TPU v7x, 32 devices: a whole 2x2x4 slice. The times are simulated.
32 devices in a mesh: blk: 16 (over z, x, core), fsdp: 2 (over y).
Axes of the slice: x: 2, y: 2, z: 4, core: 2. Of those that a mesh axis runs over, the one named last changes fastest.
Arguments:
- tokens: bfloat16 [32, 2048, 768], P('blk', 'fsdp'), may hold values from -6 to 6
- cotangent: bfloat16 [32, 2048, 768], P('blk', 'fsdp'), may hold values from -6 to 6
- segments: int32 [32, 2048], P('blk', 'fsdp'), may hold values from 0 to 7, as said below
- doc_lengths: int32 [32, 8], P('blk'), may hold values from 20 to 1026, as said below
- positions: int32 [32, 2048], P('blk', 'fsdp'), may hold values from 0 to 1025, as said below
- pairing: int32 [128], P('blk'), may hold values from 0 to 127, each once
- qkv_weight: bfloat16 [768, 2304], P('fsdp'), may hold values from -0.21875 to 0.21875
- out_weight: bfloat16 [768, 768], P('fsdp'), may hold values from -1.25 to 1.25
- swiglu_weight: bfloat16 [768, 6144], P('fsdp'), may hold values from -0.21875 to 0.21875
- down_weight: bfloat16 [3072, 768], P('fsdp'), may hold values from -0.109375 to 0.109375
- attn_gain: bfloat16 [768], P('fsdp'), may hold values from 0.5 to 1.5
- ffn_gain: bfloat16 [768], P('fsdp'), may hold values from 0.5 to 1.5
Outputs:
- loss_value: float32 [], replicated
- layer_output: bfloat16 [32, 2048, 768], P('blk', 'fsdp')
- input_grad: float32 [32, 2048, 768], P('blk', 'fsdp')
- qkv_grad: float32 [768, 2304], P('fsdp')
- out_grad: float32 [768, 768], P('fsdp')
- swiglu_grad: float32 [768, 6144], P('fsdp')
- down_grad: float32 [3072, 768], P('fsdp')
- attn_gain_grad: float32 [768], P('fsdp')
- ffn_gain_grad: float32 [768], P('fsdp')
Inputs may be any that keep to these rules, and one draw needn't show every extreme that they name: `doc_lengths`: in each row, one segment at a place drawn from the seed has exactly the most tokens; the 7 other segments, among them one of exactly 20 tokens, add up to 7 * ((1024 - 1) // 7), each 20 or more, and the row's lengths add up to 2048. `segments`: segment numbers never fall along a row, and segment s covers doc_lengths[r, s] tokens. `positions`: A token's place within its segment, counted from 0. `pairing`: each document number once.
All inputs are finite; a program needn't handle non-finite values.
Results may differ from a plain program's by a relative error of at most 0.024.
Values may be sent and summed in bfloat16 or wider, within the bound.
No kernel may reach another device: no remote copies, remote signals or barrier semaphores. Data moves between devices by JAX's collectives and lax.ppermute only.
A program may use at most 384 MiB of HBM per device.

v0:
```python
import math

import jax
import jax.numpy as jnp
from jax import lax
from jax.sharding import PartitionSpec as P

HEADS = 12
HDIM = 64


EPSILON = 1e-05
EMB_EPSILON = 1e-06
SOFTMAX_WARMTH = 0.05
ROPE_BASE = 1000.0
CONTRAST_WEIGHT = 512.0
NEGATIVE = -1e30
TOP_PRECISION = lax.Precision.HIGHEST


def from_behind(block, axis, distance):
    devices = range(lax.axis_size(axis))
    route = [((i - distance) % len(devices), i) for i in devices]
    return lax.ppermute(block, axis, route)


def rope_tables(positions):
    half_dim = HDIM // 2
    frequency = ROPE_BASE ** (-2.0 * jnp.arange(half_dim, dtype=jnp.float32) / HDIM)
    angles = positions.astype(jnp.float32)[..., None] * frequency
    return (jnp.cos(angles), jnp.sin(angles))


def rotate(heads_in, cosine, sine):
    half_dim = HDIM // 2
    first_half = heads_in[..., :half_dim]
    second_half = heads_in[..., half_dim:]
    cosine = cosine[..., None, :]
    sine = sine[..., None, :]
    return jnp.concatenate(
        [first_half * cosine - second_half * sine, second_half * cosine + first_half * sine],
        axis=-1,
    )


def unrotate(grad_in, cosine, sine):
    half_dim = HDIM // 2
    first_half = grad_in[..., :half_dim]
    second_half = grad_in[..., half_dim:]
    cosine = cosine[..., None, :]
    sine = sine[..., None, :]
    return jnp.concatenate(
        [first_half * cosine + second_half * sine, second_half * cosine - first_half * sine],
        axis=-1,
    )


def norm_forward(hidden_in, gain):
    average = jnp.mean(hidden_in, -1, keepdims=True)
    centred = hidden_in - average
    inverse = lax.rsqrt(jnp.mean(centred * centred, -1, keepdims=True) + EPSILON)
    normalized = centred * inverse
    return (normalized * gain, normalized, inverse)


def norm_backward(upstream, normalized, inverse, gain):
    scaled = upstream * gain
    inner = (
        scaled
        - jnp.mean(scaled, -1, keepdims=True)
        - normalized * jnp.mean(scaled * normalized, -1, keepdims=True)
    )
    return (inverse * inner, jnp.sum(upstream * normalized, 0))


def segment_bounds(segments, doc_lengths):
    ends = jnp.cumsum(doc_lengths, axis=1)
    starts = ends - doc_lengths
    member = segments[..., None] == jnp.arange(doc_lengths.shape[1], dtype=jnp.int32)
    first_key = jnp.sum(jnp.where(member, starts[:, None, :], 0), -1)
    last_key = jnp.sum(jnp.where(member, ends[:, None, :], 0), -1)
    return (first_key, last_key, member)


def score_block(query_heads, key_block, first_key, last_key, key_offset):
    scale = 1.0 / math.sqrt(HDIM)
    scores = (
        jnp.einsum("rqhd,rkhd->rhqk", query_heads, key_block, preferred_element_type=jnp.float32)
        * scale
    )
    key_place = key_offset + jnp.arange(key_block.shape[1], dtype=jnp.int32)
    allowed = (key_place[None, None, :] >= first_key[:, :, None]) & (
        key_place[None, None, :] < last_key[:, :, None]
    )
    allowed = allowed[:, None]
    return (jnp.where(allowed, scores, NEGATIVE), allowed)


def shards(
    tokens,
    cotangent,
    segments,
    doc_lengths,
    positions,
    pairing,
    qkv_weight,
    out_weight,
    swiglu_weight,
    down_weight,
    attn_gain,
    ffn_gain,
):
    bf16 = jnp.bfloat16
    single_document = jnp.float32
    rows_here, shard_len, model_width = tokens.shape
    tok_count = rows_here * shard_len
    scale = 1.0 / math.sqrt(HDIM)
    full_weights = (
        lax.all_gather(qkv_weight, "fsdp", axis=0, tiled=True),
        lax.all_gather(out_weight, "fsdp", axis=0, tiled=True),
        lax.all_gather(swiglu_weight, "fsdp", axis=0, tiled=True),
        lax.all_gather(down_weight, "fsdp", axis=0, tiled=True),
        lax.all_gather(attn_gain, "fsdp", axis=0, tiled=True),
        lax.all_gather(ffn_gain, "fsdp", axis=0, tiled=True),
    )
    qkv_full, out_full, swiglu_full, down_full, attn_gain_full, ffn_gain_full = full_weights
    flat_tokens = tokens.reshape(tok_count, model_width)
    projected = jnp.dot(flat_tokens, qkv_full, preferred_element_type=single_document)
    cosine, sine = rope_tables(positions)
    query_heads = projected[:, :model_width].reshape(rows_here, shard_len, HEADS, HDIM)
    key_heads = projected[:, model_width : 2 * model_width].reshape(
        rows_here, shard_len, HEADS, HDIM
    )
    value_heads = projected[:, 2 * model_width :].reshape(rows_here, shard_len, HEADS, HDIM)
    query_low = rotate(query_heads, cosine, sine).astype(bf16)
    key_low = (
        rotate(key_heads, cosine, sine).astype(bf16).reshape(rows_here, shard_len, model_width)
    )
    value_low = value_heads.astype(bf16).reshape(rows_here, shard_len, model_width)
    first_key, last_key, member = segment_bounds(segments, doc_lengths)
    start_state = (
        jnp.full((rows_here, HEADS, shard_len), NEGATIVE, single_document),
        jnp.zeros((rows_here, HEADS, shard_len), single_document),
        jnp.zeros((rows_here, shard_len, HEADS, HDIM), single_document),
    )
    key_piece = lax.all_gather(key_low, "fsdp", axis=1, tiled=True)
    value_piece = lax.all_gather(value_low, "fsdp", axis=1, tiled=True)
    piece_rows = key_piece.shape[1]
    fold_span_rows = math.gcd(piece_rows, 512)

    def one_span(turn_index, state):
        run_max, run_sum, accum = state
        offset = turn_index * fold_span_rows
        key_block = lax.dynamic_slice_in_dim(key_piece, offset, fold_span_rows, 1).reshape(
            rows_here, fold_span_rows, HEADS, HDIM
        )
        value_block = lax.dynamic_slice_in_dim(value_piece, offset, fold_span_rows, 1).reshape(
            rows_here, fold_span_rows, HEADS, HDIM
        )
        scores, allowed = score_block(query_low, key_block, first_key, last_key, offset)
        new_max = jnp.maximum(run_max, jnp.max(scores, -1))
        factor = jnp.exp(run_max - new_max)
        weights_soft = jnp.where(allowed, jnp.exp(scores - new_max[..., None]), 0.0)
        run_sum = run_sum * factor + jnp.sum(weights_soft, -1)
        accum = accum * jnp.transpose(factor, (0, 2, 1))[..., None] + jnp.einsum(
            "rhqk,rkhd->rqhd",
            weights_soft.astype(bf16),
            value_block,
            preferred_element_type=single_document,
        )
        return (new_max, run_sum, accum)

    run_max, run_sum, accum = lax.fori_loop(0, piece_rows // fold_span_rows, one_span, start_state)
    log_norm = run_max + jnp.log(run_sum)
    attended = (
        (accum / jnp.transpose(run_sum, (0, 2, 1))[..., None])
        .astype(bf16)
        .reshape(tok_count, model_width)
    )
    branch = jnp.dot(attended, out_full, preferred_element_type=single_document)
    residual_in = flat_tokens.astype(single_document)
    normed, normed_unit, normed_inv = norm_forward(
        residual_in + branch, attn_gain_full.astype(single_document)
    )
    normed_low = normed.astype(bf16)
    gate_up = jnp.dot(normed_low, swiglu_full, preferred_element_type=single_document)
    ff_width = gate_up.shape[1] // 2
    hidden_low = (jax.nn.silu(gate_up[:, :ff_width]) * gate_up[:, ff_width:]).astype(bf16)
    ffn_out = jnp.dot(hidden_low, down_full, preferred_element_type=single_document)
    output, output_unit, output_inv = norm_forward(
        normed + ffn_out, ffn_gain_full.astype(single_document)
    )
    member_f = member.astype(single_document)
    partial_sums = jnp.einsum(
        "rts,rtd->rsd",
        member_f,
        output.reshape(rows_here, shard_len, model_width),
        precision=TOP_PRECISION,
    )
    pooled_total = lax.psum(partial_sums.astype(jnp.bfloat16), "fsdp").astype(jnp.float32)
    lengths_f = doc_lengths.astype(single_document)[..., None]
    pooled = pooled_total / lengths_f
    inverse_norm = lax.rsqrt(jnp.sum(pooled * pooled, -1, keepdims=True) + EMB_EPSILON)
    embedded = pooled * inverse_norm
    embedded_low = embedded.astype(bf16)
    half_segs = doc_lengths.shape[1] // 2
    per_block = rows_here * half_segs
    query_vectors = embedded_low[:, 0::2].reshape(per_block, model_width)
    document_rows = embedded_low[:, 1::2].reshape(per_block, model_width)
    devices = lax.axis_size("blk")
    own_index = lax.axis_index("blk")
    local_ids = jnp.arange(per_block, dtype=jnp.int32)

    def similarity(document_block, source):
        similarity_matrix = (
            jnp.einsum(
                "lx,gx->lg", query_vectors, document_block, preferred_element_type=single_document
            )
            / SOFTMAX_WARMTH
        )
        target = pairing[:, None] == (source * per_block + local_ids)[None, :]
        return (similarity_matrix, target)

    similarity_matrix, target = similarity(document_rows, own_index)
    first_max = jnp.max(similarity_matrix, -1)
    first_sum = jnp.sum(jnp.exp(similarity_matrix - first_max[:, None]), -1)
    first_pos = jnp.sum(jnp.where(target, similarity_matrix, 0.0), -1)

    def visit(turn_index, state):
        document_block, best, total, positive = state
        document_block = from_behind(document_block, "blk", 1)
        source = (own_index - turn_index) % devices
        similarity_matrix, target = similarity(document_block, source)
        new_best = jnp.maximum(best, jnp.max(similarity_matrix, -1))
        total = total * jnp.exp(best - new_best) + jnp.sum(
            jnp.exp(similarity_matrix - new_best[:, None]), -1
        )
        positive = positive + jnp.sum(jnp.where(target, similarity_matrix, 0.0), -1)
        return (document_block, new_best, total, positive)

    visited = lax.fori_loop(1, devices, visit, (document_rows, first_max, first_sum, first_pos))
    log_total = visited[1] + jnp.log(visited[2])
    positive = visited[3]
    local_loss = jnp.sum(log_total - positive)

    def revisit(turn_index, state):
        doc_float, doc_grad, query_gradient = state
        source = (own_index - turn_index) % devices
        document_block = doc_float.astype(bf16)
        similarity_matrix, target = similarity(document_block, source)
        similarity_grad = (
            CONTRAST_WEIGHT
            * (jnp.exp(similarity_matrix - log_total[:, None]) - target.astype(single_document))
        ).astype(bf16)
        query_gradient = (
            query_gradient
            + jnp.dot(similarity_grad, document_block, preferred_element_type=single_document)
            / SOFTMAX_WARMTH
        )
        doc_grad = (
            doc_grad
            + jnp.einsum(
                "bv,bs->vs", similarity_grad, query_vectors, preferred_element_type=single_document
            )
            / SOFTMAX_WARMTH
        )
        moved = (
            from_behind(doc_float.astype(jnp.bfloat16), "blk", 1).astype(doc_float.dtype),
            from_behind(doc_grad.astype(jnp.bfloat16), "blk", 1).astype(doc_grad.dtype),
        )
        return (moved[0], moved[1], query_gradient)

    zero_grad = jnp.zeros((per_block, model_width), single_document)
    revisited = lax.fori_loop(
        0, devices, revisit, (document_rows.astype(single_document), zero_grad, zero_grad)
    )
    doc_grad = revisited[1]
    query_gradient = revisited[2]
    emb_grad = jnp.stack(
        [
            query_gradient.reshape(rows_here, half_segs, model_width),
            doc_grad.reshape(rows_here, half_segs, model_width),
        ],
        axis=2,
    ).reshape(rows_here, 2 * half_segs, model_width)
    along = jnp.sum(embedded * emb_grad, -1, keepdims=True)
    pooled_grad = inverse_norm * (emb_grad - embedded * along) / lengths_f
    spread_grad = jnp.einsum(
        "rts,rsd->rtd", member_f, pooled_grad, precision=TOP_PRECISION
    ).reshape(tok_count, model_width)
    output_grad = cotangent.reshape(tok_count, model_width).astype(single_document) + spread_grad
    back_weights = (
        lax.all_gather(qkv_weight, "fsdp", axis=0, tiled=True),
        lax.all_gather(out_weight, "fsdp", axis=0, tiled=True),
        lax.all_gather(swiglu_weight, "fsdp", axis=0, tiled=True),
        lax.all_gather(down_weight, "fsdp", axis=0, tiled=True),
        lax.all_gather(attn_gain, "fsdp", axis=0, tiled=True),
        lax.all_gather(ffn_gain, "fsdp", axis=0, tiled=True),
    )
    qkv_full, out_full, swiglu_full, down_full, attn_gain_full, ffn_gain_full = back_weights
    second_grad, ffn_gain_part = norm_backward(
        output_grad, output_unit, output_inv, ffn_gain_full.astype(single_document)
    )
    ffn_grad_low = second_grad.astype(bf16)
    down_part = jnp.einsum(
        "tf,td->fd", hidden_low, ffn_grad_low, preferred_element_type=single_document
    )
    hidden_grad = jnp.einsum(
        "td,fd->tf", ffn_grad_low, down_full, preferred_element_type=single_document
    )
    gate_again = jnp.dot(normed_low, swiglu_full, preferred_element_type=single_document)
    gate_value = gate_again[:, :ff_width]
    up_value = gate_again[:, ff_width:]
    sigmoid_gate = jax.nn.sigmoid(gate_value)
    gate_grad = hidden_grad * up_value * sigmoid_gate * (1.0 + gate_value * (1.0 - sigmoid_gate))
    up_grad = hidden_grad * gate_value * sigmoid_gate
    gate_up_grad = jnp.concatenate([gate_grad, up_grad], axis=-1).astype(bf16)
    swiglu_part = jnp.einsum(
        "td,te->de", normed_low, gate_up_grad, preferred_element_type=single_document
    )
    normed_grad = second_grad + jnp.einsum(
        "te,de->td", gate_up_grad, swiglu_full, preferred_element_type=single_document
    )
    first_grad, attn_gain_part = norm_backward(
        normed_grad, normed_unit, normed_inv, attn_gain_full.astype(single_document)
    )
    branch_grad_low = first_grad.astype(bf16)
    out_part = jnp.einsum(
        "td,te->de", attended, branch_grad_low, preferred_element_type=single_document
    )
    attended_grad = jnp.einsum(
        "te,de->td", branch_grad_low, out_full, preferred_element_type=single_document
    ).astype(bf16)
    attended_heads = attended_grad.reshape(rows_here, shard_len, HEADS, HDIM)
    delta_rows = jnp.sum(
        attended_grad.astype(single_document).reshape(rows_here, shard_len, HEADS, HDIM)
        * attended.astype(single_document).reshape(rows_here, shard_len, HEADS, HDIM),
        -1,
    )
    delta_rows = jnp.transpose(delta_rows, (0, 2, 1))
    gathered_back = (
        lax.all_gather(key_low, "fsdp", axis=1, tiled=True),
        lax.all_gather(value_low, "fsdp", axis=1, tiled=True),
    )
    key_all, value_all = gathered_back
    row_len = key_all.shape[1]
    span_rows = math.gcd(row_len, 512)
    zero_heads = jnp.zeros((rows_here, shard_len, HEADS, HDIM), single_document)

    def span_terms(offset):
        key_block = lax.dynamic_slice_in_dim(key_all, offset, span_rows, 1).reshape(
            rows_here, span_rows, HEADS, HDIM
        )
        value_block = lax.dynamic_slice_in_dim(value_all, offset, span_rows, 1).reshape(
            rows_here, span_rows, HEADS, HDIM
        )
        scores, allowed = score_block(query_low, key_block, first_key, last_key, offset)
        soft = jnp.where(allowed, jnp.exp(scores - log_norm[..., None]), 0.0)
        soft_grad = jnp.einsum(
            "rqhd,rkhd->rhqk", attended_heads, value_block, preferred_element_type=single_document
        )
        score_grad = (soft * (soft_grad - delta_rows[..., None])).astype(bf16)
        query_part = (
            jnp.einsum(
                "rhqk,rkhd->rqhd", score_grad, key_block, preferred_element_type=single_document
            )
            * scale
        )
        return (soft, score_grad, query_part)

    def back_span(query_acc, turn_index):
        soft, score_grad, query_part = span_terms(turn_index * span_rows)
        key_grad_block = (
            jnp.einsum(
                "rhqk,rqhd->rkhd", score_grad, query_low, preferred_element_type=single_document
            )
            * scale
        )
        value_grad_block = jnp.einsum(
            "rhqk,rqhd->rkhd",
            soft.astype(bf16),
            attended_heads,
            preferred_element_type=single_document,
        )
        return (query_acc + query_part, (key_grad_block, value_grad_block))

    query_grad_heads, span_grads = lax.scan(back_span, zero_heads, jnp.arange(row_len // span_rows))
    key_grad_all = jnp.moveaxis(span_grads[0], 0, 1).reshape(rows_here, row_len, model_width)
    value_grad_all = jnp.moveaxis(span_grads[1], 0, 1).reshape(rows_here, row_len, model_width)
    owned_grads = (
        lax.psum_scatter(
            key_grad_all.astype(jnp.bfloat16), "fsdp", scatter_dimension=1, tiled=True
        ).astype(jnp.float32),
        lax.psum_scatter(
            value_grad_all.astype(jnp.bfloat16), "fsdp", scatter_dimension=1, tiled=True
        ).astype(jnp.float32),
    )
    key_grad_heads = owned_grads[0].reshape(rows_here, shard_len, HEADS, HDIM)
    value_grad_flat = owned_grads[1].reshape(tok_count, model_width)
    query_back = unrotate(query_grad_heads, cosine, sine).reshape(tok_count, model_width)
    key_back = unrotate(key_grad_heads, cosine, sine).reshape(tok_count, model_width)
    projected_grad = jnp.concatenate([query_back, key_back, value_grad_flat], axis=-1).astype(bf16)
    qkv_part = jnp.einsum(
        "td,te->de", flat_tokens, projected_grad, preferred_element_type=single_document
    )
    input_grad = first_grad + jnp.einsum(
        "te,de->td", projected_grad, qkv_full, preferred_element_type=single_document
    )
    shares = (
        lax.psum_scatter(
            qkv_part.astype(jnp.bfloat16), "fsdp", scatter_dimension=0, tiled=True
        ).astype(jnp.float32),
        lax.psum_scatter(
            out_part.astype(jnp.bfloat16), "fsdp", scatter_dimension=0, tiled=True
        ).astype(jnp.float32),
        lax.psum_scatter(
            swiglu_part.astype(jnp.bfloat16), "fsdp", scatter_dimension=0, tiled=True
        ).astype(jnp.float32),
        lax.psum_scatter(
            down_part.astype(jnp.bfloat16), "fsdp", scatter_dimension=0, tiled=True
        ).astype(jnp.float32),
        lax.psum_scatter(
            attn_gain_part.astype(jnp.bfloat16), "fsdp", scatter_dimension=0, tiled=True
        ).astype(jnp.float32),
        lax.psum_scatter(
            ffn_gain_part.astype(jnp.bfloat16), "fsdp", scatter_dimension=0, tiled=True
        ).astype(jnp.float32),
    )
    totals = (
        lax.psum(shares[0].astype(jnp.bfloat16), "blk").astype(jnp.float32),
        lax.psum(shares[1].astype(jnp.bfloat16), "blk").astype(jnp.float32),
        lax.psum(shares[2].astype(jnp.bfloat16), "blk").astype(jnp.float32),
        lax.psum(shares[3].astype(jnp.bfloat16), "blk").astype(jnp.float32),
        lax.psum(shares[4].astype(jnp.bfloat16), "blk").astype(jnp.float32),
        lax.psum(shares[5].astype(jnp.bfloat16), "blk").astype(jnp.float32),
        lax.psum(local_loss.astype(jnp.bfloat16), "blk").astype(jnp.float32),
    )
    loss_value = totals[6] / (per_block * devices)
    layer_output = output.astype(bf16).reshape(rows_here, shard_len, model_width)
    return (
        loss_value,
        layer_output,
        input_grad.reshape(rows_here, shard_len, model_width),
        totals[0],
        totals[1],
        totals[2],
        totals[3],
        totals[4],
        totals[5],
    )


def solution(mesh):
    in_specs = (
        P("blk", "fsdp", None),
        P("blk", "fsdp", None),
        P("blk", "fsdp"),
        P("blk", None),
        P("blk", "fsdp"),
        P("blk"),
        P("fsdp", None),
        P("fsdp", None),
        P("fsdp", None),
        P("fsdp", None),
        P("fsdp"),
        P("fsdp"),
    )
    out_specs = (
        P(),
        P("blk", "fsdp", None),
        P("blk", "fsdp", None),
        P("fsdp", None),
        P("fsdp", None),
        P("fsdp", None),
        P("fsdp", None),
        P("fsdp"),
        P("fsdp"),
    )
    return jax.shard_map(shards, mesh=mesh, in_specs=in_specs, out_specs=out_specs, check_vma=False)
```

profile of v0, /device:TPU:0, one launch (start us, length us, event | category | flops | bytes accessed | tf_op | source)
XLA Modules:
  0.0 2108.1 jit_solution(14323608477122718204)
XLA Ops:
  12.7 49.0 %all-gather.9.cloned.1.call-done = bf16[768,2304]{1,0:T(8,128)(2,1)} async-done(((bf16[384,2304]{1,0:T(8,128)(2,1)}), bf16[768,2304]{1,0:T(8,128)(2,1)}) %all-gather.9.cloned.1.call-update) | async-done | bytes 3538960 | tf_op jit(solution)/shard_map/all_gather | solution.py:119
  158.5 56.3 %all-gather.11.cloned.1.call-done = bf16[2,2048,768]{1,2,0:T(8,128)(2,1)} async-done(((bf16[2,1024,768]{1,2,0:T(8,128)(2,1)}), bf16[2,2048,768]{1,2,0:T(8,128)(2,1)}) %all-gather.11.cloned.1.call-update) | async-done | bytes 6291472 | tf_op jit(solution)/shard_map/all_gather | solution.py:146
  214.8 82.5 %all-gather.13.cloned.1.call-done = bf16[2,2048,768]{1,2,0:T(8,128)(2,1)} async-done(((bf16[2,1024,768]{1,2,0:T(8,128)(2,1)}), bf16[2,2048,768]{1,2,0:T(8,128)(2,1)}) %all-gather.13.cloned.1.call-update) | async-done | bytes 6291472 | tf_op jit(solution)/shard_map/all_gather | solution.py:147
  297.3 293.7 %while.76 = (s32[]{:T(128)}, f32[2,12,1024]{2,1,0:T(8,128)S(1)}, f32[2,12,1024]{2,1,0:T(8,128)S(1)}, f32[2,1024,12,64]{1,3,2,0:T(8,128)}, s32[2,1024]{1,0:T(2,12...) while((s32[]{:T(128)}, f32[2,12,1024]{2,1,0:T(8,128)S(1)}, ...), condition=%wide.region_6.7_spmd.clone, body=%wide.region_3.6_spmd.clone.sunk | while | flops 3392815616 | bytes 186142928 | solution.py:173
  303.1 21.4 %fusion.157 = (f32[2,12,1024]{2,1,0:T(8,128)S(1)}, f32[2,12,512,1024]{3,2,1,0:T(8,128)}) fusion(pred[2,1024,512]{1,2,0:T(8,128)(4,1)} %compare_and_fusion.4, bf16[2,512,12,64]{1,3,2,0:T(8,128)(2,1)} %bitcast.225, bf16[2,1024,12,64]{1,3,2,0:T(8,128)(2,1)S(1)} %get-tuple-element.1323), kind=kOutput, calls=%fused_computation.9.clone.1 | convolution fusion | flops 1648336896 | bytes 56197120 | tf_op jit(solution)/shard_map/while/body/eval_jaxpr/rqhd,rkhd->rhqk/dot_general | solution.py:88
  324.6 26.2 %bitcast_add_fusion.4 = f32[2,1024,12,64]{1,3,2,0:T(8,128)} fusion(f32[2,1024,12,64]{1,3,2,0:T(8,128)} %get-tuple-element.1306, f32[2,1024,12]{1,2,0:T(8,128)S(1)} %get-tuple-element.1265, pred[]{:T(512)S(6)} %compare.11, bf16[2,512,12,64]{1,3,2,0:T(8,128)(2,1)} %bitcast.228, f32[2,12,512,1024]{3,2,1,0:T(8,128)} %get-tuple-element.1264, ...), kind=kOutput, calls=%fused_computation.14.clone.1 | convolution fusion | flops 1678245888 | bytes 65732608 | tf_op jit(solution)/shard_map/while/body/eval_jaxpr/rhqk,rkhd->rqhd/dot_general | solution.py:165
  350.8 21.7 %fusion.159 = f32[2,12,1024]{2,1,0:T(8,128)S(1)} fusion(f32[2,12,512,1024]{3,2,1,0:T(8,128)} %get-tuple-element.1264, f32[2,12,1024]{2,1,0:T(8,128)S(1)} %get-tuple-element.1317, pred[2,1024,512]{1,2,0:T(8,128)(4,1)S(1)} %copy-done.2), kind=kLoop, calls=%fused_computation.11.clone.1 | loop fusion | flops 62889984 | bytes 51576832 | tf_op jit(solution)/shard_map/while/body/eval_jaxpr/reduce_sum | solution.py:164
  399.7 23.8 %bitcast_add_fusion.4 = f32[2,1024,12,64]{1,3,2,0:T(8,128)} fusion(f32[2,1024,12,64]{1,3,2,0:T(8,128)} %get-tuple-element.1306, f32[2,1024,12]{1,2,0:T(8,128)S(1)} %get-tuple-element.1265, pred[]{:T(512)S(6)} %compare.11, bf16[2,512,12,64]{1,3,2,0:T(8,128)(2,1)} %bitcast.228, f32[2,12,512,1024]{3,2,1,0:T(8,128)} %get-tuple-element.1264, ...), kind=kOutput, calls=%fused_computation.14.clone.1 | convolution fusion | flops 1678245888 | bytes 65732608 | tf_op jit(solution)/shard_map/while/body/eval_jaxpr/rhqk,rkhd->rqhd/dot_general | solution.py:165
  423.5 21.7 %fusion.159 = f32[2,12,1024]{2,1,0:T(8,128)S(1)} fusion(f32[2,12,512,1024]{3,2,1,0:T(8,128)} %get-tuple-element.1264, f32[2,12,1024]{2,1,0:T(8,128)S(1)} %get-tuple-element.1317, pred[2,1024,512]{1,2,0:T(8,128)(4,1)S(1)} %copy-done.2), kind=kLoop, calls=%fused_computation.11.clone.1 | loop fusion | flops 62889984 | bytes 51576832 | tf_op jit(solution)/shard_map/while/body/eval_jaxpr/reduce_sum | solution.py:164
  450.9 21.6 %fusion.157 = (f32[2,12,1024]{2,1,0:T(8,128)S(1)}, f32[2,12,512,1024]{3,2,1,0:T(8,128)}) fusion(pred[2,1024,512]{1,2,0:T(8,128)(4,1)} %compare_and_fusion.4, bf16[2,512,12,64]{1,3,2,0:T(8,128)(2,1)} %bitcast.225, bf16[2,1024,12,64]{1,3,2,0:T(8,128)(2,1)S(1)} %get-tuple-element.1323), kind=kOutput, calls=%fused_computation.9.clone.1 | convolution fusion | flops 1648336896 | bytes 56197120 | tf_op jit(solution)/shard_map/while/body/eval_jaxpr/rqhd,rkhd->rhqk/dot_general | solution.py:88
  472.6 23.8 %bitcast_add_fusion.4 = f32[2,1024,12,64]{1,3,2,0:T(8,128)} fusion(f32[2,1024,12,64]{1,3,2,0:T(8,128)} %get-tuple-element.1306, f32[2,1024,12]{1,2,0:T(8,128)S(1)} %get-tuple-element.1265, pred[]{:T(512)S(6)} %compare.11, bf16[2,512,12,64]{1,3,2,0:T(8,128)(2,1)} %bitcast.228, f32[2,12,512,1024]{3,2,1,0:T(8,128)} %get-tuple-element.1264, ...), kind=kOutput, calls=%fused_computation.14.clone.1 | convolution fusion | flops 1678245888 | bytes 65732608 | tf_op jit(solution)/shard_map/while/body/eval_jaxpr/rhqk,rkhd->rqhd/dot_general | solution.py:165
  496.4 21.7 %fusion.159 = f32[2,12,1024]{2,1,0:T(8,128)S(1)} fusion(f32[2,12,512,1024]{3,2,1,0:T(8,128)} %get-tuple-element.1264, f32[2,12,1024]{2,1,0:T(8,128)S(1)} %get-tuple-element.1317, pred[2,1024,512]{1,2,0:T(8,128)(4,1)S(1)} %copy-done.2), kind=kLoop, calls=%fused_computation.11.clone.1 | loop fusion | flops 62889984 | bytes 51576832 | tf_op jit(solution)/shard_map/while/body/eval_jaxpr/reduce_sum | solution.py:164
  545.3 23.8 %bitcast_add_fusion.4 = f32[2,1024,12,64]{1,3,2,0:T(8,128)} fusion(f32[2,1024,12,64]{1,3,2,0:T(8,128)} %get-tuple-element.1306, f32[2,1024,12]{1,2,0:T(8,128)S(1)} %get-tuple-element.1265, pred[]{:T(512)S(6)} %compare.11, bf16[2,512,12,64]{1,3,2,0:T(8,128)(2,1)} %bitcast.228, f32[2,12,512,1024]{3,2,1,0:T(8,128)} %get-tuple-element.1264, ...), kind=kOutput, calls=%fused_computation.14.clone.1 | convolution fusion | flops 1678245888 | bytes 65732608 | tf_op jit(solution)/shard_map/while/body/eval_jaxpr/rhqk,rkhd->rqhd/dot_general | solution.py:165
  569.1 21.7 %fusion.159 = f32[2,12,1024]{2,1,0:T(8,128)S(1)} fusion(f32[2,12,512,1024]{3,2,1,0:T(8,128)} %get-tuple-element.1264, f32[2,12,1024]{2,1,0:T(8,128)S(1)} %get-tuple-element.1317, pred[2,1024,512]{1,2,0:T(8,128)(4,1)S(1)} %copy-done.2), kind=kLoop, calls=%fused_computation.11.clone.1 | loop fusion | flops 62889984 | bytes 51576832 | tf_op jit(solution)/shard_map/while/body/eval_jaxpr/reduce_sum | solution.py:164
  612.5 30.9 %fusion.67 = f32[2048,6144]{1,0:T(8,128)} fusion(bf16[768,6144]{1,0:T(8,128)(2,1)} %all-gather.17.cloned.1.call-done, f32[2048,768]{1,0:T(8,128)} %copy-done.6, f32[768]{0:T(1024)S(1)} %copy-done.40, f32[2048]{0:T(1024)S(1)} %add_rsqrt_fusion.1, f32[2048]{0:T(1024)S(1)} %broadcast_multiply_fusion.4), kind=kOutput, calls=%fused_computation.163 | convolution fusion | flops 19333644288 | bytes 66079744 | tf_op jit(solution)/shard_map/dot_general | solution.py:186
  643.4 21.6 %multiply_convert_fusion.2 = bf16[2048,3072]{1,0:T(8,128)(2,1)} fusion(f32[2048,6144]{1,0:T(8,128)} %fusion.67), kind=kLoop, calls=%fused_computation.63 | loop fusion | flops 37748736 | bytes 62914560 | tf_op jit(solution)/shard_map/convert_element_type | solution.py:188
  695.0 92.2 %while.75 = (s32[]{:T(128)}, bf16[8,768]{1,0:T(8,128)(2,1)S(1)}, f32[8]{0:T(128)S(1)}, f32[8]{0:T(128)S(1)}, f32[8]{0:T(128)S(1)}, /*index=5*/bf16[8,768]{1,0:T(...) while((s32[]{:T(128)}, bf16[8,768]{1,0:T(8,128)(2,1)S(1)}, ...), condition=%wide.region_20.21_spmd.clone, body=%wide.region_16.20_spmd.clone.sunk | while | flops 98791 | bytes 99758 | solution.py:241
  787.8 100.1 %while.77 = (s32[]{:T(128)}, bf16[8,768]{1,0:T(8,128)(2,1)S(1)}, f32[8,768]{1,0:T(8,128)S(1)}, f32[8,768]{1,0:T(8,128)S(1)}, bf16[8,768]{1,0:T(8,128)(2,1)S(1)},...) while((s32[]{:T(128)}, bf16[8,768]{1,0:T(8,128)(2,1)S(1)}, ...), condition=%wide.region_24.25_spmd.clone, body=%wide.region_23.24_spmd.clone.sunk | while | flops 344536 | bytes 295777 | solution.py:274
  901.1 34.2 %multiply_convert_fusion.1 = (bf16[2048,3072]{1,0:T(8,128)(2,1)}, bf16[2048,3072]{1,0:T(8,128)(2,1)}) fusion(f32[2048,6144]{1,0:T(8,128)} %fusion.67, bf16[3072,768]{1,0:T(8,128)(2,1)} %all-gather.19.cloned.1.call-done, f32[2048,768]{1,0:T(8,128)} %subtract_multiply_fusion.1), kind=kOutput, calls=%fused_computation.62 | convolution fusion | flops 9747038208 | bytes 86507520 | tf_op jit(solution)/shard_map/td,fd->tf/dot_general | solution.py:308
  935.3 35.5 %multiply_reduce_fusion = (bf16[768]{0:T(1024)(128)(2,1)}, f32[2048]{0:T(1024)S(1)}, f32[2048]{0:T(1024)S(1)}, f32[2048,768]{1,0:T(8,128)}) fusion(f32[2048,768]{1,0:T(8,128)} %copy-done.6, f32[2048]{0:T(1024)S(1)} %add_rsqrt_fusion.1, f32[2048]{0:T(1024)S(1)} %broadcast_multiply_fusion.4, f32[768]{0:T(1024)S(1)} %copy-done.40, ...), kind=kOutput, calls=%fused_computation.73 | convolution fusion | flops 19391836160 | bytes 53514752 | tf_op jit(solution)/shard_map/te,de->td/dot_general | solution.py:321
  1008.8 441.8 %while.78 = (s32[]{:T(128)}, f32[2,1024,12,64]{1,3,2,0:T(8,128)}, bf16[4,2,512,12,64]{2,4,3,1,0:T(8,128)(2,1)}, bf16[4,2,512,12,64]{2,4,3,1,0:T(8,128)(2,1)}, s3...) while((s32[]{:T(128)}, f32[2,1024,12,64]{1,3,2,0:T(8,128)}, ...), condition=%wide.region_32.33_spmd.clone, body=%wide.region_31.32_spmd.clone.sunk | while | flops 8212709888 | bytes 289199392 | solution.py:387
  1036.6 30.5 %fusion.181 = bf16[2,12,1024,512]{2,3,1,0:T(8,128)(2,1)} fusion(f32[2,12,512,1024]{3,2,1,0:T(8,128)} %fusion.180, f32[2,12,1024]{2,1,0:T(8,128)S(1)} %get-tuple-element.1453, f32[2,12,1024]{2,1,0:T(8,128)S(1)} %get-tuple-element.1450, pred[2,1024,512]{1,2,0:T(8,128)(4,1)} %compare_and_fusion.5, bf16[2,512,12,64]{1,3,2,0:T(8,128)(2,1)} %bitcast.229, ...), kind=kOutput, calls=%fused_computation.41.clone.1 | convolution fusion | flops 1698693120 | bytes 81461248 | tf_op jit(solution)/shard_map/while/body/eval_jaxpr/rqhd,rkhd->rhqk/dot_general | solution.py:359
  1145.5 30.5 %fusion.181 = bf16[2,12,1024,512]{2,3,1,0:T(8,128)(2,1)} fusion(f32[2,12,512,1024]{3,2,1,0:T(8,128)} %fusion.180, f32[2,12,1024]{2,1,0:T(8,128)S(1)} %get-tuple-element.1453, f32[2,12,1024]{2,1,0:T(8,128)S(1)} %get-tuple-element.1450, pred[2,1024,512]{1,2,0:T(8,128)(4,1)} %compare_and_fusion.5, bf16[2,512,12,64]{1,3,2,0:T(8,128)(2,1)} %bitcast.229, ...), kind=kOutput, calls=%fused_computation.41.clone.1 | convolution fusion | flops 1698693120 | bytes 81461248 | tf_op jit(solution)/shard_map/while/body/eval_jaxpr/rqhd,rkhd->rhqk/dot_general | solution.py:359
  1256.3 30.5 %fusion.181 = bf16[2,12,1024,512]{2,3,1,0:T(8,128)(2,1)} fusion(f32[2,12,512,1024]{3,2,1,0:T(8,128)} %fusion.180, f32[2,12,1024]{2,1,0:T(8,128)S(1)} %get-tuple-element.1453, f32[2,12,1024]{2,1,0:T(8,128)S(1)} %get-tuple-element.1450, pred[2,1024,512]{1,2,0:T(8,128)(4,1)} %compare_and_fusion.5, bf16[2,512,12,64]{1,3,2,0:T(8,128)(2,1)} %bitcast.229, ...), kind=kOutput, calls=%fused_computation.41.clone.1 | convolution fusion | flops 1698693120 | bytes 81461248 | tf_op jit(solution)/shard_map/while/body/eval_jaxpr/rqhd,rkhd->rhqk/dot_general | solution.py:359
  1367.0 30.5 %fusion.181 = bf16[2,12,1024,512]{2,3,1,0:T(8,128)(2,1)} fusion(f32[2,12,512,1024]{3,2,1,0:T(8,128)} %fusion.180, f32[2,12,1024]{2,1,0:T(8,128)S(1)} %get-tuple-element.1453, f32[2,12,1024]{2,1,0:T(8,128)S(1)} %get-tuple-element.1450, pred[2,1024,512]{1,2,0:T(8,128)(4,1)} %compare_and_fusion.5, bf16[2,512,12,64]{1,3,2,0:T(8,128)(2,1)} %bitcast.229, ...), kind=kOutput, calls=%fused_computation.41.clone.1 | convolution fusion | flops 1698693120 | bytes 81461248 | tf_op jit(solution)/shard_map/while/body/eval_jaxpr/rqhd,rkhd->rhqk/dot_general | solution.py:359
  1506.2 40.6 %reduce-scatter.9.cloned.1.call-done = bf16[2,1024,768]{1,2,0:T(8,128)(2,1)} async-done(((bf16[2,2048,768]{1,2,0:T(8,128)(2,1)}), bf16[2,1024,768]{1,2,0:T(8,128)(2,1)}) %reduce-scatter.9.cloned.1.call-update) | async-done | bytes 3145744 | tf_op jit(solution)/shard_map/reduce_scatter | solution.py:391
  1575.6 50.7 %reduce-scatter.11.cloned.1.call-done = bf16[2,1024,768]{1,2,0:T(8,128)(2,1)} async-done(((bf16[2,2048,768]{1,2,0:T(8,128)(2,1)}), bf16[2,1024,768]{1,2,0:T(8,128)(2,1)}) %reduce-scatter.11.cloned.1.call-update) | async-done | bytes 3145744 | tf_op jit(solution)/shard_map/reduce_scatter | solution.py:394
  1671.1 29.6 %fusion.41 = bf16[768,6144]{1,0:T(8,128)(2,1)} fusion(bf16[2048,3072]{1,0:T(8,128)(2,1)} %get-tuple-element.1004, bf16[2048,3072]{1,0:T(8,128)(2,1)} %get-tuple-element.1003, f32[2048,768]{1,0:T(8,128)} %copy-done.6, f32[768]{0:T(1024)S(1)} %copy-done.41, f32[2048]{0:T(1024)S(1)} %copy-done.38, f32[2048]{0:T(1024)S(1)} %copy-done.36), kind=kOutput, calls=%fused_computation.67 | convolution fusion | flops 19388694528 | bytes 40913920 | tf_op jit(solution)/shard_map/td,te->de/dot_general | solution.py:318
  1719.4 62.9 %reduce-scatter.17.cloned.1.call-done = bf16[1536,768]{1,0:T(8,128)(2,1)} async-done(((bf16[3072,768]{1,0:T(8,128)(2,1)}), bf16[1536,768]{1,0:T(8,128)(2,1)}) %reduce-scatter.17.cloned.1.call-update) | async-done | bytes 2359312 | tf_op jit(solution)/shard_map/reduce_scatter | solution.py:419
  1782.2 112.9 %reduce-scatter.15.cloned.1.call-done = bf16[384,6144]{1,0:T(8,128)(2,1)} async-done(((bf16[768,6144]{1,0:T(8,128)(2,1)}), bf16[384,6144]{1,0:T(8,128)(2,1)}) %reduce-scatter.15.cloned.1.call-update) | async-done | bytes 4718608 | tf_op jit(solution)/shard_map/reduce_scatter | solution.py:416
  1901.5 34.3 %all-reduce.2 = (bf16[]{:T(256)}, bf16[384]{0:T(512)(128)(2,1)S(1)}, bf16[384]{0:T(512)(128)(2,1)S(1)}) all-reduce(bf16[]{:T(256)} %get-tuple-element.993, bf16[384]{0:T(512)(128)(2,1)S(1)} %dynamic-slice.1, bf16[384]{0:T(512)(128)(2,1)S(1)} %dynamic-slice.3), channel_id=1, replica_groups=mesh['blk'=16,'fsdp'=2] {'blk'}, use_global_device_ids=true, to_apply=%region_22.23 | all-reduce | flops 769 | bytes 3076 | tf_op jit(solution)/shard_map/psum | solution.py:436
  1950.5 136.1 %all-reduce.7.cloned.1.call-done = (bf16[384,2304]{0,1:T(8,128)(2,1)}, bf16[384,768]{1,0:T(8,128)(2,1)}, bf16[384,6144]{1,0:T(8,128)(2,1)}, bf16[1536,768]{1,0:T(8,128)(2,1)}) async-done(((bf16[384,2304]{0,1:T(8,128)(2,1)}, bf16[384,768]{1,0:T(8,128)(2,1)}, bf16[384,6144]{1,0:T(8,128)(2,1)}, bf16[1536,768]{1,0:T(8,128)(2,1)}), (bf16[384,2304]{0,1:T(8,128)(2,1)}, bf16[384,768]{1,0:T(8,128)(2,1)}, ...) | async-done | bytes 9437200 | tf_op jit(solution)/shard_map/psum | solution.py:430
  (641 shorter events, 958.9 us)
Async XLA Ops:
  7.2 54.5 %all-gather.9.cloned.1.call-start = ((), (), s32[]{:S(2)}) async-start(), calls=%async_computation.6 | async-start | bytes 5308416 | tf_op jit(solution)/shard_map/all_gather | solution.py:119
  7.9 206.9 %all-gather.11.cloned.1.call-start = ((), (), s32[]{:S(2)}) async-start(), calls=%async_computation.7 | async-start | bytes 9437184 | tf_op jit(solution)/shard_map/all_gather | solution.py:146
  134.2 163.1 %all-gather.13.cloned.1.call-start = ((), (), s32[]{:S(2)}) async-start(), calls=%async_computation.8 | async-start | bytes 9437184 | tf_op jit(solution)/shard_map/all_gather | solution.py:147
  140.3 462.5 %all-gather.15.cloned.1.call-start = ((), (), s32[]{:S(2)}) async-start(), calls=%async_computation.9 | async-start | bytes 1769472 | tf_op jit(solution)/shard_map/all_gather | solution.py:120
  140.9 471.6 %all-gather.17.cloned.1.call-start = ((), (), s32[]{:S(2)}) async-start(), calls=%async_computation.10 | async-start | bytes 14155776 | tf_op jit(solution)/shard_map/all_gather | solution.py:121
  141.4 523.5 %all-gather.19.cloned.1.call-start = ((), (), s32[]{:S(2)}) async-start(), calls=%async_computation.11 | async-start | bytes 7077888 | tf_op jit(solution)/shard_map/all_gather | solution.py:122
  142.0 1404.8 %reduce-scatter.9.cloned.1.call-start = ((), (), s32[]{:S(2)}) async-start(), calls=%async_computation.12 | async-start | bytes 9437184 | tf_op jit(solution)/shard_map/reduce_scatter | solution.py:391
  701.1 5.9 collective-permute-start
  707.3 5.9 collective-permute-start
  713.4 5.9 collective-permute-start
  787.8 6.2 collective-permute-start.1
  794.1 6.3 collective-permute-start.1
  800.4 6.3 collective-permute-start.1
  806.6 6.3 collective-permute-start.1
  812.9 6.3 collective-permute-start.1
  819.1 6.3 collective-permute-start.1
  825.4 6.3 collective-permute-start.1
  831.7 6.3 collective-permute-start.1
  837.9 6.3 collective-permute-start.1
  844.2 6.3 collective-permute-start.1
  850.4 6.3 collective-permute-start.1
  856.7 6.3 collective-permute-start.1
  863.0 6.3 collective-permute-start.1
  869.2 6.3 collective-permute-start.1
  875.5 6.3 collective-permute-start.1
  881.7 6.3 collective-permute-start.1
  1472.8 153.5 %reduce-scatter.11.cloned.1.call-start = ((), (), s32[]{:S(2)}) async-start(), calls=%async_computation.13 | async-start | bytes 9437184 | tf_op jit(solution)/shard_map/reduce_scatter | solution.py:394
  1495.3 205.5 %reduce-scatter.19.cloned.1.call-start = ((), (), s32[]{:S(2)}) async-start(), calls=%async_computation.17 | async-start | bytes 5308416
  1647.0 72.4 %reduce-scatter.13.cloned.1.call-start = ((), (), s32[]{:S(2)}) async-start(), calls=%async_computation.14 | async-start | bytes 1769472 | tf_op jit(solution)/shard_map/reduce_scatter | solution.py:413
  1654.4 127.8 %reduce-scatter.17.cloned.1.call-start = ((), (), s32[]{:S(2)}) async-start(), calls=%async_computation.16 | async-start | bytes 7077888 | tf_op jit(solution)/shard_map/reduce_scatter | solution.py:419
  1671.0 224.1 %reduce-scatter.15.cloned.1.call-start = ((), (), s32[]{:S(2)}) async-start(), calls=%async_computation.15 | async-start | bytes 14155776 | tf_op jit(solution)/shard_map/reduce_scatter | solution.py:416
  1700.8 385.8 %all-reduce.7.cloned.1.call-start = ((), (), s32[]{:S(2)}) async-start(), calls=%async_computation.18 | async-start | bytes 18874368 | tf_op jit(solution)/shard_map/psum | solution.py:430
  (92 other events, 2998.9 us)
Sparse Core Ops, SparseCore 0:
  9.6 52.0 all-gather.8
  134.3 80.4 all-gather.10
  216.9 80.3 all-gather.12
  298.7 22.7 all-gather.14
  322.9 117.9 all-gather.16
  442.4 62.6 all-gather.18
  1473.0 73.8 reduce-scatter.8
  1549.3 77.0 reduce-scatter.10
  1647.1 47.6 reduce-scatter.18
  1697.5 21.7 reduce-scatter.12
  1722.2 59.9 reduce-scatter.16
  1784.5 110.5 reduce-scatter.14
  1900.3 186.2 all-reduce.6
where the time goes:
time: 2120 us; the launch traced here: 2110 us
  matrix products  831 us (39%)
  waiting for transfers between devices  786 us (37%)
  other arithmetic  225 us (11%)
  local copies, waits for them, and re-layouts  185 us (9%)
  blocking collectives  55.7 us (3%)
    ppermute x47, waiting for transfers between devices, from_behind(): return lax.ppermute(block, axis, route)  178 us
    dot_general x8, matrix products, score_block(): jnp.einsum('rqhd,rkhd->rhqk', query_heads, key_block, preferred_element_t...  169 us
    psum x1, waiting for transfers between devices, shards(): lax.psum(shares[0].astype(jnp.bfloat16), 'blk').astype(jnp.float32)  136 us
    dot_general x4, matrix products, span_terms(): jnp.einsum('rqhd,rkhd->rhqk', attended_heads, value_block, preferred_elem...  122 us
    reduce_scatter x1, waiting for transfers between devices, shards(): lax.psum_scatter(swiglu_part.astype(jnp.bfloat16), 'fsdp', scatter_dimens...  113 us
    dot_general x4, matrix products, one_span(): jnp.einsum('rhqk,rkhd->rqhd', weights_soft.astype(bf16), value_block, pre...  97.7 us
    reduce_sum x4, other arithmetic, one_span(): run_sum = run_sum * factor + jnp.sum(weights_soft, -1)  86.7 us
    dot_general x4, matrix products, back_span(): jnp.einsum('rhqk,rqhd->rkhd', soft.astype(bf16), attended_heads, preferre...  85.1 us
  transfers between devices with their start and end apart: 60, of which 40 were waited for; matrix products, arithmetic and copies ran while one was open for 25% of the time, Pallas kernels for 0%

commit v1 on v0

v1 whole, which is shorter than its diff:
```python
import functools
import math

import jax
import jax.numpy as jnp
from jax import lax
from jax.experimental import pallas as pl
from jax.experimental.pallas import tpu as pltpu
from jax.sharding import PartitionSpec as P

HEADS = 12
HDIM = 64
PAIRS = HEADS // 2
LANES = 128
SEG = 8

EPSILON = 1e-05
EMB_EPSILON = 1e-06
SOFTMAX_WARMTH = 0.05
ROPE_BASE = 1000.0
CONTRAST_WEIGHT = 512.0
NEGATIVE = -1e30

BF = jnp.bfloat16
F32 = jnp.float32
MIB = 1 << 20


def dot(a, b):
    return lax.dot_general(a, b, (((1,), (0,)), ((), ())), preferred_element_type=F32)


def dot_bt(a, b):
    return lax.dot_general(a, b, (((1,), (1,)), ((), ())), preferred_element_type=F32)


def dot_at(a, b):
    return lax.dot_general(a, b, (((0,), (0,)), ((), ())), preferred_element_type=F32)


def lane_iota(shape):
    return lax.broadcasted_iota(jnp.int32, shape, len(shape) - 1)


def halves_swapped(block):
    low = lane_iota(block.shape) % HDIM < HDIM // 2
    return jnp.where(low, pltpu.roll(block, LANES - 32, 1), pltpu.roll(block, 32, 1))


def weight_pieces(weight, flip):
    rows, cols = weight.shape
    shards = lax.axis_size("fsdp")
    mine = lax.axis_index("fsdp")
    blocks = lax.axis_size("blk")
    if shards != 2 or blocks % 4:
        return [lax.all_gather(weight, "fsdp", axis=0, tiled=True)], [(0, 0)]
    place = lax.axis_index("blk")
    core, side = place % 2, (place // 2) % 2
    r2, c2 = rows // 2, cols // 2
    piece = lax.dynamic_slice(weight, (side * r2, core * c2), (r2, c2))
    first = lax.ppermute(piece, "fsdp", [(0, 1), (1, 0)])
    second = lax.ppermute(first, "blk", [(i, i ^ 2) for i in range(blocks)])
    over = [(i, i ^ 1) for i in range(blocks)]
    third = lax.ppermute(first, "blk", over)
    fourth = lax.ppermute(second, "blk", over)
    other = (1 - mine) * rows
    return [weight, first, second, third, fourth], [
        (mine * rows, 0),
        (other + side * r2, core * c2),
        (other + (1 - side) * r2, core * c2),
        (other + side * r2, (1 - core) * c2),
        (other + (1 - side) * r2, (1 - core) * c2),
    ]


def as_table(offsets):
    return jnp.stack([jnp.asarray(v, jnp.int32) for pair in offsets for v in pair])


def weight_copies(table, base, pieces, whole, sems):
    copies = []
    for n, piece in enumerate(pieces):
        rows, cols = piece.shape
        row = pl.multiple_of(table[2 * (base + n)], 16)
        col = pl.multiple_of(table[2 * (base + n) + 1], LANES)
        copies.append(
            pltpu.make_async_copy(
                piece, whole.at[pl.ds(row, rows), pl.ds(col, cols)], sems.at[base + n]
            )
        )
    return copies


ANY = pl.BlockSpec(memory_space=pl.ANY)


def params(limit_mib):
    return pltpu.CompilerParams(vmem_limit_bytes=limit_mib * MIB)


def qkv_kernel(count, table, x_ref, cos_ref, sin_ref, *rest):
    pieces, (q_ref, k_ref, v_ref, whole, sems) = rest[:count], rest[count:]
    width = q_ref.shape[1]

    @pl.when(pl.program_id(0) == 0)
    def _():
        copies = weight_copies(table, 0, pieces, whole, sems)
        for copy in copies:
            copy.start()
        for copy in copies:
            copy.wait()

    x = x_ref[...]
    cosine, sine = cos_ref[...], sin_ref[...]
    for ref, start, factor in ((q_ref, 0, 1.0 / math.sqrt(HDIM)), (k_ref, width, 1.0)):
        projected = dot(x, whole[:, start : start + width])
        for b in range(0, width, LANES):
            block = projected[:, b : b + LANES]
            turned = block * cosine + halves_swapped(block) * sine
            ref[:, b : b + LANES] = turned.astype(BF) * jnp.asarray(factor, BF)
    v_ref[...] = dot(x, whole[:, 2 * width :]).astype(BF)


def project(x, cosine, sine, weight, tile):
    pieces, offsets = weight
    tokens, width = x.shape
    row = lambda i, *_: (i, 0)
    return pl.pallas_call(
        functools.partial(qkv_kernel, len(pieces)),
        grid_spec=pltpu.PrefetchScalarGridSpec(
            num_scalar_prefetch=1,
            grid=(tokens // tile,),
            in_specs=[
                pl.BlockSpec((tile, width), row),
                pl.BlockSpec((tile, LANES), row),
                pl.BlockSpec((tile, LANES), row),
            ]
            + [ANY] * len(pieces),
            out_specs=[pl.BlockSpec((tile, width), row)] * 3,
            scratch_shapes=[
                pltpu.VMEM((width, 3 * width), BF),
                pltpu.SemaphoreType.DMA((len(pieces),)),
            ],
        ),
        out_shape=[jax.ShapeDtypeStruct((tokens, width), BF)] * 3,
        compiler_params=params(40),
        cost_estimate=pl.CostEstimate(
            flops=6 * tokens * width * width, bytes_accessed=16 * MIB, transcendentals=0
        ),
    )(as_table(offsets), x, cosine, sine, *pieces)


def input_grad_kernel(count, table, dbr_ref, dq_ref, dk_ref, dv_ref, *rest):
    pieces, (out_ref, whole, sems) = rest[:count], rest[count:]
    width = dq_ref.shape[1]

    @pl.when(pl.program_id(0) == 0)
    def _():
        copies = weight_copies(table, 1, pieces, whole, sems)
        for copy in copies:
            copy.start()
        for copy in copies:
            copy.wait()

    total = dbr_ref[...].astype(F32)
    for n, ref in enumerate((dq_ref, dk_ref, dv_ref)):
        total += dot_bt(ref[...], whole[:, n * width : (n + 1) * width])
    out_ref[...] = total.astype(out_ref.dtype)


def input_grad_part(dbr, dq, dk, dv, weight, start, tokens, dtype, tile):
    pieces, offsets = weight
    width = dq.shape[1]
    table = as_table([(start // tile, 0), *offsets])
    shifted = lambda i, t: (i + t[0], 0)
    return pl.pallas_call(
        functools.partial(input_grad_kernel, len(pieces)),
        grid_spec=pltpu.PrefetchScalarGridSpec(
            num_scalar_prefetch=1,
            grid=(tokens // tile,),
            in_specs=[pl.BlockSpec((tile, width), shifted)] * 4 + [ANY] * len(pieces),
            out_specs=pl.BlockSpec((tile, width), lambda i, t: (i, 0)),
            scratch_shapes=[
                pltpu.VMEM((width, 3 * width), BF),
                pltpu.SemaphoreType.DMA((len(pieces) + 1,)),
            ],
        ),
        out_shape=jax.ShapeDtypeStruct((tokens, width), dtype),
        compiler_params=params(40),
        cost_estimate=pl.CostEstimate(
            flops=6 * tokens * width * width, bytes_accessed=16 * MIB, transcendentals=0
        ),
    )(table, dbr, dq, dk, dv, *pieces)


BQ = 256
BK = 256


def attend_kernel(spans, q_ref, k_ref, v_ref, kf_ref, qf_ref, o_ref, lse_ref, kx, vte, vto):
    block = pl.program_id(2)
    where = (pl.program_id(0) * pl.num_programs(2) + block) * 2
    row_len = k_ref.shape[0]

    @pl.when(block == 0)
    def _():
        kx[:, :LANES] = k_ref[...]
        kx[:, LANES:] = kf_ref[...]
        for b in range(0, row_len, BK):
            turned = v_ref[b : b + BK, :].astype(F32).T
            upper = lax.broadcasted_iota(jnp.int32, turned.shape, 0) < HDIM
            vte[:, b : b + BK] = jnp.where(upper, turned, 1.0).astype(BF)
            vto[:, b : b + BK] = jnp.where(upper, 1.0, turned).astype(BF)

    q, qf = q_ref[...], qf_ref[...]
    even = lane_iota(q.shape) < HDIM
    zero = jnp.zeros_like(q)
    queries = (
        jnp.concatenate([jnp.where(even, q, zero), qf], axis=1),
        jnp.concatenate([jnp.where(even, zero, q), qf], axis=1),
    )
    first, count = spans[where], spans[where + 1]

    def step(j, state):
        at = pl.multiple_of(first + j * BK, LANES)
        keys = kx[pl.ds(at, BK), :]
        values = (vte[:, pl.ds(at, BK)], vto[:, pl.ds(at, BK)])
        out = []
        for h in range(2):
            best, accum = state[2 * h], state[2 * h + 1]
            scores = dot_bt(keys, queries[h])
            new = jnp.maximum(best, jnp.max(scores, axis=0, keepdims=True))
            soft = jnp.exp(scores - new).astype(BF)
            accum = accum * jnp.exp(best - new) + dot(values[h], soft)
            out += [new, accum]
        return tuple(out)

    start = (jnp.full((1, BQ), NEGATIVE, F32), jnp.zeros((LANES, BQ), F32)) * 2
    best_e, acc_e, best_o, acc_o = lax.fori_loop(0, count, step, start)
    sum_e, sum_o = acc_e[HDIM : HDIM + 1], acc_o[0:1]
    turned = jnp.concatenate([acc_e[:HDIM] / sum_e, acc_o[HDIM:] / sum_o], axis=0)
    o_ref[...] = turned.T.astype(BF)
    lse_ref[0, 0:1, :] = best_e + jnp.log(sum_e)
    lse_ref[0, 1:2, :] = best_o + jnp.log(sum_o)


def attend(q, k, v, key_feat, query_feat, spans, rows):
    tokens, width = q.shape
    row_len = k.shape[0] // rows
    blocks = tokens // rows // BQ
    of_q = lambda r, p, i, *_: (r * blocks + i, p)
    of_k = lambda r, p, i, *_: (r, p)
    return pl.pallas_call(
        attend_kernel,
        grid_spec=pltpu.PrefetchScalarGridSpec(
            num_scalar_prefetch=1,
            grid=(rows, PAIRS, blocks),
            in_specs=[
                pl.BlockSpec((BQ, LANES), of_q),
                pl.BlockSpec((row_len, LANES), of_k),
                pl.BlockSpec((row_len, LANES), of_k),
                pl.BlockSpec((row_len, LANES), lambda r, p, i, *_: (r, 0)),
                pl.BlockSpec((BQ, LANES), lambda r, p, i, *_: (r * blocks + i, 0)),
            ],
            out_specs=[
                pl.BlockSpec((BQ, LANES), of_q),
                pl.BlockSpec((1, 2, BQ), lambda r, p, i, *_: (p, 0, r * blocks + i)),
            ],
            scratch_shapes=[
                pltpu.VMEM((row_len, 2 * LANES), BF),
                pltpu.VMEM((LANES, row_len), BF),
                pltpu.VMEM((LANES, row_len), BF),
            ],
        ),
        out_shape=[
            jax.ShapeDtypeStruct((tokens, width), BF),
            jax.ShapeDtypeStruct((PAIRS, 2, tokens), F32),
        ],
        compiler_params=params(40),
        cost_estimate=pl.CostEstimate(
            flops=tokens * row_len * width * 4, bytes_accessed=16 * MIB, transcendentals=0
        ),
    )(spans, q, k, v, key_feat, query_feat)


def attend_back_kernel(
    spans, q_ref, do_ref, k_ref, v_ref, kf_ref, qf_ref, cq_ref, sq_ref, ck_ref, sk_ref,
    dq_ref, dk_ref, dv_ref, kx, vx, kt, dk_acc, dv_acc,
):
    pair, block = pl.program_id(1), pl.program_id(2)
    where = (pl.program_id(0) * pl.num_programs(2) + block) * 2
    row_len = k_ref.shape[0]

    @pl.when(block == 0)
    def _():
        kx[:, :LANES] = k_ref[...]
        kx[:, LANES:] = kf_ref[...]
        vx[:, :LANES] = v_ref[...]
        vx[:, LANES:] = kf_ref[...]
        for b in range(0, row_len, BK):
            kt[:, b : b + BK] = k_ref[b : b + BK, :].astype(F32).T.astype(BF)
        dk_acc[...] = jnp.zeros_like(dk_acc)
        dv_acc[...] = jnp.zeros_like(dv_acc)

    q, do, qf = q_ref[...], do_ref[...], qf_ref[...]
    lanes = lane_iota(q.shape)
    even = lanes < HDIM
    zero = jnp.zeros_like(q)
    split_q = (jnp.where(even, q, zero), jnp.where(even, zero, q))
    split_do = (jnp.where(even, do, zero), jnp.where(even, zero, do))
    queries, upstream = [], []
    for h in range(2):
        lane = lanes - (2 * pair + h)
        of_lse = (lanes < SEG) | (lane == 8) | (lane == 20) | (lane == 32)
        of_delta = (lane == 44) | (lane == 56) | (lane == 68)
        queries.append(jnp.concatenate([split_q[h], jnp.where(of_lse, qf, zero)], axis=1))
        upstream.append(jnp.concatenate([split_do[h], jnp.where(of_delta, qf, zero)], axis=1))
    stacked_q = jnp.concatenate(split_q, axis=0)
    stacked_do = jnp.concatenate(split_do, axis=0)
    first, count = spans[where], spans[where + 1]

    def step(j, state):
        at = pl.multiple_of(first + j * BK, LANES)
        keys, values = kx[pl.ds(at, BK), :], vx[pl.ds(at, BK), :]
        turned_keys = kt[:, pl.ds(at, BK)]
        soft, grads, out = [], [], []
        for h in range(2):
            probs = jnp.exp(dot_bt(keys, queries[h]))
            grad = (probs * dot_bt(values, upstream[h])).astype(BF)
            soft.append(probs.astype(BF))
            grads.append(grad)
            out.append(state[h] + dot(turned_keys[h * HDIM : (h + 1) * HDIM], grad))
        dv_acc[pl.ds(at, BK), :] += dot(jnp.concatenate(soft, axis=1), stacked_do)
        dk_acc[pl.ds(at, BK), :] += dot(jnp.concatenate(grads, axis=1), stacked_q)
        return tuple(out)

    start = (jnp.zeros((HDIM, BQ), F32),) * 2
    turned = jnp.concatenate(lax.fori_loop(0, count, step, start), axis=0)
    dq = turned.T * (1.0 / math.sqrt(HDIM))
    dq_ref[...] = (dq * cq_ref[...] - halves_swapped(dq) * sq_ref[...]).astype(BF)

    @pl.when(block == pl.num_programs(2) - 1)
    def _():
        for b in range(0, row_len, BK):
            part = pl.ds(b, BK)
            dk = dk_acc[part, :]
            dk_ref[part, :] = (dk * ck_ref[part, :] - halves_swapped(dk) * sk_ref[part, :]).astype(BF)
            dv_ref[part, :] = dv_acc[part, :].astype(BF)


def attend_back(q, do, k, v, key_feat, query_feat, spans, tables_q, tables_k, rows):
    tokens, width = q.shape
    row_len = k.shape[0] // rows
    blocks = tokens // rows // BQ
    of_q = lambda r, p, i, *_: (r * blocks + i, p)
    of_k = lambda r, p, i, *_: (r, p)
    per_q = pl.BlockSpec((BQ, LANES), lambda r, p, i, *_: (r * blocks + i, 0))
    per_k = pl.BlockSpec((row_len, LANES), lambda r, p, i, *_: (r, 0))
    return pl.pallas_call(
        attend_back_kernel,
        grid_spec=pltpu.PrefetchScalarGridSpec(
            num_scalar_prefetch=1,
            grid=(rows, PAIRS, blocks),
            in_specs=[
                pl.BlockSpec((BQ, LANES), of_q),
                pl.BlockSpec((BQ, LANES), of_q),
                pl.BlockSpec((row_len, LANES), of_k),
                pl.BlockSpec((row_len, LANES), of_k),
                per_k,
                per_q,
                per_q,
                per_q,
                per_k,
                per_k,
            ],
            out_specs=[
                pl.BlockSpec((BQ, LANES), of_q),
                pl.BlockSpec((row_len, LANES), of_k),
                pl.BlockSpec((row_len, LANES), of_k),
            ],
            scratch_shapes=[
                pltpu.VMEM((row_len, 2 * LANES), BF),
                pltpu.VMEM((row_len, 2 * LANES), BF),
                pltpu.VMEM((LANES, row_len), BF),
                pltpu.VMEM((row_len, LANES), F32),
                pltpu.VMEM((row_len, LANES), F32),
            ],
        ),
        out_shape=[
            jax.ShapeDtypeStruct((tokens, width), BF),
            jax.ShapeDtypeStruct((rows * row_len, width), BF),
            jax.ShapeDtypeStruct((rows * row_len, width), BF),
        ],
        compiler_params=params(48),
        cost_estimate=pl.CostEstimate(
            flops=tokens * row_len * width * 10, bytes_accessed=24 * MIB, transcendentals=0
        ),
    )(spans, q, do, k, v, key_feat, query_feat, *tables_q, *tables_k)


FF_CHUNK = 512


def normalize(hidden):
    average = jnp.mean(hidden, -1, keepdims=True)
    centred = hidden - average
    inverse = lax.rsqrt(jnp.mean(centred * centred, -1, keepdims=True) + EPSILON)
    return centred * inverse, inverse


def norm_back(scaled, normalized, inverse):
    return inverse * (
        scaled
        - jnp.mean(scaled, -1, keepdims=True)
        - normalized * jnp.mean(scaled * normalized, -1, keepdims=True)
    )


def split_two(value):
    high = value.astype(BF)
    return high, (value - high.astype(F32)).astype(BF)


def mix_kernel(counts, table, att_ref, x_ref, qf_ref, g1_ref, g2_ref, *rest):
    total = sum(counts)
    pieces, (nl_ref, stat_ref, gu_ref, out_ref, pool_ref, wo, ws, wd, sems) = rest[:total], rest[total:]
    groups, base = [], 0
    for count, whole in zip(counts, (wo, ws, wd)):
        groups.append(weight_copies(table, base, pieces[base : base + count], whole, sems))
        base += count
    step, begin = pl.program_id(1), (pl.program_id(0) == 0) & (pl.program_id(1) == 0)

    @pl.when(begin)
    def _():
        for group in groups:
            for copy in group:
                copy.start()
        for copy in groups[0]:
            copy.wait()

    branch = dot(att_ref[...], wo[...])
    unit, inverse1 = normalize(x_ref[...].astype(F32) + branch)
    normed = unit * g1_ref[...]
    low = normed.astype(BF)
    nl_ref[...] = low

    @pl.when(begin)
    def _():
        for group in groups[1:]:
            for copy in group:
                copy.wait()

    ff = wd.shape[0]
    hidden_sum = normed
    for c in range(0, ff, FF_CHUNK):
        gate = dot(low, ws[:, c : c + FF_CHUNK])
        up = dot(low, ws[:, ff + c : ff + c + FF_CHUNK])
        gu_ref[:, c : c + FF_CHUNK] = gate.astype(BF)
        gu_ref[:, ff + c : ff + c + FF_CHUNK] = up.astype(BF)
        hidden = (gate * (0.5 + 0.5 * jnp.tanh(0.5 * gate)) * up).astype(BF)
        hidden_sum = hidden_sum + dot(hidden, wd[c : c + FF_CHUNK, :])
    unit2, inverse2 = normalize(hidden_sum)
    output = unit2 * g2_ref[...]
    out_ref[...] = output.astype(BF)
    lanes = lane_iota(stat_ref.shape)
    stat_ref[...] = jnp.where(lanes == 0, inverse1, inverse2)
    high, rest_low = split_two(output)
    member = qf_ref[...]
    sums = (dot_at(member, high) + dot_at(member, rest_low))[:SEG]

    @pl.when(step == 0)
    def _():
        pool_ref[0] = sums

    @pl.when(step > 0)
    def _():
        pool_ref[0] += sums


def mix(attended, x, query_feat, gain1, gain2, weights, rows, tile):
    tokens, width = x.shape
    counts = [len(w[0]) for w in weights]
    pieces = [p for w in weights for p in w[0]]
    offsets = [o for w in weights for o in w[1]]
    steps = tokens // rows // tile
    ff = sum_rows(weights[2])
    row = lambda r, i, *_: (r * steps + i, 0)
    fixed = lambda r, i, *_: (0, 0)
    return pl.pallas_call(
        functools.partial(mix_kernel, counts),
        grid_spec=pltpu.PrefetchScalarGridSpec(
            num_scalar_prefetch=1,
            grid=(rows, steps),
            in_specs=[
                pl.BlockSpec((tile, width), row),
                pl.BlockSpec((tile, width), row),
                pl.BlockSpec((tile, LANES), row),
                pl.BlockSpec((1, width), fixed),
                pl.BlockSpec((1, width), fixed),
            ]
            + [ANY] * len(pieces),
            out_specs=[
                pl.BlockSpec((tile, width), row),
                pl.BlockSpec((tile, LANES), row),
                pl.BlockSpec((tile, 2 * ff), row),
                pl.BlockSpec((tile, width), row),
                pl.BlockSpec((1, SEG, width), lambda r, i, *_: (r, 0, 0)),
            ],
            scratch_shapes=[
                pltpu.VMEM((width, width), BF),
                pltpu.VMEM((width, 2 * ff), BF),
                pltpu.VMEM((ff, width), BF),
                pltpu.SemaphoreType.DMA((len(pieces),)),
            ],
        ),
        out_shape=[
            jax.ShapeDtypeStruct((tokens, width), BF),
            jax.ShapeDtypeStruct((tokens, LANES), F32),
            jax.ShapeDtypeStruct((tokens, 2 * ff), BF),
            jax.ShapeDtypeStruct((tokens, width), BF),
            jax.ShapeDtypeStruct((rows, SEG, width), F32),
        ],
        compiler_params=params(56),
        cost_estimate=pl.CostEstimate(
            flops=2 * tokens * width * (width + 3 * ff), bytes_accessed=64 * MIB, transcendentals=0
        ),
    )(as_table(offsets), attended, x, query_feat, gain1, gain2, *pieces)


def sum_rows(weight):
    pieces, offsets = weight
    return pieces[0].shape[0] * (1 if len(pieces) == 1 else 2)


def mix_back_kernel(
    counts, table, cot_ref, out_ref, nl_ref, stat_ref, qf_ref, dp_ref, gu_ref, att_ref, lse_ref, g1_ref, g2_ref, head_ref,
    *rest,
):
    total = sum(counts)
    pieces = rest[:total]
    dffn_ref, hid_ref, dgu_ref, dbr_ref, datt_ref, feat_ref, ga_ref, gf_ref, wo, ws, wd, sems = rest[total:]
    groups, base = [], 0
    for count, whole in zip(counts, (wo, ws, wd)):
        groups.append(weight_copies(table, base, pieces[base : base + count], whole, sems))
        base += count
    begin = (pl.program_id(0) == 0) & (pl.program_id(1) == 0)

    @pl.when(begin)
    def _():
        for group in groups[::-1]:
            for copy in group:
                copy.start()

    stat = stat_ref[...]
    inverse1, inverse2 = stat[:, 0:1], stat[:, 1:2]
    member = qf_ref[...]
    high, rest_low = split_two(dp_ref[0])
    upstream = cot_ref[...].astype(F32) + dot(member, high) + dot(member, rest_low)
    gain2 = g2_ref[...]
    unit2 = out_ref[...].astype(F32) / gain2
    second = norm_back(upstream * gain2, unit2, inverse2)
    gain2_part = upstream * unit2
    dffn = second.astype(BF)
    dffn_ref[...] = dffn

    @pl.when(begin)
    def _():
        ga_ref[...] = jnp.zeros_like(ga_ref)
        gf_ref[...] = jnp.zeros_like(gf_ref)
        for group in groups:
            for copy in group:
                copy.wait()

    ff = wd.shape[0]
    dnormed = second
    for c in range(0, ff, FF_CHUNK):
        dhid = dot_bt(dffn, wd[c : c + FF_CHUNK, :])
        gate = gu_ref[:, c : c + FF_CHUNK].astype(F32)
        up = gu_ref[:, ff + c : ff + c + FF_CHUNK].astype(F32)
        sig = 0.5 + 0.5 * jnp.tanh(0.5 * gate)
        silu = gate * sig
        hid_ref[:, c : c + FF_CHUNK] = (silu * up).astype(BF)
        dgate = (dhid * up * (sig + silu * (1.0 - sig))).astype(BF)
        dup = (dhid * silu).astype(BF)
        dgu_ref[:, c : c + FF_CHUNK] = dgate
        dgu_ref[:, ff + c : ff + c + FF_CHUNK] = dup
        dnormed = dnormed + dot_bt(dgate, ws[:, c : c + FF_CHUNK])
        dnormed = dnormed + dot_bt(dup, ws[:, ff + c : ff + c + FF_CHUNK])
    gain1 = g1_ref[...]
    unit1 = nl_ref[...].astype(F32) / gain1
    first = norm_back(dnormed * gain1, unit1, inverse1)
    gain1_part = dnormed * unit1
    dbr = first.astype(BF)
    dbr_ref[...] = dbr
    datt = dot_bt(dbr, wo[...]).astype(BF)
    datt_ref[...] = datt
    tile, width = datt.shape
    ga_ref[...] += jnp.sum(gain1_part.reshape(tile // 8, 8, width), axis=0)
    gf_ref[...] += jnp.sum(gain2_part.reshape(tile // 8, 8, width), axis=0)

    high, rest_low = split_two(datt.astype(F32) * att_ref[...].astype(F32))
    heads = head_ref[...]
    delta = dot(high, heads) + dot(rest_low, heads)
    feat = member.astype(F32)
    for value, start in ((lse_ref[...], 8), (delta, 44)):
        left = -value
        for n in range(3):
            part = left.astype(BF).astype(F32)
            left = left - part
            feat = feat + pltpu.roll(part, start + HEADS * n, 1)
    feat_ref[...] = feat.astype(BF)


def mix_back(cot, output, low, stat, query_feat, dpool, gate_up, attended, lse, gain1, gain2, weights, rows, tile):
    tokens, width = cot.shape
    counts = [len(w[0]) for w in weights]
    pieces = [p for w in weights for p in w[0]]
    offsets = [o for w in weights for o in w[1]]
    steps = tokens // rows // tile
    ff = sum_rows(weights[2])
    row = lambda r, i, *_: (r * steps + i, 0)
    fixed = lambda r, i, *_: (0, 0)
    wide, narrow = pl.BlockSpec((tile, width), row), pl.BlockSpec((tile, LANES), row)
    heads = (jnp.arange(width)[:, None] // HDIM == jnp.arange(LANES)[None, :]).astype(BF)
    return pl.pallas_call(
        functools.partial(mix_back_kernel, counts),
        grid_spec=pltpu.PrefetchScalarGridSpec(
            num_scalar_prefetch=1,
            grid=(rows, steps),
            in_specs=[
                wide,
                wide,
                wide,
                narrow,
                narrow,
                pl.BlockSpec((1, LANES, width), lambda r, i, *_: (r, 0, 0)),
                pl.BlockSpec((tile, 2 * ff), row),
                wide,
                narrow,
                pl.BlockSpec((1, width), fixed),
                pl.BlockSpec((1, width), fixed),
                pl.BlockSpec((width, LANES), fixed),
            ]
            + [ANY] * len(pieces),
            out_specs=[
                wide,
                pl.BlockSpec((tile, ff), row),
                pl.BlockSpec((tile, 2 * ff), row),
                wide,
                wide,
                narrow,
                pl.BlockSpec((8, width), fixed),
                pl.BlockSpec((8, width), fixed),
            ],
            scratch_shapes=[
                pltpu.VMEM((width, width), BF),
                pltpu.VMEM((width, 2 * ff), BF),
                pltpu.VMEM((ff, width), BF),
                pltpu.SemaphoreType.DMA((len(pieces),)),
            ],
        ),
        out_shape=[
            jax.ShapeDtypeStruct((tokens, width), BF),
            jax.ShapeDtypeStruct((tokens, ff), BF),
            jax.ShapeDtypeStruct((tokens, 2 * ff), BF),
            jax.ShapeDtypeStruct((tokens, width), BF),
            jax.ShapeDtypeStruct((tokens, width), BF),
            jax.ShapeDtypeStruct((tokens, LANES), BF),
            jax.ShapeDtypeStruct((8, width), F32),
            jax.ShapeDtypeStruct((8, width), F32),
        ],
        compiler_params=params(56),
        cost_estimate=pl.CostEstimate(
            flops=2 * tokens * width * (width + 3 * ff), bytes_accessed=96 * MIB, transcendentals=0
        ),
    )(
        as_table(offsets), cot, output, low, stat, query_feat, dpool, gate_up, attended, lse, gain1, gain2, heads, *pieces,
    )


def flipped(block, axis, bit):
    route = [(i, i ^ bit) for i in range(lax.axis_size(axis))]
    return lax.ppermute(block, axis, route)


def bits_of(axis):
    size, bit = lax.axis_size(axis), 1
    while bit < size:
        yield bit
        bit *= 2


def summed_everywhere(value):
    for axis in ("fsdp", "blk"):
        for bit in bits_of(axis):
            value = value + flipped(value, axis, bit)
    return value


def contrast(sums, lengths, pairing, row_mode, row_ids):
    rows, segs, width = sums.shape
    lengths = lengths.astype(F32)[..., None]
    pooled = sums / lengths
    inverse = lax.rsqrt(jnp.sum(pooled * pooled, -1, keepdims=True) + EMB_EPSILON)
    embedded = pooled * inverse
    own = rows * segs
    pair = jnp.stack([pairing, jnp.zeros_like(pairing)], axis=-1).reshape(own, 1)
    spare = jnp.concatenate([pair // 128, pair % 128, jnp.zeros((own, 126), jnp.int32)], axis=1)
    buffer = jnp.concatenate([embedded.reshape(own, width).astype(BF), spare.astype(BF)], axis=1)
    ids = row_ids
    for axis in ("fsdp", "blk") if row_mode else ("blk",):
        for bit in bits_of(axis):
            buffer = jnp.concatenate([buffer, flipped(buffer, axis, bit)], axis=0)
            if axis == "fsdp":
                ids = jnp.concatenate([ids, ids ^ bit])
            else:
                ids = jnp.concatenate([ids, ids ^ (bit * ROWS_PER_BLOCK)])
    total = buffer.shape[0]
    every = buffer[:, :width]
    pair_all = (buffer[:, width].astype(jnp.int32) * 128 + buffer[:, width + 1].astype(jnp.int32))[:, None]
    seg = jnp.arange(total, dtype=jnp.int32) % segs
    number = jnp.repeat(ids, segs, total_repeat_length=total) * (segs // 2) + seg // 2
    is_query = (seg % 2 == 0)[:, None]
    is_doc = (seg % 2 == 1)[None, :]
    target = is_query & is_doc & (pair_all == number[None, :])
    sims = dot_bt(every, every) / SOFTMAX_WARMTH
    masked = jnp.where(is_doc, sims, NEGATIVE)
    best = jnp.max(masked, -1, keepdims=True)
    log_total = best + jnp.log(jnp.sum(jnp.exp(masked - best), -1, keepdims=True))
    positive = jnp.sum(jnp.where(target, sims, 0.0), -1, keepdims=True)
    loss = jnp.sum(jnp.where(is_query[:own], log_total[:own] - positive[:own], 0.0))
    d_sims = CONTRAST_WEIGHT * (jnp.exp(masked - log_total) - target.astype(F32))
    d_sims = jnp.where(is_query, d_sims, 0.0).astype(BF)
    grad = (dot(d_sims[:own], every) + dot_at(d_sims[:, :own], every)) / SOFTMAX_WARMTH
    grad = grad.reshape(rows, segs, width)
    along = jnp.sum(embedded * grad, -1, keepdims=True)
    return loss, inverse * (grad - embedded * along) / lengths


ROWS_PER_BLOCK = 2


def half_row(kept, moved, first):
    return jnp.concatenate([jnp.where(first, kept, moved), jnp.where(first, moved, kept)], axis=0)


def shards(
    tokens,
    cotangent,
    segments,
    doc_lengths,
    positions,
    pairing,
    qkv_weight,
    out_weight,
    swiglu_weight,
    down_weight,
    attn_gain,
    ffn_gain,
):
    rows_here, shard_len, width = tokens.shape
    split = lax.axis_size("fsdp")
    mine = lax.axis_index("fsdp")
    place = lax.axis_index("blk")
    row_len = shard_len * split
    row_mode = split == rows_here == 2
    swap = [(0, 1), (1, 0)]

    if row_mode:

        def to_rows(array):
            kept = lax.dynamic_index_in_dim(array, mine, 0, keepdims=False)
            moved = lax.dynamic_index_in_dim(array, 1 - mine, 0, keepdims=False)
            return half_row(kept, lax.ppermute(moved, "fsdp", swap), mine == 0)

        def to_shards(kept, moved):
            came = lax.ppermute(moved, "fsdp", swap).astype(kept.dtype)
            first = mine == 0
            return jnp.stack([jnp.where(first, kept, came), jnp.where(first, came, kept)])

        rows, per_row, query_start = 1, row_len, 0
        lengths = lax.dynamic_slice_in_dim(doc_lengths, mine, 1, 0)
        own_pairing = lax.dynamic_slice_in_dim(pairing.reshape(rows_here, -1), mine, 1, 0)
        row_ids = (place * rows_here + mine)[None]
    else:

        def to_rows(array):
            return array.reshape(-1, width)

        rows, per_row, query_start = rows_here, shard_len, mine * shard_len
        lengths, own_pairing = doc_lengths, pairing.reshape(rows_here, -1)
        row_ids = place * rows_here + jnp.arange(rows_here, dtype=jnp.int32)
    tokens_here = rows * per_row
    tile = 256

    order = jnp.arange(SEG, dtype=jnp.int32)
    ends = jnp.sum(jnp.where(order[None, :] <= order[:, None], lengths[:, None, :], 0), -1)
    starts = ends - lengths
    token = jnp.arange(row_len, dtype=jnp.int32)
    at = token[None, :, None]
    member = (at >= starts[:, None, :]) & (at < ends[:, None, :])
    first_of = jnp.max(jnp.where(at >= starts[:, None, :], starts[:, None, :], 0), -1)
    lane = jnp.arange(LANES, dtype=jnp.int32)
    frequency = ROPE_BASE ** (-2.0 * (lane % 32).astype(F32) / HDIM)
    angles = (token[None, :] - first_of).astype(F32)[..., None] * frequency
    cosine = jnp.cos(angles).reshape(-1, LANES)
    sine = (jnp.sin(angles) * jnp.where(lane % HDIM < 32, -1.0, 1.0)).reshape(-1, LANES)
    key_feat = jnp.where(member, 0.0, NEGATIVE)
    key_feat = jnp.concatenate([key_feat, jnp.ones((rows, row_len, 120), F32)], -1)
    key_feat = key_feat.astype(BF).reshape(-1, LANES)
    query_feat = jnp.pad(member.astype(BF), ((0, 0), (0, 0), (0, 120))).reshape(-1, LANES)

    def of_queries(table):
        if row_mode:
            return table
        table = table.reshape(rows, row_len, LANES)
        return lax.dynamic_slice_in_dim(table, query_start, per_row, 1).reshape(-1, LANES)

    tables_k = (cosine, sine)
    tables_q = (of_queries(cosine), of_queries(sine))
    query_feat = of_queries(query_feat)
    block_first = query_start + BQ * jnp.arange(per_row // BQ, dtype=jnp.int32)[None, :, None]
    low = jnp.max(jnp.where(block_first >= starts[:, None, :], starts[:, None, :], 0), -1)
    high = jnp.min(jnp.where(block_first + BQ - 1 < ends[:, None, :], ends[:, None, :], row_len), -1)
    low = low // LANES * LANES
    count = (high - low + BK - 1) // BK
    low = jnp.minimum(low, row_len - count * BK)
    spans = jnp.stack([low, count], axis=-1).reshape(-1).astype(jnp.int32)

    qkv = weight_pieces(qkv_weight, 0)
    x = to_rows(tokens)
    out_w, swiglu_w, down_w = lax.optimization_barrier((out_weight, swiglu_weight, down_weight, x))[:3]
    outer = weight_pieces(out_w, 0)
    swiglu = weight_pieces(swiglu_w, 0)
    down = weight_pieces(down_w, 0)
    gains = jnp.stack([attn_gain, ffn_gain])
    if row_mode:
        other = lax.ppermute(gains, "fsdp", swap)
        gains = jnp.where(mine == 0, jnp.concatenate([gains, other], 1), jnp.concatenate([other, gains], 1))
    else:
        gains = lax.all_gather(gains, "fsdp", axis=1, tiled=True)
    gain1, gain2 = gains[0:1].astype(F32), gains[1:2].astype(F32)

    query, key, value = project(x, *tables_q, qkv, tile)
    if row_mode:
        key_all, value_all = key, value
    else:

        def along_row(part):
            part = part.reshape(rows, per_row, width)
            return lax.all_gather(part, "fsdp", axis=1, tiled=True).reshape(-1, width)

        key_all, value_all = along_row(key), along_row(value)
    attended, lse = attend(query, key_all, value_all, key_feat, query_feat, spans, rows)
    cot = to_rows(lax.optimization_barrier((cotangent, query))[0])
    low_normed, stat, gate_up, output, sums = mix(
        attended, x, query_feat, gain1, gain2, (outer, swiglu, down), rows, tile
    )
    if not row_mode:
        sums = lax.psum(sums, "fsdp")
    loss, d_pool = contrast(sums, lengths, own_pairing, row_mode, row_ids)
    d_pool = jnp.pad(d_pool, ((0, 0), (0, LANES - SEG), (0, 0)))
    lse_columns = jnp.pad(lse.reshape(HEADS, tokens_here).T, ((0, 0), (0, LANES - HEADS)))
    d_ffn, hidden, d_gate_up, d_branch, d_attended, back_feat, gain1_part, gain2_part = mix_back(
        cot, output, low_normed, stat, query_feat, d_pool, gate_up, attended, lse_columns, gain1, gain2,
        (outer, swiglu, down), rows, tile,
    )
    down_part = dot_at(hidden, d_ffn).astype(BF)
    swiglu_part = dot_at(low_normed, d_gate_up).astype(BF)
    out_part = dot_at(attended, d_branch).astype(BF)
    if not row_mode:
        loss = loss / split
    small = jnp.concatenate([jnp.sum(gain1_part, 0), jnp.sum(gain2_part, 0), jnp.full((LANES,), loss)])
    small = summed_everywhere(small.reshape(-1, LANES))
    d_query, d_key, d_value = attend_back(
        query, d_attended, key_all, value_all, key_feat, back_feat, spans, tables_q, tables_k, rows
    )
    if not row_mode:

        def own_part(grad):
            grad = grad.reshape(rows, row_len, width)
            return lax.psum_scatter(grad, "fsdp", scatter_dimension=1, tiled=True).reshape(-1, width)

        d_key, d_value = own_part(d_key), own_part(d_value)
    grads_in = (d_branch, d_query, d_key, d_value, qkv)
    if row_mode:
        moved = input_grad_part(*grads_in, (1 - mine) * shard_len, shard_len, BF, tile)
        kept = input_grad_part(*grads_in, mine * shard_len, shard_len, F32, tile)
        input_grad = to_shards(kept, moved)
        halves = [lax.dynamic_slice_in_dim(output, h * shard_len, shard_len, 0) for h in (mine, 1 - mine)]
        layer_output = to_shards(*halves)
    else:
        input_grad = input_grad_part(*grads_in, 0, tokens_here, F32, tile).reshape(tokens.shape)
        layer_output = output.reshape(tokens.shape)
    qkv_part = jnp.concatenate([dot_at(x, g).astype(BF) for g in (d_query, d_key, d_value)], axis=1)

    def reduced(part):
        part = lax.psum_scatter(part, "fsdp", scatter_dimension=0, tiled=True)
        return lax.psum(part, "blk").astype(F32)

    small = small.reshape(-1)
    half = width // split
    gain1_grad = lax.dynamic_slice_in_dim(small, mine * half, half, 0)
    gain2_grad = lax.dynamic_slice_in_dim(small, width + mine * half, half, 0)
    queries = lax.axis_size("blk") * pairing.shape[0]
    return (
        small[2 * width] / queries,
        layer_output,
        input_grad,
        reduced(qkv_part),
        reduced(out_part),
        reduced(swiglu_part),
        reduced(down_part),
        gain1_grad,
        gain2_grad,
    )


def solution(mesh):
    in_specs = (
        P("blk", "fsdp", None),
        P("blk", "fsdp", None),
        P("blk", "fsdp"),
        P("blk", None),
        P("blk", "fsdp"),
        P("blk"),
        P("fsdp", None),
        P("fsdp", None),
        P("fsdp", None),
        P("fsdp", None),
        P("fsdp"),
        P("fsdp"),
    )
    out_specs = (
        P(),
        P("blk", "fsdp", None),
        P("blk", "fsdp", None),
        P("fsdp", None),
        P("fsdp", None),
        P("fsdp", None),
        P("fsdp", None),
        P("fsdp"),
        P("fsdp"),
    )
    return jax.shard_map(shards, mesh=mesh, in_specs=in_specs, out_specs=out_specs, check_vma=False)
```

time: 2120 us -> 1140 us (0.54)
  matrix products: 831 us -> 58.7 us
  Pallas kernels: 0 us -> 487 us
  waiting for transfers between devices: 786 us -> 405 us
  other arithmetic: 225 us -> 58.3 us
  local copies, waits for them, and re-layouts: 185 us -> 63.7 us
  blocking collectives: 55.7 us -> 0 us
  starting transfers between devices: 2.5 us -> 46.1 us
    dot_general x106 -> x9, matrix products: 831 us -> 58.7 us  [the longest x7 58 us: dot_at(): lax.dot_general(a, b, (((0,), (0,)), ((), ())), preferred_element_type=F32)]
    pallas_call x0 -> x7, Pallas kernels: none -> 487 us  [the longest x1 181 us: attend_back(): pl.pallas_call(attend_back_kernel, grid_spec=pltpu.PrefetchScalarGridSpec...]
    all_gather x6 -> x0, waiting for transfers between devices: 188 us -> none  [the longest x1 82.5 us: shards(): value_piece = lax.all_gather(value_low, 'fsdp', axis=1, tiled=True)]
    reduce_sum x27 -> x6, other arithmetic: 109 us -> 1.87 us  [the longest x1 0.93 us: contrast(): jnp.sum(pooled * pooled, -1, keepdims=True) + EMB_EPSILON]
    ppermute x47 -> x31, waiting for transfers between devices: 178 us -> 80.8 us  [the longest x10 39.3 us: flipped(): return lax.ppermute(block, axis, route)]
    reduce_scatter x5 -> x3, waiting for transfers between devices: 282 us -> 197 us  [reduced(): part = lax.psum_scatter(part, 'fsdp', scatter_dimension=0, tiled=True)]
    convert_element_type x9 -> x0, local copies, waits for them, and re-layouts: 54.5 us -> none  [the longest x2 22.4 us: shards(): value_grad_all.astype(jnp.bfloat16)]
    ppermute x47 -> x31, starting transfers between devices: 1.8 us -> 45.9 us  [the longest x10 18 us: flipped(): return lax.ppermute(block, axis, route)]
  transfers between devices with their start and end apart: 60 -> 36, of which waited for: 40 -> 20; matrix products, arithmetic and copies ran while one was open for 25% -> 10% of each run, Pallas kernels for 0% -> 16%
where the time goes in v1:
time: 1140 us
  Pallas kernels  487 us (43%)
  waiting for transfers between devices  405 us (36%)
  local copies, waits for them, and re-layouts  63.7 us (6%)
  matrix products  58.7 us (5%)
  other arithmetic  58.3 us (5%)
  starting transfers between devices  46.1 us (4%)
  between operations  16.8 us (1%)
    reduce_scatter x3, waiting for transfers between devices, reduced(): part = lax.psum_scatter(part, 'fsdp', scatter_dimension=0, tiled=True)  197 us
    pallas_call x1, Pallas kernels, attend_back(): pl.pallas_call(attend_back_kernel, grid_spec=pltpu.PrefetchScalarGridSpec...  181 us
    pallas_call x1, Pallas kernels, attend(): pl.pallas_call(attend_kernel, grid_spec=pltpu.PrefetchScalarGridSpec(num_...  158 us
    psum x1, waiting for transfers between devices, reduced(): return lax.psum(part, 'blk').astype(F32)  113 us
    pallas_call x1, Pallas kernels, mix_back(): pl.pallas_call(functools.partial(mix_back_kernel, counts), grid_spec=pltp...  64.3 us
    dot_general x7, matrix products, dot_at(): lax.dot_general(a, b, (((0,), (0,)), ((), ())), preferred_element_type=F32)  58 us
    pallas_call x1, Pallas kernels, mix(): pl.pallas_call(functools.partial(mix_kernel, counts), grid_spec=pltpu.Pre...  56.2 us
    unnamed x110, local copies, waits for them, and re-layouts  44.4 us
  transfers between devices with their start and end apart: 36, of which 20 were waited for; matrix products, arithmetic and copies ran while one was open for 10% of the time, Pallas kernels for 16%

profile of v1, /device:TPU:0, one launch (start us, length us, event | category | flops | bytes accessed | tf_op | source)
XLA Modules:
  0.0 1135.5 jit_solution(9090098052134349269)
XLA Ops:
  22.7 15.7 %fusion.23 = s32[256]{0:T(256)S(1)} fusion(pred[256]{0:T(512)(128)(4,1)S(1)} %get-tuple-element.133, pred[256]{0:T(512)(128)(4,1)S(1)} %get-tuple-element.132, pred[256]{0:T(512)(128)(4,1)S(1)} %get-tuple-element.131, pred[256]{0:T(512)(128)(4,1)S(1)} %get-tuple-element.130, pred[256]{0:T(512)(128)(4,1)S(1)} %get-tuple-element.129, ...), kind=kLoop, calls=%fused_computation.159 | loop fusion | flops 14592 | bytes 9580 | tf_op jit(solution)/shard_map/add | solution.py:722
  40.5 8.0 collective-permute-done
  60.9 7.5 collective-permute-done.2.rest_2_
  68.5 3.7 fusion.4
  76.6 7.2 collective-permute-done.11.rest_6_
  85.8 12.8 %shard_map.169 = (bf16[2048,768]{1,0:T(8,128)(2,1)S(1)}, bf16[2048,768]{1,0:T(8,128)(2,1)S(1)}, bf16[2048,768]{1,0:T(8,128)(2,1)}) custom-call(s32[10]{0:T(128)S(1)} %stack.73.table, bf16[2048,768]{1,0:T(8,128)(2,1)} %pad_maximum_fusion.2.x_ref, f32[2048,128]{1,0:T(8,128)S(1)} %get-tuple-element.159.cos_ref.cq_ref.ck_ref, ...), custom_call_target="tpu_custom_call" | custom-call | flops 7247757312 | bytes 16777216 | tf_op jit(solution)/shard_map/pallas_call | solution.py:128
  108.4 16.9 %collective-permute-done.8.rest_2_ = bf16[192,384]{1,0:T(8,128)(2,1)S(1)} collective-permute-done((bf16[192,384]{1,0:T(8,128)(2,1)}, bf16[192,384]{1,0:T(8,128)(2,1)S(1)}, u32[]{:S(2)}, u32[]{:S(2)}) %collective-permute-start.8) | collective-permute-done | bytes 147488 | tf_op jit(solution)/shard_map/ppermute | solution.py:62
  132.0 158.0 %shard_map.170 = (bf16[2048,768]{1,0:T(8,128)(2,1)S(1)}, f32[6,2,2048]{2,1,0:T(2,128)S(1)}) custom-call(s32[16]{0:T(128)S(1)} %reshape.1101.spans, bf16[2048,768]{1,0:T(8,128)(2,1)S(1)} %copy-done.27, bf16[2048,768]{1,0:T(8,128)(2,1)S(1)} %copy-done.29, bf16[2048,768]{1,0:T(8,128)(2,1)S(1)} %copy-done.30, bf16[2048,128]{1,0:T(8,128)(2,1)S(1)} %copy-done.24, ...), custom_call_target="tpu_custom_call" | custom-call | flops 12884901888 | bytes 16777216 | tf_op jit(solution)/shard_map/pallas_call | solution.py:253
  293.2 9.4 collective-permute-start.10
  305.4 56.2 %shard_map.171 = (bf16[2048,768]{1,0:T(8,128)(2,1)}, f32[2048,128]{1,0:T(8,128)}, bf16[2048,6144]{1,0:T(8,128)(2,1)}, bf16[2048,768]{1,0:T(8,128)(2,1)}, f32[1,8,768]{2,1,0:T(8,128)}) custom-call(s32[30]{0:T(128)} %stack.70.table, bf16[2048,768]{1,0:T(8,128)(2,1)} %copy-done.25, bf16[2048,768]{1,0:T(8,128)(2,1)} %pad_maximum_fusion.2.x_ref, ...), custom_call_target="tpu_custom_call" | custom-call | flops 31406948352 | bytes 67108864 | tf_op jit(solution)/shard_map/pallas_call | solution.py:489
  373.9 3.6 collective-permute-done.22
  377.6 6.6 collective-permute-start.23
  386.1 7.0 collective-permute-done.23
  395.4 64.3 %shard_map.172 = (bf16[2048,768]{1,0:T(8,128)(2,1)}, bf16[2048,3072]{1,0:T(8,128)(2,1)}, bf16[2048,6144]{1,0:T(8,128)(2,1)}, bf16[2048,768]{1,0:T(8,128)(2,1)}, ...) custom-call(s32[30]{0:T(128)} %stack.70.table, ...), custom_call_target="tpu_custom_call" | custom-call | flops 31406948352 | bytes 100663296 | tf_op jit(solution)/shard_map/pallas_call | solution.py:625
  460.8 180.6 %shard_map.173 = (bf16[2048,768]{1,0:T(8,128)(2,1)}, bf16[2048,768]{1,0:T(8,128)(2,1)}, bf16[2048,768]{1,0:T(8,128)(2,1)}) custom-call(s32[16]{0:T(128)S(1)} %reshape.1101.spans, bf16[2048,768]{1,0:T(8,128)(2,1)} %copy-done.26, bf16[2048,768]{1,0:T(8,128)(2,1)} %get-tuple-element.63.do_ref, bf16[2048,768]{1,0:T(8,128)(2,1)} %copy-done.28, ...), custom_call_target="tpu_custom_call" | custom-call | flops 32212254720 | bytes 25165824 | tf_op jit(solution)/shard_map/pallas_call | solution.py:359
  641.5 4.7 convolution_convert_fusion.3
  652.0 3.8 copy.51
  657.7 5.6 convolution_convert_fusion.2
  663.4 15.7 %convolution_convert_fusion.1 = bf16[3072,768]{1,0:T(8,128)(2,1)} fusion(bf16[2048,3072]{1,0:T(8,128)(2,1)} %get-tuple-element.69, bf16[2048,768]{1,0:T(8,128)(2,1)} %get-tuple-element.70), kind=kOutput, calls=%fused_computation.2 | convolution fusion | flops 9666035712 | bytes 20447232 | tf_op jit(solution)/shard_map/dot_general | solution.py:38
  679.2 26.4 %convolution_convert_fusion = bf16[768,6144]{1,0:T(8,128)(2,1)} fusion(bf16[2048,768]{1,0:T(8,128)(2,1)} %get-tuple-element.55.nl_ref, bf16[2048,6144]{1,0:T(8,128)(2,1)} %get-tuple-element.68), kind=kOutput, calls=%fused_computation | convolution fusion | flops 19332071424 | bytes 37748736 | tf_op jit(solution)/shard_map/dot_general | solution.py:38
  705.7 14.2 %reduce-scatter.13.cloned.1.call-done = bf16[384,2304]{1,0:T(8,128)(2,1)} async-done(((bf16[768,2304]{1,0:T(8,128)(2,1)}), bf16[384,2304]{1,0:T(8,128)(2,1)}) %reduce-scatter.13.cloned.1.call-update) | async-done | bytes 1769488
  719.9 4.1 copy.52
  724.0 20.6 %reduce-scatter.7.cloned.1.call-done = bf16[384,768]{1,0:T(8,128)(2,1)} async-done(((bf16[768,768]{1,0:T(8,128)(2,1)}), bf16[384,768]{1,0:T(8,128)(2,1)}) %reduce-scatter.7.cloned.1.call-update) | async-done | bytes 589840 | tf_op jit(solution)/shard_map/reduce_scatter | solution.py:898
  744.6 62.9 %reduce-scatter.11.cloned.1.call-done = bf16[1536,768]{1,0:T(8,128)(2,1)} async-done(((bf16[3072,768]{1,0:T(8,128)(2,1)}), bf16[1536,768]{1,0:T(8,128)(2,1)}) %reduce-scatter.11.cloned.1.call-update) | async-done | bytes 2359312 | tf_op jit(solution)/shard_map/reduce_scatter | solution.py:898
  807.5 113.4 %reduce-scatter.9.cloned.1.call-done = bf16[384,6144]{1,0:T(8,128)(2,1)} async-done(((bf16[768,6144]{1,0:T(8,128)(2,1)}), bf16[384,6144]{1,0:T(8,128)(2,1)}) %reduce-scatter.9.cloned.1.call-update) | async-done | bytes 4718608 | tf_op jit(solution)/shard_map/reduce_scatter | solution.py:898
  937.0 7.5 shard_map.175
  944.5 16.9 %collective-permute-done.24 = f32[13,128]{1,0:T(8,128)S(1)} collective-permute-done((f32[13,128]{1,0:T(8,128)S(1)}, f32[13,128]{1,0:T(8,128)S(1)}, u32[]{:S(2)}, u32[]{:S(2)}) %collective-permute-start.24) | collective-permute-done | bytes 6688 | tf_op jit(solution)/shard_map/ppermute | solution.py:683
  980.3 7.2 shard_map.174
  995.9 3.1 pad_maximum_fusion
  999.1 113.2 %all-reduce.8.cloned.1.call-done = (bf16[384,2304]{0,1:T(8,128)(2,1)}, bf16[384,768]{1,0:T(8,128)(2,1)}, bf16[384,6144]{1,0:T(8,128)(2,1)}, bf16[1536,768]{1,0:T(8,128)(2,1)}) async-done(((bf16[384,2304]{0,1:T(8,128)(2,1)}, bf16[384,768]{1,0:T(8,128)(2,1)}, bf16[384,6144]{1,0:T(8,128)(2,1)}, bf16[1536,768]{1,0:T(8,128)(2,1)}), (bf16[384,2304]{0,1:T(8,128)(2,1)}, bf16[384,768]{1,0:T(8,128)(2,1)}, ...) | async-done | bytes 9437200 | tf_op jit(solution)/shard_map/psum | solution.py:899
  1112.2 4.1 copy.50
  1117.4 7.4 convert_element_type.118
  (270 shorter events, 130.1 us)
Async XLA Ops:
  7.2 712.6 %reduce-scatter.13.cloned.1.call-start = ((), (), s32[]{:S(2)}) async-start(), calls=%async_computation.7 | async-start | bytes 5308416
  10.1 38.5 %collective-permute-start = (bf16[1024,768]{1,0:T(8,128)(2,1)}, bf16[1024,768]{1,0:T(8,128)(2,1)}, u32[]{:S(2)}, u32[]{:S(2)}) collective-permute-start(bf16[1024,768]{1,0:T(8,128)(2,1)} %dynamic-slice_bitcast_fusion.1), channel_id=1, source_target_pairs={{0,1},{1,0},{2,3},{3,2},{4,5},{5,4},{6,7},{7,6},{8,9},{9,8},{10,11... | collective-permute-start | bytes 4718600 | tf_op jit(solution)/shard_map/ppermute | solution.py:774
  13.1 44.9 %collective-permute-start.1 = (bf16[192,1152]{1,0:T(8,128)(2,1)S(1)}, bf16[192,1152]{1,0:T(8,128)(2,1)S(1)}, u32[]{:S(2)}, u32[]{:S(2)}) collective-permute-start(bf16[192,1152]{1,0:T(8,128)(2,1)S(1)} %dynamic_slice.46), channel_id=1, source_target_pairs={{0,1},{1,0},{2,3},{3,2},{4,5},{5,4},{6,7},{7,6},{8,9},{9,8},{10,11... | collective-permute-start | bytes 1327112 | tf_op jit(solution)/shard_map/ppermute | solution.py:61
  13.2 93.0 %collective-permute-start.6 = (bf16[2,384]{1,0:T(2,128)(2,1)S(1)}, bf16[2,384]{1,0:T(2,128)(2,1)S(1)}, u32[]{:S(2)}, u32[]{:S(2)}) collective-permute-start(bf16[2,384]{1,0:T(2,128)(2,1)S(1)} %pad_maximum_fusion.9), channel_id=1, source_target_pairs={{0,1},{1,0},{2,3},{3,2},{4,5},{5,4},{6,7},{7,6},{8,9},{9,8},{10,11... | collective-permute-start | bytes 4616 | tf_op jit(solution)/shard_map/ppermute | solution.py:838
  54.7 29.1 %collective-permute-start.11 = (bf16[192,3072]{1,0:T(8,128)(2,1)S(1)}, bf16[192,3072]{1,0:T(8,128)(2,1)}, u32[]{:S(2)}, u32[]{:S(2)}) collective-permute-start(bf16[192,3072]{1,0:T(8,128)(2,1)S(1)} %dynamic_slice.50), channel_id=1, source_target_pairs={{0,1},{1,0},{2,3},{3,2},{4,5},{5,4},{6,7},{7,6},{8,9},{9,8},{10,11... | collective-permute-start | bytes 3538952 | tf_op jit(solution)/shard_map/ppermute | solution.py:61
  57.9 10.5 collective-permute-start.2
  60.9 15.0 %collective-permute-start.3 = (bf16[192,1152]{1,0:T(8,128)(2,1)S(1)}, bf16[192,1152]{1,0:T(8,128)(2,1)S(1)}, u32[]{:S(2)}, u32[]{:S(2)}) collective-permute-start(bf16[192,1152]{1,0:T(8,128)(2,1)S(1)} %collective-permute-done.1.rest_1_), channel_id=1, source_target_pairs={{0,2},{2,0},{4,6},{6,4},{8,10},{10,8},{12,14},{14,12},{16,18},{18,... | collective-permute-start | bytes 1327112 | tf_op jit(solution)/shard_map/ppermute | solution.py:64
  68.5 17.3 %collective-permute-start.4 = (bf16[192,1152]{1,0:T(8,128)(2,1)S(1)}, bf16[192,1152]{1,0:T(8,128)(2,1)S(1)}, u32[]{:S(2)}, u32[]{:S(2)}) collective-permute-start(bf16[192,1152]{1,0:T(8,128)(2,1)S(1)} %collective-permute-done.2.rest_2_), channel_id=1, source_target_pairs={{0,2},{2,0},{4,6},{6,4},{8,10},{10,8},{12,14},{14,12},{16,18},{18,... | collective-permute-start | bytes 1327112 | tf_op jit(solution)/shard_map/ppermute | solution.py:65
  73.3 32.9 %collective-permute-start.7 = (bf16[192,384]{1,0:T(8,128)(2,1)S(1)}, bf16[192,384]{1,0:T(8,128)(2,1)}, u32[]{:S(2)}, u32[]{:S(2)}) collective-permute-start(bf16[192,384]{1,0:T(8,128)(2,1)S(1)} %dynamic_slice.49), channel_id=1, source_target_pairs={{0,1},{1,0},{2,3},{3,2},{4,5},{5,4},{6,7},{7,6},{8,9},{9,8},{10,11... | collective-permute-start | bytes 442376 | tf_op jit(solution)/shard_map/ppermute | solution.py:61
  75.9 26.0 %collective-permute-start.15 = (bf16[768,384]{1,0:T(8,128)(2,1)S(1)}, bf16[768,384]{1,0:T(8,128)(2,1)}, u32[]{:S(2)}, u32[]{:S(2)}) collective-permute-start(bf16[768,384]{1,0:T(8,128)(2,1)S(1)} %dynamic_slice.51), channel_id=1, source_target_pairs={{0,1},{1,0},{2,3},{3,2},{4,5},{5,4},{6,7},{7,6},{8,9},{9,8},{10,11... | collective-permute-start | bytes 1769480 | tf_op jit(solution)/shard_map/ppermute | solution.py:61
  83.8 42.1 %collective-permute-start.12 = (bf16[192,3072]{1,0:T(8,128)(2,1)}, bf16[192,3072]{1,0:T(8,128)(2,1)}, u32[]{:S(2)}, u32[]{:S(2)}) collective-permute-start(bf16[192,3072]{1,0:T(8,128)(2,1)} %collective-permute-done.11.rest_6_), channel_id=1, source_target_pairs={{0,4},{2,6},{4,0},{6,2},{8,12},{10,14},{12,8},{14,10},{16,20},{18,... | collective-permute-start | bytes 3538952 | tf_op jit(solution)/shard_map/ppermute | solution.py:62
  102.0 23.8 %collective-permute-start.16 = (bf16[768,384]{1,0:T(8,128)(2,1)}, bf16[768,384]{1,0:T(8,128)(2,1)}, u32[]{:S(2)}, u32[]{:S(2)}) collective-permute-start(bf16[768,384]{1,0:T(8,128)(2,1)} %collective-permute-done.15.rest_11_), channel_id=1, source_target_pairs={{0,4},{2,6},{4,0},{6,2},{8,12},{10,14},{12,8},{14,10},{16,20},{18,... | collective-permute-start | bytes 1769480 | tf_op jit(solution)/shard_map/ppermute | solution.py:62
  103.3 189.9 %collective-permute-start.5 = (bf16[1024,768]{1,0:T(8,128)(2,1)}, bf16[1024,768]{1,0:T(8,128)(2,1)}, u32[]{:S(2)}, u32[]{:S(2)}) collective-permute-start(bf16[1024,768]{1,0:T(8,128)(2,1)} %dynamic-slice_bitcast_fusion), channel_id=1, source_target_pairs={{0,1},{1,0},{2,3},{3,2},{4,5},{5,4},{6,7},{7,6},{8,9},{9,8},{10,11... | collective-permute-start | bytes 4718600 | tf_op jit(solution)/shard_map/ppermute | solution.py:774
  106.2 19.1 %collective-permute-start.8 = (bf16[192,384]{1,0:T(8,128)(2,1)}, bf16[192,384]{1,0:T(8,128)(2,1)S(1)}, u32[]{:S(2)}, u32[]{:S(2)}) collective-permute-start(bf16[192,384]{1,0:T(8,128)(2,1)} %collective-permute-done.7.rest_1_), channel_id=1, source_target_pairs={{0,4},{2,6},{4,0},{6,2},{8,12},{10,14},{12,8},{14,10},{16,20},{18,... | collective-permute-start | bytes 442376 | tf_op jit(solution)/shard_map/ppermute | solution.py:62
  107.8 17.5 %collective-permute-start.9 = (bf16[192,384]{1,0:T(8,128)(2,1)}, bf16[192,384]{1,0:T(8,128)(2,1)S(1)}, u32[]{:S(2)}, u32[]{:S(2)}) collective-permute-start(bf16[192,384]{1,0:T(8,128)(2,1)} %collective-permute-done.7.rest_1_), channel_id=1, source_target_pairs={{0,2},{2,0},{4,6},{6,4},{8,10},{10,8},{12,14},{14,12},{16,18},{18,... | collective-permute-start | bytes 442376 | tf_op jit(solution)/shard_map/ppermute | solution.py:64
  125.3 179.5 %collective-permute-start.17 = (bf16[768,384]{1,0:T(8,128)(2,1)}, bf16[768,384]{1,0:T(8,128)(2,1)}, u32[]{:S(2)}, u32[]{:S(2)}) collective-permute-start(bf16[768,384]{1,0:T(8,128)(2,1)} %collective-permute-done.15.rest_11_), channel_id=1, source_target_pairs={{0,2},{2,0},{4,6},{6,4},{8,10},{10,8},{12,14},{14,12},{16,18},{18,... | collective-permute-start | bytes 1769480 | tf_op jit(solution)/shard_map/ppermute | solution.py:64
  125.3 179.5 %collective-permute-start.13 = (bf16[192,3072]{1,0:T(8,128)(2,1)}, bf16[192,3072]{1,0:T(8,128)(2,1)}, u32[]{:S(2)}, u32[]{:S(2)}) collective-permute-start(bf16[192,3072]{1,0:T(8,128)(2,1)} %collective-permute-done.11.rest_6_), channel_id=1, source_target_pairs={{0,2},{2,0},{4,6},{6,4},{8,10},{10,8},{12,14},{14,12},{16,18},{18,... | collective-permute-start | bytes 3538952 | tf_op jit(solution)/shard_map/ppermute | solution.py:64
  125.8 179.0 %collective-permute-start.18 = (bf16[768,384]{1,0:T(8,128)(2,1)}, bf16[768,384]{1,0:T(8,128)(2,1)}, u32[]{:S(2)}, u32[]{:S(2)}) collective-permute-start(bf16[768,384]{1,0:T(8,128)(2,1)} %collective-permute-done.16.rest_12_), channel_id=1, source_target_pairs={{0,2},{2,0},{4,6},{6,4},{8,10},{10,8},{12,14},{14,12},{16,18},{18,... | collective-permute-start | bytes 1769480 | tf_op jit(solution)/shard_map/ppermute | solution.py:65
  125.9 178.9 %collective-permute-start.14 = (bf16[192,3072]{1,0:T(8,128)(2,1)}, bf16[192,3072]{1,0:T(8,128)(2,1)}, u32[]{:S(2)}, u32[]{:S(2)}) collective-permute-start(bf16[192,3072]{1,0:T(8,128)(2,1)} %collective-permute-done.12.rest_7_), channel_id=1, source_target_pairs={{0,2},{2,0},{4,6},{6,4},{8,10},{10,8},{12,14},{14,12},{16,18},{18,... | collective-permute-start | bytes 3538952 | tf_op jit(solution)/shard_map/ppermute | solution.py:65
  293.2 11.5 %collective-permute-start.10 = (bf16[192,384]{1,0:T(8,128)(2,1)S(1)}, bf16[192,384]{1,0:T(8,128)(2,1)S(1)}, u32[]{:S(2)}, u32[]{:S(2)}) collective-permute-start(bf16[192,384]{1,0:T(8,128)(2,1)S(1)} %collective-permute-done.8.rest_2_), channel_id=1, source_target_pairs={{0,2},{2,0},{4,6},{6,4},{8,10},{10,8},{12,14},{14,12},{16,18},{18,... | collective-permute-start | bytes 442376 | tf_op jit(solution)/shard_map/ppermute | solution.py:65
  368.5 4.2 collective-permute-start.21
  372.7 4.8 collective-permute-start.22
  377.6 15.5 %collective-permute-start.23 = (bf16[128,896]{1,0:T(8,128)(2,1)S(1)}, bf16[128,896]{1,0:T(8,128)(2,1)S(1)}, u32[]{:S(2)}, u32[]{:S(2)}) collective-permute-start(bf16[128,896]{1,0:T(8,128)(2,1)S(1)} %get-tuple-element.150), channel_id=1, source_target_pairs={{0,16},{2,18},{4,20},{6,22},{8,24},{10,26},{12,28},{14,30},{16,0},... | collective-permute-start | bytes 688136 | tf_op jit(solution)/shard_map/ppermute | solution.py:683
  655.8 88.7 %reduce-scatter.7.cloned.1.call-start = ((), (), s32[]{:S(2)}) async-start(), calls=%async_computation.4 | async-start | bytes 1769472 | tf_op jit(solution)/shard_map/reduce_scatter | solution.py:898
  663.3 144.2 %reduce-scatter.11.cloned.1.call-start = ((), (), s32[]{:S(2)}) async-start(), calls=%async_computation.6 | async-start | bytes 7077888 | tf_op jit(solution)/shard_map/reduce_scatter | solution.py:898
  679.1 241.8 %reduce-scatter.9.cloned.1.call-start = ((), (), s32[]{:S(2)}) async-start(), calls=%async_computation.5 | async-start | bytes 14155776 | tf_op jit(solution)/shard_map/reduce_scatter | solution.py:898
  705.6 406.6 %all-reduce.8.cloned.1.call-start = ((), (), s32[]{:S(2)}) async-start(), calls=%async_computation.8 | async-start | bytes 18874368 | tf_op jit(solution)/shard_map/psum | solution.py:899
  923.7 65.6 %collective-permute-start.29 = (bf16[1024,768]{1,0:T(8,128)(2,1)}, bf16[1024,768]{1,0:T(8,128)(2,1)}, u32[]{:S(2)}, u32[]{:S(2)}) collective-permute-start(bf16[1024,768]{1,0:T(8,128)(2,1)} %constant_dynamic-slice_fusion), channel_id=1, source_target_pairs={{0,1},{1,0},{2,3},{3,2},{4,5},{5,4},{6,7},{7,6},{8,9},{9,8},{10,11... | collective-permute-start | bytes 4718600 | tf_op jit(solution)/shard_map/ppermute | solution.py:777
  925.3 36.0 %collective-permute-start.24 = (f32[13,128]{1,0:T(8,128)S(1)}, f32[13,128]{1,0:T(8,128)S(1)}, u32[]{:S(2)}, u32[]{:S(2)}) collective-permute-start(f32[13,128]{1,0:T(8,128)S(1)} %maximum_bitcast_fusion), channel_id=1, source_target_pairs={{0,1},{1,0},{2,3},{3,2},{4,5},{5,4},{6,7},{7,6},{8,9},{9,8},{10,11... | collective-permute-start | bytes 19976 | tf_op jit(solution)/shard_map/ppermute | solution.py:683
  944.4 49.6 %collective-permute-start.30 = (bf16[1024,768]{1,0:T(8,128)(2,1)}, bf16[1024,768]{1,0:T(8,128)(2,1)}, u32[]{:S(2)}, u32[]{:S(2)}) collective-permute-start(bf16[1024,768]{1,0:T(8,128)(2,1)} %shard_map.175), channel_id=1, source_target_pairs={{0,1},{1,0},{2,3},{3,2},{4,5},{5,4},{6,7},{7,6},{8,9},{9,8},{10,11... | collective-permute-start | bytes 4718600 | tf_op jit(solution)/shard_map/ppermute | solution.py:777
  966.3 4.0 collective-permute-start.27
  970.3 17.2 %collective-permute-start.28 = (f32[13,128]{1,0:T(8,128)S(1)}, f32[13,128]{1,0:T(8,128)S(1)}, u32[]{:S(2)}, u32[]{:S(2)}) collective-permute-start(f32[13,128]{1,0:T(8,128)S(1)} %add.416), channel_id=1, source_target_pairs={{0,16},{2,18},{4,20},{6,22},{8,24},{10,26},{12,28},{14,30},{16,0},... | collective-permute-start | bytes 19976 | tf_op jit(solution)/shard_map/ppermute | solution.py:683
  (55 other events, 932.6 us)
Sparse Core Ops, SparseCore 0:
  656.0 63.8 reduce-scatter.12
  722.8 21.7 reduce-scatter.6
  747.5 59.9 reduce-scatter.10
  810.3 110.5 reduce-scatter.8
  925.9 186.2 all-reduce.7

commit v2 on v1

v2 whole, which is shorter than its diff:
```python
import functools
import math

import jax
import jax.numpy as jnp
from jax import lax
from jax.experimental import pallas as pl
from jax.experimental.pallas import tpu as pltpu
from jax.sharding import PartitionSpec as P

HEADS = 12
HDIM = 64
PAIRS = HEADS // 2
LANES = 128
SEG = 8

EPSILON = 1e-05
EMB_EPSILON = 1e-06
SOFTMAX_WARMTH = 0.05
ROPE_BASE = 1000.0
CONTRAST_WEIGHT = 512.0
NEGATIVE = -1e30

BF = jnp.bfloat16
F32 = jnp.float32
MIB = 1 << 20
CHEAP = pl.CostEstimate(flops=1024, bytes_accessed=1024, transcendentals=0)


def cost(flops):
    return pl.CostEstimate(flops=4 * flops, bytes_accessed=MIB, transcendentals=0)


def dot(a, b):
    return lax.dot_general(a, b, (((1,), (0,)), ((), ())), preferred_element_type=F32)


def dot_bt(a, b):
    return lax.dot_general(a, b, (((1,), (1,)), ((), ())), preferred_element_type=F32)


def dot_at(a, b):
    return lax.dot_general(a, b, (((0,), (0,)), ((), ())), preferred_element_type=F32)


def lane_iota(shape):
    return lax.broadcasted_iota(jnp.int32, shape, len(shape) - 1)


def halves_swapped(block):
    low = lane_iota(block.shape) % HDIM < HDIM // 2
    return jnp.where(low, pltpu.roll(block, LANES - 32, 1), pltpu.roll(block, 32, 1))


def flipped(block, axis, bit):
    route = [(i, i ^ bit) for i in range(lax.axis_size(axis))]
    return lax.ppermute(block, axis, route)


def take(array, index, dim):
    return lax.dynamic_index_in_dim(array, index, dim, keepdims=False)


class Weight:
    def __init__(self, pieces, offsets, shape):
        self.pieces, self.offsets, self.shape = pieces, offsets, shape


def whole_weight(weight):
    rows, cols = weight.shape
    shape = (rows * lax.axis_size("fsdp"), cols)
    return Weight([lax.all_gather(weight, "fsdp", axis=0, tiled=True)], [(0, 0)], shape)


def half_of(weight, shift):
    half = weight.shape[0] // 2
    return lax.dynamic_slice_in_dim(weight, lax.axis_index("blk") % 2 * half + shift, half, 0)


def from_halves(weight, first):
    rows, cols = weight.shape
    core, mine = lax.axis_index("blk") % 2, lax.axis_index("fsdp")
    second = flipped(first, "blk", 1)
    other = (1 - mine) * rows
    offsets = [
        (mine * rows, 0),
        (other + core * (rows // 2), 0),
        (other + (1 - core) * (rows // 2), 0),
    ]
    return Weight([weight, first, second], offsets, (2 * rows, cols))


def share_of(weight, shift=0):
    share = weight.shape[0] // lax.axis_size("blk")
    return lax.dynamic_slice_in_dim(weight, lax.axis_index("blk") * share + shift, share, 0)


def from_shares(weight, share):
    rows, cols = weight.shape
    mine = lax.axis_index("fsdp")
    other = lax.all_gather(share, "blk", axis=0, tiled=True)
    return Weight([weight, other], [(mine * rows, 0), ((1 - mine) * rows, 0)], (2 * rows, cols))


def as_table(offsets):
    return jnp.stack([jnp.asarray(v, jnp.int32) for pair in offsets for v in pair])


def weight_copies(table, base, pieces, whole, sems):
    copies = []
    for n, piece in enumerate(pieces):
        rows, cols = piece.shape
        row = pl.multiple_of(table[2 * (base + n)], 16)
        col = pl.multiple_of(table[2 * (base + n) + 1], LANES)
        copies.append(
            pltpu.make_async_copy(
                piece, whole.at[pl.ds(row, rows), pl.ds(col, cols)], sems.at[base + n]
            )
        )
    return copies


def grouped_copies(counts, table, pieces, wholes, sems):
    groups, base = [], 1
    for count, whole in zip(counts, wholes):
        groups.append(weight_copies(table, base, pieces[base - 1 : base - 1 + count], whole, sems))
        base += count
    return groups


def start_all(*groups):
    for group in groups:
        for copy in group:
            copy.start()


def wait_all(*groups):
    for group in groups:
        for copy in group:
            copy.wait()


def weight_operands(weights, lead, after=()):
    counts = [len(w.pieces) for w in weights] + [len(after)]
    pieces = [p for w in weights for p in w.pieces]
    table = as_table([lead] + [o for w in weights for o in w.offsets])
    scratch = [pltpu.VMEM(w.shape, BF) for w in weights]
    return counts, pieces + list(after), table, scratch + [pltpu.SemaphoreType.DMA((len(pieces) + 1,))]


def zero_after(array):
    return jnp.minimum(jnp.abs(array[(0,) * array.ndim].astype(F32)), 0.0).astype(jnp.int32)


ANY = pl.BlockSpec(memory_space=pl.ANY)


def params(limit_mib):
    return pltpu.CompilerParams(vmem_limit_bytes=limit_mib * MIB)


def tied_kernel(*refs):
    del refs


def tied(values, after=()):
    if len(values) + len(after) < 2:
        return list(values)
    return pl.pallas_call(
        tied_kernel,
        in_specs=[ANY] * (len(values) + len(after)),
        out_specs=[ANY] * len(values),
        out_shape=[jax.ShapeDtypeStruct(v.shape, v.dtype) for v in values],
        input_output_aliases={n: n for n in range(len(values))},
        cost_estimate=CHEAP,
    )(*values, *after)


def row_specs(parts, tile, width, steps):
    if len(parts) == 1:
        return [pl.BlockSpec((tile, width), lambda r, i, *_: (r * steps + i, 0))]
    half = steps // 2

    def kept(r, i, t):
        return jnp.where(i // half == t[0], i % half, jnp.where(t[0] == 0, half - 1, 0)), 0

    def moved(r, i, t):
        return jnp.where(i // half != t[0], i % half, jnp.where(t[0] == 0, 0, half - 1)), 0

    return [pl.BlockSpec((tile, width), kept), pl.BlockSpec((tile, width), moved)]


def row_tile(table, refs):
    if len(refs) == 1:
        return refs[0][...]
    own = pl.program_id(1) // (pl.num_programs(1) // 2) == table[0]
    return jnp.where(own, refs[0][...], refs[1][...])


def qkv_kernel(counts, old, table, cos_ref, sin_ref, in_ref, *rest):
    pieces, rest = rest[: sum(counts)], rest[sum(counts) + old :]
    q_ref, k_ref, v_ref, x_ref, whole, sems = rest
    width = q_ref.shape[1]

    @pl.when(pl.program_id(0) == 0)
    def _():
        groups = grouped_copies(counts, table, pieces, [whole], sems)
        start_all(*groups)
        wait_all(*groups)

    x = in_ref[...]
    x_ref[...] = x
    cosine, sine = cos_ref[...], sin_ref[...]
    for ref, start, factor in ((q_ref, 0, 1.0 / math.sqrt(HDIM)), (k_ref, width, 1.0)):
        projected = dot(x, whole[:, start : start + width])
        for b in range(0, width, LANES):
            block = projected[:, b : b + LANES]
            turned = block * cosine + halves_swapped(block) * sine
            ref[:, b : b + LANES] = turned.astype(BF) * jnp.asarray(factor, BF)
    v_ref[...] = dot(x, whole[:, 2 * width :]).astype(BF)


def project(x, start, cosine, sine, weight, old, tile, after=()):
    tokens, width = cosine.shape[0], weight.shape[0]
    counts, pieces, table, scratch = weight_operands([weight], (start // tile, 0), after)
    shifted = lambda i, t: (i + t[0], 0)
    narrow, wide = pl.BlockSpec((tile, LANES), shifted), pl.BlockSpec((tile, width), shifted)
    first = 4 + len(pieces)
    return pl.pallas_call(
        functools.partial(qkv_kernel, counts, len(old)),
        grid_spec=pltpu.PrefetchScalarGridSpec(
            num_scalar_prefetch=1,
            grid=(x.shape[0] // tile,),
            in_specs=[narrow, narrow, pl.BlockSpec((tile, width), lambda i, t: (i, 0))] + [ANY] * (len(pieces) + len(old)),
            out_specs=[wide] * 4,
            scratch_shapes=scratch,
        ),
        out_shape=[jax.ShapeDtypeStruct((tokens, width), BF)] * 4,
        input_output_aliases={first + n: n for n in range(len(old))},
        compiler_params=params(48),
        cost_estimate=cost(6 * x.shape[0] * width * width),
    )(table, cosine, sine, x, *pieces, *old)


def input_grad_kernel(counts, groups, table, dbr_ref, *rest):
    grads, rest = rest[: 3 * groups], rest[3 * groups :]
    pieces, (out_ref, whole, sems) = rest[: sum(counts)], rest[sum(counts) :]
    width = dbr_ref.shape[1]

    @pl.when(pl.program_id(0) == 0)
    def _():
        copies = grouped_copies(counts, table, pieces, [whole], sems)
        start_all(*copies)
        wait_all(*copies)

    total = dbr_ref[...].astype(F32)
    for n, ref in enumerate(grads):
        wide = ref.shape[1]
        start = n % 3 * width + n // 3 * wide
        total += dot_bt(ref[...], whole[:, start : start + wide])
    out_ref[...] = total.astype(out_ref.dtype)


def input_grad_part(dbr, grads, weight, start, tokens, dtype, tile, after=()):
    width = dbr.shape[1]
    counts, pieces, table, scratch = weight_operands([weight], (start // tile, 0), after)
    shifted = lambda i, t: (i + t[0], 0)
    return pl.pallas_call(
        functools.partial(input_grad_kernel, counts, len(grads) // 3),
        grid_spec=pltpu.PrefetchScalarGridSpec(
            num_scalar_prefetch=1,
            grid=(tokens // tile,),
            in_specs=[pl.BlockSpec((tile, width), shifted)]
            + [pl.BlockSpec((tile, g.shape[1]), shifted) for g in grads]
            + [ANY] * len(pieces),
            out_specs=pl.BlockSpec((tile, width), lambda i, t: (i, 0)),
            scratch_shapes=scratch,
        ),
        out_shape=jax.ShapeDtypeStruct((tokens, width), dtype),
        compiler_params=params(48),
        cost_estimate=cost(6 * tokens * width * width),
    )(table, dbr, *grads, *pieces)


BQ = 256
BK_FWD = 512
BK_BACK = 256
VROWS = HDIM + 16


def spread_pairs(whole, source, features, group):
    for g in range(group):
        whole[:, 2 * g * LANES : (2 * g + 1) * LANES] = source[:, g * LANES : (g + 1) * LANES]
        whole[:, (2 * g + 1) * LANES : (2 * g + 2) * LANES] = features[...]


def staggered(count, load, work, finish):
    loaded, worked = load(0), None
    for g in range(count):
        ahead = load(g + 1) if g + 1 < count else None
        result = work(g, loaded)
        if worked is not None:
            finish(g - 1, worked)
        worked, loaded = result, ahead
    finish(count - 1, worked)


def attend_kernel(group, extra, spans, q_ref, k_ref, v_ref, kf_ref, qf_ref, *rest):
    o_ref, lse_ref, kx, vt, qx, best, accum = rest[extra:]
    block = pl.program_id(2)
    where = (pl.program_id(0) * pl.num_programs(2) + block) * 2
    row_len = k_ref.shape[0]

    @pl.when(block == 0)
    def _():
        spread_pairs(kx, k_ref, kf_ref, group)
        for g in range(group):
            for b in range(0, row_len, 256):
                turned = v_ref[b : b + 256, g * LANES : (g + 1) * LANES].astype(F32).T.astype(BF)
                for h in range(2):
                    vt[2 * g + h, :HDIM, b : b + 256] = turned[h * HDIM : (h + 1) * HDIM]
                    vt[2 * g + h, HDIM:, b : b + 256] = jnp.ones((16, 256), BF)

    qf = qf_ref[...]
    even = lane_iota(qf.shape) < HDIM
    zero = jnp.zeros_like(qf)
    for g in range(group):
        q = q_ref[:, g * LANES : (g + 1) * LANES]
        qx[g, :BQ, :LANES] = jnp.where(even, q, zero)
        qx[g, BQ:, :LANES] = jnp.where(even, zero, q)
        qx[g, :BQ, LANES:] = qf
        qx[g, BQ:, LANES:] = qf
    best[...] = jnp.full_like(best, NEGATIVE)
    accum[...] = jnp.zeros_like(accum)
    first, count = spans[where], spans[where + 1]

    def step(j, state):
        at = pl.multiple_of(first + j * BK_FWD, LANES)

        def load(g):
            return dot_bt(kx[pl.ds(at, BK_FWD), 2 * g * LANES : 2 * (g + 1) * LANES], qx[g])

        def work(g, scores):
            old = best[g]
            new = jnp.maximum(old, jnp.max(scores, axis=0, keepdims=True))
            best[g] = new
            return jnp.exp(scores - new).astype(BF), jnp.exp(old - new)

        def finish(g, worked):
            soft, factor = worked
            for h in range(2):
                cols = slice(h * BQ, (h + 1) * BQ)
                values = vt[2 * g + h, :, pl.ds(at, BK_FWD)]
                accum[g, :, cols] = accum[g, :, cols] * factor[:, cols] + dot(values, soft[:, cols])

        staggered(group, load, work, finish)
        return state

    lax.fori_loop(0, count, step, 0)
    for g in range(group):
        total = accum[g, HDIM : HDIM + 1]
        lse = best[g] + jnp.log(total)
        lse_ref[2 * g] = lse[:, :BQ]
        lse_ref[2 * g + 1] = lse[:, BQ:]
        turned = accum[g, :HDIM] / total
        turned = jnp.concatenate([turned[:, :BQ], turned[:, BQ:]], axis=0)
        o_ref[:, g * LANES : (g + 1) * LANES] = turned.T.astype(BF)


def attend(q, k, v, key_feat, query_feat, spans, rows, group, after=()):
    tokens, width = q.shape
    row_len = k.shape[0] // rows
    blocks = tokens // rows // BQ
    of_q = lambda r, p, i, *_: (r * blocks + i, p)
    of_k = lambda r, p, i, *_: (r, p)
    wide = group * LANES
    return pl.pallas_call(
        functools.partial(attend_kernel, group, len(after)),
        grid_spec=pltpu.PrefetchScalarGridSpec(
            num_scalar_prefetch=1,
            grid=(rows, PAIRS // group, blocks),
            in_specs=[
                pl.BlockSpec((BQ, wide), of_q),
                pl.BlockSpec((row_len, wide), of_k),
                pl.BlockSpec((row_len, wide), of_k),
                pl.BlockSpec((row_len, LANES), lambda r, p, i, *_: (r, 0)),
                pl.BlockSpec((BQ, LANES), lambda r, p, i, *_: (r * blocks + i, 0)),
            ]
            + [ANY] * len(after),
            out_specs=[
                pl.BlockSpec((BQ, wide), of_q),
                pl.BlockSpec((2 * group, 1, BQ), lambda r, p, i, *_: (p, 0, r * blocks + i)),
            ],
            scratch_shapes=[
                pltpu.VMEM((row_len, 2 * wide), BF),
                pltpu.VMEM((2 * group, VROWS, row_len), BF),
                pltpu.VMEM((group, 2 * BQ, 2 * LANES), BF),
                pltpu.VMEM((group, 1, 2 * BQ), F32),
                pltpu.VMEM((group, VROWS, 2 * BQ), F32),
            ],
        ),
        out_shape=[
            jax.ShapeDtypeStruct((tokens, width), BF),
            jax.ShapeDtypeStruct((HEADS, 1, tokens), F32),
        ],
        compiler_params=params(56),
        cost_estimate=cost(4 * tokens * row_len * width),
    )(spans, q, k, v, key_feat, query_feat, *after)


def attend_back_kernel(
    group, base, extra, spans, q_ref, do_ref, k_ref, v_ref, kf_ref, qf_ref, cq_ref, sq_ref, ck_ref, sk_ref, *rest,
):
    dq_ref, dk_ref, dv_ref, kx, vx, kt, qx, dox, dq_acc, dk_acc, dv_acc = rest[extra:]
    block = pl.program_id(2)
    pair = base + pl.program_id(1) * group
    where = (pl.program_id(0) * pl.num_programs(2) + block) * 2
    row_len = k_ref.shape[0]

    @pl.when(block == 0)
    def _():
        spread_pairs(kx, k_ref, kf_ref, group)
        spread_pairs(vx, v_ref, kf_ref, group)
        for g in range(group):
            for b in range(0, row_len, 256):
                turned = k_ref[b : b + 256, g * LANES : (g + 1) * LANES].astype(F32).T.astype(BF)
                kt[g * LANES : (g + 1) * LANES, b : b + 256] = turned
        dk_acc[...] = jnp.zeros_like(dk_acc)
        dv_acc[...] = jnp.zeros_like(dv_acc)

    qf = qf_ref[...]
    lanes = lane_iota(qf.shape)
    even = lanes < HDIM
    zero = jnp.zeros_like(qf)
    for g in range(group):
        cols = slice(g * LANES, (g + 1) * LANES)
        for whole, source in ((qx, q_ref[:, cols]), (dox, do_ref[:, cols])):
            whole[g, :BQ, :LANES] = jnp.where(even, source, zero)
            whole[g, BQ:, :LANES] = jnp.where(even, zero, source)
        for h in range(2):
            lane = lanes - (2 * (pair + g) + h)
            of_lse = (lanes < SEG) | (lane == 8) | (lane == 20) | (lane == 32)
            of_delta = (lane == 44) | (lane == 56) | (lane == 68)
            qx[g, h * BQ : (h + 1) * BQ, LANES:] = jnp.where(of_lse, qf, zero)
            dox[g, h * BQ : (h + 1) * BQ, LANES:] = jnp.where(of_delta, qf, zero)
    dq_acc[...] = jnp.zeros_like(dq_acc)
    first, count = spans[where], spans[where + 1]

    def step(j, state):
        at = pl.multiple_of(first + j * BK_BACK, LANES)

        def load(g):
            twice = slice(2 * g * LANES, (2 * g + 2) * LANES)
            return dot_bt(kx[pl.ds(at, BK_BACK), twice], qx[g]), dot_bt(vx[pl.ds(at, BK_BACK), twice], dox[g])

        def work(g, loaded):
            probs = jnp.exp(loaded[0])
            return probs.astype(BF), (probs * loaded[1]).astype(BF)

        def finish(g, worked):
            probs, grad = worked
            cols = slice(g * LANES, (g + 1) * LANES)
            dv_acc[pl.ds(at, BK_BACK), cols] += dot(probs, dox[g, :, :LANES])
            dk_acc[pl.ds(at, BK_BACK), cols] += dot(grad, qx[g, :, :LANES])
            for h in range(2):
                rows = slice(g * LANES + h * HDIM, g * LANES + (h + 1) * HDIM)
                dq_acc[rows] += dot(kt[rows, pl.ds(at, BK_BACK)], grad[:, h * BQ : (h + 1) * BQ])

        staggered(group, load, work, finish)
        return state

    lax.fori_loop(0, count, step, 0)
    for g in range(group):
        cols = slice(g * LANES, (g + 1) * LANES)
        dq = dq_acc[cols].T * (1.0 / math.sqrt(HDIM))
        dq_ref[:, cols] = (dq * cq_ref[...] - halves_swapped(dq) * sq_ref[...]).astype(BF)

    @pl.when(block == pl.num_programs(2) - 1)
    def _():
        for b in range(0, row_len, 256):
            part = pl.ds(b, 256)
            cosine, sine = ck_ref[part, :], sk_ref[part, :]
            for g in range(group):
                cols = slice(g * LANES, (g + 1) * LANES)
                dk = dk_acc[part, cols]
                dk_ref[part, cols] = (dk * cosine - halves_swapped(dk) * sine).astype(BF)
            dv_ref[part, :] = dv_acc[part, :].astype(BF)


def attend_back(q, do, k, v, key_feat, query_feat, spans, tables_q, tables_k, rows, group, base, pairs, after=()):
    tokens, width = q.shape
    row_len = k.shape[0] // rows
    blocks = tokens // rows // BQ
    start = base // group
    of_q = lambda r, p, i, *_: (r * blocks + i, start + p)
    of_k = lambda r, p, i, *_: (r, start + p)
    per_q = pl.BlockSpec((BQ, LANES), lambda r, p, i, *_: (r * blocks + i, 0))
    per_k = pl.BlockSpec((row_len, LANES), lambda r, p, i, *_: (r, 0))
    wide = group * LANES
    return pl.pallas_call(
        functools.partial(attend_back_kernel, group, base, len(after)),
        grid_spec=pltpu.PrefetchScalarGridSpec(
            num_scalar_prefetch=1,
            grid=(rows, pairs // group, blocks),
            in_specs=[
                pl.BlockSpec((BQ, wide), of_q),
                pl.BlockSpec((BQ, wide), of_q),
                pl.BlockSpec((row_len, wide), of_k),
                pl.BlockSpec((row_len, wide), of_k),
                per_k,
                per_q,
                per_q,
                per_q,
                per_k,
                per_k,
            ]
            + [ANY] * len(after),
            out_specs=[
                pl.BlockSpec((BQ, wide), lambda r, p, i, *_: (r * blocks + i, p)),
                pl.BlockSpec((row_len, wide), lambda r, p, i, *_: (r, p)),
                pl.BlockSpec((row_len, wide), lambda r, p, i, *_: (r, p)),
            ],
            scratch_shapes=[
                pltpu.VMEM((row_len, 2 * wide), BF),
                pltpu.VMEM((row_len, 2 * wide), BF),
                pltpu.VMEM((wide, row_len), BF),
                pltpu.VMEM((group, 2 * BQ, 2 * LANES), BF),
                pltpu.VMEM((group, 2 * BQ, 2 * LANES), BF),
                pltpu.VMEM((wide, BQ), F32),
                pltpu.VMEM((row_len, wide), F32),
                pltpu.VMEM((row_len, wide), F32),
            ],
        ),
        out_shape=[
            jax.ShapeDtypeStruct((tokens, pairs * LANES), BF),
            jax.ShapeDtypeStruct((rows * row_len, pairs * LANES), BF),
            jax.ShapeDtypeStruct((rows * row_len, pairs * LANES), BF),
        ],
        compiler_params=params(56),
        cost_estimate=cost(8 * tokens * row_len * pairs * LANES),
    )(spans, q, do, k, v, key_feat, query_feat, *tables_q, *tables_k, *after)


FF_CHUNK = 512


def normalize(hidden):
    average = jnp.mean(hidden, -1, keepdims=True)
    centred = hidden - average
    inverse = lax.rsqrt(jnp.mean(centred * centred, -1, keepdims=True) + EPSILON)
    return centred * inverse, inverse


def norm_back(scaled, normalized, inverse):
    return inverse * (
        scaled
        - jnp.mean(scaled, -1, keepdims=True)
        - normalized * jnp.mean(scaled * normalized, -1, keepdims=True)
    )


def split_two(value):
    high = value.astype(BF)
    return high, (value - high.astype(F32)).astype(BF)


def mix_kernel(counts, table, att_ref, x_ref, qf_ref, g1_ref, g2_ref, *rest):
    pieces, rest = rest[: sum(counts)], rest[sum(counts) :]
    nl_ref, stat_ref, hid_ref, fg_ref, fu_ref, out_ref, pool_ref, wo, ws, wd, sems = rest
    groups = grouped_copies(counts, table, pieces, (wo, ws, wd), sems)
    step, begin = pl.program_id(1), (pl.program_id(0) == 0) & (pl.program_id(1) == 0)

    @pl.when(begin)
    def _():
        start_all(*groups)
        wait_all(groups[0])

    branch = dot(att_ref[...], wo[...])
    unit, inverse1 = normalize(x_ref[...].astype(F32) + branch)
    normed = unit * g1_ref[...]
    low = normed.astype(BF)
    nl_ref[...] = low

    @pl.when(begin)
    def _():
        wait_all(*groups[1:])

    ff = wd.shape[0]
    hidden_sum = [normed]

    def load(c):
        cols = slice(c * FF_CHUNK, (c + 1) * FF_CHUNK)
        return dot(low, ws[:, cols]), dot(low, ws[:, ff + c * FF_CHUNK : ff + (c + 1) * FF_CHUNK])

    def work(c, loaded):
        cols = slice(c * FF_CHUNK, (c + 1) * FF_CHUNK)
        gate, up = loaded
        sig = 0.5 + 0.5 * jnp.tanh(0.5 * gate)
        silu = gate * sig
        hidden = (silu * up).astype(BF)
        hid_ref[:, cols] = hidden
        fg_ref[:, cols] = (up * (sig + silu * (1.0 - sig))).astype(BF)
        fu_ref[:, cols] = silu.astype(BF)
        return hidden

    def finish(c, hidden):
        hidden_sum[0] = hidden_sum[0] + dot(hidden, wd[c * FF_CHUNK : (c + 1) * FF_CHUNK, :])

    staggered(ff // FF_CHUNK, load, work, finish)
    unit2, inverse2 = normalize(hidden_sum[0])
    output = unit2 * g2_ref[...]
    out_ref[...] = output.astype(BF)
    lanes = lane_iota(stat_ref.shape)
    stat_ref[...] = jnp.where(lanes == 0, inverse1, inverse2)
    high, rest_low = split_two(output)
    member = qf_ref[...]
    sums = (dot_at(member, high) + dot_at(member, rest_low))[:SEG]

    @pl.when(step == 0)
    def _():
        pool_ref[0] = sums

    @pl.when(step > 0)
    def _():
        pool_ref[0] += sums


def mix(attended, x, query_feat, gain1, gain2, weights, rows, tile, after):
    tokens, width = x.shape
    steps = tokens // rows // tile
    ff = weights[2].shape[0]
    counts, pieces, table, scratch = weight_operands(weights, (0, 0), after)
    wide, narrow = row_specs([None], tile, width, steps), row_specs([None], tile, LANES, steps)
    hidden, fixed = row_specs([None], tile, ff, steps), [pl.BlockSpec((1, width), lambda r, i, *_: (0, 0))]
    return pl.pallas_call(
        functools.partial(mix_kernel, counts),
        grid_spec=pltpu.PrefetchScalarGridSpec(
            num_scalar_prefetch=1,
            grid=(rows, steps),
            in_specs=wide * 2 + narrow + fixed * 2 + [ANY] * len(pieces),
            out_specs=wide + narrow + hidden * 3 + wide + [pl.BlockSpec((1, SEG, width), lambda r, i, *_: (r, 0, 0))],
            scratch_shapes=scratch,
        ),
        out_shape=[
            jax.ShapeDtypeStruct((tokens, width), BF),
            jax.ShapeDtypeStruct((tokens, LANES), F32),
            jax.ShapeDtypeStruct((tokens, ff), BF),
            jax.ShapeDtypeStruct((tokens, ff), BF),
            jax.ShapeDtypeStruct((tokens, ff), BF),
            jax.ShapeDtypeStruct((tokens, width), BF),
            jax.ShapeDtypeStruct((rows, SEG, width), F32),
        ],
        compiler_params=params(58),
        cost_estimate=cost(2 * tokens * width * (width + 3 * ff)),
    )(table, attended, x, query_feat, gain1, gain2, *pieces)


def hidden_back_kernel(counts, parts, table, *rest):
    cot_refs, rest = rest[:parts], rest[parts:]
    out_ref, stat_ref, qf_ref, dp_ref, fg_ref, fu_ref, g2_ref = rest[:7]
    pieces, rest = rest[7 : 7 + sum(counts)], rest[7 + sum(counts) :]
    dffn_ref, dgate_ref, dup_ref, gf_ref, wd, sems = rest
    groups = grouped_copies(counts, table, pieces, [wd], sems)
    begin = (pl.program_id(0) == 0) & (pl.program_id(1) == 0)

    @pl.when(begin)
    def _():
        start_all(*groups)
        gf_ref[...] = jnp.zeros_like(gf_ref)

    inverse2 = stat_ref[:, 1:2]
    member = qf_ref[...]
    high, rest_low = split_two(dp_ref[0])
    upstream = row_tile(table, cot_refs).astype(F32) + dot(member, high) + dot(member, rest_low)
    gain2 = g2_ref[...]
    unit2 = out_ref[...].astype(F32) / gain2
    dffn = norm_back(upstream * gain2, unit2, inverse2).astype(BF)
    dffn_ref[...] = dffn
    tile, width = dffn.shape
    gf_ref[...] += jnp.sum((upstream * unit2).reshape(tile // 8, 8, width), axis=0)

    @pl.when(begin)
    def _():
        wait_all(*groups)

    def load(c):
        return dot_bt(dffn, wd[c * FF_CHUNK : (c + 1) * FF_CHUNK, :])

    def work(c, dhid):
        cols = slice(c * FF_CHUNK, (c + 1) * FF_CHUNK)
        dgate_ref[:, cols] = (dhid * fg_ref[:, cols].astype(F32)).astype(BF)
        dup_ref[:, cols] = (dhid * fu_ref[:, cols].astype(F32)).astype(BF)

    staggered(wd.shape[0] // FF_CHUNK, load, work, lambda c, worked: None)


def hidden_back(cots, lead, output, stat, query_feat, dpool, factors, gain2, down, rows, tile):
    tokens, width = output.shape
    ff = down.shape[0]
    steps = tokens // rows // tile
    counts, pieces, table, scratch = weight_operands([down], (lead, 0))
    wide, narrow = row_specs([None], tile, width, steps), row_specs([None], tile, LANES, steps)
    hidden = row_specs([None], tile, ff, steps)
    return pl.pallas_call(
        functools.partial(hidden_back_kernel, counts, len(cots)),
        grid_spec=pltpu.PrefetchScalarGridSpec(
            num_scalar_prefetch=1,
            grid=(rows, steps),
            in_specs=row_specs(cots, tile, width, steps)
            + wide
            + narrow * 2
            + [pl.BlockSpec((1, LANES, width), lambda r, i, *_: (r, 0, 0))]
            + hidden * 2
            + [pl.BlockSpec((1, width), lambda r, i, *_: (0, 0))]
            + [ANY] * len(pieces),
            out_specs=wide + hidden * 2 + [pl.BlockSpec((8, width), lambda r, i, *_: (0, 0))],
            scratch_shapes=scratch,
        ),
        out_shape=[
            jax.ShapeDtypeStruct((tokens, width), BF),
            jax.ShapeDtypeStruct((tokens, ff), BF),
            jax.ShapeDtypeStruct((tokens, ff), BF),
            jax.ShapeDtypeStruct((8, width), F32),
        ],
        compiler_params=params(58),
        cost_estimate=cost(4 * tokens * width * ff),
    )(table, *cots, output, stat, query_feat, dpool, *factors, gain2, *pieces)


def branch_back_kernel(counts, table, *refs):
    dffn_ref, nl_ref, stat_ref, qf_ref, dgate_ref, dup_ref, att_ref, lse_ref, g1_ref, head_ref = refs[:10]
    rest = refs[10:]
    pieces, rest = rest[: sum(counts)], rest[sum(counts) :]
    dbr_ref, datt_ref, feat_ref, ga_ref, wo, ws, sems = rest
    groups = grouped_copies(counts, table, pieces, (wo, ws), sems)
    begin = (pl.program_id(0) == 0) & (pl.program_id(1) == 0)

    @pl.when(begin)
    def _():
        start_all(*groups)
        ga_ref[...] = jnp.zeros_like(ga_ref)
        wait_all(*groups)

    ff = dgate_ref.shape[1]
    dnormed = dffn_ref[...].astype(F32) + dot_bt(dgate_ref[...], ws[:, :ff]) + dot_bt(dup_ref[...], ws[:, ff:])
    gain1 = g1_ref[...]
    unit1 = nl_ref[...].astype(F32) / gain1
    dbr = norm_back(dnormed * gain1, unit1, stat_ref[:, 0:1]).astype(BF)
    dbr_ref[...] = dbr
    datt = dot_bt(dbr, wo[...]).astype(BF)
    datt_ref[...] = datt
    tile, width = datt.shape
    ga_ref[...] += jnp.sum((dnormed * unit1).reshape(tile // 8, 8, width), axis=0)

    high, rest_low = split_two(datt.astype(F32) * att_ref[...].astype(F32))
    heads = head_ref[...]
    delta = dot(high, heads) + dot(rest_low, heads)
    feat = qf_ref[...].astype(F32)
    for value, start in ((lse_ref[...], 8), (delta, 44)):
        left = -value
        for n in range(3):
            part = left.astype(BF).astype(F32)
            left = left - part
            feat = feat + pltpu.roll(part, start + HEADS * n, 1)
    feat_ref[...] = feat.astype(BF)


def branch_back(dffn, low, stat, query_feat, dgate, dup, attended, lse, gain1, weights, rows, tile, after=()):
    tokens, width = low.shape
    ff = dgate.shape[1]
    steps = tokens // rows // tile
    counts, pieces, table, scratch = weight_operands(weights, (0, 0), after)
    wide, narrow = row_specs([None], tile, width, steps), row_specs([None], tile, LANES, steps)
    hidden = row_specs([None], tile, ff, steps)
    heads = (jnp.arange(width)[:, None] // HDIM == jnp.arange(LANES)[None, :]).astype(BF)
    return pl.pallas_call(
        functools.partial(branch_back_kernel, counts),
        grid_spec=pltpu.PrefetchScalarGridSpec(
            num_scalar_prefetch=1,
            grid=(rows, steps),
            in_specs=wide * 2
            + narrow * 2
            + hidden * 2
            + wide
            + narrow
            + [pl.BlockSpec((1, width), lambda r, i, *_: (0, 0))]
            + [pl.BlockSpec((width, LANES), lambda r, i, *_: (0, 0))]
            + [ANY] * len(pieces),
            out_specs=wide * 2 + narrow + [pl.BlockSpec((8, width), lambda r, i, *_: (0, 0))],
            scratch_shapes=scratch,
        ),
        out_shape=[
            jax.ShapeDtypeStruct((tokens, width), BF),
            jax.ShapeDtypeStruct((tokens, width), BF),
            jax.ShapeDtypeStruct((tokens, LANES), BF),
            jax.ShapeDtypeStruct((8, width), F32),
        ],
        compiler_params=params(58),
        cost_estimate=cost(2 * tokens * width * (width + 2 * ff)),
    )(table, dffn, low, stat, query_feat, dgate, dup, attended, lse, gain1, heads, *pieces)


def bits_of(axis):
    size, bit = lax.axis_size(axis), 1
    while bit < size:
        yield bit
        bit *= 2


def in_order(parts, index):
    shape = (2,) + (1,) * parts[0].ndim
    first = lax.broadcasted_iota(jnp.int32, shape, 0) == index
    return jnp.where(first, parts[0][None], parts[1][None])


def add(first, *others):
    total = first.astype(F32)
    for other in others:
        total = total + other.astype(F32)
    return total.astype(BF)


def reduction(part, short):
    rows, cols = part.shape
    shards = lax.axis_size("fsdp")
    mine, place = lax.axis_index("fsdp"), lax.axis_index("blk")
    core, side = place % 2, place // 2 % 2
    now = part.reshape(shards, 2, rows // shards // 2, cols)
    (came,) = yield [take(now, 1 - core, 1)], [("blk", 1)]
    now = add(take(now, core, 1), came)
    bit = shards // 2
    while bit:
        now = now.reshape(2, bit, -1, cols)
        own = mine // bit % 2
        (came,) = yield [take(now, 1 - own, 0)], [("fsdp", bit)]
        now = add(take(now, own, 0), came)
        bit //= 2
    now = now.reshape(2, -1, cols)
    (came,) = yield [take(now, 1 - side, 0)], [("blk", 2)]
    now = add(take(now, side, 0), came)
    bits = [bit for bit in bits_of("blk") if bit > 2]
    if short:
        for bit in bits:
            (came,) = yield [now], [("blk", bit)]
            now = add(now, came)
    else:
        for bit in bits:
            now = now.reshape(2, -1, cols)
            own = place // bit % 2
            (came,) = yield [take(now, 1 - own, 0)], [("blk", bit)]
            now = add(take(now, own, 0), came)
        for bit in bits[::-1]:
            (came,) = yield [now], [("blk", bit)]
            now = in_order([now, came], place // bit % 2).reshape(-1, cols)
    now = now.reshape(-1, cols)
    (came,) = yield [now], [("blk", 2)]
    now = in_order([now, came], side).reshape(-1, cols)
    (came,) = yield [now], [("blk", 1)]
    yield [now, came], None


class Reduction:
    def __init__(self, part, short=False):
        self.stages = reduction(part, short)
        self.sends, self.routes = next(self.stages)

    @property
    def done(self):
        return self.routes is None

    @property
    def result(self):
        return self.sends

    def launch(self):
        came = [flipped(a, *route) for a, route in zip(self.sends, self.routes)]
        return self.sends, came

    def take_in(self, came):
        self.sends, self.routes = self.stages.send(came)


def beside(work, launches, joins=None):
    sent, flights = [], []
    for r in launches:
        if not r.done:
            sends, came = r.launch()
            sent += sends
            flights.append((r, came))
    values = list(work(sent))
    late = []
    if joins is not None:
        late = [f for f in flights if f[0] not in [j for j in joins if isinstance(j, Reduction)]]
        flights = [f for f in flights if f not in late] + [j for j in joins if not isinstance(j, Reduction)]
    count = len(values)
    both = tied(values + [a for _, came in flights for a in came])
    at = count
    for r, came in flights:
        r.take_in(both[at : at + len(came)])
        at += len(came)
    return both[:count], late


def reduced(part):
    part = lax.psum_scatter(part, ("fsdp", "blk"), scatter_dimension=0, tiled=True)
    return lax.all_gather(part, "blk", axis=0, tiled=True)


def weight_grad(pairs, beside_it=None):
    arrays, left = [], []
    for a, b in pairs:
        place = [n for n, other in enumerate(arrays) if other is a]
        if not place:
            arrays.append(a)
            place = [len(arrays) - 1]
        arrays.append(b)
        left.append((place[0], len(arrays) - 1))
    cols = sum(b.shape[1] for _, b in pairs)
    last = []
    if beside_it is not None:
        last = [beside_it]
        cols += beside_it.shape[1]

    def kernel(*refs):
        out_ref, at = refs[-1], 0
        for a, b in left:
            part = dot_at(refs[a][...], refs[b][...]).astype(BF)
            out_ref[:, at : at + part.shape[1]] = part
            at += part.shape[1]
        if last:
            out_ref[:, at:] = refs[-2][...]

    return pl.pallas_call(
        kernel,
        out_shape=jax.ShapeDtypeStruct((pairs[0][0].shape[1], cols), BF),
        compiler_params=params(56),
        cost_estimate=cost(2 * pairs[0][0].shape[0] * pairs[0][0].shape[1] * cols),
    )(*arrays, *last)


def unfold_kernel(columns, table, *refs):
    pairs = 2 * (1 + max(n for parts in columns for n, _, _ in parts))
    own = pl.program_id(0) == table[0]
    values = [jnp.where(own, refs[n][...], refs[n + 1][...]) for n in range(0, pairs, 2)]
    for ref, parts in zip(refs[pairs:], columns):
        at = 0
        for n, start, wide in parts:
            ref[:, at : at + wide] = values[n][:, start : start + wide].astype(F32)
            at += wide


def unfold(pairs, columns):
    rows = pairs[0][0].shape[0]
    block = rows // 2 if rows % 32 == 0 else rows
    steps = rows // block
    return pl.pallas_call(
        functools.partial(unfold_kernel, columns),
        grid_spec=pltpu.PrefetchScalarGridSpec(
            num_scalar_prefetch=1,
            grid=(2, steps),
            in_specs=[pl.BlockSpec((block, a.shape[1]), lambda c, i, t: (i, 0)) for pair in pairs for a in pair],
            out_specs=[pl.BlockSpec((block, sum(p[2] for p in parts)), lambda c, i, t: (c * steps + i, 0)) for parts in columns],
        ),
        out_shape=[jax.ShapeDtypeStruct((2 * rows, sum(p[2] for p in parts)), F32) for parts in columns],
        compiler_params=params(40),
        cost_estimate=CHEAP,
    )((lax.axis_index("blk") % 2).reshape(1), *[a for pair in pairs for a in pair])


def contrast(sums, lengths, pairing, row_mode, row_ids):
    rows, segs, width = sums.shape
    lengths = lengths.astype(F32)[..., None]
    pooled = sums / lengths
    inverse = lax.rsqrt(jnp.sum(pooled * pooled, -1, keepdims=True) + EMB_EPSILON)
    embedded = pooled * inverse
    own = rows * segs
    pair = jnp.stack([pairing, jnp.zeros_like(pairing)], axis=-1).reshape(own, 1)
    spare = jnp.concatenate([pair // 128, pair % 128, jnp.zeros((own, 126), jnp.int32)], axis=1)
    buffer = jnp.concatenate([embedded.reshape(own, width).astype(BF), spare.astype(BF)], axis=1)
    ids = row_ids
    for axis in ("fsdp", "blk") if row_mode else ("blk",):
        for bit in bits_of(axis):
            buffer = jnp.concatenate([buffer, flipped(buffer, axis, bit)], axis=0)
            if axis == "fsdp":
                ids = jnp.concatenate([ids, ids ^ bit])
            else:
                ids = jnp.concatenate([ids, ids ^ (bit * ROWS_PER_BLOCK)])
    total = buffer.shape[0]
    every = buffer[:, :width]
    pair_all = (buffer[:, width].astype(jnp.int32) * 128 + buffer[:, width + 1].astype(jnp.int32))[:, None]
    seg = jnp.arange(total, dtype=jnp.int32) % segs
    number = jnp.broadcast_to(ids[:, None], (total // segs, segs)).reshape(total) * (segs // 2) + seg // 2
    is_query = (seg % 2 == 0)[:, None]
    is_doc = (seg % 2 == 1)[None, :]
    target = is_query & is_doc & (pair_all == number[None, :])
    sims = dot_bt(every, every) / SOFTMAX_WARMTH
    masked = jnp.where(is_doc, sims, NEGATIVE)
    best = jnp.max(masked, -1, keepdims=True)
    log_total = best + jnp.log(jnp.sum(jnp.exp(masked - best), -1, keepdims=True))
    positive = jnp.sum(jnp.where(target, sims, 0.0), -1, keepdims=True)
    loss = jnp.sum(jnp.where(is_query[:own], log_total[:own] - positive[:own], 0.0))
    d_sims = CONTRAST_WEIGHT * (jnp.exp(masked - log_total) - target.astype(F32))
    d_sims = jnp.where(is_query, d_sims, 0.0).astype(BF)
    grad = (dot(d_sims[:own], every) + dot_at(d_sims[:, :own], every)) / SOFTMAX_WARMTH
    grad = grad.reshape(rows, segs, width)
    along = jnp.sum(embedded * grad, -1, keepdims=True)
    return loss, inverse * (grad - embedded * along) / lengths


ROWS_PER_BLOCK = 2


def shards(
    tokens,
    cotangent,
    segments,
    doc_lengths,
    positions,
    pairing,
    qkv_weight,
    out_weight,
    swiglu_weight,
    down_weight,
    attn_gain,
    ffn_gain,
):
    rows_here, shard_len, width = tokens.shape
    split = lax.axis_size("fsdp")
    mine = lax.axis_index("fsdp")
    place = lax.axis_index("blk")
    row_len = shard_len * split
    row_mode = split == rows_here == 2

    if row_mode:
        rows, per_row, query_start, lead = 1, row_len, 0, mine
        lengths = lax.dynamic_slice_in_dim(doc_lengths, mine, 1, 0)
        own_pairing = lax.dynamic_slice_in_dim(pairing.reshape(rows_here, -1), mine, 1, 0)
        row_ids = (place * rows_here + mine)[None]
    else:
        rows, per_row, query_start, lead = rows_here, shard_len, mine * shard_len, 0
        lengths, own_pairing = doc_lengths, pairing.reshape(rows_here, -1)
        row_ids = place * rows_here + jnp.arange(rows_here, dtype=jnp.int32)
    tokens_here = rows * per_row
    tile = min(512, per_row)
    small_tile = min(256, per_row)

    gains = jnp.stack([attn_gain, ffn_gain])
    if row_mode:
        qkv_share = flipped(share_of(qkv_weight), "fsdp", 1)
        qkv = from_shares(qkv_weight, qkv_share)
        moved = flipped(take(tokens, 1 - mine + zero_after(qkv_share), 0), "fsdp", 1)
        swiglu_share = flipped(share_of(swiglu_weight, zero_after(moved)), "fsdp", 1)
        swiglu = from_shares(swiglu_weight, swiglu_share)
        gains = in_order([gains, flipped(gains, "fsdp", 1)], mine)
        gains = jnp.concatenate([gains[0], gains[1]], axis=1)
    else:
        qkv, swiglu = whole_weight(qkv_weight), whole_weight(swiglu_weight)
        gains = lax.all_gather(gains, "fsdp", axis=1, tiled=True)
    gain1, gain2 = gains[0:1].astype(F32), gains[1:2].astype(F32)

    order = jnp.arange(SEG, dtype=jnp.int32)
    ends = jnp.sum(jnp.where(order[None, :] <= order[:, None], lengths[:, None, :], 0), -1)
    starts = ends - lengths
    token = jnp.arange(row_len, dtype=jnp.int32)
    at = token[None, :, None]
    member = (at >= starts[:, None, :]) & (at < ends[:, None, :])
    first_of = jnp.max(jnp.where(at >= starts[:, None, :], starts[:, None, :], 0), -1)
    lane = jnp.arange(LANES, dtype=jnp.int32)
    frequency = ROPE_BASE ** (-2.0 * (lane % 32).astype(F32) / HDIM)
    angles = (token[None, :] - first_of).astype(F32)[..., None] * frequency
    cosine = jnp.cos(angles).reshape(-1, LANES)
    sine = (jnp.sin(angles) * jnp.where(lane % HDIM < 32, -1.0, 1.0)).reshape(-1, LANES)
    key_feat = jnp.where(member, 0.0, NEGATIVE)
    key_feat = jnp.concatenate([key_feat, jnp.ones((rows, row_len, 120), F32)], -1)
    key_feat = key_feat.astype(BF).reshape(-1, LANES)
    query_feat = jnp.pad(member.astype(BF), ((0, 0), (0, 0), (0, 120))).reshape(-1, LANES)

    def of_queries(table):
        if row_mode:
            return table
        table = table.reshape(rows, row_len, LANES)
        return lax.dynamic_slice_in_dim(table, query_start, per_row, 1).reshape(-1, LANES)

    tables_k = (cosine, sine)
    tables_q = (of_queries(cosine), of_queries(sine))
    query_feat = of_queries(query_feat)
    block_first = query_start + BQ * jnp.arange(per_row // BQ, dtype=jnp.int32)[None, :, None]
    low = jnp.max(jnp.where(block_first >= starts[:, None, :], starts[:, None, :], 0), -1)
    high = jnp.min(jnp.where(block_first + BQ - 1 < ends[:, None, :], ends[:, None, :], row_len), -1)
    low = low // LANES * LANES

    def spans_of(size):
        count = (high - low + size - 1) // size
        return jnp.stack([jnp.minimum(low, row_len - count * size), count], axis=-1).reshape(-1).astype(jnp.int32)

    spans, spans_back = spans_of(BK_FWD), spans_of(BK_BACK)

    if row_mode:
        tables = (*tables_q, qkv)
        shift = zero_after(moved)
        halves = [half_of(w, shift) for w in (out_weight, down_weight)]
        firsts = [flipped(h, "fsdp", 1) for h in halves]
        query, key, value, x = project(take(tokens, mine, 0), mine * shard_len, *tables, [], small_tile, halves)
        old = [query, key, value, x]
        query, key, value, x = project(moved, (1 - mine) * shard_len, *tables, old, small_tile)
        key_all, value_all = key, value
    else:
        query, key, value, x = project(tokens.reshape(-1, width), 0, *tables_q, qkv, [], small_tile)

        def along_row(part):
            part = part.reshape(rows, per_row, width)
            return lax.all_gather(part, "fsdp", axis=1, tiled=True).reshape(-1, width)

        key_all, value_all = along_row(key), along_row(value)
    attended, lse = attend(query, key_all, value_all, key_feat, query_feat, spans, rows, PAIRS)
    if row_mode:
        attended, *firsts = tied([attended, *firsts], [lse])
        outer, down = from_halves(out_weight, firsts[0]), from_halves(down_weight, firsts[1])
        cot_send = take(cotangent, 1 - mine + zero_after(firsts[1]), 0)
        cots = [take(cotangent, mine, 0), flipped(cot_send, "fsdp", 1)]
        after = [cot_send]
    else:
        outer, down = whole_weight(out_weight), whole_weight(down_weight)
        cots, after = [cotangent.reshape(-1, width)], []
    low_normed, stat, hidden, *factors, output, sums = mix(
        attended, x, query_feat, gain1, gain2, (outer, swiglu, down), rows, small_tile, after
    )
    if row_mode:
        sums, cots[1] = tied([sums, cots[1]])
        output_came = flipped(lax.dynamic_slice_in_dim(output, (1 - mine) * shard_len, shard_len, 0), "fsdp", 1)
    else:
        layer_output = output.reshape(tokens.shape)
        sums = lax.psum(sums, "fsdp")
    loss, d_pool = contrast(sums, lengths, own_pairing, row_mode, row_ids)
    d_pool = jnp.pad(d_pool, ((0, 0), (0, LANES - SEG), (0, 0)))
    lse_columns = jnp.pad(lse.reshape(HEADS, tokens_here).T, ((0, 0), (0, LANES - HEADS)))

    d_ffn, d_gate, d_up, gain2_part = hidden_back(
        cots, lead, output, stat, query_feat, d_pool, factors, gain2, down, rows, small_tile
    )
    if row_mode:
        d_gate, output_came = tied([d_gate, output_came])
        layer_output = lax.dynamic_slice_in_dim(output, mine * shard_len, shard_len, 0)
        layer_output = in_order([layer_output, output_came], mine)
    down_rows = reduced(dot_at(hidden, d_ffn).astype(BF))
    gate_rows = reduced(dot_at(low_normed, d_gate).astype(BF))
    up_sum = Reduction(dot_at(low_normed, d_up).astype(BF))
    (d_branch, d_attended, back_feat, gain1_part), _ = beside(
        lambda sent: branch_back(
            d_ffn, low_normed, stat, query_feat, d_gate, d_up, attended, lse_columns, gain1, (outer, swiglu), rows,
            small_tile, sent,
        ),
        [up_sum],
    )
    part_rows = jnp.arange(width, dtype=jnp.int32) % (width // split)
    losses = jnp.where(part_rows == place, loss if row_mode else loss / split, 0.0)
    losses_high = lax.reduce_precision(losses, 8, 7)
    small = jnp.stack([jnp.sum(gain1_part, 0), jnp.sum(gain2_part, 0), losses_high, losses - losses_high], axis=1)
    small = jnp.pad(small, ((0, 0), (0, LANES - 4))).astype(BF)
    grads, qkv_sums = [], []
    running = [up_sum]
    for n in range(PAIRS // BACK_PAIRS):
        columns, _ = beside(
            lambda sent: attend_back(
                query, d_attended, key_all, value_all, key_feat, back_feat, spans_back, tables_q, tables_k, rows,
                BACK_PAIRS, n * BACK_PAIRS, BACK_PAIRS, sent,
            ),
            running,
        )
        if not row_mode:

            def own_part(grad):
                grad = grad.reshape(rows, row_len, -1)
                grad = lax.psum_scatter(grad, "fsdp", scatter_dimension=1, tiled=True)
                return grad.reshape(tokens_here, -1)

            columns = [columns[0], own_part(columns[1]), own_part(columns[2])]
        grads += columns
        pairs = [(x, g) for g in columns]
        if n == 0:
            qkv_sums.append(Reduction(weight_grad([*pairs, (attended, d_branch)], small), True))
        else:
            qkv_sums.append(Reduction(weight_grad(pairs), True))
        running = [up_sum, *qkv_sums]
    if row_mode:
        (moved,), _ = beside(
            lambda sent: [
                input_grad_part(d_branch, grads, qkv, (1 - mine) * shard_len, shard_len, BF, small_tile, sent)
            ],
            running,
        )
        came = flipped(moved, "fsdp", 1)
        (kept,), _ = beside(
            lambda sent: [input_grad_part(d_branch, grads, qkv, mine * shard_len, shard_len, F32, small_tile, sent)],
            running,
        )
        input_grad = in_order([kept, came.astype(F32)], mine)
    else:
        input_grad = input_grad_part(d_branch, grads, qkv, 0, tokens_here, F32, small_tile).reshape(tokens.shape)
    while any(not r.done for r in running):
        beside(lambda _: [], running)
    wide, groups = BACK_PAIRS * LANES, PAIRS // BACK_PAIRS
    ff = d_gate.shape[1]
    half = width // split // 2
    up_rows = in_order(up_sum.result, place % 2).reshape(2 * half, ff)
    swiglu_grad = jnp.concatenate([gate_rows, up_rows], axis=1).astype(F32)
    qkv_columns = [(g, part * wide, wide) for part in range(3) for g in range(groups)]
    qkv_grad, out_grad, small = unfold(
        [r.result for r in qkv_sums], [qkv_columns, [(0, 3 * wide, width)], [(0, 3 * wide + width, LANES)]]
    )
    queries = lax.axis_size("blk") * pairing.shape[0]
    return (
        jnp.sum(small[:, 2:4]) / queries,
        layer_output,
        input_grad,
        qkv_grad,
        out_grad,
        swiglu_grad,
        down_rows.astype(F32),
        small[:, 0],
        small[:, 1],
    )


BACK_PAIRS = 2


def solution(mesh):
    in_specs = (
        P("blk", "fsdp", None),
        P("blk", "fsdp", None),
        P("blk", "fsdp"),
        P("blk", None),
        P("blk", "fsdp"),
        P("blk"),
        P("fsdp", None),
        P("fsdp", None),
        P("fsdp", None),
        P("fsdp", None),
        P("fsdp"),
        P("fsdp"),
    )
    out_specs = (
        P(),
        P("blk", "fsdp", None),
        P("blk", "fsdp", None),
        P("fsdp", None),
        P("fsdp", None),
        P("fsdp", None),
        P("fsdp", None),
        P("fsdp"),
        P("fsdp"),
    )
    return jax.shard_map(shards, mesh=mesh, in_specs=in_specs, out_specs=out_specs, check_vma=False)
```

time: 1140 us -> 741 us (0.65)
  waiting for transfers between devices: 405 us -> 122 us
  Pallas kernels: 487 us -> 359 us
  other arithmetic: 58.3 us -> 72.5 us
  matrix products: 58.7 us -> 45 us
    reduce_scatter x3 -> x2, waiting for transfers between devices: 197 us -> 0.01 us  [reduced(): lax.psum_scatter(part, ('fsdp', 'blk'), scatter_dimension=0, tiled=True)]
    pallas_call x6 -> x27, Pallas kernels: 430 us -> 304 us  [the longest x3 110 us: attend_back(): pl.pallas_call(functools.partial(attend_back_kernel, group, base, len(aft...]
    psum x1 -> x0, waiting for transfers between devices: 113 us -> none  [reduced(): return lax.psum(part, 'blk').astype(F32)]
    ppermute x10 -> x46, waiting for transfers between devices: 39.3 us -> 122 us  [flipped(): return lax.ppermute(block, axis, route)]
    ppermute x21 -> x0, waiting for transfers between devices: 41.5 us -> none  [the longest x4 24.4 us: weight_pieces(): second = lax.ppermute(first, 'blk', [(i, i ^ 2) for i in range(blocks)])]
    ppermute x10 -> x46, starting transfers between devices: 18 us -> 52.3 us  [flipped(): return lax.ppermute(block, axis, route)]
    ppermute x21 -> x0, starting transfers between devices: 27.8 us -> none  [the longest x4 9.94 us: weight_pieces(): fourth = lax.ppermute(second, 'blk', over)]
    convert_element_type x4 -> x24, other arithmetic: 11.9 us -> 36.2 us  [the longest x20 21.3 us: add(): return total.astype(BF)]
  transfers between devices with their start and end apart: 36 -> 52, of which waited for: 20 -> 15; matrix products, arithmetic and copies ran while one was open for 10% -> 18% of each run, Pallas kernels for 16% -> 45%
where the time goes in v2:
time: 741 us; the launch traced here: 731 us
  Pallas kernels  359 us (48%)
  waiting for transfers between devices  122 us (16%)
  other arithmetic  72.5 us (10%)
  local copies, waits for them, and re-layouts  60.4 us (8%)
  starting transfers between devices  52.5 us (7%)
  matrix products  45 us (6%)
  between operations  19.7 us (3%)
    ppermute x46, waiting for transfers between devices, flipped(): return lax.ppermute(block, axis, route)  122 us
    pallas_call x3, Pallas kernels, attend_back(): pl.pallas_call(functools.partial(attend_back_kernel, group, base, len(aft...  110 us
    pallas_call x1, Pallas kernels, mix(): pl.pallas_call(functools.partial(mix_kernel, counts), grid_spec=pltpu.Pre...  54.7 us
    pallas_call x1, Pallas kernels, attend(): pl.pallas_call(functools.partial(attend_kernel, group, len(after)), grid_...  53.5 us
    ppermute x46, starting transfers between devices, flipped(): return lax.ppermute(block, axis, route)  52.3 us
    pallas_call x1, Pallas kernels, branch_back(): pl.pallas_call(functools.partial(branch_back_kernel, counts), grid_spec=p...  45.6 us
    dot_general x4, matrix products, dot_at(): lax.dot_general(a, b, (((0,), (0,)), ((), ())), preferred_element_type=F32)  44.3 us
    pallas_call x1, Pallas kernels, hidden_back(): pl.pallas_call(functools.partial(hidden_back_kernel, counts, len(cots)),...  29.9 us
  transfers between devices with their start and end apart: 52, of which 15 were waited for; matrix products, arithmetic and copies ran while one was open for 18% of the time, Pallas kernels for 45%

profile of v2, /device:TPU:0, one launch (start us, length us, event | category | flops | bytes accessed | tf_op | source)
XLA Modules:
  0.0 731.4 jit_solution(1180137671081885830)
XLA Ops:
  28.3 5.5 fusion.7
  33.8 25.4 %collective-permute-done.1.in_ref = bf16[1024,768]{1,0:T(8,128)(2,1)} collective-permute-done((bf16[1024,768]{1,0:T(8,128)(2,1)}, bf16[1024,768]{1,0:T(8,128)(2,1)}, u32[]{:S(2)}, u32[]{:S(2)}) %collective-permute-start.1) | collective-permute-done | bytes 1572896 | tf_op jit(solution)/shard_map/ppermute | solution.py:57
  64.9 7.2 collective-permute-done.6
  78.7 8.6 %shard_map.169 = (bf16[2048,768]{1,0:T(8,128)(2,1)}, bf16[2048,768]{1,0:T(8,128)(2,1)}, bf16[2048,768]{1,0:T(8,128)(2,1)}, bf16[2048,768]{1,0:T(8,128)(2,1)}) custom-call(s32[6]{0:T(128)S(1)} %stack.110.table, f32[2048,128]{1,0:T(8,128)S(1)} %copy-done.8, f32[2048,128]{1,0:T(8,128)S(1)} %copy-done.6, bf16[1024,768]{1,0:T(8,128)(2,1)S(1)} %get-tuple-element.195.in_ref, ...), custom_call_target="tpu_custom_call" | custom-call | flops 14495514624 | bytes 1048576 | tf_op jit(solution)/shard_map/pallas_call | solution.py:229
  87.4 9.3 %shard_map.170 = (bf16[2048,768]{1,0:T(8,128)(2,1)}, bf16[2048,768]{1,0:T(8,128)(2,1)}, bf16[2048,768]{1,0:T(8,128)(2,1)}, bf16[2048,768]{1,0:T(8,128)(2,1)}) custom-call(s32[6]{0:T(128)S(1)} %stack.108.table, f32[2048,128]{1,0:T(8,128)S(1)} %copy-done.8, ...), custom_call_target="tpu_custom_call", output_to_operand_aliasing={{0}: (6, {}), {1}: (7, {}), {2}: (8, {}), {3}: (9, {})} | custom-call | flops 14495514624 | bytes 1048576 | tf_op jit(solution)/shard_map/pallas_call | solution.py:229
  96.7 53.5 %shard_map.171 = (bf16[2048,768]{1,0:T(8,128)(2,1)}, f32[12,1,2048]{2,1,0:T(1,128)}) custom-call(s32[16]{0:T(128)} %reshape.1371.spans, bf16[2048,768]{1,0:T(8,128)(2,1)} %get-tuple-element.102.q_ref, bf16[2048,768]{1,0:T(8,128)(2,1)} %get-tuple-element.103.k_ref, bf16[2048,768]{1,0:T(8,128)(2,1)} %get-tuple-element.104.v_ref, ...), custom_call_target="tpu_custom_call" | custom-call | flops 51539607552 | bytes 1048576 | tf_op jit(solution)/shard_map/pallas_call | solution.py:377
  159.7 54.7 %shard_map.173 = (bf16[2048,768]{1,0:T(8,128)(2,1)}, f32[2048,128]{1,0:T(8,128)}, bf16[2048,3072]{1,0:T(8,128)(2,1)}, bf16[2048,3072]{1,0:T(8,128)(2,1)}, bf16[2...) custom-call(s32[18]{0:T(128)} %stack.120.table, ...), custom_call_target="tpu_custom_call" | custom-call | flops 125627793408 | bytes 1048576 | tf_op jit(solution)/shard_map/pallas_call | solution.py:635
  217.6 3.7 collective-permute-done.9
  234.8 8.2 %collective-permute-done.13 = bf16[128,896]{1,0:T(8,128)(2,1)S(1)} collective-permute-done((bf16[128,896]{1,0:T(8,128)(2,1)S(1)}, bf16[128,896]{1,0:T(8,128)(2,1)S(1)}, u32[]{:S(2)}, u32[]{:S(2)}) %collective-permute-start.13) | collective-permute-done | bytes 229408 | tf_op jit(solution)/shard_map/ppermute | solution.py:57
  245.3 29.9 %shard_map.175 = (bf16[2048,768]{1,0:T(8,128)(2,1)}, bf16[2048,3072]{1,0:T(8,128)(2,1)}, bf16[2048,3072]{1,0:T(8,128)(2,1)}, f32[8,768]{1,0:T(8,128)}) custom-call(s32[8]{0:T(128)} %stack.119.table, bf16[1024,768]{1,0:T(8,128)(2,1)} %get-tuple-element.194.rest_0_, bf16[1024,768]{1,0:T(8,128)(2,1)} %get-tuple-element.111.rest_1_, ...), custom_call_target="tpu_custom_call" | custom-call | flops 77309411328 | bytes 1048576 | tf_op jit(solution)/shard_map/pallas_call | solution.py:704
  275.3 15.4 %convolution_convert_fusion = bf16[3072,768]{1,0:T(8,128)(2,1)} fusion(bf16[2048,3072]{1,0:T(8,128)(2,1)} %get-tuple-element.184, bf16[2048,768]{1,0:T(8,128)(2,1)} %get-tuple-element.117.refs_0_), kind=kOutput, calls=%fused_computation | convolution fusion | flops 9666035712 | bytes 20447232 | tf_op jit(solution)/shard_map/dot_general | solution.py:43
  295.6 4.0 constant_dynamic-slice_fusion
  301.8 13.4 %convolution_convert_fusion.2 = bf16[768,3072]{1,0:T(8,128)(2,1)S(1)} fusion(bf16[2048,768]{1,0:T(8,128)(2,1)S(1)} %copy-done.86, bf16[2048,3072]{1,0:T(8,128)(2,1)} %get-tuple-element.121.refs_5_), kind=kOutput, calls=%fused_computation.2 | convolution fusion | flops 9666035712 | bytes 20447232 | tf_op jit(solution)/shard_map/dot_general | solution.py:43
  320.0 15.9 %collective-permute-done.14.refs_1_ = bf16[1024,768]{1,0:T(8,128)(2,1)} collective-permute-done((bf16[1024,768]{1,0:T(8,128)(2,1)}, bf16[1024,768]{1,0:T(8,128)(2,1)}, u32[]{:S(2)}, u32[]{:S(2)}) %collective-permute-start.14) | collective-permute-done | bytes 1572896 | tf_op jit(solution)/shard_map/ppermute | solution.py:57
  336.0 15.3 %convolution_convert_fusion.1 = bf16[768,3072]{1,0:T(8,128)(2,1)} fusion(bf16[2048,768]{1,0:T(8,128)(2,1)} %get-tuple-element.118.refs_1_, bf16[2048,3072]{1,0:T(8,128)(2,1)} %get-tuple-element.120.refs_4_), kind=kOutput, calls=%fused_computation.1 | convolution fusion | flops 9666035712 | bytes 20447232 | tf_op jit(solution)/shard_map/dot_general | solution.py:43
  351.4 45.6 %shard_map.177 = (bf16[2048,768]{1,0:T(8,128)(2,1)}, bf16[2048,768]{1,0:T(8,128)(2,1)}, bf16[2048,128]{1,0:T(8,128)(2,1)}, f32[8,768]{1,0:T(8,128)}) custom-call(s32[12]{0:T(128)} %stack.114.table, bf16[2048,768]{1,0:T(8,128)(2,1)} %get-tuple-element.117.refs_0_, bf16[2048,768]{1,0:T(8,128)(2,1)} %get-tuple-element.118.refs_1_, ...), custom_call_target="tpu_custom_call" | custom-call | flops 86973087744 | bytes 1048576 | tf_op jit(solution)/shard_map/pallas_call | solution.py:776
  404.5 36.8 %shard_map.179 = (bf16[2048,256]{1,0:T(8,128)(2,1)}, bf16[2048,256]{1,0:T(8,128)(2,1)}, bf16[2048,256]{1,0:T(8,128)(2,1)}) custom-call(s32[16]{0:T(128)} %reshape.1370.spans, bf16[2048,768]{1,0:T(8,128)(2,1)} %get-tuple-element.102.q_ref, bf16[2048,768]{1,0:T(8,128)(2,1)} %get-tuple-element.126.do_ref, bf16[2048,768]{1,0:T(8,128)(2,1)} %get-tuple-element.103.k_ref, ...), custom_call_target="tpu_custom_call" | custom-call | flops 34359738368 | bytes 1048576 | tf_op jit(solution)/shard_map/pallas_call | solution.py:500
  446.3 11.2 %shard_map.181 = bf16[768,1664]{1,0:T(8,128)(2,1)} custom-call(bf16[2048,768]{1,0:T(8,128)(2,1)} %get-tuple-element.101.x_ref.refs_0_, bf16[2048,256]{1,0:T(8,128)(2,1)} %get-tuple-element.132.refs_1_.rest_0_, bf16[2048,256]{1,0:T(8,128)(2,1)} %get-tuple-element.133.refs_2_.rest_1_, bf16[2048,256]{1,0:T(8,128)(2,1)} %get-tuple-element.134.refs_3_.rest_2_, ...), custom_call_target="tpu_custom_call" | custom-call | flops 20937965568 | bytes 1048576 | tf_op jit(solution)/shard_map/pallas_call | solution.py:933
  461.7 36.9 %shard_map.182 = (bf16[2048,256]{1,0:T(8,128)(2,1)}, bf16[2048,256]{1,0:T(8,128)(2,1)}, bf16[2048,256]{1,0:T(8,128)(2,1)}) custom-call(s32[16]{0:T(128)} %reshape.1370.spans, bf16[2048,768]{1,0:T(8,128)(2,1)} %get-tuple-element.102.q_ref, bf16[2048,768]{1,0:T(8,128)(2,1)} %get-tuple-element.126.do_ref, bf16[2048,768]{1,0:T(8,128)(2,1)} %get-tuple-element.103.k_ref, ...), custom_call_target="tpu_custom_call" | custom-call | flops 34359738368 | bytes 1048576 | tf_op jit(solution)/shard_map/pallas_call | solution.py:500
  501.5 6.7 shard_map.184
  513.2 36.7 %shard_map.185 = (bf16[2048,256]{1,0:T(8,128)(2,1)}, bf16[2048,256]{1,0:T(8,128)(2,1)}, bf16[2048,256]{1,0:T(8,128)(2,1)}) custom-call(s32[16]{0:T(128)} %reshape.1370.spans, bf16[2048,768]{1,0:T(8,128)(2,1)} %get-tuple-element.102.q_ref, bf16[2048,768]{1,0:T(8,128)(2,1)} %get-tuple-element.126.do_ref, bf16[2048,768]{1,0:T(8,128)(2,1)} %get-tuple-element.103.k_ref, ...), custom_call_target="tpu_custom_call" | custom-call | flops 34359738368 | bytes 1048576 | tf_op jit(solution)/shard_map/pallas_call | solution.py:500
  558.9 6.6 shard_map.187
  570.8 9.8 %shard_map.188.refs_0_ = bf16[1024,768]{1,0:T(8,128)(2,1)} custom-call(s32[6]{0:T(128)S(1)} %copy-done.19, bf16[2048,768]{1,0:T(8,128)(2,1)} %get-tuple-element.135.refs_5_.dbr_ref, bf16[2048,256]{1,0:T(8,128)(2,1)S(1)} %copy-done.9, bf16[2048,256]{1,0:T(8,128)(2,1)S(1)} %copy-done.10, bf16[2048,256]{1,0:T(8,128)(2,1)S(1)} %copy-done.11, ...), custom_call_target="tpu_custom_call" | custom-call | flops 14495514624 | bytes 1048576 | tf_op jit(solution)/shard_map/pallas_call | solution.py:268
  589.9 9.8 %shard_map.190.refs_0_ = f32[1024,768]{1,0:T(8,128)} custom-call(s32[6]{0:T(128)S(1)} %copy-done.17, bf16[2048,768]{1,0:T(8,128)(2,1)} %get-tuple-element.135.refs_5_.dbr_ref, bf16[2048,256]{1,0:T(8,128)(2,1)S(1)} %copy-done.9, bf16[2048,256]{1,0:T(8,128)(2,1)S(1)} %copy-done.10, bf16[2048,256]{1,0:T(8,128)(2,1)S(1)} %copy-done.12, ...), custom_call_target="tpu_custom_call" | custom-call | flops 14495514624 | bytes 1048576 | tf_op jit(solution)/shard_map/pallas_call | solution.py:268
  610.4 15.6 %collective-permute-done.32.refs_2_ = bf16[96,768]{1,0:T(8,128)(2,1)S(1)} collective-permute-done((bf16[96,768]{1,0:T(8,128)(2,1)S(1)}, bf16[96,768]{1,0:T(8,128)(2,1)S(1)}, u32[]{:S(2)}, u32[]{:S(2)}) %collective-permute-start.32) | collective-permute-done | bytes 147488 | tf_op jit(solution)/shard_map/ppermute | solution.py:57
  636.2 8.5 %collective-permute-done.36.refs_2_ = bf16[96,768]{1,0:T(8,128)(2,1)S(1)} collective-permute-done((bf16[96,768]{1,0:T(8,128)(2,1)S(1)}, bf16[96,768]{1,0:T(8,128)(2,1)S(1)}, u32[]{:S(2)}, u32[]{:S(2)}) %collective-permute-start.36) | collective-permute-done | bytes 147488 | tf_op jit(solution)/shard_map/ppermute | solution.py:57
  644.9 7.6 %collective-permute-done.35.refs_1_ = bf16[96,1664]{1,0:T(8,128)(2,1)S(1)} collective-permute-done((bf16[96,1664]{1,0:T(8,128)(2,1)S(1)}, bf16[96,1664]{1,0:T(8,128)(2,1)S(1)}, u32[]{:S(2)}, u32[]{:S(2)}) %collective-permute-start.35) | collective-permute-done | bytes 319520 | tf_op jit(solution)/shard_map/ppermute | solution.py:57
  664.7 6.4 collective-permute-done.41.refs_3_
  678.5 15.0 %collective-permute-done.45 = bf16[1024,768]{1,0:T(8,128)(2,1)} collective-permute-done((bf16[1024,768]{1,0:T(8,128)(2,1)}, bf16[1024,768]{1,0:T(8,128)(2,1)}, u32[]{:S(2)}, u32[]{:S(2)}) %collective-permute-start.45) | collective-permute-done | bytes 1572896 | tf_op jit(solution)/shard_map/ppermute | solution.py:57
  699.3 6.0 broadcast_select_fusion
  712.2 4.2 convert_element_type.432
  716.4 6.6 maximum_convert_fusion
  (443 shorter events, 171.4 us)
Async XLA Ops:
  7.2 69.1 %all-gather.5.cloned.1.call-start = ((), (), s32[]{:S(2)}) async-start(), calls=%async_computation.2 | async-start | bytes 1880064 | tf_op jit(solution)/shard_map/all_gather | solution.py:101
  12.5 139.2 %collective-permute-start.4 = (bf16[2,384]{1,0:T(2,128)(2,1)S(1)}, bf16[2,384]{1,0:T(2,128)(2,1)}, u32[]{:S(2)}, u32[]{:S(2)}) collective-permute-start(bf16[2,384]{1,0:T(2,128)(2,1)S(1)} %pad_maximum_fusion.6), channel_id=1, source_target_pairs={{0,1},{1,0},{2,3},{3,2},{4,5},{5,4},{6,7},{7,6},{8,9},{9,8},{10,11... | collective-permute-start | bytes 4616 | tf_op jit(solution)/shard_map/ppermute | solution.py:57
  17.6 142.1 %all-gather.7.cloned.1.call-start = ((), (), s32[]{:S(2)}) async-start(), calls=%async_computation.3 | async-start | bytes 5013504 | tf_op jit(solution)/shard_map/all_gather | solution.py:101
  23.0 36.2 %collective-permute-start.1 = (bf16[1024,768]{1,0:T(8,128)(2,1)}, bf16[1024,768]{1,0:T(8,128)(2,1)}, u32[]{:S(2)}, u32[]{:S(2)}) collective-permute-start(bf16[1024,768]{1,0:T(8,128)(2,1)} %get-tuple-element.196), channel_id=1, source_target_pairs={{0,1},{1,0},{2,3},{3,2},{4,5},{5,4},{6,7},{7,6},{8,9},{9,8},{10,11... | collective-permute-start | bytes 4718600 | tf_op jit(solution)/shard_map/ppermute | solution.py:57
  64.5 85.7 %collective-permute-start.2 = (bf16[192,768]{1,0:T(8,128)(2,1)S(1)}, bf16[192,768]{1,0:T(8,128)(2,1)S(1)}, u32[]{:S(2)}, u32[]{:S(2)}) collective-permute-start(bf16[192,768]{1,0:T(8,128)(2,1)S(1)} %constant_dynamic-slice_fusion.9.rest_2_), channel_id=1, source_target_pairs={{0,1},{1,0},{2,3},{3,2},{4,5},{5,4},{6,7},{7,6},{8,9},{9,8},{10,11... | collective-permute-start | bytes 884744 | tf_op jit(solution)/shard_map/ppermute | solution.py:57
  72.8 496.7 %reduce-scatter.5.cloned.1.call-start = ((), (), s32[]{:S(2)}) async-start(), calls=%async_computation.6 | async-start | bytes 4866048 | tf_op jit(solution)/shard_map/reduce_scatter | solution.py:905
  74.5 75.7 %collective-permute-start.3 = (bf16[768,768]{1,0:T(8,128)(2,1)S(1)}, bf16[768,768]{1,0:T(8,128)(2,1)}, u32[]{:S(2)}, u32[]{:S(2)}) collective-permute-start(bf16[768,768]{1,0:T(8,128)(2,1)S(1)} %constant_dynamic-slice_fusion.8.rest_3_), channel_id=1, source_target_pairs={{0,1},{1,0},{2,3},{3,2},{4,5},{5,4},{6,7},{7,6},{8,9},{9,8},{10,11... | collective-permute-start | bytes 3538952 | tf_op jit(solution)/shard_map/ppermute | solution.py:57
  157.3 57.1 %collective-permute-start.8 = (bf16[1024,768]{1,0:T(8,128)(2,1)}, bf16[1024,768]{1,0:T(8,128)(2,1)S(1)}, u32[]{:S(2)}, u32[]{:S(2)}) collective-permute-start(bf16[1024,768]{1,0:T(8,128)(2,1)} %get-tuple-element.193.rest_8_), channel_id=1, source_target_pairs={{0,1},{1,0},{2,3},{3,2},{4,5},{5,4},{6,7},{7,6},{8,9},{9,8},{10,11... | collective-permute-start | bytes 4718600 | tf_op jit(solution)/shard_map/ppermute | solution.py:57
  290.7 313.3 %reduce-scatter.3.cloned.1.call-start = ((), (), s32[]{:S(2)}) async-start(), calls=%async_computation.4 | async-start | bytes 4866048 | tf_op jit(solution)/shard_map/reduce_scatter | solution.py:905
  299.6 36.4 %collective-permute-start.14 = (bf16[1024,768]{1,0:T(8,128)(2,1)}, bf16[1024,768]{1,0:T(8,128)(2,1)}, u32[]{:S(2)}, u32[]{:S(2)}) collective-permute-start(bf16[1024,768]{1,0:T(8,128)(2,1)} %get-tuple-element.192), channel_id=1, source_target_pairs={{0,1},{1,0},{2,3},{3,2},{4,5},{5,4},{6,7},{7,6},{8,9},{9,8},{10,11... | collective-permute-start | bytes 4718600 | tf_op jit(solution)/shard_map/ppermute | solution.py:57
  318.1 78.8 %collective-permute-start.15 = (bf16[2,192,3072]{2,1,0:T(8,128)(2,1)}, bf16[2,192,3072]{2,1,0:T(8,128)(2,1)S(1)}, u32[]{:S(2)}, u32[]{:S(2)}) collective-permute-start(bf16[2,192,3072]{2,1,0:T(8,128)(2,1)} %dynamic-slice_bitcast_fusion.refs_15_), channel_id=1, source_target_pairs={{0,2},{2,0},{4,6},{6,4},{8,10},{10,8},{12,14},{14,12},{16,18},{18,... | collective-permute-start | bytes 7077896 | tf_op jit(solution)/shard_map/ppermute | solution.py:57
  351.3 360.9 %all-gather.11.cloned.1.call-start = ((), (), s32[]{:S(2)}) async-start(), calls=%async_computation.7 | async-start | bytes 2506752 | tf_op jit(solution)/shard_map/all_gather | solution.py:906
  402.7 42.6 %collective-permute-start.16 = (bf16[1,192,3072]{2,1,0:T(8,128)(2,1)}, bf16[1,192,3072]{2,1,0:T(8,128)(2,1)S(1)}, u32[]{:S(2)}, u32[]{:S(2)}) collective-permute-start(bf16[1,192,3072]{2,1,0:T(8,128)(2,1)} %constant_dynamic-slice_fusion.4.rest_0_), channel_id=1, source_target_pairs={{0,1},{1,0},{2,3},{3,2},{4,5},{5,4},{6,7},{7,6},{8,9},{9,8},{10,11... | collective-permute-start | bytes 3538952 | tf_op jit(solution)/shard_map/ppermute | solution.py:57
  459.7 38.9 %collective-permute-start.17 = (bf16[96,3072]{1,0:T(8,128)(2,1)S(1)}, bf16[96,3072]{1,0:T(8,128)(2,1)S(1)}, u32[]{:S(2)}, u32[]{:S(2)}) collective-permute-start(bf16[96,3072]{1,0:T(8,128)(2,1)S(1)} %dynamic-slice_bitcast_fusion.8.rest_0_), channel_id=1, source_target_pairs={{0,4},{2,6},{4,0},{6,2},{8,12},{10,14},{12,8},{14,10},{16,20},{18,... | collective-permute-start | bytes 1769480 | tf_op jit(solution)/shard_map/ppermute | solution.py:57
  461.7 36.9 %collective-permute-start.18 = (bf16[2,192,1664]{2,1,0:T(8,128)(2,1)S(1)}, bf16[2,192,1664]{2,1,0:T(8,128)(2,1)}, u32[]{:S(2)}, u32[]{:S(2)}) collective-permute-start(bf16[2,192,1664]{2,1,0:T(8,128)(2,1)S(1)} %dynamic-slice_bitcast_fusion.5.rest_1_), channel_id=1, source_target_pairs={{0,2},{2,0},{4,6},{6,4},{8,10},{10,8},{12,14},{14,12},{16,18},{18,... | collective-permute-start | bytes 3833864 | tf_op jit(solution)/shard_map/ppermute | solution.py:57
  509.6 40.3 %collective-permute-start.19 = (bf16[48,3072]{1,0:T(8,128)(2,1)S(1)}, bf16[48,3072]{1,0:T(8,128)(2,1)S(1)}, u32[]{:S(2)}, u32[]{:S(2)}) collective-permute-start(bf16[48,3072]{1,0:T(8,128)(2,1)S(1)} %dynamic-slice_bitcast_fusion.10.rest_0_), channel_id=1, source_target_pairs={{0,8},{2,10},{4,12},{6,14},{8,0},{10,2},{12,4},{14,6},{16,24},{18,... | collective-permute-start | bytes 884744 | tf_op jit(solution)/shard_map/ppermute | solution.py:57
  510.7 39.2 %collective-permute-start.20 = (bf16[1,192,1664]{2,1,0:T(8,128)(2,1)S(1)}, bf16[1,192,1664]{2,1,0:T(8,128)(2,1)S(1)}, u32[]{:S(2)}, u32[]{:S(2)}) collective-permute-start(bf16[1,192,1664]{2,1,0:T(8,128)(2,1)S(1)} %constant_dynamic-slice_fusion.3.rest_1_), channel_id=1, source_target_pairs={{0,1},{1,0},{2,3},{3,2},{4,5},{5,4},{6,7},{7,6},{8,9},{9,8},{10,11... | collective-permute-start | bytes 1916936 | tf_op jit(solution)/shard_map/ppermute | solution.py:57
  511.4 38.5 %collective-permute-start.21 = (bf16[2,192,768]{2,1,0:T(8,128)(2,1)S(1)}, bf16[2,192,768]{2,1,0:T(8,128)(2,1)S(1)}, u32[]{:S(2)}, u32[]{:S(2)}) collective-permute-start(bf16[2,192,768]{2,1,0:T(8,128)(2,1)S(1)} %dynamic-slice_bitcast_fusion.7.rest_2_), channel_id=1, source_target_pairs={{0,2},{2,0},{4,6},{6,4},{8,10},{10,8},{12,14},{14,12},{16,18},{18,... | collective-permute-start | bytes 1769480 | tf_op jit(solution)/shard_map/ppermute | solution.py:57
  553.2 27.4 %collective-permute-start.22 = (bf16[24,3072]{1,0:T(8,128)(2,1)}, bf16[24,3072]{1,0:T(8,128)(2,1)}, u32[]{:S(2)}, u32[]{:S(2)}) collective-permute-start(bf16[24,3072]{1,0:T(8,128)(2,1)} %dynamic-slice_bitcast_fusion.13.rest_11_), channel_id=1, source_target_pairs={{0,16},{2,18},{4,20},{6,22},{8,24},{10,26},{12,28},{14,30},{16,0},... | collective-permute-start | bytes 442376 | tf_op jit(solution)/shard_map/ppermute | solution.py:57
  556.4 24.2 %collective-permute-start.23 = (bf16[96,1664]{1,0:T(8,128)(2,1)S(1)}, bf16[96,1664]{1,0:T(8,128)(2,1)}, u32[]{:S(2)}, u32[]{:S(2)}) collective-permute-start(bf16[96,1664]{1,0:T(8,128)(2,1)S(1)} %dynamic-slice_bitcast_fusion.9.rest_12_), channel_id=1, source_target_pairs={{0,4},{2,6},{4,0},{6,2},{8,12},{10,14},{12,8},{14,10},{16,20},{18,... | collective-permute-start | bytes 958472 | tf_op jit(solution)/shard_map/ppermute | solution.py:57
  558.5 22.1 %collective-permute-start.24 = (bf16[1,192,768]{2,1,0:T(8,128)(2,1)}, bf16[1,192,768]{2,1,0:T(8,128)(2,1)}, u32[]{:S(2)}, u32[]{:S(2)}) collective-permute-start(bf16[1,192,768]{2,1,0:T(8,128)(2,1)} %constant_dynamic-slice_fusion.2.rest_13_), channel_id=1, source_target_pairs={{0,1},{1,0},{2,3},{3,2},{4,5},{5,4},{6,7},{7,6},{8,9},{9,8},{10,11... | collective-permute-start | bytes 884744 | tf_op jit(solution)/shard_map/ppermute | solution.py:57
  569.5 146.9 %all-gather.9.cloned.1.call-start = ((), (), s32[]{:S(2)}) async-start(), calls=%async_computation.5 | async-start | bytes 2506752 | tf_op jit(solution)/shard_map/all_gather | solution.py:906
  581.8 17.9 %collective-permute-start.26 = (bf16[24,3072]{1,0:T(8,128)(2,1)S(1)}, bf16[24,3072]{1,0:T(8,128)(2,1)S(1)}, u32[]{:S(2)}, u32[]{:S(2)}) collective-permute-start(bf16[24,3072]{1,0:T(8,128)(2,1)S(1)} %fusion.19.rest_11_), channel_id=1, source_target_pairs={{0,16},{2,18},{4,20},{6,22},{8,24},{10,26},{12,28},{14,30},{16,0},... | collective-permute-start | bytes 442376 | tf_op jit(solution)/shard_map/ppermute | solution.py:57
  583.6 17.6 %collective-permute-start.27 = (bf16[96,1664]{1,0:T(8,128)(2,1)S(1)}, bf16[96,1664]{1,0:T(8,128)(2,1)}, u32[]{:S(2)}, u32[]{:S(2)}) collective-permute-start(bf16[96,1664]{1,0:T(8,128)(2,1)S(1)} %fusion.9.rest_12_), channel_id=1, source_target_pairs={{0,8},{2,10},{4,12},{6,14},{8,0},{10,2},{12,4},{14,6},{16,24},{18,... | collective-permute-start | bytes 958472 | tf_op jit(solution)/shard_map/ppermute | solution.py:57
  602.2 23.8 %collective-permute-start.30 = (bf16[48,3072]{1,0:T(8,128)(2,1)S(1)}, bf16[48,3072]{1,0:T(8,128)(2,1)S(1)}, u32[]{:S(2)}, u32[]{:S(2)}) collective-permute-start(bf16[48,3072]{1,0:T(8,128)(2,1)S(1)} %bitcast_select_fusion.6), channel_id=1, source_target_pairs={{0,8},{2,10},{4,12},{6,14},{8,0},{10,2},{12,4},{14,6},{16,24},{18,... | collective-permute-start | bytes 884744 | tf_op jit(solution)/shard_map/ppermute | solution.py:57
  605.2 20.8 %collective-permute-start.31 = (bf16[96,1664]{1,0:T(8,128)(2,1)S(1)}, bf16[96,1664]{1,0:T(8,128)(2,1)S(1)}, u32[]{:S(2)}, u32[]{:S(2)}) collective-permute-start(bf16[96,1664]{1,0:T(8,128)(2,1)S(1)} %add_convert_fusion.3), channel_id=1, source_target_pairs={{0,16},{2,18},{4,20},{6,22},{8,24},{10,26},{12,28},{14,30},{16,0},... | collective-permute-start | bytes 958472 | tf_op jit(solution)/shard_map/ppermute | solution.py:57
  608.6 17.4 %collective-permute-start.32 = (bf16[96,768]{1,0:T(8,128)(2,1)S(1)}, bf16[96,768]{1,0:T(8,128)(2,1)S(1)}, u32[]{:S(2)}, u32[]{:S(2)}) collective-permute-start(bf16[96,768]{1,0:T(8,128)(2,1)S(1)} %fusion.18), channel_id=1, source_target_pairs={{0,8},{2,10},{4,12},{6,14},{8,0},{10,2},{12,4},{14,6},{16,24},{18,... | collective-permute-start | bytes 442376 | tf_op jit(solution)/shard_map/ppermute | solution.py:57
  628.6 23.9 %collective-permute-start.34 = (bf16[96,3072]{1,0:T(8,128)(2,1)S(1)}, bf16[96,3072]{1,0:T(8,128)(2,1)S(1)}, u32[]{:S(2)}, u32[]{:S(2)}) collective-permute-start(bf16[96,3072]{1,0:T(8,128)(2,1)S(1)} %bitcast_select_fusion.3), channel_id=1, source_target_pairs={{0,4},{2,6},{4,0},{6,2},{8,12},{10,14},{12,8},{14,10},{16,20},{18,... | collective-permute-start | bytes 1769480 | tf_op jit(solution)/shard_map/ppermute | solution.py:57
  631.0 21.6 %collective-permute-start.35 = (bf16[96,1664]{1,0:T(8,128)(2,1)S(1)}, bf16[96,1664]{1,0:T(8,128)(2,1)S(1)}, u32[]{:S(2)}, u32[]{:S(2)}) collective-permute-start(bf16[96,1664]{1,0:T(8,128)(2,1)S(1)} %add_convert_fusion.2), channel_id=1, source_target_pairs={{0,4},{2,6},{4,0},{6,2},{8,12},{10,14},{12,8},{14,10},{16,20},{18,... | collective-permute-start | bytes 958472 | tf_op jit(solution)/shard_map/ppermute | solution.py:57
  656.4 37.1 %collective-permute-start.45 = (bf16[1024,768]{1,0:T(8,128)(2,1)}, bf16[1024,768]{1,0:T(8,128)(2,1)}, u32[]{:S(2)}, u32[]{:S(2)}) collective-permute-start(bf16[1024,768]{1,0:T(8,128)(2,1)} %get-tuple-element.180), channel_id=1, source_target_pairs={{0,1},{1,0},{2,3},{3,2},{4,5},{5,4},{6,7},{7,6},{8,9},{9,8},{10,11... | collective-permute-start | bytes 4718600 | tf_op jit(solution)/shard_map/ppermute | solution.py:57
  673.0 23.8 %collective-permute-start.42 = (bf16[192,768]{1,0:T(8,128)(2,1)S(1)}, bf16[192,768]{1,0:T(8,128)(2,1)S(1)}, u32[]{:S(2)}, u32[]{:S(2)}) collective-permute-start(bf16[192,768]{1,0:T(8,128)(2,1)S(1)} %bitcast_select_fusion.5.refs_2_), channel_id=1, source_target_pairs={{0,2},{2,0},{4,6},{6,4},{8,10},{10,8},{12,14},{14,12},{16,18},{18,... | collective-permute-start | bytes 884744 | tf_op jit(solution)/shard_map/ppermute | solution.py:57
  674.0 22.8 %collective-permute-start.43 = (bf16[96,768]{1,0:T(8,128)(2,1)S(1)}, bf16[96,768]{1,0:T(8,128)(2,1)S(1)}, u32[]{:S(2)}, u32[]{:S(2)}) collective-permute-start(bf16[96,768]{1,0:T(8,128)(2,1)S(1)} %add_convert_fusion.6), channel_id=1, source_target_pairs={{0,4},{2,6},{4,0},{6,2},{8,12},{10,14},{12,8},{14,10},{16,20},{18,... | collective-permute-start | bytes 442376 | tf_op jit(solution)/shard_map/ppermute | solution.py:57
  (107 other events, 847.1 us)
Sparse Core Ops, SparseCore 0:
  17.7 42.0 all-gather.4
  73.0 54.6 all-gather.6
  290.9 109.7 reduce-scatter.4
  407.4 113.6 reduce-scatter.2
  569.6 50.5 all-gather.10
  622.4 44.0 all-gather.8

commit v3 on v2

--- a/solution.py
+++ b/solution.py
@@ -261,7 +261,7 @@
     out_ref[...] = total.astype(out_ref.dtype)
 
 
-def input_grad_part(dbr, grads, weight, start, tokens, dtype, tile, after=()):
+def input_grad_part(dbr, grads, weight, start, tokens, dtype, tile, after=(), whole=False):
     width = dbr.shape[1]
     counts, pieces, table, scratch = weight_operands([weight], (start // tile, 0), after)
     shifted = lambda i, t: (i + t[0], 0)
@@ -273,19 +273,44 @@
             in_specs=[pl.BlockSpec((tile, width), shifted)]
             + [pl.BlockSpec((tile, g.shape[1]), shifted) for g in grads]
             + [ANY] * len(pieces),
-            out_specs=pl.BlockSpec((tile, width), lambda i, t: (i, 0)),
+            out_specs=pl.BlockSpec((tile, width), shifted if whole else lambda i, t: (i, 0)),
             scratch_shapes=scratch,
         ),
-        out_shape=jax.ShapeDtypeStruct((tokens, width), dtype),
+        out_shape=jax.ShapeDtypeStruct((dbr.shape[0] if whole else tokens, width), dtype),
         compiler_params=params(48),
         cost_estimate=cost(6 * tokens * width * width),
     )(table, dbr, *grads, *pieces)
+
+
+def place_kernel(table, in_ref, old_ref, out_ref):
+    del table, old_ref
+    out_ref[...] = in_ref[...].astype(out_ref.dtype)
+
+
+def placed(part, array, start, tile):
+    rows, width = part.shape
+    return pl.pallas_call(
+        place_kernel,
+        grid_spec=pltpu.PrefetchScalarGridSpec(
+            num_scalar_prefetch=1,
+            grid=(rows // tile,),
+            in_specs=[pl.BlockSpec((tile, width), lambda i, t: (i, 0)), ANY],
+            out_specs=pl.BlockSpec((tile, width), lambda i, t: (i + t[0], 0)),
+        ),
+        out_shape=jax.ShapeDtypeStruct(array.shape, array.dtype),
+        input_output_aliases={2: 0},
+        cost_estimate=CHEAP,
+    )((start // tile).astype(jnp.int32).reshape(1), part, array)
 
 
 BQ = 256
 BK_FWD = 512
 BK_BACK = 256
 VROWS = HDIM + 16
+
+
+def lanes_where(condition):
+    return jnp.where(condition(lane_iota((1, LANES))), 1.0, 0.0).astype(BF)
 
 
 def spread_pairs(whole, source, features, group):
@@ -322,12 +347,11 @@
                     vt[2 * g + h, HDIM:, b : b + 256] = jnp.ones((16, 256), BF)
 
     qf = qf_ref[...]
-    even = lane_iota(qf.shape) < HDIM
-    zero = jnp.zeros_like(qf)
+    even, odd = lanes_where(lambda lane: lane < HDIM), lanes_where(lambda lane: lane >= HDIM)
     for g in range(group):
         q = q_ref[:, g * LANES : (g + 1) * LANES]
-        qx[g, :BQ, :LANES] = jnp.where(even, q, zero)
-        qx[g, BQ:, :LANES] = jnp.where(even, zero, q)
+        qx[g, :BQ, :LANES] = q * even
+        qx[g, BQ:, :LANES] = q * odd
         qx[g, :BQ, LANES:] = qf
         qx[g, BQ:, LANES:] = qf
     best[...] = jnp.full_like(best, NEGATIVE)
@@ -429,20 +453,22 @@
         dv_acc[...] = jnp.zeros_like(dv_acc)
 
     qf = qf_ref[...]
-    lanes = lane_iota(qf.shape)
-    even = lanes < HDIM
-    zero = jnp.zeros_like(qf)
+    even, odd = lanes_where(lambda lane: lane < HDIM), lanes_where(lambda lane: lane >= HDIM)
     for g in range(group):
         cols = slice(g * LANES, (g + 1) * LANES)
         for whole, source in ((qx, q_ref[:, cols]), (dox, do_ref[:, cols])):
-            whole[g, :BQ, :LANES] = jnp.where(even, source, zero)
-            whole[g, BQ:, :LANES] = jnp.where(even, zero, source)
+            whole[g, :BQ, :LANES] = source * even
+            whole[g, BQ:, :LANES] = source * odd
         for h in range(2):
-            lane = lanes - (2 * (pair + g) + h)
-            of_lse = (lanes < SEG) | (lane == 8) | (lane == 20) | (lane == 32)
-            of_delta = (lane == 44) | (lane == 56) | (lane == 68)
-            qx[g, h * BQ : (h + 1) * BQ, LANES:] = jnp.where(of_lse, qf, zero)
-            dox[g, h * BQ : (h + 1) * BQ, LANES:] = jnp.where(of_delta, qf, zero)
+            head = 2 * (pair + g) + h
+
+            def at(lane, starts):
+                return functools.reduce(jnp.logical_or, [lane == start + head for start in starts])
+
+            of_lse = lanes_where(lambda lane: (lane < SEG) | at(lane, (8, 20, 32)))
+            of_delta = lanes_where(lambda lane: at(lane, (44, 56, 68)))
+            qx[g, h * BQ : (h + 1) * BQ, LANES:] = qf * of_lse
+            dox[g, h * BQ : (h + 1) * BQ, LANES:] = qf * of_delta
     dq_acc[...] = jnp.zeros_like(dq_acc)
     first, count = spans[where], spans[where + 1]
 
@@ -659,7 +685,7 @@
     cot_refs, rest = rest[:parts], rest[parts:]
     out_ref, stat_ref, qf_ref, dp_ref, fg_ref, fu_ref, g2_ref = rest[:7]
     pieces, rest = rest[7 : 7 + sum(counts)], rest[7 + sum(counts) :]
-    dffn_ref, dgate_ref, dup_ref, gf_ref, wd, sems = rest
+    dffn_ref, dgu_ref, gf_ref, wd, sems = rest
     groups = grouped_copies(counts, table, pieces, [wd], sems)
     begin = (pl.program_id(0) == 0) & (pl.program_id(1) == 0)
 
@@ -683,15 +709,18 @@
     def _():
         wait_all(*groups)
 
+    ff = wd.shape[0]
+
     def load(c):
         return dot_bt(dffn, wd[c * FF_CHUNK : (c + 1) * FF_CHUNK, :])
 
     def work(c, dhid):
         cols = slice(c * FF_CHUNK, (c + 1) * FF_CHUNK)
-        dgate_ref[:, cols] = (dhid * fg_ref[:, cols].astype(F32)).astype(BF)
-        dup_ref[:, cols] = (dhid * fu_ref[:, cols].astype(F32)).astype(BF)
-
-    staggered(wd.shape[0] // FF_CHUNK, load, work, lambda c, worked: None)
+        dgu_ref[:, cols] = (dhid * fg_ref[:, cols].astype(F32)).astype(BF)
+        after = slice(ff + c * FF_CHUNK, ff + (c + 1) * FF_CHUNK)
+        dgu_ref[:, after] = (dhid * fu_ref[:, cols].astype(F32)).astype(BF)
+
+    staggered(ff // FF_CHUNK, load, work, lambda c, worked: None)
 
 
 def hidden_back(cots, lead, output, stat, query_feat, dpool, factors, gain2, down, rows, tile):
@@ -713,13 +742,12 @@
             + hidden * 2
             + [pl.BlockSpec((1, width), lambda r, i, *_: (0, 0))]
             + [ANY] * len(pieces),
-            out_specs=wide + hidden * 2 + [pl.BlockSpec((8, width), lambda r, i, *_: (0, 0))],
+            out_specs=wide + row_specs([None], tile, 2 * ff, steps) + [pl.BlockSpec((8, width), lambda r, i, *_: (0, 0))],
             scratch_shapes=scratch,
         ),
         out_shape=[
             jax.ShapeDtypeStruct((tokens, width), BF),
-            jax.ShapeDtypeStruct((tokens, ff), BF),
-            jax.ShapeDtypeStruct((tokens, ff), BF),
+            jax.ShapeDtypeStruct((tokens, 2 * ff), BF),
             jax.ShapeDtypeStruct((8, width), F32),
         ],
         compiler_params=params(58),
@@ -728,8 +756,8 @@
 
 
 def branch_back_kernel(counts, table, *refs):
-    dffn_ref, nl_ref, stat_ref, qf_ref, dgate_ref, dup_ref, att_ref, lse_ref, g1_ref, head_ref = refs[:10]
-    rest = refs[10:]
+    dffn_ref, nl_ref, stat_ref, qf_ref, dgu_ref, att_ref, lse_ref, g1_ref, head_ref = refs[:9]
+    rest = refs[9:]
     pieces, rest = rest[: sum(counts)], rest[sum(counts) :]
     dbr_ref, datt_ref, feat_ref, ga_ref, wo, ws, sems = rest
     groups = grouped_copies(counts, table, pieces, (wo, ws), sems)
@@ -741,8 +769,7 @@
         ga_ref[...] = jnp.zeros_like(ga_ref)
         wait_all(*groups)
 
-    ff = dgate_ref.shape[1]
-    dnormed = dffn_ref[...].astype(F32) + dot_bt(dgate_ref[...], ws[:, :ff]) + dot_bt(dup_ref[...], ws[:, ff:])
+    dnormed = dffn_ref[...].astype(F32) + dot_bt(dgu_ref[...], ws[...])
     gain1 = g1_ref[...]
     unit1 = nl_ref[...].astype(F32) / gain1
     dbr = norm_back(dnormed * gain1, unit1, stat_ref[:, 0:1]).astype(BF)
@@ -765,13 +792,13 @@
     feat_ref[...] = feat.astype(BF)
 
 
-def branch_back(dffn, low, stat, query_feat, dgate, dup, attended, lse, gain1, weights, rows, tile, after=()):
+def branch_back(dffn, low, stat, query_feat, dgu, attended, lse, gain1, weights, rows, tile, after=()):
     tokens, width = low.shape
-    ff = dgate.shape[1]
+    ff = dgu.shape[1] // 2
     steps = tokens // rows // tile
     counts, pieces, table, scratch = weight_operands(weights, (0, 0), after)
     wide, narrow = row_specs([None], tile, width, steps), row_specs([None], tile, LANES, steps)
-    hidden = row_specs([None], tile, ff, steps)
+    hidden = row_specs([None], tile, 2 * ff, steps)
     heads = (jnp.arange(width)[:, None] // HDIM == jnp.arange(LANES)[None, :]).astype(BF)
     return pl.pallas_call(
         functools.partial(branch_back_kernel, counts),
@@ -780,7 +807,7 @@
             grid=(rows, steps),
             in_specs=wide * 2
             + narrow * 2
-            + hidden * 2
+            + hidden
             + wide
             + narrow
             + [pl.BlockSpec((1, width), lambda r, i, *_: (0, 0))]
@@ -797,7 +824,7 @@
         ],
         compiler_params=params(58),
         cost_estimate=cost(2 * tokens * width * (width + 2 * ff)),
-    )(table, dffn, low, stat, query_feat, dgate, dup, attended, lse, gain1, heads, *pieces)
+    )(table, dffn, low, stat, query_feat, dgu, attended, lse, gain1, heads, *pieces)
 
 
 def bits_of(axis):
@@ -861,6 +888,8 @@
 
 class Reduction:
     def __init__(self, part, short=False):
+        fsdp_bits, lines = len(list(bits_of("fsdp"))), len(list(bits_of("blk"))) - 2
+        self.left = 4 + fsdp_bits + lines * (1 if short else 2)
         self.stages = reduction(part, short)
         self.sends, self.routes = next(self.stages)
 
@@ -877,6 +906,7 @@
         return self.sends, came
 
     def take_in(self, came):
+        self.left -= 1
         self.sends, self.routes = self.stages.send(came)
 
 
@@ -901,12 +931,80 @@
     return both[:count], late
 
 
-def reduced(part):
-    part = lax.psum_scatter(part, ("fsdp", "blk"), scatter_dimension=0, tiled=True)
-    return lax.all_gather(part, "blk", axis=0, tiled=True)
-
-
-def weight_grad(pairs, beside_it=None):
+def turned(block):
+    return block.astype(F32).T.astype(BF)
+
+
+def swiglu_part_kernel(low_ref, grad_ref, out_ref, low_turned):
+    tokens = low_ref.shape[0]
+
+    @pl.when(pl.program_id(0) == 0)
+    def _():
+        for b in range(0, tokens, 256):
+            low_turned[:, b : b + 256] = turned(low_ref[b : b + 256, :])
+
+    part = dot(low_turned[...], grad_ref[...]).astype(BF)
+    rows = out_ref.shape[2]
+    for f in range(out_ref.shape[1]):
+        out_ref[0, f] = part[f * rows : (f + 1) * rows]
+
+
+def down_part_kernel(hidden_ref, dffn_ref, old_ref, out_ref):
+    del old_ref
+    part = dot(turned(hidden_ref[...]), dffn_ref[...]).astype(BF)
+    rows, cols = out_ref.shape[2:]
+    across = part.shape[1] // cols
+    for n in range(out_ref.shape[0]):
+        down, along = n // across * rows, n % across * cols
+        out_ref[n, 0] = part[down : down + rows, along : along + cols]
+
+
+def shares_fit(low, hidden):
+    blocks, split = lax.axis_size("blk"), lax.axis_size("fsdp")
+    width, ff = low.shape[1], hidden.shape[1]
+    cols = 2 * ff // blocks
+    return cols % LANES == 0 and width % cols == 0 and ff * width // (split * blocks * cols) * 2 == width // split
+
+
+def feed_forward_shares(low, d_gate_up, hidden, d_ffn):
+    blocks, split = lax.axis_size("blk"), lax.axis_size("fsdp")
+    tokens, width = low.shape
+    ff = hidden.shape[1]
+    cols, rows = 2 * ff // blocks, width // split
+    down_rows = rows // 2
+    across = width // cols
+    shape = jax.ShapeDtypeStruct((blocks, split, rows + down_rows, cols), BF)
+    whole = lambda a: pl.BlockSpec(a.shape, lambda *_: (0, 0))
+    shares = pl.pallas_call(
+        swiglu_part_kernel,
+        grid=(blocks,),
+        in_specs=[whole(low), pl.BlockSpec((tokens, cols), lambda j: (0, j))],
+        out_specs=pl.BlockSpec((1, split, rows, cols), lambda j: (j, 0, 0, 0)),
+        out_shape=shape,
+        scratch_shapes=[pltpu.VMEM((width, tokens), BF)],
+        compiler_params=params(48),
+        cost_estimate=cost(4 * tokens * width * ff),
+    )(low, d_gate_up)
+    taken = 2 * down_rows
+    steps = ff // split // taken
+    return pl.pallas_call(
+        down_part_kernel,
+        grid=(split, steps),
+        in_specs=[pl.BlockSpec((tokens, taken), lambda f, j: (0, f * steps + j)), whole(d_ffn), ANY],
+        out_specs=pl.BlockSpec((2 * across, 1, down_rows, cols), lambda f, j: (j, f, 2, 0)),
+        out_shape=shape,
+        input_output_aliases={2: 0},
+        compiler_params=params(48),
+        cost_estimate=cost(2 * tokens * width * ff),
+    )(hidden, d_ffn, shares)
+
+
+def plain_sum(part):
+    part = lax.psum_scatter(part, "fsdp", scatter_dimension=0, tiled=True)
+    return lax.psum(part, "blk").astype(F32)
+
+
+def weight_grad(pairs, beside_it=None, after=()):
     arrays, left = [], []
     for a, b in pairs:
         place = [n for n, other in enumerate(arrays) if other is a]
@@ -928,43 +1026,75 @@
             out_ref[:, at : at + part.shape[1]] = part
             at += part.shape[1]
         if last:
-            out_ref[:, at:] = refs[-2][...]
-
+            out_ref[:, at:] = refs[len(arrays)][...]
+
+    whole = pl.BlockSpec(memory_space=pltpu.VMEM)
     return pl.pallas_call(
         kernel,
+        in_specs=[whole] * (len(arrays) + len(last)) + [ANY] * len(after),
         out_shape=jax.ShapeDtypeStruct((pairs[0][0].shape[1], cols), BF),
         compiler_params=params(56),
         cost_estimate=cost(2 * pairs[0][0].shape[0] * pairs[0][0].shape[1] * cols),
-    )(*arrays, *last)
-
-
-def unfold_kernel(columns, table, *refs):
-    pairs = 2 * (1 + max(n for parts in columns for n, _, _ in parts))
+    )(*arrays, *last, *after)
+
+
+def unfold_kernel(kinds, columns, table, *refs):
     own = pl.program_id(0) == table[0]
-    values = [jnp.where(own, refs[n][...], refs[n + 1][...]) for n in range(0, pairs, 2)]
-    for ref, parts in zip(refs[pairs:], columns):
-        at = 0
+    values, at = [], 0
+    for kind in kinds:
+        values.append(refs[at][...] if kind == 1 else jnp.where(own, refs[at][...], refs[at + 1][...]))
+        at += kind
+    for ref, parts in zip(refs[at:], columns):
+        to = 0
         for n, start, wide in parts:
-            ref[:, at : at + wide] = values[n][:, start : start + wide].astype(F32)
-            at += wide
-
-
-def unfold(pairs, columns):
-    rows = pairs[0][0].shape[0]
+            ref[:, to : to + wide] = values[n][:, start : start + wide].astype(F32)
+            to += wide
+
+
+def unfold(results, columns):
+    rows = sum(a.shape[0] for a in results[0]) // 2
     block = rows // 2 if rows % 32 == 0 else rows
     steps = rows // block
+    maps = {2: lambda c, i, t: (i, 0), 1: lambda c, i, t: (c * steps + i, 0)}
     return pl.pallas_call(
-        functools.partial(unfold_kernel, columns),
+        functools.partial(unfold_kernel, [len(r) for r in results], columns),
         grid_spec=pltpu.PrefetchScalarGridSpec(
             num_scalar_prefetch=1,
             grid=(2, steps),
-            in_specs=[pl.BlockSpec((block, a.shape[1]), lambda c, i, t: (i, 0)) for pair in pairs for a in pair],
-            out_specs=[pl.BlockSpec((block, sum(p[2] for p in parts)), lambda c, i, t: (c * steps + i, 0)) for parts in columns],
+            in_specs=[pl.BlockSpec((block, a.shape[1]), maps[len(r)]) for r in results for a in r],
+            out_specs=[pl.BlockSpec((block, sum(p[2] for p in parts)), maps[1]) for parts in columns],
         ),
         out_shape=[jax.ShapeDtypeStruct((2 * rows, sum(p[2] for p in parts)), F32) for parts in columns],
         compiler_params=params(40),
         cost_estimate=CHEAP,
-    )((lax.axis_index("blk") % 2).reshape(1), *[a for pair in pairs for a in pair])
+    )((lax.axis_index("blk") % 2).reshape(1), *[a for r in results for a in r])
+
+
+def spread_kernel(both_ref, swiglu_ref, down_ref):
+    rows = swiglu_ref.shape[0]
+    swiglu_ref[...] = both_ref[0, :rows, :].astype(F32)
+    down_ref[...] = both_ref[0, rows:, :].astype(F32)
+
+
+def spread(both, width):
+    blocks, height, cols = both.shape
+    rows = height * 2 // 3
+    across = width // cols
+    return pl.pallas_call(
+        spread_kernel,
+        grid=(blocks,),
+        in_specs=[pl.BlockSpec((1, height, cols), lambda n: (n, 0, 0))],
+        out_specs=[
+            pl.BlockSpec((rows, cols), lambda n: (0, n)),
+            pl.BlockSpec((rows // 2, cols), lambda n: (n // across, n % across)),
+        ],
+        out_shape=[
+            jax.ShapeDtypeStruct((rows, blocks * cols), F32),
+            jax.ShapeDtypeStruct((blocks // across * (rows // 2), width), F32),
+        ],
+        compiler_params=params(40),
+        cost_estimate=CHEAP,
+    )(both)
 
 
 def contrast(sums, lengths, pairing, row_mode, row_ids):
@@ -1047,10 +1177,9 @@
     gains = jnp.stack([attn_gain, ffn_gain])
     if row_mode:
         qkv_share = flipped(share_of(qkv_weight), "fsdp", 1)
+        moved, qkv_share = tied([take(tokens, 1 - mine, 0), qkv_share])
+        moved = flipped(moved, "fsdp", 1)
         qkv = from_shares(qkv_weight, qkv_share)
-        moved = flipped(take(tokens, 1 - mine + zero_after(qkv_share), 0), "fsdp", 1)
-        swiglu_share = flipped(share_of(swiglu_weight, zero_after(moved)), "fsdp", 1)
-        swiglu = from_shares(swiglu_weight, swiglu_share)
         gains = in_order([gains, flipped(gains, "fsdp", 1)], mine)
         gains = jnp.concatenate([gains[0], gains[1]], axis=1)
     else:
@@ -1097,12 +1226,15 @@
 
     if row_mode:
         tables = (*tables_q, qkv)
-        shift = zero_after(moved)
-        halves = [half_of(w, shift) for w in (out_weight, down_weight)]
+        share = share_of(swiglu_weight, zero_after(moved))
+        share_came = flipped(share, "fsdp", 1)
+        old = project(take(tokens, mine, 0), mine * shard_len, *tables, [], small_tile, [moved, share])
+        *old, share_came = tied([*old, share_came])
+        swiglu = from_shares(swiglu_weight, share_came)
+        shift = zero_after(old[0])
+        halves = [half_of(out_weight, shift), half_of(down_weight, shift)]
         firsts = [flipped(h, "fsdp", 1) for h in halves]
-        query, key, value, x = project(take(tokens, mine, 0), mine * shard_len, *tables, [], small_tile, halves)
-        old = [query, key, value, x]
-        query, key, value, x = project(moved, (1 - mine) * shard_len, *tables, old, small_tile)
+        query, key, value, x = project(moved, (1 - mine) * shard_len, *tables, old, small_tile, halves)
         key_all, value_all = key, value
     else:
         query, key, value, x = project(tokens.reshape(-1, width), 0, *tables_q, qkv, [], small_tile)
@@ -1135,30 +1267,33 @@
     d_pool = jnp.pad(d_pool, ((0, 0), (0, LANES - SEG), (0, 0)))
     lse_columns = jnp.pad(lse.reshape(HEADS, tokens_here).T, ((0, 0), (0, LANES - HEADS)))
 
-    d_ffn, d_gate, d_up, gain2_part = hidden_back(
+    d_ffn, d_gate_up, gain2_part = hidden_back(
         cots, lead, output, stat, query_feat, d_pool, factors, gain2, down, rows, small_tile
     )
+    fast = row_mode and shares_fit(low_normed, hidden)
+    if fast:
+        share = feed_forward_shares(low_normed, d_gate_up, hidden, d_ffn)
+        after = [share]
+        share = lax.psum_scatter(share.reshape(-1, share.shape[-1]), ("blk", "fsdp"), scatter_dimension=0, tiled=True)
+    else:
+        swiglu_grad = plain_sum(dot_at(low_normed, d_gate_up).astype(BF))
+        down_grad = plain_sum(dot_at(hidden, d_ffn).astype(BF))
+        after = []
+    d_branch, d_attended, back_feat, gain1_part = branch_back(
+        d_ffn, low_normed, stat, query_feat, d_gate_up, attended, lse_columns, gain1, (outer, swiglu), rows, small_tile,
+        after,
+    )
     if row_mode:
-        d_gate, output_came = tied([d_gate, output_came])
+        d_branch, output_came = tied([d_branch, output_came])
         layer_output = lax.dynamic_slice_in_dim(output, mine * shard_len, shard_len, 0)
         layer_output = in_order([layer_output, output_came], mine)
-    down_rows = reduced(dot_at(hidden, d_ffn).astype(BF))
-    gate_rows = reduced(dot_at(low_normed, d_gate).astype(BF))
-    up_sum = Reduction(dot_at(low_normed, d_up).astype(BF))
-    (d_branch, d_attended, back_feat, gain1_part), _ = beside(
-        lambda sent: branch_back(
-            d_ffn, low_normed, stat, query_feat, d_gate, d_up, attended, lse_columns, gain1, (outer, swiglu), rows,
-            small_tile, sent,
-        ),
-        [up_sum],
-    )
     part_rows = jnp.arange(width, dtype=jnp.int32) % (width // split)
     losses = jnp.where(part_rows == place, loss if row_mode else loss / split, 0.0)
     losses_high = lax.reduce_precision(losses, 8, 7)
     small = jnp.stack([jnp.sum(gain1_part, 0), jnp.sum(gain2_part, 0), losses_high, losses - losses_high], axis=1)
     small = jnp.pad(small, ((0, 0), (0, LANES - 4))).astype(BF)
-    grads, qkv_sums = [], []
-    running = [up_sum]
+    out_sum = Reduction(weight_grad([(attended, d_branch)], small))
+    grads, running = [], [out_sum]
     for n in range(PAIRS // BACK_PAIRS):
         columns, _ = beside(
             lambda sent: attend_back(
@@ -1175,13 +1310,13 @@
                 return grad.reshape(tokens_here, -1)
 
             columns = [columns[0], own_part(columns[1]), own_part(columns[2])]
+        if fast and n == PAIRS // BACK_PAIRS - 1:
+            *columns, share = tied([*columns, share])
+            both = lax.all_gather(share, "blk", axis=0)
         grads += columns
-        pairs = [(x, g) for g in columns]
-        if n == 0:
-            qkv_sums.append(Reduction(weight_grad([*pairs, (attended, d_branch)], small), True))
-        else:
-            qkv_sums.append(Reduction(weight_grad(pairs), True))
-        running = [up_sum, *qkv_sums]
+        (part,), _ = beside(lambda sent: [weight_grad([(x, g) for g in columns], None, sent)], running)
+        running.append(Reduction(part, True))
+    qkv_sums = running[1:]
     if row_mode:
         (moved,), _ = beside(
             lambda sent: [
@@ -1189,25 +1324,30 @@
             ],
             running,
         )
-        came = flipped(moved, "fsdp", 1)
+        exchange = flipped(moved, "fsdp", 1)
         (kept,), _ = beside(
-            lambda sent: [input_grad_part(d_branch, grads, qkv, mine * shard_len, shard_len, F32, small_tile, sent)],
+            lambda sent: [
+                input_grad_part(d_branch, grads, qkv, mine * shard_len, shard_len, F32, small_tile, sent, True)
+            ],
             running,
         )
-        input_grad = in_order([kept, came.astype(F32)], mine)
+        for _ in range(2):
+            beside(lambda _: [], running)
+        kept, exchange = tied([kept, exchange])
+        (input_grad,), _ = beside(
+            lambda _: [placed(exchange, kept, (1 - mine) * shard_len, small_tile)], running
+        )
+        input_grad = input_grad.reshape(tokens.shape)
     else:
         input_grad = input_grad_part(d_branch, grads, qkv, 0, tokens_here, F32, small_tile).reshape(tokens.shape)
+    if fast:
+        (swiglu_grad, down_grad), _ = beside(lambda _: spread(both, width), running)
     while any(not r.done for r in running):
         beside(lambda _: [], running)
     wide, groups = BACK_PAIRS * LANES, PAIRS // BACK_PAIRS
-    ff = d_gate.shape[1]
-    half = width // split // 2
-    up_rows = in_order(up_sum.result, place % 2).reshape(2 * half, ff)
-    swiglu_grad = jnp.concatenate([gate_rows, up_rows], axis=1).astype(F32)
     qkv_columns = [(g, part * wide, wide) for part in range(3) for g in range(groups)]
-    qkv_grad, out_grad, small = unfold(
-        [r.result for r in qkv_sums], [qkv_columns, [(0, 3 * wide, width)], [(0, 3 * wide + width, LANES)]]
-    )
+    (qkv_grad,) = unfold([r.result for r in qkv_sums], [qkv_columns])
+    out_grad, small = unfold([out_sum.result], [[(0, 0, width)], [(0, width, LANES)]])
     queries = lax.axis_size("blk") * pairing.shape[0]
     return (
         jnp.sum(small[:, 2:4]) / queries,
@@ -1216,13 +1356,13 @@
         qkv_grad,
         out_grad,
         swiglu_grad,
-        down_rows.astype(F32),
+        down_grad,
         small[:, 0],
         small[:, 1],
     )
 
 
-BACK_PAIRS = 2
+BACK_PAIRS = 3
 
 
 def solution(mesh):

time: 741 us -> 660 us (0.89); the launches traced: 731 us -> 658 us
  Pallas kernels: 359 us -> 418 us
  waiting for transfers between devices: 122 us -> 74.4 us
  matrix products: 45 us -> 0.85 us
  other arithmetic: 72.5 us -> 44 us
  starting transfers between devices: 52.5 us -> 42.3 us
    pallas_call x4 -> x9, Pallas kernels: 27.1 us -> 88.1 us  [the longest x1 32.3 us: feed_forward_shares(): pl.pallas_call(swiglu_part_kernel, grid=(blocks,), in_specs=[whole(low),...]
    ppermute x46 -> x39, waiting for transfers between devices: 122 us -> 73.7 us  [flipped(): return lax.ppermute(block, axis, route)]
    dot_general x4 -> x1, matrix products: 44.3 us -> 0.17 us  [dot_at(): lax.dot_general(a, b, (((0,), (0,)), ((), ())), preferred_element_type=F32)]
    convert_element_type x3 -> x0, other arithmetic: 14.1 us -> none  [the longest x1 6.56 us: shards(): swiglu_grad = jnp.concatenate([gate_rows, up_rows], axis=1).astype(F32)]
    ppermute x46 -> x39, starting transfers between devices: 52.3 us -> 42.2 us  [flipped(): return lax.ppermute(block, axis, route)]
    select_n x10 -> x7, other arithmetic: 19 us -> 9.07 us  [in_order(): return jnp.where(first, parts[0][None], parts[1][None])]
    pallas_call x3 -> x2, Pallas kernels: 110 us -> 103 us  [attend_back(): pl.pallas_call(functools.partial(attend_back_kernel, group, base, len(aft...]
    unnamed x179 -> x163, local copies, waits for them, and re-layouts: 20.3 us -> 26.8 us
  transfers between devices with their start and end apart: 52 -> 43, of which waited for: 15 -> 14; matrix products, arithmetic and copies ran while one was open for 18% -> 11% of each run, Pallas kernels for 45% -> 63%
where the time goes in v3:
time: 660 us; the launch traced here: 658 us
  Pallas kernels  418 us (63%)
  waiting for transfers between devices  74.4 us (11%)
  local copies, waits for them, and re-layouts  59.1 us (9%)
  other arithmetic  44 us (7%)
  starting transfers between devices  42.3 us (6%)
  between operations  19.1 us (3%)
    pallas_call x2, Pallas kernels, attend_back(): pl.pallas_call(functools.partial(attend_back_kernel, group, base, len(aft...  103 us
    ppermute x39, waiting for transfers between devices, flipped(): return lax.ppermute(block, axis, route)  73.7 us
    pallas_call x1, Pallas kernels, attend(): pl.pallas_call(functools.partial(attend_kernel, group, len(after)), grid_...  57.6 us
    pallas_call x1, Pallas kernels, mix(): pl.pallas_call(functools.partial(mix_kernel, counts), grid_spec=pltpu.Pre...  54.9 us
    pallas_call x1, Pallas kernels, branch_back(): pl.pallas_call(functools.partial(branch_back_kernel, counts), grid_spec=p...  46 us
    ppermute x39, starting transfers between devices, flipped(): return lax.ppermute(block, axis, route)  42.2 us
    pallas_call x1, Pallas kernels, feed_forward_shares(): pl.pallas_call(swiglu_part_kernel, grid=(blocks,), in_specs=[whole(low),...  32.3 us
    pallas_call x1, Pallas kernels, hidden_back(): pl.pallas_call(functools.partial(hidden_back_kernel, counts, len(cots)),...  30.1 us
  transfers between devices with their start and end apart: 43, of which 14 were waited for; matrix products, arithmetic and copies ran while one was open for 11% of the time, Pallas kernels for 63%

profile of v3, /device:TPU:0, one launch (start us, length us, event | category | flops | bytes accessed | tf_op | source)
XLA Modules:
  0.0 658.2 jit_solution(10862760210021948549)
XLA Ops:
  15.6 3.2 dynamic-slice_bitcast_fusion.2
  23.9 5.0 fusion.5
  28.9 27.7 %collective-permute-done.1.rest_2_.in_ref = bf16[1024,768]{1,0:T(8,128)(2,1)} collective-permute-done((bf16[1024,768]{1,0:T(8,128)(2,1)}, bf16[1024,768]{1,0:T(8,128)(2,1)}, u32[]{:S(2)}, u32[]{:S(2)}) %collective-permute-start.1) | collective-permute-done | bytes 1572896 | tf_op jit(solution)/shard_map/ppermute | solution.py:57
  63.1 8.4 %shard_map.170 = (bf16[2048,768]{1,0:T(8,128)(2,1)}, bf16[2048,768]{1,0:T(8,128)(2,1)}, bf16[2048,768]{1,0:T(8,128)(2,1)}, bf16[2048,768]{1,0:T(8,128)(2,1)}) custom-call(s32[6]{0:T(128)S(1)} %stack.111.table, f32[2048,128]{1,0:T(8,128)S(1)} %copy-done.11, f32[2048,128]{1,0:T(8,128)S(1)} %get-tuple-element.207.sin_ref.sq_ref.sk_ref, ...), custom_call_target="tpu_custom_call" | custom-call | flops 14495514624 | bytes 1048576 | tf_op jit(solution)/shard_map/pallas_call | solution.py:229
  82.0 9.7 %shard_map.172 = (bf16[2048,768]{1,0:T(8,128)(2,1)}, bf16[2048,768]{1,0:T(8,128)(2,1)}, bf16[2048,768]{1,0:T(8,128)(2,1)}, bf16[2048,768]{1,0:T(8,128)(2,1)}) custom-call(s32[6]{0:T(128)S(1)} %stack.109.table, f32[2048,128]{1,0:T(8,128)S(1)} %copy-done.12, ...), custom_call_target="tpu_custom_call", output_to_operand_aliasing={{0}: (8, {}), {1}: (9, {}), {2}: (10, {}), {3}: (11, {})} | custom-call | flops 14495514624 | bytes 1048576 | tf_op jit(solution)/shard_map/pallas_call | solution.py:229
  91.6 57.6 %shard_map.173 = (bf16[2048,768]{1,0:T(8,128)(2,1)}, f32[12,1,2048]{2,1,0:T(1,128)}) custom-call(s32[16]{0:T(128)} %reshape.1323.spans, bf16[2048,768]{1,0:T(8,128)(2,1)} %get-tuple-element.108.q_ref, bf16[2048,768]{1,0:T(8,128)(2,1)} %get-tuple-element.109.k_ref, bf16[2048,768]{1,0:T(8,128)(2,1)} %get-tuple-element.110.v_ref, ...), custom_call_target="tpu_custom_call" | custom-call | flops 51539607552 | bytes 1048576 | tf_op jit(solution)/shard_map/pallas_call | solution.py:401
  158.4 54.9 %shard_map.175 = (bf16[2048,768]{1,0:T(8,128)(2,1)}, f32[2048,128]{1,0:T(8,128)}, bf16[2048,3072]{1,0:T(8,128)(2,1)}, bf16[2048,3072]{1,0:T(8,128)(2,1)}, bf16[2...) custom-call(s32[18]{0:T(128)} %stack.120.table, ...), custom_call_target="tpu_custom_call" | custom-call | flops 125627793408 | bytes 1048576 | tf_op jit(solution)/shard_map/pallas_call | solution.py:661
  221.5 3.5 collective-permute-start.11
  227.4 4.8 collective-permute-done.12
  235.7 3.7 constant_dynamic-slice_fusion
  247.0 30.1 %shard_map.177 = (bf16[2048,768]{1,0:T(8,128)(2,1)}, bf16[2048,6144]{1,0:T(8,128)(2,1)}, f32[8,768]{1,0:T(8,128)}) custom-call(s32[8]{0:T(128)} %stack.119.table, bf16[1024,768]{1,0:T(8,128)(2,1)} %get-tuple-element.196.rest_0_, bf16[1024,768]{1,0:T(8,128)(2,1)} %get-tuple-element.119.rest_1_, bf16[2048,768]{1,0:T(8,128)(2,1)} %get-tuple-element.120.rest_2_, ...), custom_call_target="tpu_custom_call" | custom-call | flops 77309411328 | bytes 1048576 | tf_op jit(solution)/shard_map/pallas_call | solution.py:733
  279.1 32.3 %shard_map.178.old_ref = bf16[16,2,576,384]{3,2,1,0:T(8,128)(2,1)} custom-call(bf16[2048,768]{1,0:T(8,128)(2,1)S(1)} %copy-done.18, bf16[2048,6144]{1,0:T(8,128)(2,1)} %get-tuple-element.127.grad_ref.refs_4_), custom_call_target="tpu_custom_call" | custom-call | flops 77309411328 | bytes 1048576 | tf_op jit(solution)/shard_map/pallas_call | solution.py:978
  311.3 14.5 %shard_map.179.refs_14_ = bf16[16,2,576,384]{3,2,1,0:T(8,128)(2,1)} custom-call(bf16[2048,3072]{1,0:T(8,128)(2,1)} %get-tuple-element.128.hidden_ref, bf16[2048,768]{1,0:T(8,128)(2,1)S(1)} %copy-done.17, bf16[16,2,576,384]{3,2,1,0:T(8,128)(2,1)} %shard_map.178.old_ref), custom_call_target="tpu_custom_call", output_to_operand_aliasing={{}: (2, {})} | custom-call | flops 38654705664 | bytes 1048576 | tf_op jit(solution)/shard_map/pallas_call | solution.py:990
  326.0 46.0 %shard_map.180 = (bf16[2048,768]{1,0:T(8,128)(2,1)}, bf16[2048,768]{1,0:T(8,128)(2,1)}, bf16[2048,128]{1,0:T(8,128)(2,1)}, f32[8,768]{1,0:T(8,128)}) custom-call(s32[12]{0:T(128)} %stack.114.table, bf16[2048,768]{1,0:T(8,128)(2,1)} %get-tuple-element.125.dffn_ref.refs_0_, bf16[2048,768]{1,0:T(8,128)(2,1)} %get-tuple-element.126.low_ref.refs_1_, ...), custom_call_target="tpu_custom_call" | custom-call | flops 86973087744 | bytes 1048576 | tf_op jit(solution)/shard_map/pallas_call | solution.py:803
  375.0 6.6 %shard_map.182 = bf16[768,896]{1,0:T(8,128)(2,1)} custom-call(bf16[2048,768]{1,0:T(8,128)(2,1)} %get-tuple-element.113.att_ref.refs_5_.refs_0_, bf16[2048,768]{1,0:T(8,128)(2,1)} %get-tuple-element.130.refs_1_.dbr_ref, bf16[768,128]{1,0:T(8,128)(2,1)} %pad.24.refs_2_), custom_call_target="tpu_custom_call" | custom-call | flops 11274289152 | bytes 1048576 | tf_op jit(solution)/shard_map/pallas_call | solution.py:1032
  383.7 51.4 %shard_map.183 = (bf16[2048,384]{1,0:T(8,128)(2,1)}, bf16[2048,384]{1,0:T(8,128)(2,1)}, bf16[2048,384]{1,0:T(8,128)(2,1)}) custom-call(s32[16]{0:T(128)} %reshape.1332.spans, bf16[2048,768]{1,0:T(8,128)(2,1)} %get-tuple-element.108.q_ref, bf16[2048,768]{1,0:T(8,128)(2,1)} %get-tuple-element.133.do_ref, bf16[2048,768]{1,0:T(8,128)(2,1)} %get-tuple-element.109.k_ref, ...), custom_call_target="tpu_custom_call" | custom-call | flops 51539607552 | bytes 1048576 | tf_op jit(solution)/shard_map/pallas_call | solution.py:526
  440.9 9.6 %shard_map.185.refs_0_ = bf16[768,1152]{1,0:T(8,128)(2,1)} custom-call(bf16[2048,768]{1,0:T(8,128)(2,1)} %get-tuple-element.114.x_ref.refs_0_, bf16[2048,384]{1,0:T(8,128)(2,1)} %get-tuple-element.139.refs_1_.rest_0_, bf16[2048,384]{1,0:T(8,128)(2,1)} %get-tuple-element.140.refs_2_.rest_1_, bf16[2048,384]{1,0:T(8,128)(2,1)} %get-tuple-element.141.refs_3_.rest_2_, ...), custom_call_target="tpu_custom_call" | custom-call | flops 14495514624 | bytes 1048576 | tf_op jit(solution)/shard_map/pallas_call | solution.py:1032
  450.4 4.1 collective-permute-done.16.refs_1_
  456.4 3.3 collective-permute-start.17
  461.8 51.8 %shard_map.187 = (bf16[2048,384]{1,0:T(8,128)(2,1)}, bf16[2048,384]{1,0:T(8,128)(2,1)}, bf16[2048,384]{1,0:T(8,128)(2,1)}) custom-call(s32[16]{0:T(128)} %reshape.1332.spans, bf16[2048,768]{1,0:T(8,128)(2,1)} %get-tuple-element.108.q_ref, bf16[2048,768]{1,0:T(8,128)(2,1)} %get-tuple-element.133.do_ref, bf16[2048,768]{1,0:T(8,128)(2,1)} %get-tuple-element.109.k_ref, ...), custom_call_target="tpu_custom_call" | custom-call | flops 51539607552 | bytes 1048576 | tf_op jit(solution)/shard_map/pallas_call | solution.py:526
  518.4 9.7 %shard_map.190.refs_0_ = bf16[768,1152]{1,0:T(8,128)(2,1)} custom-call(bf16[2048,768]{1,0:T(8,128)(2,1)} %get-tuple-element.114.x_ref.refs_0_, bf16[2048,384]{1,0:T(8,128)(2,1)} %get-tuple-element.151.refs_1_.rest_3_, bf16[2048,384]{1,0:T(8,128)(2,1)} %get-tuple-element.152.refs_2_.rest_4_, bf16[2048,384]{1,0:T(8,128)(2,1)} %get-tuple-element.153.refs_3_.rest_5_, ...), custom_call_target="tpu_custom_call" | custom-call | flops 14495514624 | bytes 1048576 | tf_op jit(solution)/shard_map/pallas_call | solution.py:1032
  532.0 3.8 collective-permute-start.22
  537.1 9.8 %shard_map.192.refs_0_ = bf16[1024,768]{1,0:T(8,128)(2,1)S(1)} custom-call(s32[6]{0:T(128)S(1)} %copy-done.16, bf16[2048,768]{1,0:T(8,128)(2,1)} %get-tuple-element.130.refs_1_.dbr_ref, bf16[2048,384]{1,0:T(8,128)(2,1)S(1)} %copy-done.5, bf16[2048,384]{1,0:T(8,128)(2,1)S(1)} %copy-done.6, bf16[2048,384]{1,0:T(8,128)(2,1)} %get-tuple-element.141.refs_3_.rest_2_, ...), custom_call_target="tpu_custom_call" | custom-call | flops 14495514624 | bytes 1048576 | tf_op jit(solution)/shard_map/pallas_call | solution.py:268
  558.2 10.6 %shard_map.194.refs_0_ = f32[2048,768]{1,0:T(8,128)} custom-call(s32[6]{0:T(128)S(1)} %copy-done.14, bf16[2048,768]{1,0:T(8,128)(2,1)} %get-tuple-element.130.refs_1_.dbr_ref, bf16[2048,384]{1,0:T(8,128)(2,1)S(1)} %copy-done.5, bf16[2048,384]{1,0:T(8,128)(2,1)S(1)} %copy-done.6, bf16[2048,384]{1,0:T(8,128)(2,1)S(1)} %copy-done.7, ...), custom_call_target="tpu_custom_call" | custom-call | flops 14495514624 | bytes 1048576 | tf_op jit(solution)/shard_map/pallas_call | solution.py:268
  568.8 7.0 %collective-permute-done.25.refs_2_ = bf16[96,1152]{1,0:T(8,128)(2,1)S(1)} collective-permute-done((bf16[96,1152]{1,0:T(8,128)(2,1)S(1)}, bf16[96,1152]{1,0:T(8,128)(2,1)S(1)}, u32[]{:S(2)}, u32[]{:S(2)}) %collective-permute-start.25) | collective-permute-done | bytes 221216 | tf_op jit(solution)/shard_map/ppermute | solution.py:57
  584.3 3.3 collective-permute-done.27.refs_0_
  587.6 4.3 collective-permute-done.28.refs_1_
  598.9 6.2 collective-permute-done.30.refs_0_
  611.9 6.4 collective-permute-done.33.refs_1_
  618.3 3.9 shard_map.199.refs_0_
  630.6 7.8 %shard_map.202 = (f32[384,6144]{1,0:T(8,128)}, f32[1536,768]{1,0:T(8,128)}) custom-call(bf16[16,576,384]{2,1,0:T(8,128)(2,1)S(1)} %bitcast.159), custom_call_target="tpu_custom_call" | custom-call | flops 1024 | bytes 1024 | tf_op jit(solution)/shard_map/pallas_call | solution.py:1083
  640.3 4.0 broadcast_select_fusion
  (395 shorter events, 134.2 us)
Async XLA Ops:
  7.2 54.7 %all-gather.5.cloned.1.call-start = ((), (), s32[]{:S(2)}) async-start(), calls=%async_computation.1 | async-start | bytes 1880064 | tf_op jit(solution)/shard_map/all_gather | solution.py:101
  8.1 10.8 %collective-permute-start = (bf16[24,2304]{1,0:T(8,128)(2,1)S(1)}, bf16[24,2304]{1,0:T(8,128)(2,1)S(1)}, u32[]{:S(2)}, u32[]{:S(2)}) collective-permute-start(bf16[24,2304]{1,0:T(8,128)(2,1)S(1)} %constant_dynamic-slice_fusion.9), channel_id=1, source_target_pairs={{0,1},{1,0},{2,3},{3,2},{4,5},{5,4},{6,7},{7,6},{8,9},{9,8},{10,11... | collective-permute-start | bytes 331784 | tf_op jit(solution)/shard_map/ppermute | solution.py:57
  13.1 138.9 %collective-permute-start.5 = (bf16[2,384]{1,0:T(2,128)(2,1)}, bf16[2,384]{1,0:T(2,128)(2,1)}, u32[]{:S(2)}, u32[]{:S(2)}) collective-permute-start(bf16[2,384]{1,0:T(2,128)(2,1)} %pad_maximum_fusion.6), channel_id=1, source_target_pairs={{0,1},{1,0},{2,3},{3,2},{4,5},{5,4},{6,7},{7,6},{8,9},{9,8},{10,11... | collective-permute-start | bytes 4616 | tf_op jit(solution)/shard_map/ppermute | solution.py:57
  19.6 138.2 %all-gather.7.cloned.1.call-start = ((), (), s32[]{:S(2)}) async-start(), calls=%async_computation.2 | async-start | bytes 5013504 | tf_op jit(solution)/shard_map/all_gather | solution.py:101
  20.4 36.2 %collective-permute-start.1 = (bf16[1024,768]{1,0:T(8,128)(2,1)}, bf16[1024,768]{1,0:T(8,128)(2,1)}, u32[]{:S(2)}, u32[]{:S(2)}) collective-permute-start(bf16[1024,768]{1,0:T(8,128)(2,1)} %get-tuple-element.98), channel_id=1, source_target_pairs={{0,1},{1,0},{2,3},{3,2},{4,5},{5,4},{6,7},{7,6},{8,9},{9,8},{10,11... | collective-permute-start | bytes 4718600 | tf_op jit(solution)/shard_map/ppermute | solution.py:57
  59.5 12.0 %collective-permute-start.2 = (bf16[24,6144]{1,0:T(8,128)(2,1)S(1)}, bf16[24,6144]{1,0:T(8,128)(2,1)}, u32[]{:S(2)}, u32[]{:S(2)}) collective-permute-start(bf16[24,6144]{1,0:T(8,128)(2,1)S(1)} %constant_dynamic-slice_fusion.8.rest_3_), channel_id=1, source_target_pairs={{0,1},{1,0},{2,3},{3,2},{4,5},{5,4},{6,7},{7,6},{8,9},{9,8},{10,11... | collective-permute-start | bytes 884744 | tf_op jit(solution)/shard_map/ppermute | solution.py:57
  71.5 443.0 %reduce-scatter.2.cloned.1.call-start = ((), (), s32[]{:S(2)}) async-start(), calls=%async_computation.3 | async-start | bytes 14598144 | tf_op jit(solution)/shard_map/reduce_scatter | solution.py:1277
  78.2 71.1 %collective-permute-start.3 = (bf16[192,768]{1,0:T(8,128)(2,1)S(1)}, bf16[192,768]{1,0:T(8,128)(2,1)S(1)}, u32[]{:S(2)}, u32[]{:S(2)}) collective-permute-start(bf16[192,768]{1,0:T(8,128)(2,1)S(1)} %constant_dynamic-slice_fusion.7.rest_2_), channel_id=1, source_target_pairs={{0,1},{1,0},{2,3},{3,2},{4,5},{5,4},{6,7},{7,6},{8,9},{9,8},{10,11... | collective-permute-start | bytes 884744 | tf_op jit(solution)/shard_map/ppermute | solution.py:57
  81.3 68.0 %collective-permute-start.4 = (bf16[768,768]{1,0:T(8,128)(2,1)S(1)}, bf16[768,768]{1,0:T(8,128)(2,1)S(1)}, u32[]{:S(2)}, u32[]{:S(2)}) collective-permute-start(bf16[768,768]{1,0:T(8,128)(2,1)S(1)} %constant_dynamic-slice_fusion.6.rest_3_), channel_id=1, source_target_pairs={{0,1},{1,0},{2,3},{3,2},{4,5},{5,4},{6,7},{7,6},{8,9},{9,8},{10,11... | collective-permute-start | bytes 3538952 | tf_op jit(solution)/shard_map/ppermute | solution.py:57
  157.7 55.7 %collective-permute-start.8 = (bf16[1024,768]{1,0:T(8,128)(2,1)}, bf16[1024,768]{1,0:T(8,128)(2,1)S(1)}, u32[]{:S(2)}, u32[]{:S(2)}) collective-permute-start(bf16[1024,768]{1,0:T(8,128)(2,1)} %get-tuple-element.195.rest_8_), channel_id=1, source_target_pairs={{0,1},{1,0},{2,3},{3,2},{4,5},{5,4},{6,7},{7,6},{8,9},{9,8},{10,11... | collective-permute-start | bytes 4718600 | tf_op jit(solution)/shard_map/ppermute | solution.py:57
  232.2 11.9 %collective-permute-start.13 = (bf16[128,896]{1,0:T(8,128)(2,1)S(1)}, bf16[128,896]{1,0:T(8,128)(2,1)S(1)}, u32[]{:S(2)}, u32[]{:S(2)}) collective-permute-start(bf16[128,896]{1,0:T(8,128)(2,1)S(1)} %get-tuple-element.199), channel_id=1, source_target_pairs={{0,16},{2,18},{4,20},{6,22},{8,24},{10,26},{12,28},{14,30},{16,0},... | collective-permute-start | bytes 688136 | tf_op jit(solution)/shard_map/ppermute | solution.py:57
  239.4 135.6 %collective-permute-start.14 = (bf16[1024,768]{1,0:T(8,128)(2,1)}, bf16[1024,768]{1,0:T(8,128)(2,1)}, u32[]{:S(2)}, u32[]{:S(2)}) collective-permute-start(bf16[1024,768]{1,0:T(8,128)(2,1)} %get-tuple-element.194), channel_id=1, source_target_pairs={{0,1},{1,0},{2,3},{3,2},{4,5},{5,4},{6,7},{7,6},{8,9},{9,8},{10,11... | collective-permute-start | bytes 4718600 | tf_op jit(solution)/shard_map/ppermute | solution.py:57
  325.9 301.7 %all-gather.9.cloned.1.call-start = ((), (), s32[]{:S(2)}) async-start(), calls=%async_computation.4 | async-start | bytes 7520256 | tf_op jit(solution)/shard_map/all_gather | solution.py:1315
  382.8 52.3 %collective-permute-start.15 = (bf16[2,192,896]{2,1,0:T(8,128)(2,1)S(1)}, bf16[2,192,896]{2,1,0:T(8,128)(2,1)S(1)}, u32[]{:S(2)}, u32[]{:S(2)}) collective-permute-start(bf16[2,192,896]{2,1,0:T(8,128)(2,1)S(1)} %dynamic-slice_bitcast_fusion.6.rest_0_), channel_id=1, source_target_pairs={{0,2},{2,0},{4,6},{6,4},{8,10},{10,8},{12,14},{14,12},{16,18},{18,... | collective-permute-start | bytes 2064392 | tf_op jit(solution)/shard_map/ppermute | solution.py:57
  438.6 16.0 %collective-permute-start.16 = (bf16[1,192,896]{2,1,0:T(8,128)(2,1)S(1)}, bf16[1,192,896]{2,1,0:T(8,128)(2,1)S(1)}, u32[]{:S(2)}, u32[]{:S(2)}) collective-permute-start(bf16[1,192,896]{2,1,0:T(8,128)(2,1)S(1)} %constant_dynamic-slice_fusion.3.refs_4_), channel_id=1, source_target_pairs={{0,1},{1,0},{2,3},{3,2},{4,5},{5,4},{6,7},{7,6},{8,9},{9,8},{10,11... | collective-permute-start | bytes 1032200 | tf_op jit(solution)/shard_map/ppermute | solution.py:57
  456.4 57.2 %collective-permute-start.17 = (bf16[96,896]{1,0:T(8,128)(2,1)S(1)}, bf16[96,896]{1,0:T(8,128)(2,1)S(1)}, u32[]{:S(2)}, u32[]{:S(2)}) collective-permute-start(bf16[96,896]{1,0:T(8,128)(2,1)S(1)} %dynamic-slice_bitcast_fusion.9.rest_0_), channel_id=1, source_target_pairs={{0,4},{2,6},{4,0},{6,2},{8,12},{10,14},{12,8},{14,10},{16,20},{18,... | collective-permute-start | bytes 516104 | tf_op jit(solution)/shard_map/ppermute | solution.py:57
  460.9 52.7 %collective-permute-start.18 = (bf16[2,192,1152]{2,1,0:T(8,128)(2,1)S(1)}, bf16[2,192,1152]{2,1,0:T(8,128)(2,1)S(1)}, u32[]{:S(2)}, u32[]{:S(2)}) collective-permute-start(bf16[2,192,1152]{2,1,0:T(8,128)(2,1)S(1)} %dynamic-slice_bitcast_fusion.5.rest_1_), channel_id=1, source_target_pairs={{0,2},{2,0},{4,6},{6,4},{8,10},{10,8},{12,14},{14,12},{16,18},{18,... | collective-permute-start | bytes 2654216 | tf_op jit(solution)/shard_map/ppermute | solution.py:57
  515.6 12.5 %collective-permute-start.19 = (bf16[48,896]{1,0:T(8,128)(2,1)S(1)}, bf16[48,896]{1,0:T(8,128)(2,1)S(1)}, u32[]{:S(2)}, u32[]{:S(2)}) collective-permute-start(bf16[48,896]{1,0:T(8,128)(2,1)S(1)} %dynamic-slice_bitcast_fusion.10.refs_4_), channel_id=1, source_target_pairs={{0,8},{2,10},{4,12},{6,14},{8,0},{10,2},{12,4},{14,6},{16,24},{18,... | collective-permute-start | bytes 258056 | tf_op jit(solution)/shard_map/ppermute | solution.py:57
  530.4 17.7 %collective-permute-start.21 = (bf16[24,896]{1,0:T(8,128)(2,1)S(1)}, bf16[24,896]{1,0:T(8,128)(2,1)S(1)}, u32[]{:S(2)}, u32[]{:S(2)}) collective-permute-start(bf16[24,896]{1,0:T(8,128)(2,1)S(1)} %dynamic-slice_bitcast_fusion.11.rest_8_), channel_id=1, source_target_pairs={{0,16},{2,18},{4,20},{6,22},{8,24},{10,26},{12,28},{14,30},{16,0},... | collective-permute-start | bytes 129032 | tf_op jit(solution)/shard_map/ppermute | solution.py:57
  532.0 16.1 %collective-permute-start.22 = (bf16[96,1152]{1,0:T(8,128)(2,1)S(1)}, bf16[96,1152]{1,0:T(8,128)(2,1)S(1)}, u32[]{:S(2)}, u32[]{:S(2)}) collective-permute-start(bf16[96,1152]{1,0:T(8,128)(2,1)S(1)} %dynamic-slice_bitcast_fusion.8.rest_9_), channel_id=1, source_target_pairs={{0,4},{2,6},{4,0},{6,2},{8,12},{10,14},{12,8},{14,10},{16,20},{18,... | collective-permute-start | bytes 663560 | tf_op jit(solution)/shard_map/ppermute | solution.py:57
  537.0 11.1 %collective-permute-start.23 = (bf16[2,192,1152]{2,1,0:T(8,128)(2,1)S(1)}, bf16[2,192,1152]{2,1,0:T(8,128)(2,1)}, u32[]{:S(2)}, u32[]{:S(2)}) collective-permute-start(bf16[2,192,1152]{2,1,0:T(8,128)(2,1)S(1)} %dynamic-slice_bitcast_fusion.4.rest_10_), channel_id=1, source_target_pairs={{0,2},{2,0},{4,6},{6,4},{8,10},{10,8},{12,14},{14,12},{16,18},{18,... | collective-permute-start | bytes 2654216 | tf_op jit(solution)/shard_map/ppermute | solution.py:57
  549.6 19.1 %collective-permute-start.24 = (bf16[24,896]{1,0:T(8,128)(2,1)S(1)}, bf16[24,896]{1,0:T(8,128)(2,1)S(1)}, u32[]{:S(2)}, u32[]{:S(2)}) collective-permute-start(bf16[24,896]{1,0:T(8,128)(2,1)S(1)} %fusion.17.rest_8_), channel_id=1, source_target_pairs={{0,16},{2,18},{4,20},{6,22},{8,24},{10,26},{12,28},{14,30},{16,0},... | collective-permute-start | bytes 129032 | tf_op jit(solution)/shard_map/ppermute | solution.py:57
  553.7 22.1 %collective-permute-start.25 = (bf16[96,1152]{1,0:T(8,128)(2,1)S(1)}, bf16[96,1152]{1,0:T(8,128)(2,1)S(1)}, u32[]{:S(2)}, u32[]{:S(2)}) collective-permute-start(bf16[96,1152]{1,0:T(8,128)(2,1)S(1)} %fusion.9.rest_9_), channel_id=1, source_target_pairs={{0,8},{2,10},{4,12},{6,14},{8,0},{10,2},{12,4},{14,6},{16,24},{18,... | collective-permute-start | bytes 663560 | tf_op jit(solution)/shard_map/ppermute | solution.py:57
  556.8 19.7 %collective-permute-start.26 = (bf16[1,192,1152]{2,1,0:T(8,128)(2,1)S(1)}, bf16[1,192,1152]{2,1,0:T(8,128)(2,1)}, u32[]{:S(2)}, u32[]{:S(2)}) collective-permute-start(bf16[1,192,1152]{2,1,0:T(8,128)(2,1)S(1)} %constant_dynamic-slice_fusion.1.rest_10_), channel_id=1, source_target_pairs={{0,1},{1,0},{2,3},{3,2},{4,5},{5,4},{6,7},{7,6},{8,9},{9,8},{10,11... | collective-permute-start | bytes 1327112 | tf_op jit(solution)/shard_map/ppermute | solution.py:57
  578.3 13.6 %collective-permute-start.28 = (bf16[96,1152]{1,0:T(8,128)(2,1)}, bf16[96,1152]{1,0:T(8,128)(2,1)S(1)}, u32[]{:S(2)}, u32[]{:S(2)}) collective-permute-start(bf16[96,1152]{1,0:T(8,128)(2,1)} %add_convert_fusion.6), channel_id=1, source_target_pairs={{0,16},{2,18},{4,20},{6,22},{8,24},{10,26},{12,28},{14,30},{16,0},... | collective-permute-start | bytes 663560 | tf_op jit(solution)/shard_map/ppermute | solution.py:57
  579.5 12.4 %collective-permute-start.29 = (bf16[96,1152]{1,0:T(8,128)(2,1)S(1)}, bf16[96,1152]{1,0:T(8,128)(2,1)S(1)}, u32[]{:S(2)}, u32[]{:S(2)}) collective-permute-start(bf16[96,1152]{1,0:T(8,128)(2,1)S(1)} %dynamic-slice_bitcast_fusion.7), channel_id=1, source_target_pairs={{0,4},{2,6},{4,0},{6,2},{8,12},{10,14},{12,8},{14,10},{16,20},{18,... | collective-permute-start | bytes 663560 | tf_op jit(solution)/shard_map/ppermute | solution.py:57
  583.0 35.3 %collective-permute-start.33 = (bf16[1024,768]{1,0:T(8,128)(2,1)S(1)}, bf16[1024,768]{1,0:T(8,128)(2,1)}, u32[]{:S(2)}, u32[]{:S(2)}) collective-permute-start(bf16[1024,768]{1,0:T(8,128)(2,1)S(1)} %copy-done.4), channel_id=1, source_target_pairs={{0,1},{1,0},{2,3},{3,2},{4,5},{5,4},{6,7},{7,6},{8,9},{9,8},{10,11... | collective-permute-start | bytes 4718600 | tf_op jit(solution)/shard_map/ppermute | solution.py:57
  594.4 10.8 %collective-permute-start.31 = (bf16[96,1152]{1,0:T(8,128)(2,1)S(1)}, bf16[96,1152]{1,0:T(8,128)(2,1)S(1)}, u32[]{:S(2)}, u32[]{:S(2)}) collective-permute-start(bf16[96,1152]{1,0:T(8,128)(2,1)S(1)} %add_convert_fusion.5), channel_id=1, source_target_pairs={{0,4},{2,6},{4,0},{6,2},{8,12},{10,14},{12,8},{14,10},{16,20},{18,... | collective-permute-start | bytes 663560 | tf_op jit(solution)/shard_map/ppermute | solution.py:57
  607.6 16.7 %collective-permute-start.34 = (bf16[192,896]{1,0:T(8,128)(2,1)S(1)}, bf16[192,896]{1,0:T(8,128)(2,1)S(1)}, u32[]{:S(2)}, u32[]{:S(2)}) collective-permute-start(bf16[192,896]{1,0:T(8,128)(2,1)S(1)} %bitcast_select_fusion.2.refs_0_), channel_id=1, source_target_pairs={{0,2},{2,0},{4,6},{6,4},{8,10},{10,8},{12,14},{14,12},{16,18},{18,... | collective-permute-start | bytes 1032200 | tf_op jit(solution)/shard_map/ppermute | solution.py:57
  608.9 15.4 %collective-permute-start.35 = (bf16[192,1152]{1,0:T(8,128)(2,1)S(1)}, bf16[192,1152]{1,0:T(8,128)(2,1)S(1)}, u32[]{:S(2)}, u32[]{:S(2)}) collective-permute-start(bf16[192,1152]{1,0:T(8,128)(2,1)S(1)} %bitcast_select_fusion.1.refs_0_), channel_id=1, source_target_pairs={{0,2},{2,0},{4,6},{6,4},{8,10},{10,8},{12,14},{14,12},{16,18},{18,... | collective-permute-start | bytes 1327112 | tf_op jit(solution)/shard_map/ppermute | solution.py:57
  611.1 13.2 %collective-permute-start.36 = (bf16[96,1152]{1,0:T(8,128)(2,1)}, bf16[96,1152]{1,0:T(8,128)(2,1)S(1)}, u32[]{:S(2)}, u32[]{:S(2)}) collective-permute-start(bf16[96,1152]{1,0:T(8,128)(2,1)} %add_convert_fusion.4), channel_id=1, source_target_pairs={{0,16},{2,18},{4,20},{6,22},{8,24},{10,26},{12,28},{14,30},{16,0},... | collective-permute-start | bytes 663560 | tf_op jit(solution)/shard_map/ppermute | solution.py:57
  627.0 11.4 %collective-permute-start.37 = (bf16[96,1152]{1,0:T(8,128)(2,1)S(1)}, bf16[96,1152]{1,0:T(8,128)(2,1)S(1)}, u32[]{:S(2)}, u32[]{:S(2)}) collective-permute-start(bf16[96,1152]{1,0:T(8,128)(2,1)S(1)} %add_convert_fusion.3), channel_id=1, source_target_pairs={{0,4},{2,6},{4,0},{6,2},{8,12},{10,14},{12,8},{14,10},{16,20},{18,... | collective-permute-start | bytes 663560 | tf_op jit(solution)/shard_map/ppermute | solution.py:57
  (90 other events, 863.0 us)
Sparse Core Ops, SparseCore 0:
  19.7 42.1 all-gather.4
  71.7 52.9 all-gather.6
  326.0 164.8 reduce-scatter.1
  514.7 70.8 all-gather.8

commit v4 on v3

--- a/solution.py
+++ b/solution.py
@@ -190,11 +190,11 @@
     return [pl.BlockSpec((tile, width), kept), pl.BlockSpec((tile, width), moved)]
 
 
-def row_tile(table, refs):
+def row_tile(table, refs, rows):
     if len(refs) == 1:
-        return refs[0][...]
+        return refs[0][rows]
     own = pl.program_id(1) // (pl.num_programs(1) // 2) == table[0]
-    return jnp.where(own, refs[0][...], refs[1][...])
+    return jnp.where(own, refs[0][rows], refs[1][rows])
 
 
 def qkv_kernel(counts, old, table, cos_ref, sin_ref, in_ref, *rest):
@@ -568,6 +568,7 @@
 
 
 FF_CHUNK = 512
+SUB = 256
 
 
 def normalize(hidden):
@@ -599,48 +600,61 @@
     @pl.when(begin)
     def _():
         start_all(*groups)
-        wait_all(groups[0])
-
-    branch = dot(att_ref[...], wo[...])
-    unit, inverse1 = normalize(x_ref[...].astype(F32) + branch)
-    normed = unit * g1_ref[...]
-    low = normed.astype(BF)
-    nl_ref[...] = low
-
-    @pl.when(begin)
-    def _():
-        wait_all(*groups[1:])
+        wait_all(*groups)
 
     ff = wd.shape[0]
-    hidden_sum = [normed]
-
-    def load(c):
+    tile, chunks = att_ref.shape[0], wd.shape[0] // FF_CHUNK
+    subs, opened, pools = tile // SUB, [], []
+    lanes = lane_iota((SUB, LANES))
+
+    def open_next():
+        rows = slice(len(opened) * SUB, (len(opened) + 1) * SUB)
+        branch = dot(att_ref[rows], wo[...])
+        unit, inverse1 = normalize(x_ref[rows].astype(F32) + branch)
+        normed = unit * g1_ref[...]
+        low = normed.astype(BF)
+        nl_ref[rows] = low
+        opened.append([low, normed, inverse1, rows])
+
+    def close(sub):
+        _, hidden_sum, inverse1, rows = opened[sub]
+        unit2, inverse2 = normalize(hidden_sum)
+        output = unit2 * g2_ref[...]
+        out_ref[rows] = output.astype(BF)
+        stat_ref[rows] = jnp.where(lanes == 0, inverse1, inverse2)
+        high, rest_low = split_two(output)
+        member = qf_ref[rows]
+        pools.append((dot_at(member, high) + dot_at(member, rest_low))[:SEG])
+
+    def load(n):
+        low, c = opened[n // chunks][0], n % chunks
         cols = slice(c * FF_CHUNK, (c + 1) * FF_CHUNK)
         return dot(low, ws[:, cols]), dot(low, ws[:, ff + c * FF_CHUNK : ff + (c + 1) * FF_CHUNK])
 
-    def work(c, loaded):
-        cols = slice(c * FF_CHUNK, (c + 1) * FF_CHUNK)
+    def work(n, loaded):
+        sub, c = n // chunks, n % chunks
+        if c == 1 and sub + 1 < subs:
+            open_next()
+        if c == 2 and sub > 0:
+            close(sub - 1)
+        rows, cols = opened[sub][3], slice(c * FF_CHUNK, (c + 1) * FF_CHUNK)
         gate, up = loaded
         sig = 0.5 + 0.5 * jnp.tanh(0.5 * gate)
         silu = gate * sig
         hidden = (silu * up).astype(BF)
-        hid_ref[:, cols] = hidden
-        fg_ref[:, cols] = (up * (sig + silu * (1.0 - sig))).astype(BF)
-        fu_ref[:, cols] = silu.astype(BF)
+        hid_ref[rows, cols] = hidden
+        fg_ref[rows, cols] = (up * (sig + silu * (1.0 - sig))).astype(BF)
+        fu_ref[rows, cols] = silu.astype(BF)
         return hidden
 
-    def finish(c, hidden):
-        hidden_sum[0] = hidden_sum[0] + dot(hidden, wd[c * FF_CHUNK : (c + 1) * FF_CHUNK, :])
-
-    staggered(ff // FF_CHUNK, load, work, finish)
-    unit2, inverse2 = normalize(hidden_sum[0])
-    output = unit2 * g2_ref[...]
-    out_ref[...] = output.astype(BF)
-    lanes = lane_iota(stat_ref.shape)
-    stat_ref[...] = jnp.where(lanes == 0, inverse1, inverse2)
-    high, rest_low = split_two(output)
-    member = qf_ref[...]
-    sums = (dot_at(member, high) + dot_at(member, rest_low))[:SEG]
+    def finish(n, hidden):
+        c = n % chunks
+        opened[n // chunks][1] = opened[n // chunks][1] + dot(hidden, wd[c * FF_CHUNK : (c + 1) * FF_CHUNK, :])
+
+    open_next()
+    staggered(subs * chunks, load, work, finish)
+    close(subs - 1)
+    sums = functools.reduce(jnp.add, pools)
 
     @pl.when(step == 0)
     def _():
@@ -694,33 +708,42 @@
         start_all(*groups)
         gf_ref[...] = jnp.zeros_like(gf_ref)
 
-    inverse2 = stat_ref[:, 1:2]
-    member = qf_ref[...]
+    gain2 = g2_ref[...]
     high, rest_low = split_two(dp_ref[0])
-    upstream = row_tile(table, cot_refs).astype(F32) + dot(member, high) + dot(member, rest_low)
-    gain2 = g2_ref[...]
-    unit2 = out_ref[...].astype(F32) / gain2
-    dffn = norm_back(upstream * gain2, unit2, inverse2).astype(BF)
-    dffn_ref[...] = dffn
-    tile, width = dffn.shape
-    gf_ref[...] += jnp.sum((upstream * unit2).reshape(tile // 8, 8, width), axis=0)
+    tile, width = out_ref.shape
+    ff = wd.shape[0]
+    subs, chunks, opened = tile // SUB, ff // FF_CHUNK, []
+
+    def open_next():
+        rows = slice(len(opened) * SUB, (len(opened) + 1) * SUB)
+        member = qf_ref[rows]
+        upstream = row_tile(table, cot_refs, rows).astype(F32) + dot(member, high) + dot(member, rest_low)
+        unit2 = out_ref[rows].astype(F32) / gain2
+        dffn = norm_back(upstream * gain2, unit2, stat_ref[rows, 1:2]).astype(BF)
+        dffn_ref[rows] = dffn
+        gf_ref[...] += jnp.sum((upstream * unit2).reshape(SUB // 8, 8, width), axis=0)
+        opened.append((dffn, rows))
+
+    def load(n):
+        c = n % chunks
+        return dot_bt(opened[n // chunks][0], wd[c * FF_CHUNK : (c + 1) * FF_CHUNK, :])
+
+    def work(n, dhid):
+        sub, c = n // chunks, n % chunks
+        if c == 1 and sub + 1 < subs:
+            open_next()
+        rows, cols = opened[sub][1], slice(c * FF_CHUNK, (c + 1) * FF_CHUNK)
+        dgu_ref[rows, cols] = (dhid * fg_ref[rows, cols].astype(F32)).astype(BF)
+        after = slice(ff + c * FF_CHUNK, ff + (c + 1) * FF_CHUNK)
+        dgu_ref[rows, after] = (dhid * fu_ref[rows, cols].astype(F32)).astype(BF)
+
+    open_next()
 
     @pl.when(begin)
     def _():
         wait_all(*groups)
 
-    ff = wd.shape[0]
-
-    def load(c):
-        return dot_bt(dffn, wd[c * FF_CHUNK : (c + 1) * FF_CHUNK, :])
-
-    def work(c, dhid):
-        cols = slice(c * FF_CHUNK, (c + 1) * FF_CHUNK)
-        dgu_ref[:, cols] = (dhid * fg_ref[:, cols].astype(F32)).astype(BF)
-        after = slice(ff + c * FF_CHUNK, ff + (c + 1) * FF_CHUNK)
-        dgu_ref[:, after] = (dhid * fu_ref[:, cols].astype(F32)).astype(BF)
-
-    staggered(ff // FF_CHUNK, load, work, lambda c, worked: None)
+    staggered(subs * chunks, load, work, lambda n, worked: None)
 
 
 def hidden_back(cots, lead, output, stat, query_feat, dpool, factors, gain2, down, rows, tile):
@@ -769,27 +792,38 @@
         ga_ref[...] = jnp.zeros_like(ga_ref)
         wait_all(*groups)
 
-    dnormed = dffn_ref[...].astype(F32) + dot_bt(dgu_ref[...], ws[...])
-    gain1 = g1_ref[...]
-    unit1 = nl_ref[...].astype(F32) / gain1
-    dbr = norm_back(dnormed * gain1, unit1, stat_ref[:, 0:1]).astype(BF)
-    dbr_ref[...] = dbr
-    datt = dot_bt(dbr, wo[...]).astype(BF)
-    datt_ref[...] = datt
-    tile, width = datt.shape
-    ga_ref[...] += jnp.sum((dnormed * unit1).reshape(tile // 8, 8, width), axis=0)
-
-    high, rest_low = split_two(datt.astype(F32) * att_ref[...].astype(F32))
-    heads = head_ref[...]
-    delta = dot(high, heads) + dot(rest_low, heads)
-    feat = qf_ref[...].astype(F32)
-    for value, start in ((lse_ref[...], 8), (delta, 44)):
-        left = -value
-        for n in range(3):
-            part = left.astype(BF).astype(F32)
-            left = left - part
-            feat = feat + pltpu.roll(part, start + HEADS * n, 1)
-    feat_ref[...] = feat.astype(BF)
+    gain1, heads = g1_ref[...], head_ref[...]
+    width = nl_ref.shape[1]
+    rows_of = lambda n: slice(n * SUB, (n + 1) * SUB)
+
+    def load(n):
+        rows = rows_of(n)
+        return dffn_ref[rows].astype(F32) + dot_bt(dgu_ref[rows], ws[...])
+
+    def work(n, dnormed):
+        rows = rows_of(n)
+        unit1 = nl_ref[rows].astype(F32) / gain1
+        dbr = norm_back(dnormed * gain1, unit1, stat_ref[rows, 0:1]).astype(BF)
+        dbr_ref[rows] = dbr
+        ga_ref[...] += jnp.sum((dnormed * unit1).reshape(SUB // 8, 8, width), axis=0)
+        return dbr
+
+    def finish(n, dbr):
+        rows = rows_of(n)
+        datt = dot_bt(dbr, wo[...]).astype(BF)
+        datt_ref[rows] = datt
+        high, rest_low = split_two(datt.astype(F32) * att_ref[rows].astype(F32))
+        delta = dot(high, heads) + dot(rest_low, heads)
+        feat = qf_ref[rows].astype(F32)
+        for value, start in ((lse_ref[rows], 8), (delta, 44)):
+            left = -value
+            for part_n in range(3):
+                part = left.astype(BF).astype(F32)
+                left = left - part
+                feat = feat + pltpu.roll(part, start + HEADS * part_n, 1)
+        feat_ref[rows] = feat.astype(BF)
+
+    staggered(dgu_ref.shape[0] // SUB, load, work, finish)
 
 
 def branch_back(dffn, low, stat, query_feat, dgu, attended, lse, gain1, weights, rows, tile, after=()):
@@ -944,9 +978,10 @@
             low_turned[:, b : b + 256] = turned(low_ref[b : b + 256, :])
 
     part = dot(low_turned[...], grad_ref[...]).astype(BF)
-    rows = out_ref.shape[2]
-    for f in range(out_ref.shape[1]):
-        out_ref[0, f] = part[f * rows : (f + 1) * rows]
+    taken, split, rows, cols = out_ref.shape
+    for n in range(taken):
+        for f in range(split):
+            out_ref[n, f] = part[f * rows : (f + 1) * rows, n * cols : (n + 1) * cols]
 
 
 def down_part_kernel(hidden_ref, dffn_ref, old_ref, out_ref):
@@ -977,9 +1012,9 @@
     whole = lambda a: pl.BlockSpec(a.shape, lambda *_: (0, 0))
     shares = pl.pallas_call(
         swiglu_part_kernel,
-        grid=(blocks,),
-        in_specs=[whole(low), pl.BlockSpec((tokens, cols), lambda j: (0, j))],
-        out_specs=pl.BlockSpec((1, split, rows, cols), lambda j: (j, 0, 0, 0)),
+        grid=(blocks // 2,),
+        in_specs=[whole(low), pl.BlockSpec((tokens, 2 * cols), lambda j: (0, j))],
+        out_specs=pl.BlockSpec((2, split, rows, cols), lambda j: (j, 0, 0, 0)),
         out_shape=shape,
         scratch_shapes=[pltpu.VMEM((width, tokens), BF)],
         compiler_params=params(48),
@@ -1177,7 +1212,7 @@
     gains = jnp.stack([attn_gain, ffn_gain])
     if row_mode:
         qkv_share = flipped(share_of(qkv_weight), "fsdp", 1)
-        moved, qkv_share = tied([take(tokens, 1 - mine, 0), qkv_share])
+        (moved,) = tied([take(tokens, 1 - mine, 0)], [qkv_share])
         moved = flipped(moved, "fsdp", 1)
         qkv = from_shares(qkv_weight, qkv_share)
         gains = in_order([gains, flipped(gains, "fsdp", 1)], mine)
@@ -1255,7 +1290,7 @@
         outer, down = whole_weight(out_weight), whole_weight(down_weight)
         cots, after = [cotangent.reshape(-1, width)], []
     low_normed, stat, hidden, *factors, output, sums = mix(
-        attended, x, query_feat, gain1, gain2, (outer, swiglu, down), rows, small_tile, after
+        attended, x, query_feat, gain1, gain2, (outer, swiglu, down), rows, tile, after
     )
     if row_mode:
         sums, cots[1] = tied([sums, cots[1]])
@@ -1268,7 +1303,7 @@
     lse_columns = jnp.pad(lse.reshape(HEADS, tokens_here).T, ((0, 0), (0, LANES - HEADS)))
 
     d_ffn, d_gate_up, gain2_part = hidden_back(
-        cots, lead, output, stat, query_feat, d_pool, factors, gain2, down, rows, small_tile
+        cots, lead, output, stat, query_feat, d_pool, factors, gain2, down, rows, tile
     )
     fast = row_mode and shares_fit(low_normed, hidden)
     if fast:
@@ -1280,7 +1315,7 @@
         down_grad = plain_sum(dot_at(hidden, d_ffn).astype(BF))
         after = []
     d_branch, d_attended, back_feat, gain1_part = branch_back(
-        d_ffn, low_normed, stat, query_feat, d_gate_up, attended, lse_columns, gain1, (outer, swiglu), rows, small_tile,
+        d_ffn, low_normed, stat, query_feat, d_gate_up, attended, lse_columns, gain1, (outer, swiglu), rows, tile,
         after,
     )
     if row_mode:
@@ -1331,8 +1366,10 @@
             ],
             running,
         )
-        for _ in range(2):
-            beside(lambda _: [], running)
+        beside(lambda _: [], running)
+        if fast:
+            (swiglu_grad, down_grad), _ = beside(lambda _: spread(both, width), running)
+        (layer_output,), _ = beside(lambda _: [layer_output], running)
         kept, exchange = tied([kept, exchange])
         (input_grad,), _ = beside(
             lambda _: [placed(exchange, kept, (1 - mine) * shard_len, small_tile)], running
@@ -1340,8 +1377,6 @@
         input_grad = input_grad.reshape(tokens.shape)
     else:
         input_grad = input_grad_part(d_branch, grads, qkv, 0, tokens_here, F32, small_tile).reshape(tokens.shape)
-    if fast:
-        (swiglu_grad, down_grad), _ = beside(lambda _: spread(both, width), running)
     while any(not r.done for r in running):
         beside(lambda _: [], running)
     wide, groups = BACK_PAIRS * LANES, PAIRS // BACK_PAIRS

time: 660 us -> 631 us (0.956)
  Pallas kernels: 418 us -> 395 us
  waiting for transfers between devices: 74.4 us -> 63.8 us
    ppermute x39, waiting for transfers between devices: 73.7 us -> 63.7 us  [flipped(): return lax.ppermute(block, axis, route)]
    pallas_call x1, Pallas kernels: 32.3 us -> 25 us  [feed_forward_shares(): pl.pallas_call(swiglu_part_kernel, grid=(blocks // 2,), in_specs=[whole(l...]
    pallas_call x1, Pallas kernels: 46 us -> 39.3 us  [branch_back(): pl.pallas_call(functools.partial(branch_back_kernel, counts), grid_spec=p...]
    unnamed x163 -> x169, local copies, waits for them, and re-layouts: 26.8 us -> 26.7 us
  transfers between devices with their start and end apart: 43 -> 43, of which waited for: 14 -> 13; matrix products, arithmetic and copies ran while one was open for 11% -> 11% of each run, Pallas kernels for 63% -> 63%
where the time goes in v4:
time: 631 us; the launch traced here: 624 us
  Pallas kernels  395 us (63%)
  waiting for transfers between devices  63.8 us (10%)
  local copies, waits for them, and re-layouts  58 us (9%)
  starting transfers between devices  44.3 us (7%)
  other arithmetic  42.9 us (7%)
  between operations  19.2 us (3%)
    pallas_call x2, Pallas kernels, attend_back(): pl.pallas_call(functools.partial(attend_back_kernel, group, base, len(aft...  99.7 us
    ppermute x39, waiting for transfers between devices, flipped(): return lax.ppermute(block, axis, route)  63.7 us
    pallas_call x1, Pallas kernels, attend(): pl.pallas_call(functools.partial(attend_kernel, group, len(after)), grid_...  53.1 us
    pallas_call x1, Pallas kernels, mix(): pl.pallas_call(functools.partial(mix_kernel, counts), grid_spec=pltpu.Pre...  52.7 us
    ppermute x39, starting transfers between devices, flipped(): return lax.ppermute(block, axis, route)  43.9 us
    pallas_call x1, Pallas kernels, branch_back(): pl.pallas_call(functools.partial(branch_back_kernel, counts), grid_spec=p...  39.3 us
    pallas_call x1, Pallas kernels, hidden_back(): pl.pallas_call(functools.partial(hidden_back_kernel, counts, len(cots)),...  30.2 us
    unnamed x169, local copies, waits for them, and re-layouts  26.7 us
  transfers between devices with their start and end apart: 43, of which 13 were waited for; matrix products, arithmetic and copies ran while one was open for 11% of the time, Pallas kernels for 63%

profile of v4, /device:TPU:0, one launch (start us, length us, event | category | flops | bytes accessed | tf_op | source)
XLA Modules:
  0.0 623.9 jit_solution(3324295879822807199)
XLA Ops:
  8.1 3.0 collective-permute-start
  17.3 3.2 dynamic-slice_bitcast_fusion.2
  24.0 5.0 fusion.5
  29.0 27.7 %collective-permute-done.1.rest_2_.in_ref = bf16[1024,768]{1,0:T(8,128)(2,1)} collective-permute-done((bf16[1024,768]{1,0:T(8,128)(2,1)}, bf16[1024,768]{1,0:T(8,128)(2,1)}, u32[]{:S(2)}, u32[]{:S(2)}) %collective-permute-start.1) | collective-permute-done | bytes 1572896 | tf_op jit(solution)/shard_map/ppermute | solution.py:57
  62.7 8.4 %shard_map.170 = (bf16[2048,768]{1,0:T(8,128)(2,1)}, bf16[2048,768]{1,0:T(8,128)(2,1)}, bf16[2048,768]{1,0:T(8,128)(2,1)}, bf16[2048,768]{1,0:T(8,128)(2,1)}) custom-call(s32[6]{0:T(128)S(1)} %stack.111.table, f32[2048,128]{1,0:T(8,128)S(1)} %copy-done.11, f32[2048,128]{1,0:T(8,128)S(1)} %get-tuple-element.205.sin_ref.sq_ref.sk_ref, ...), custom_call_target="tpu_custom_call" | custom-call | flops 14495514624 | bytes 1048576 | tf_op jit(solution)/shard_map/pallas_call | solution.py:229
  80.8 9.5 %shard_map.172 = (bf16[2048,768]{1,0:T(8,128)(2,1)}, bf16[2048,768]{1,0:T(8,128)(2,1)}, bf16[2048,768]{1,0:T(8,128)(2,1)}, bf16[2048,768]{1,0:T(8,128)(2,1)}) custom-call(s32[6]{0:T(128)S(1)} %stack.109.table, f32[2048,128]{1,0:T(8,128)S(1)} %copy-done.12, ...), custom_call_target="tpu_custom_call", output_to_operand_aliasing={{0}: (8, {}), {1}: (9, {}), {2}: (10, {}), {3}: (11, {})} | custom-call | flops 14495514624 | bytes 1048576 | tf_op jit(solution)/shard_map/pallas_call | solution.py:229
  90.3 53.1 %shard_map.173 = (bf16[2048,768]{1,0:T(8,128)(2,1)}, f32[12,1,2048]{2,1,0:T(1,128)}) custom-call(s32[16]{0:T(128)} %reshape.1323.spans, bf16[2048,768]{1,0:T(8,128)(2,1)} %get-tuple-element.105.q_ref, bf16[2048,768]{1,0:T(8,128)(2,1)} %get-tuple-element.106.k_ref, bf16[2048,768]{1,0:T(8,128)(2,1)} %get-tuple-element.107.v_ref, ...), custom_call_target="tpu_custom_call" | custom-call | flops 51539607552 | bytes 1048576 | tf_op jit(solution)/shard_map/pallas_call | solution.py:401
  152.5 52.7 %shard_map.175 = (bf16[2048,768]{1,0:T(8,128)(2,1)}, f32[2048,128]{1,0:T(8,128)}, bf16[2048,3072]{1,0:T(8,128)(2,1)}, bf16[2048,3072]{1,0:T(8,128)(2,1)}, bf16[2...) custom-call(s32[18]{0:T(128)} %stack.120.table, ...), custom_call_target="tpu_custom_call" | custom-call | flops 125627793408 | bytes 1048576 | tf_op jit(solution)/shard_map/pallas_call | solution.py:675
  213.3 3.7 collective-permute-start.11
  219.4 4.3 collective-permute-start.12
  223.7 2.8 collective-permute-done.12
  230.9 3.7 constant_dynamic-slice_fusion
  241.0 30.2 %shard_map.177 = (bf16[2048,768]{1,0:T(8,128)(2,1)}, bf16[2048,6144]{1,0:T(8,128)(2,1)}, f32[8,768]{1,0:T(8,128)}) custom-call(s32[8]{0:T(128)} %stack.119.table, bf16[1024,768]{1,0:T(8,128)(2,1)} %get-tuple-element.194.rest_0_, bf16[1024,768]{1,0:T(8,128)(2,1)} %get-tuple-element.116.rest_1_, bf16[2048,768]{1,0:T(8,128)(2,1)} %get-tuple-element.117.rest_2_, ...), custom_call_target="tpu_custom_call" | custom-call | flops 77309411328 | bytes 1048576 | tf_op jit(solution)/shard_map/pallas_call | solution.py:756
  273.0 25.0 %shard_map.178.old_ref = bf16[16,2,576,384]{3,2,1,0:T(8,128)(2,1)} custom-call(bf16[2048,768]{1,0:T(8,128)(2,1)S(1)} %copy-done.18, bf16[2048,6144]{1,0:T(8,128)(2,1)} %get-tuple-element.124.grad_ref.refs_4_), custom_call_target="tpu_custom_call" | custom-call | flops 77309411328 | bytes 1048576 | tf_op jit(solution)/shard_map/pallas_call | solution.py:1013
  298.0 14.6 %shard_map.179.refs_14_ = bf16[16,2,576,384]{3,2,1,0:T(8,128)(2,1)} custom-call(bf16[2048,3072]{1,0:T(8,128)(2,1)} %get-tuple-element.125.hidden_ref, bf16[2048,768]{1,0:T(8,128)(2,1)S(1)} %copy-done.17, bf16[16,2,576,384]{3,2,1,0:T(8,128)(2,1)} %shard_map.178.old_ref), custom_call_target="tpu_custom_call", output_to_operand_aliasing={{}: (2, {})} | custom-call | flops 38654705664 | bytes 1048576 | tf_op jit(solution)/shard_map/pallas_call | solution.py:1025
  312.7 39.3 %shard_map.180 = (bf16[2048,768]{1,0:T(8,128)(2,1)}, bf16[2048,768]{1,0:T(8,128)(2,1)}, bf16[2048,128]{1,0:T(8,128)(2,1)}, f32[8,768]{1,0:T(8,128)}) custom-call(s32[12]{0:T(128)} %stack.114.table, bf16[2048,768]{1,0:T(8,128)(2,1)} %get-tuple-element.122.dffn_ref.refs_0_, bf16[2048,768]{1,0:T(8,128)(2,1)} %get-tuple-element.123.low_ref.refs_1_, ...), custom_call_target="tpu_custom_call" | custom-call | flops 86973087744 | bytes 1048576 | tf_op jit(solution)/shard_map/pallas_call | solution.py:837
  355.1 6.8 %shard_map.182 = bf16[768,896]{1,0:T(8,128)(2,1)} custom-call(bf16[2048,768]{1,0:T(8,128)(2,1)} %get-tuple-element.110.att_ref.refs_5_.refs_0_, bf16[2048,768]{1,0:T(8,128)(2,1)} %get-tuple-element.127.refs_1_.dbr_ref, bf16[768,128]{1,0:T(8,128)(2,1)} %pad.24.refs_2_), custom_call_target="tpu_custom_call" | custom-call | flops 11274289152 | bytes 1048576 | tf_op jit(solution)/shard_map/pallas_call | solution.py:1067
  363.9 50.1 %shard_map.183 = (bf16[2048,384]{1,0:T(8,128)(2,1)}, bf16[2048,384]{1,0:T(8,128)(2,1)}, bf16[2048,384]{1,0:T(8,128)(2,1)}) custom-call(s32[16]{0:T(128)} %reshape.1332.spans, bf16[2048,768]{1,0:T(8,128)(2,1)} %get-tuple-element.105.q_ref, bf16[2048,768]{1,0:T(8,128)(2,1)} %get-tuple-element.130.do_ref, bf16[2048,768]{1,0:T(8,128)(2,1)} %get-tuple-element.106.k_ref, ...), custom_call_target="tpu_custom_call" | custom-call | flops 51539607552 | bytes 1048576 | tf_op jit(solution)/shard_map/pallas_call | solution.py:526
  418.2 9.7 %shard_map.185.refs_0_ = bf16[768,1152]{1,0:T(8,128)(2,1)} custom-call(bf16[2048,768]{1,0:T(8,128)(2,1)} %get-tuple-element.111.x_ref.refs_0_, bf16[2048,384]{1,0:T(8,128)(2,1)} %get-tuple-element.136.refs_1_.rest_0_, bf16[2048,384]{1,0:T(8,128)(2,1)} %get-tuple-element.137.refs_2_.rest_1_, bf16[2048,384]{1,0:T(8,128)(2,1)} %get-tuple-element.138.refs_3_.rest_2_, ...), custom_call_target="tpu_custom_call" | custom-call | flops 14495514624 | bytes 1048576 | tf_op jit(solution)/shard_map/pallas_call | solution.py:1067
  434.0 49.6 %shard_map.187 = (bf16[2048,384]{1,0:T(8,128)(2,1)}, bf16[2048,384]{1,0:T(8,128)(2,1)}, bf16[2048,384]{1,0:T(8,128)(2,1)}) custom-call(s32[16]{0:T(128)} %reshape.1332.spans, bf16[2048,768]{1,0:T(8,128)(2,1)} %get-tuple-element.105.q_ref, bf16[2048,768]{1,0:T(8,128)(2,1)} %get-tuple-element.130.do_ref, bf16[2048,768]{1,0:T(8,128)(2,1)} %get-tuple-element.106.k_ref, ...), custom_call_target="tpu_custom_call" | custom-call | flops 51539607552 | bytes 1048576 | tf_op jit(solution)/shard_map/pallas_call | solution.py:526
  488.4 9.9 %shard_map.190.refs_0_ = bf16[768,1152]{1,0:T(8,128)(2,1)} custom-call(bf16[2048,768]{1,0:T(8,128)(2,1)} %get-tuple-element.111.x_ref.refs_0_, bf16[2048,384]{1,0:T(8,128)(2,1)} %get-tuple-element.148.refs_1_.rest_3_, bf16[2048,384]{1,0:T(8,128)(2,1)} %get-tuple-element.149.refs_2_.rest_4_, bf16[2048,384]{1,0:T(8,128)(2,1)} %get-tuple-element.150.refs_3_.rest_5_, ...), custom_call_target="tpu_custom_call" | custom-call | flops 14495514624 | bytes 1048576 | tf_op jit(solution)/shard_map/pallas_call | solution.py:1067
  506.4 9.8 %shard_map.192.refs_0_ = bf16[1024,768]{1,0:T(8,128)(2,1)S(1)} custom-call(s32[6]{0:T(128)S(1)} %copy-done.16, bf16[2048,768]{1,0:T(8,128)(2,1)} %get-tuple-element.127.refs_1_.dbr_ref, bf16[2048,384]{1,0:T(8,128)(2,1)S(1)} %copy-done.5, bf16[2048,384]{1,0:T(8,128)(2,1)S(1)} %copy-done.6, bf16[2048,384]{1,0:T(8,128)(2,1)} %get-tuple-element.138.refs_3_.rest_2_, ...), custom_call_target="tpu_custom_call" | custom-call | flops 14495514624 | bytes 1048576 | tf_op jit(solution)/shard_map/pallas_call | solution.py:268
  526.7 10.9 %shard_map.194.refs_0_ = f32[2048,768]{1,0:T(8,128)} custom-call(s32[6]{0:T(128)S(1)} %copy-done.14, bf16[2048,768]{1,0:T(8,128)(2,1)} %get-tuple-element.127.refs_1_.dbr_ref, bf16[2048,384]{1,0:T(8,128)(2,1)S(1)} %copy-done.5, bf16[2048,384]{1,0:T(8,128)(2,1)S(1)} %copy-done.6, bf16[2048,384]{1,0:T(8,128)(2,1)S(1)} %copy-done.7, ...), custom_call_target="tpu_custom_call" | custom-call | flops 14495514624 | bytes 1048576 | tf_op jit(solution)/shard_map/pallas_call | solution.py:268
  537.6 7.4 %collective-permute-done.25.refs_2_ = bf16[96,1152]{1,0:T(8,128)(2,1)S(1)} collective-permute-done((bf16[96,1152]{1,0:T(8,128)(2,1)S(1)}, bf16[96,1152]{1,0:T(8,128)(2,1)S(1)}, u32[]{:S(2)}, u32[]{:S(2)}) %collective-permute-start.25) | collective-permute-done | bytes 221216 | tf_op jit(solution)/shard_map/ppermute | solution.py:57
  549.9 3.6 collective-permute-start.27
  553.5 3.2 collective-permute-done.27.refs_0_
  556.7 4.3 collective-permute-done.28.refs_1_
  569.5 3.0 copy-done
  572.5 7.8 %shard_map.197 = (f32[384,6144]{1,0:T(8,128)}, f32[1536,768]{1,0:T(8,128)}) custom-call(bf16[16,576,384]{2,1,0:T(8,128)(2,1)S(1)} %bitcast.159), custom_call_target="tpu_custom_call" | custom-call | flops 1024 | bytes 1024 | tf_op jit(solution)/shard_map/pallas_call | solution.py:1118
  586.6 3.5 broadcast_select_fusion.refs_0_
  590.1 7.9 %collective-permute-done.35.refs_3_ = bf16[96,1152]{1,0:T(8,128)(2,1)S(1)} collective-permute-done((bf16[96,1152]{1,0:T(8,128)(2,1)S(1)}, bf16[96,1152]{1,0:T(8,128)(2,1)S(1)}, u32[]{:S(2)}, u32[]{:S(2)}) %collective-permute-start.35) | collective-permute-done | bytes 221216 | tf_op jit(solution)/shard_map/ppermute | solution.py:57
  603.5 3.9 shard_map.202.refs_0_
  (401 shorter events, 127.5 us)
Async XLA Ops:
  7.2 54.2 %all-gather.5.cloned.1.call-start = ((), (), s32[]{:S(2)}) async-start(), calls=%async_computation.1 | async-start | bytes 1880064 | tf_op jit(solution)/shard_map/all_gather | solution.py:101
  13.1 133.0 %collective-permute-start.5 = (bf16[2,384]{1,0:T(2,128)(2,1)}, bf16[2,384]{1,0:T(2,128)(2,1)}, u32[]{:S(2)}, u32[]{:S(2)}) collective-permute-start(bf16[2,384]{1,0:T(2,128)(2,1)} %pad_maximum_fusion.6), channel_id=1, source_target_pairs={{0,1},{1,0},{2,3},{3,2},{4,5},{5,4},{6,7},{7,6},{8,9},{9,8},{10,11... | collective-permute-start | bytes 4616 | tf_op jit(solution)/shard_map/ppermute | solution.py:57
  16.7 135.2 %all-gather.7.cloned.1.call-start = ((), (), s32[]{:S(2)}) async-start(), calls=%async_computation.2 | async-start | bytes 5013504 | tf_op jit(solution)/shard_map/all_gather | solution.py:101
  20.5 36.2 %collective-permute-start.1 = (bf16[1024,768]{1,0:T(8,128)(2,1)}, bf16[1024,768]{1,0:T(8,128)(2,1)}, u32[]{:S(2)}, u32[]{:S(2)}) collective-permute-start(bf16[1024,768]{1,0:T(8,128)(2,1)} %shard_map.169), channel_id=1, source_target_pairs={{0,1},{1,0},{2,3},{3,2},{4,5},{5,4},{6,7},{7,6},{8,9},{9,8},{10,11... | collective-permute-start | bytes 4718600 | tf_op jit(solution)/shard_map/ppermute | solution.py:57
  59.6 11.4 %collective-permute-start.2 = (bf16[24,6144]{1,0:T(8,128)(2,1)S(1)}, bf16[24,6144]{1,0:T(8,128)(2,1)}, u32[]{:S(2)}, u32[]{:S(2)}) collective-permute-start(bf16[24,6144]{1,0:T(8,128)(2,1)S(1)} %constant_dynamic-slice_fusion.8.rest_3_), channel_id=1, source_target_pairs={{0,1},{1,0},{2,3},{3,2},{4,5},{5,4},{6,7},{7,6},{8,9},{9,8},{10,11... | collective-permute-start | bytes 884744 | tf_op jit(solution)/shard_map/ppermute | solution.py:57
  71.1 413.5 %reduce-scatter.2.cloned.1.call-start = ((), (), s32[]{:S(2)}) async-start(), calls=%async_computation.3 | async-start | bytes 14598144 | tf_op jit(solution)/shard_map/reduce_scatter | solution.py:1312
  77.1 66.3 %collective-permute-start.3 = (bf16[192,768]{1,0:T(8,128)(2,1)S(1)}, bf16[192,768]{1,0:T(8,128)(2,1)S(1)}, u32[]{:S(2)}, u32[]{:S(2)}) collective-permute-start(bf16[192,768]{1,0:T(8,128)(2,1)S(1)} %constant_dynamic-slice_fusion.7.rest_2_), channel_id=1, source_target_pairs={{0,1},{1,0},{2,3},{3,2},{4,5},{5,4},{6,7},{7,6},{8,9},{9,8},{10,11... | collective-permute-start | bytes 884744 | tf_op jit(solution)/shard_map/ppermute | solution.py:57
  79.0 64.4 %collective-permute-start.4 = (bf16[768,768]{1,0:T(8,128)(2,1)S(1)}, bf16[768,768]{1,0:T(8,128)(2,1)S(1)}, u32[]{:S(2)}, u32[]{:S(2)}) collective-permute-start(bf16[768,768]{1,0:T(8,128)(2,1)S(1)} %constant_dynamic-slice_fusion.6.rest_3_), channel_id=1, source_target_pairs={{0,1},{1,0},{2,3},{3,2},{4,5},{5,4},{6,7},{7,6},{8,9},{9,8},{10,11... | collective-permute-start | bytes 3538952 | tf_op jit(solution)/shard_map/ppermute | solution.py:57
  151.6 53.6 %collective-permute-start.8 = (bf16[1024,768]{1,0:T(8,128)(2,1)}, bf16[1024,768]{1,0:T(8,128)(2,1)S(1)}, u32[]{:S(2)}, u32[]{:S(2)}) collective-permute-start(bf16[1024,768]{1,0:T(8,128)(2,1)} %get-tuple-element.193.rest_8_), channel_id=1, source_target_pairs={{0,1},{1,0},{2,3},{3,2},{4,5},{5,4},{6,7},{7,6},{8,9},{9,8},{10,11... | collective-permute-start | bytes 4718600 | tf_op jit(solution)/shard_map/ppermute | solution.py:57
  226.5 11.5 %collective-permute-start.13 = (bf16[128,896]{1,0:T(8,128)(2,1)S(1)}, bf16[128,896]{1,0:T(8,128)(2,1)S(1)}, u32[]{:S(2)}, u32[]{:S(2)}) collective-permute-start(bf16[128,896]{1,0:T(8,128)(2,1)S(1)} %get-tuple-element.197), channel_id=1, source_target_pairs={{0,16},{2,18},{4,20},{6,22},{8,24},{10,26},{12,28},{14,30},{16,0},... | collective-permute-start | bytes 688136 | tf_op jit(solution)/shard_map/ppermute | solution.py:57
  234.7 120.4 %collective-permute-start.14 = (bf16[1024,768]{1,0:T(8,128)(2,1)}, bf16[1024,768]{1,0:T(8,128)(2,1)}, u32[]{:S(2)}, u32[]{:S(2)}) collective-permute-start(bf16[1024,768]{1,0:T(8,128)(2,1)} %get-tuple-element.192), channel_id=1, source_target_pairs={{0,1},{1,0},{2,3},{3,2},{4,5},{5,4},{6,7},{7,6},{8,9},{9,8},{10,11... | collective-permute-start | bytes 4718600 | tf_op jit(solution)/shard_map/ppermute | solution.py:57
  312.6 256.8 %all-gather.9.cloned.1.call-start = ((), (), s32[]{:S(2)}) async-start(), calls=%async_computation.4 | async-start | bytes 7520256 | tf_op jit(solution)/shard_map/all_gather | solution.py:1350
  363.0 50.9 %collective-permute-start.15 = (bf16[2,192,896]{2,1,0:T(8,128)(2,1)S(1)}, bf16[2,192,896]{2,1,0:T(8,128)(2,1)S(1)}, u32[]{:S(2)}, u32[]{:S(2)}) collective-permute-start(bf16[2,192,896]{2,1,0:T(8,128)(2,1)S(1)} %dynamic-slice_bitcast_fusion.6.rest_0_), channel_id=1, source_target_pairs={{0,2},{2,0},{4,6},{6,4},{8,10},{10,8},{12,14},{14,12},{16,18},{18,... | collective-permute-start | bytes 2064392 | tf_op jit(solution)/shard_map/ppermute | solution.py:57
  429.7 53.9 %collective-permute-start.17 = (bf16[96,896]{1,0:T(8,128)(2,1)S(1)}, bf16[96,896]{1,0:T(8,128)(2,1)S(1)}, u32[]{:S(2)}, u32[]{:S(2)}) collective-permute-start(bf16[96,896]{1,0:T(8,128)(2,1)S(1)} %dynamic-slice_bitcast_fusion.9.rest_0_), channel_id=1, source_target_pairs={{0,4},{2,6},{4,0},{6,2},{8,12},{10,14},{12,8},{14,10},{16,20},{18,... | collective-permute-start | bytes 516104 | tf_op jit(solution)/shard_map/ppermute | solution.py:57
  433.1 50.5 %collective-permute-start.18 = (bf16[2,192,1152]{2,1,0:T(8,128)(2,1)S(1)}, bf16[2,192,1152]{2,1,0:T(8,128)(2,1)S(1)}, u32[]{:S(2)}, u32[]{:S(2)}) collective-permute-start(bf16[2,192,1152]{2,1,0:T(8,128)(2,1)S(1)} %dynamic-slice_bitcast_fusion.5.rest_1_), channel_id=1, source_target_pairs={{0,2},{2,0},{4,6},{6,4},{8,10},{10,8},{12,14},{14,12},{16,18},{18,... | collective-permute-start | bytes 2654216 | tf_op jit(solution)/shard_map/ppermute | solution.py:57
  485.6 12.6 %collective-permute-start.19 = (bf16[48,896]{1,0:T(8,128)(2,1)S(1)}, bf16[48,896]{1,0:T(8,128)(2,1)S(1)}, u32[]{:S(2)}, u32[]{:S(2)}) collective-permute-start(bf16[48,896]{1,0:T(8,128)(2,1)S(1)} %dynamic-slice_bitcast_fusion.10.refs_4_), channel_id=1, source_target_pairs={{0,8},{2,10},{4,12},{6,14},{8,0},{10,2},{12,4},{14,6},{16,24},{18,... | collective-permute-start | bytes 258056 | tf_op jit(solution)/shard_map/ppermute | solution.py:57
  487.6 12.5 %collective-permute-start.20 = (bf16[1,192,1152]{2,1,0:T(8,128)(2,1)S(1)}, bf16[1,192,1152]{2,1,0:T(8,128)(2,1)S(1)}, u32[]{:S(2)}, u32[]{:S(2)}) collective-permute-start(bf16[1,192,1152]{2,1,0:T(8,128)(2,1)S(1)} %constant_dynamic-slice_fusion.2.refs_5_), channel_id=1, source_target_pairs={{0,1},{1,0},{2,3},{3,2},{4,5},{5,4},{6,7},{7,6},{8,9},{9,8},{10,11... | collective-permute-start | bytes 1327112 | tf_op jit(solution)/shard_map/ppermute | solution.py:57
  501.8 15.6 %collective-permute-start.21 = (bf16[24,896]{1,0:T(8,128)(2,1)S(1)}, bf16[24,896]{1,0:T(8,128)(2,1)S(1)}, u32[]{:S(2)}, u32[]{:S(2)}) collective-permute-start(bf16[24,896]{1,0:T(8,128)(2,1)S(1)} %dynamic-slice_bitcast_fusion.11.rest_8_), channel_id=1, source_target_pairs={{0,16},{2,18},{4,20},{6,22},{8,24},{10,26},{12,28},{14,30},{16,0},... | collective-permute-start | bytes 129032 | tf_op jit(solution)/shard_map/ppermute | solution.py:57
  503.8 13.6 %collective-permute-start.22 = (bf16[96,1152]{1,0:T(8,128)(2,1)S(1)}, bf16[96,1152]{1,0:T(8,128)(2,1)S(1)}, u32[]{:S(2)}, u32[]{:S(2)}) collective-permute-start(bf16[96,1152]{1,0:T(8,128)(2,1)S(1)} %dynamic-slice_bitcast_fusion.8.rest_9_), channel_id=1, source_target_pairs={{0,4},{2,6},{4,0},{6,2},{8,12},{10,14},{12,8},{14,10},{16,20},{18,... | collective-permute-start | bytes 663560 | tf_op jit(solution)/shard_map/ppermute | solution.py:57
  506.1 11.3 %collective-permute-start.23 = (bf16[2,192,1152]{2,1,0:T(8,128)(2,1)S(1)}, bf16[2,192,1152]{2,1,0:T(8,128)(2,1)}, u32[]{:S(2)}, u32[]{:S(2)}) collective-permute-start(bf16[2,192,1152]{2,1,0:T(8,128)(2,1)S(1)} %dynamic-slice_bitcast_fusion.4.rest_10_), channel_id=1, source_target_pairs={{0,2},{2,0},{4,6},{6,4},{8,10},{10,8},{12,14},{14,12},{16,18},{18,... | collective-permute-start | bytes 2654216 | tf_op jit(solution)/shard_map/ppermute | solution.py:57
  518.9 18.7 %collective-permute-start.24 = (bf16[24,896]{1,0:T(8,128)(2,1)S(1)}, bf16[24,896]{1,0:T(8,128)(2,1)S(1)}, u32[]{:S(2)}, u32[]{:S(2)}) collective-permute-start(bf16[24,896]{1,0:T(8,128)(2,1)S(1)} %fusion.17.rest_8_), channel_id=1, source_target_pairs={{0,16},{2,18},{4,20},{6,22},{8,24},{10,26},{12,28},{14,30},{16,0},... | collective-permute-start | bytes 129032 | tf_op jit(solution)/shard_map/ppermute | solution.py:57
  522.7 22.2 %collective-permute-start.25 = (bf16[96,1152]{1,0:T(8,128)(2,1)S(1)}, bf16[96,1152]{1,0:T(8,128)(2,1)S(1)}, u32[]{:S(2)}, u32[]{:S(2)}) collective-permute-start(bf16[96,1152]{1,0:T(8,128)(2,1)S(1)} %fusion.9.rest_9_), channel_id=1, source_target_pairs={{0,8},{2,10},{4,12},{6,14},{8,0},{10,2},{12,4},{14,6},{16,24},{18,... | collective-permute-start | bytes 663560 | tf_op jit(solution)/shard_map/ppermute | solution.py:57
  526.2 19.4 %collective-permute-start.26 = (bf16[1,192,1152]{2,1,0:T(8,128)(2,1)S(1)}, bf16[1,192,1152]{2,1,0:T(8,128)(2,1)}, u32[]{:S(2)}, u32[]{:S(2)}) collective-permute-start(bf16[1,192,1152]{2,1,0:T(8,128)(2,1)S(1)} %constant_dynamic-slice_fusion.1.rest_10_), channel_id=1, source_target_pairs={{0,1},{1,0},{2,3},{3,2},{4,5},{5,4},{6,7},{7,6},{8,9},{9,8},{10,11... | collective-permute-start | bytes 1327112 | tf_op jit(solution)/shard_map/ppermute | solution.py:57
  547.4 13.6 %collective-permute-start.28 = (bf16[96,1152]{1,0:T(8,128)(2,1)}, bf16[96,1152]{1,0:T(8,128)(2,1)S(1)}, u32[]{:S(2)}, u32[]{:S(2)}) collective-permute-start(bf16[96,1152]{1,0:T(8,128)(2,1)} %add_convert_fusion.6), channel_id=1, source_target_pairs={{0,16},{2,18},{4,20},{6,22},{8,24},{10,26},{12,28},{14,30},{16,0},... | collective-permute-start | bytes 663560 | tf_op jit(solution)/shard_map/ppermute | solution.py:57
  548.7 12.3 %collective-permute-start.29 = (bf16[96,1152]{1,0:T(8,128)(2,1)S(1)}, bf16[96,1152]{1,0:T(8,128)(2,1)S(1)}, u32[]{:S(2)}, u32[]{:S(2)}) collective-permute-start(bf16[96,1152]{1,0:T(8,128)(2,1)S(1)} %dynamic-slice_bitcast_fusion.7), channel_id=1, source_target_pairs={{0,4},{2,6},{4,0},{6,2},{8,12},{10,14},{12,8},{14,10},{16,20},{18,... | collective-permute-start | bytes 663560 | tf_op jit(solution)/shard_map/ppermute | solution.py:57
  563.4 16.8 %collective-permute-start.31 = (bf16[96,1152]{1,0:T(8,128)(2,1)S(1)}, bf16[96,1152]{1,0:T(8,128)(2,1)S(1)}, u32[]{:S(2)}, u32[]{:S(2)}) collective-permute-start(bf16[96,1152]{1,0:T(8,128)(2,1)S(1)} %add_convert_fusion.5), channel_id=1, source_target_pairs={{0,4},{2,6},{4,0},{6,2},{8,12},{10,14},{12,8},{14,10},{16,20},{18,... | collective-permute-start | bytes 663560 | tf_op jit(solution)/shard_map/ppermute | solution.py:57
  566.0 14.3 %collective-permute-start.32 = (bf16[96,1152]{1,0:T(8,128)(2,1)S(1)}, bf16[96,1152]{1,0:T(8,128)(2,1)S(1)}, u32[]{:S(2)}, u32[]{:S(2)}) collective-permute-start(bf16[96,1152]{1,0:T(8,128)(2,1)S(1)} %fusion.8), channel_id=1, source_target_pairs={{0,8},{2,10},{4,12},{6,14},{8,0},{10,2},{12,4},{14,6},{16,24},{18,... | collective-permute-start | bytes 663560 | tf_op jit(solution)/shard_map/ppermute | solution.py:57
  567.2 13.1 %collective-permute-start.30 = (bf16[96,896]{1,0:T(8,128)(2,1)S(1)}, bf16[96,896]{1,0:T(8,128)(2,1)S(1)}, u32[]{:S(2)}, u32[]{:S(2)}) collective-permute-start(bf16[96,896]{1,0:T(8,128)(2,1)S(1)} %bitcast_select_fusion.3), channel_id=1, source_target_pairs={{0,4},{2,6},{4,0},{6,2},{8,12},{10,14},{12,8},{14,10},{16,20},{18,... | collective-permute-start | bytes 516104 | tf_op jit(solution)/shard_map/ppermute | solution.py:57
  567.8 35.7 %collective-permute-start.36 = (bf16[1024,768]{1,0:T(8,128)(2,1)S(1)}, bf16[1024,768]{1,0:T(8,128)(2,1)}, u32[]{:S(2)}, u32[]{:S(2)}) collective-permute-start(bf16[1024,768]{1,0:T(8,128)(2,1)S(1)} %copy-done.4), channel_id=1, source_target_pairs={{0,1},{1,0},{2,3},{3,2},{4,5},{5,4},{6,7},{7,6},{8,9},{9,8},{10,11... | collective-permute-start | bytes 4718600 | tf_op jit(solution)/shard_map/ppermute | solution.py:57
  582.2 15.8 %collective-permute-start.33 = (bf16[192,896]{1,0:T(8,128)(2,1)S(1)}, bf16[192,896]{1,0:T(8,128)(2,1)S(1)}, u32[]{:S(2)}, u32[]{:S(2)}) collective-permute-start(bf16[192,896]{1,0:T(8,128)(2,1)S(1)} %bitcast_select_fusion.2.refs_0_), channel_id=1, source_target_pairs={{0,2},{2,0},{4,6},{6,4},{8,10},{10,8},{12,14},{14,12},{16,18},{18,... | collective-permute-start | bytes 1032200 | tf_op jit(solution)/shard_map/ppermute | solution.py:57
  583.4 15.3 %collective-permute-start.34 = (bf16[192,1152]{1,0:T(8,128)(2,1)S(1)}, bf16[192,1152]{1,0:T(8,128)(2,1)S(1)}, u32[]{:S(2)}, u32[]{:S(2)}) collective-permute-start(bf16[192,1152]{1,0:T(8,128)(2,1)S(1)} %bitcast_select_fusion.1.refs_0_), channel_id=1, source_target_pairs={{0,2},{2,0},{4,6},{6,4},{8,10},{10,8},{12,14},{14,12},{16,18},{18,... | collective-permute-start | bytes 1327112 | tf_op jit(solution)/shard_map/ppermute | solution.py:57
  585.0 13.1 %collective-permute-start.35 = (bf16[96,1152]{1,0:T(8,128)(2,1)S(1)}, bf16[96,1152]{1,0:T(8,128)(2,1)S(1)}, u32[]{:S(2)}, u32[]{:S(2)}) collective-permute-start(bf16[96,1152]{1,0:T(8,128)(2,1)S(1)} %add_convert_fusion.4), channel_id=1, source_target_pairs={{0,16},{2,18},{4,20},{6,22},{8,24},{10,26},{12,28},{14,30},{16,0},... | collective-permute-start | bytes 663560 | tf_op jit(solution)/shard_map/ppermute | solution.py:57
  (93 other events, 823.5 us)
Sparse Core Ops, SparseCore 0:
  16.8 42.1 all-gather.4
  71.2 53.5 all-gather.6
  312.7 160.9 reduce-scatter.1
  484.8 69.8 all-gather.8

commit v5 on v4

--- a/solution.py
+++ b/solution.py
@@ -72,9 +72,9 @@
     return Weight([lax.all_gather(weight, "fsdp", axis=0, tiled=True)], [(0, 0)], shape)
 
 
-def half_of(weight, shift):
+def half_of(weight):
     half = weight.shape[0] // 2
-    return lax.dynamic_slice_in_dim(weight, lax.axis_index("blk") % 2 * half + shift, half, 0)
+    return lax.dynamic_slice_in_dim(weight, lax.axis_index("blk") % 2 * half, half, 0)
 
 
 def from_halves(weight, first):
@@ -90,9 +90,9 @@
     return Weight([weight, first, second], offsets, (2 * rows, cols))
 
 
-def share_of(weight, shift=0):
+def share_of(weight):
     share = weight.shape[0] // lax.axis_size("blk")
-    return lax.dynamic_slice_in_dim(weight, lax.axis_index("blk") * share + shift, share, 0)
+    return lax.dynamic_slice_in_dim(weight, lax.axis_index("blk") * share, share, 0)
 
 
 def from_shares(weight, share):
@@ -197,18 +197,19 @@
     return jnp.where(own, refs[0][rows], refs[1][rows])
 
 
-def qkv_kernel(counts, old, table, cos_ref, sin_ref, in_ref, *rest):
-    pieces, rest = rest[: sum(counts)], rest[sum(counts) + old :]
+def qkv_kernel(counts, parts, table, cos_ref, sin_ref, *rest):
+    x_refs, rest = rest[:parts], rest[parts:]
+    pieces, rest = rest[: sum(counts)], rest[sum(counts) :]
     q_ref, k_ref, v_ref, x_ref, whole, sems = rest
     width = q_ref.shape[1]
 
-    @pl.when(pl.program_id(0) == 0)
+    @pl.when((pl.program_id(0) == 0) & (pl.program_id(1) == 0))
     def _():
         groups = grouped_copies(counts, table, pieces, [whole], sems)
         start_all(*groups)
         wait_all(*groups)
 
-    x = in_ref[...]
+    x = row_tile(table, x_refs, slice(None))
     x_ref[...] = x
     cosine, sine = cos_ref[...], sin_ref[...]
     for ref, start, factor in ((q_ref, 0, 1.0 / math.sqrt(HDIM)), (k_ref, width, 1.0)):
@@ -220,26 +221,24 @@
     v_ref[...] = dot(x, whole[:, 2 * width :]).astype(BF)
 
 
-def project(x, start, cosine, sine, weight, old, tile, after=()):
+def project(xs, lead, cosine, sine, weight, rows, tile, after=()):
     tokens, width = cosine.shape[0], weight.shape[0]
-    counts, pieces, table, scratch = weight_operands([weight], (start // tile, 0), after)
-    shifted = lambda i, t: (i + t[0], 0)
-    narrow, wide = pl.BlockSpec((tile, LANES), shifted), pl.BlockSpec((tile, width), shifted)
-    first = 4 + len(pieces)
+    steps = tokens // rows // tile
+    counts, pieces, table, scratch = weight_operands([weight], (lead, 0), after)
+    wide, narrow = row_specs([None], tile, width, steps), row_specs([None], tile, LANES, steps)
     return pl.pallas_call(
-        functools.partial(qkv_kernel, counts, len(old)),
+        functools.partial(qkv_kernel, counts, len(xs)),
         grid_spec=pltpu.PrefetchScalarGridSpec(
             num_scalar_prefetch=1,
-            grid=(x.shape[0] // tile,),
-            in_specs=[narrow, narrow, pl.BlockSpec((tile, width), lambda i, t: (i, 0))] + [ANY] * (len(pieces) + len(old)),
-            out_specs=[wide] * 4,
+            grid=(rows, steps),
+            in_specs=narrow * 2 + row_specs(xs, tile, width, steps) + [ANY] * len(pieces),
+            out_specs=wide * 4,
             scratch_shapes=scratch,
         ),
         out_shape=[jax.ShapeDtypeStruct((tokens, width), BF)] * 4,
-        input_output_aliases={first + n: n for n in range(len(old))},
         compiler_params=params(48),
-        cost_estimate=cost(6 * x.shape[0] * width * width),
-    )(table, cosine, sine, x, *pieces, *old)
+        cost_estimate=cost(6 * tokens * width * width),
+    )(table, cosine, sine, *xs, *pieces)
 
 
 def input_grad_kernel(counts, groups, table, dbr_ref, *rest):
@@ -254,10 +253,9 @@
         wait_all(*copies)
 
     total = dbr_ref[...].astype(F32)
-    for n, ref in enumerate(grads):
-        wide = ref.shape[1]
-        start = n % 3 * width + n // 3 * wide
-        total += dot_bt(ref[...], whole[:, start : start + wide])
+    for n in range(3):
+        columns = jnp.concatenate([ref[...] for ref in grads[n::3]], axis=1)
+        total += dot_bt(columns, whole[:, n * width : (n + 1) * width])
     out_ref[...] = total.astype(out_ref.dtype)
 
 
@@ -1054,10 +1052,14 @@
         last = [beside_it]
         cols += beside_it.shape[1]
 
+    (shared,) = {a for a, _ in left}
+
     def kernel(*refs):
-        out_ref, at = refs[-1], 0
-        for a, b in left:
-            part = dot_at(refs[a][...], refs[b][...]).astype(BF)
+        out_ref, flipped_ref, at = refs[-2], refs[-1], 0
+        for b in range(0, flipped_ref.shape[1], 256):
+            flipped_ref[:, b : b + 256] = turned(refs[shared][b : b + 256, :])
+        for _, b in left:
+            part = dot(flipped_ref[...], refs[b][...]).astype(BF)
             out_ref[:, at : at + part.shape[1]] = part
             at += part.shape[1]
         if last:
@@ -1067,6 +1069,7 @@
     return pl.pallas_call(
         kernel,
         in_specs=[whole] * (len(arrays) + len(last)) + [ANY] * len(after),
+        scratch_shapes=[pltpu.VMEM(pairs[0][0].shape[::-1], BF)],
         out_shape=jax.ShapeDtypeStruct((pairs[0][0].shape[1], cols), BF),
         compiler_params=params(56),
         cost_estimate=cost(2 * pairs[0][0].shape[0] * pairs[0][0].shape[1] * cols),
@@ -1261,18 +1264,16 @@
 
     if row_mode:
         tables = (*tables_q, qkv)
-        share = share_of(swiglu_weight, zero_after(moved))
+        share, *halves = tied([share_of(swiglu_weight), half_of(out_weight), half_of(down_weight)], [moved])
         share_came = flipped(share, "fsdp", 1)
-        old = project(take(tokens, mine, 0), mine * shard_len, *tables, [], small_tile, [moved, share])
-        *old, share_came = tied([*old, share_came])
+        firsts = [flipped(h, "fsdp", 1) for h in halves]
+        xs = [take(tokens, mine, 0), moved]
+        projected = project(xs, lead, *tables, rows, small_tile, [share, *halves])
+        query, key, value, x, share_came = tied([*projected, share_came])
         swiglu = from_shares(swiglu_weight, share_came)
-        shift = zero_after(old[0])
-        halves = [half_of(out_weight, shift), half_of(down_weight, shift)]
-        firsts = [flipped(h, "fsdp", 1) for h in halves]
-        query, key, value, x = project(moved, (1 - mine) * shard_len, *tables, old, small_tile, halves)
         key_all, value_all = key, value
     else:
-        query, key, value, x = project(tokens.reshape(-1, width), 0, *tables_q, qkv, [], small_tile)
+        query, key, value, x = project([tokens.reshape(-1, width)], 0, *tables_q, qkv, rows, small_tile)
 
         def along_row(part):
             part = part.reshape(rows, per_row, width)

time: 631 us -> 631 us (level)
    pallas_call x2 -> x1, Pallas kernels: 17.8 us -> 14.3 us  [project(): pl.pallas_call(functools.partial(qkv_kernel, counts, len(xs)), grid_spec=...]
    unnamed x169 -> x165, local copies, waits for them, and re-layouts: 26.7 us -> 26.9 us
  transfers between devices with their start and end apart: 43 -> 43, of which waited for: 13 -> 14; matrix products, arithmetic and copies ran while one was open for 11% -> 12% of each run, Pallas kernels for 63% -> 63%
where the time goes in v5:
time: 631 us; the launch traced here: 621 us
  Pallas kernels  393 us (62%)
  waiting for transfers between devices  61 us (10%)
  local copies, waits for them, and re-layouts  59.9 us (9%)
  starting transfers between devices  46.2 us (7%)
  other arithmetic  42.8 us (7%)
  between operations  17.9 us (3%)
    pallas_call x2, Pallas kernels, attend_back(): pl.pallas_call(functools.partial(attend_back_kernel, group, base, len(aft...  101 us
    ppermute x39, waiting for transfers between devices, flipped(): return lax.ppermute(block, axis, route)  60.9 us
    pallas_call x1, Pallas kernels, attend(): pl.pallas_call(functools.partial(attend_kernel, group, len(after)), grid_...  55.2 us
    pallas_call x1, Pallas kernels, mix(): pl.pallas_call(functools.partial(mix_kernel, counts), grid_spec=pltpu.Pre...  52.6 us
    ppermute x39, starting transfers between devices, flipped(): return lax.ppermute(block, axis, route)  46.1 us
    pallas_call x1, Pallas kernels, branch_back(): pl.pallas_call(functools.partial(branch_back_kernel, counts), grid_spec=p...  39 us
    pallas_call x1, Pallas kernels, hidden_back(): pl.pallas_call(functools.partial(hidden_back_kernel, counts, len(cots)),...  30.1 us
    unnamed x165, local copies, waits for them, and re-layouts  26.9 us
  transfers between devices with their start and end apart: 43, of which 14 were waited for; matrix products, arithmetic and copies ran while one was open for 12% of the time, Pallas kernels for 63%

profile of v5, /device:TPU:0, one launch (start us, length us, event | category | flops | bytes accessed | tf_op | source)
XLA Modules:
  0.0 621.4 jit_solution(18428258637615586626)
XLA Ops:
  8.1 3.0 collective-permute-start
  19.4 3.2 dynamic-slice_bitcast_fusion.2
  27.7 5.0 fusion.5
  34.6 23.9 %collective-permute-done.1.refs_3_.rest_1_ = bf16[1024,768]{1,0:T(8,128)(2,1)} collective-permute-done((bf16[1024,768]{1,0:T(8,128)(2,1)}, bf16[1024,768]{1,0:T(8,128)(2,1)}, u32[]{:S(2)}, u32[]{:S(2)}) %collective-permute-start.1) | collective-permute-done | bytes 1572896 | tf_op jit(solution)/shard_map/ppermute | solution.py:57
  64.3 14.3 %shard_map.171 = (bf16[2048,768]{1,0:T(8,128)(2,1)}, bf16[2048,768]{1,0:T(8,128)(2,1)}, bf16[2048,768]{1,0:T(8,128)(2,1)}, bf16[2048,768]{1,0:T(8,128)(2,1)}) custom-call(s32[6]{0:T(128)S(1)} %stack.107.table, f32[2048,128]{1,0:T(8,128)S(1)} %copy-done.16, f32[2048,128]{1,0:T(8,128)S(1)} %get-tuple-element.203.sin_ref.sq_ref.sk_ref, ...), custom_call_target="tpu_custom_call" | custom-call | flops 28991029248 | bytes 1048576 | tf_op jit(solution)/shard_map/pallas_call | solution.py:229
  86.1 55.2 %shard_map.173 = (bf16[2048,768]{1,0:T(8,128)(2,1)}, f32[12,1,2048]{2,1,0:T(1,128)}) custom-call(s32[16]{0:T(128)} %reshape.1313.spans, bf16[2048,768]{1,0:T(8,128)(2,1)} %get-tuple-element.103.q_ref, bf16[2048,768]{1,0:T(8,128)(2,1)} %get-tuple-element.104.k_ref, bf16[2048,768]{1,0:T(8,128)(2,1)} %get-tuple-element.105.v_ref, ...), custom_call_target="tpu_custom_call" | custom-call | flops 51539607552 | bytes 1048576 | tf_op jit(solution)/shard_map/pallas_call | solution.py:399
  150.4 52.6 %shard_map.175 = (bf16[2048,768]{1,0:T(8,128)(2,1)}, f32[2048,128]{1,0:T(8,128)}, bf16[2048,3072]{1,0:T(8,128)(2,1)}, bf16[2048,3072]{1,0:T(8,128)(2,1)}, bf16[2...) custom-call(s32[18]{0:T(128)} %stack.115.table, ...), custom_call_target="tpu_custom_call" | custom-call | flops 125627793408 | bytes 1048576 | tf_op jit(solution)/shard_map/pallas_call | solution.py:673
  215.4 3.3 collective-permute-start.12
  218.7 2.9 collective-permute-done.12
  221.7 2.7 collective-permute-start.13
  227.8 3.7 constant_dynamic-slice_fusion
  237.1 30.1 %shard_map.177 = (bf16[2048,768]{1,0:T(8,128)(2,1)}, bf16[2048,6144]{1,0:T(8,128)(2,1)}, f32[8,768]{1,0:T(8,128)}) custom-call(s32[8]{0:T(128)} %stack.114.table, bf16[1024,768]{1,0:T(8,128)(2,1)} %get-tuple-element.192.rest_0_, bf16[1024,768]{1,0:T(8,128)(2,1)} %get-tuple-element.114.rest_1_, bf16[2048,768]{1,0:T(8,128)(2,1)} %get-tuple-element.115.rest_2_, ...), custom_call_target="tpu_custom_call" | custom-call | flops 77309411328 | bytes 1048576 | tf_op jit(solution)/shard_map/pallas_call | solution.py:754
  269.1 24.9 %shard_map.178.old_ref = bf16[16,2,576,384]{3,2,1,0:T(8,128)(2,1)} custom-call(bf16[2048,768]{1,0:T(8,128)(2,1)S(1)} %copy-done.18, bf16[2048,6144]{1,0:T(8,128)(2,1)} %get-tuple-element.122.grad_ref.refs_4_), custom_call_target="tpu_custom_call" | custom-call | flops 77309411328 | bytes 1048576 | tf_op jit(solution)/shard_map/pallas_call | solution.py:1011
  294.0 14.5 %shard_map.179.refs_14_ = bf16[16,2,576,384]{3,2,1,0:T(8,128)(2,1)} custom-call(bf16[2048,3072]{1,0:T(8,128)(2,1)} %get-tuple-element.123.hidden_ref, bf16[2048,768]{1,0:T(8,128)(2,1)S(1)} %copy-done.17, bf16[16,2,576,384]{3,2,1,0:T(8,128)(2,1)} %shard_map.178.old_ref), custom_call_target="tpu_custom_call", output_to_operand_aliasing={{}: (2, {})} | custom-call | flops 38654705664 | bytes 1048576 | tf_op jit(solution)/shard_map/pallas_call | solution.py:1023
  308.7 39.0 %shard_map.180 = (bf16[2048,768]{1,0:T(8,128)(2,1)}, bf16[2048,768]{1,0:T(8,128)(2,1)}, bf16[2048,128]{1,0:T(8,128)(2,1)}, f32[8,768]{1,0:T(8,128)}) custom-call(s32[12]{0:T(128)} %stack.110.table, bf16[2048,768]{1,0:T(8,128)(2,1)} %get-tuple-element.120.dffn_ref.refs_0_, bf16[2048,768]{1,0:T(8,128)(2,1)} %get-tuple-element.121.low_ref.refs_1_, ...), custom_call_target="tpu_custom_call" | custom-call | flops 86973087744 | bytes 1048576 | tf_op jit(solution)/shard_map/pallas_call | solution.py:835
  350.7 7.0 %shard_map.182 = bf16[768,896]{1,0:T(8,128)(2,1)} custom-call(bf16[2048,768]{1,0:T(8,128)(2,1)} %get-tuple-element.108.att_ref.refs_5_.refs_0_, bf16[2048,768]{1,0:T(8,128)(2,1)} %get-tuple-element.125.refs_1_.dbr_ref, bf16[768,128]{1,0:T(8,128)(2,1)} %pad.24.refs_2_), custom_call_target="tpu_custom_call" | custom-call | flops 11274289152 | bytes 1048576 | tf_op jit(solution)/shard_map/pallas_call | solution.py:1069
  359.7 50.4 %shard_map.183 = (bf16[2048,384]{1,0:T(8,128)(2,1)}, bf16[2048,384]{1,0:T(8,128)(2,1)}, bf16[2048,384]{1,0:T(8,128)(2,1)}) custom-call(s32[16]{0:T(128)} %reshape.1322.spans, bf16[2048,768]{1,0:T(8,128)(2,1)} %get-tuple-element.103.q_ref, bf16[2048,768]{1,0:T(8,128)(2,1)} %get-tuple-element.128.do_ref, bf16[2048,768]{1,0:T(8,128)(2,1)} %get-tuple-element.104.k_ref, ...), custom_call_target="tpu_custom_call" | custom-call | flops 51539607552 | bytes 1048576 | tf_op jit(solution)/shard_map/pallas_call | solution.py:524
  415.1 9.8 %shard_map.185.refs_0_ = bf16[768,1152]{1,0:T(8,128)(2,1)} custom-call(bf16[2048,768]{1,0:T(8,128)(2,1)} %get-tuple-element.109.x_ref.refs_0_, bf16[2048,384]{1,0:T(8,128)(2,1)} %get-tuple-element.134.refs_1_.rest_0_, bf16[2048,384]{1,0:T(8,128)(2,1)} %get-tuple-element.135.refs_2_.rest_1_, bf16[2048,384]{1,0:T(8,128)(2,1)} %get-tuple-element.136.refs_3_.rest_2_, ...), custom_call_target="tpu_custom_call" | custom-call | flops 14495514624 | bytes 1048576 | tf_op jit(solution)/shard_map/pallas_call | solution.py:1069
  430.1 50.6 %shard_map.187 = (bf16[2048,384]{1,0:T(8,128)(2,1)}, bf16[2048,384]{1,0:T(8,128)(2,1)}, bf16[2048,384]{1,0:T(8,128)(2,1)}) custom-call(s32[16]{0:T(128)} %reshape.1322.spans, bf16[2048,768]{1,0:T(8,128)(2,1)} %get-tuple-element.103.q_ref, bf16[2048,768]{1,0:T(8,128)(2,1)} %get-tuple-element.128.do_ref, bf16[2048,768]{1,0:T(8,128)(2,1)} %get-tuple-element.104.k_ref, ...), custom_call_target="tpu_custom_call" | custom-call | flops 51539607552 | bytes 1048576 | tf_op jit(solution)/shard_map/pallas_call | solution.py:524
  486.1 9.9 %shard_map.190.refs_0_ = bf16[768,1152]{1,0:T(8,128)(2,1)} custom-call(bf16[2048,768]{1,0:T(8,128)(2,1)} %get-tuple-element.109.x_ref.refs_0_, bf16[2048,384]{1,0:T(8,128)(2,1)} %get-tuple-element.146.refs_1_.rest_3_, bf16[2048,384]{1,0:T(8,128)(2,1)} %get-tuple-element.147.refs_2_.rest_4_, bf16[2048,384]{1,0:T(8,128)(2,1)} %get-tuple-element.148.refs_3_.rest_5_, ...), custom_call_target="tpu_custom_call" | custom-call | flops 14495514624 | bytes 1048576 | tf_op jit(solution)/shard_map/pallas_call | solution.py:1069
  498.4 3.5 collective-permute-start.21
  504.8 8.8 %shard_map.192.refs_0_ = bf16[1024,768]{1,0:T(8,128)(2,1)S(1)} custom-call(s32[6]{0:T(128)S(1)} %stack.126.table, bf16[2048,768]{1,0:T(8,128)(2,1)} %get-tuple-element.125.refs_1_.dbr_ref, bf16[2048,384]{1,0:T(8,128)(2,1)S(1)} %copy-done.7, bf16[2048,384]{1,0:T(8,128)(2,1)S(1)} %copy-done.8, bf16[2048,384]{1,0:T(8,128)(2,1)} %get-tuple-element.136.refs_3_.rest_2_, ...), custom_call_target="tpu_custom_call" | custom-call | flops 14495514624 | bytes 1048576 | tf_op jit(solution)/shard_map/pallas_call | solution.py:266
  522.4 10.0 %shard_map.194.refs_0_ = f32[2048,768]{1,0:T(8,128)} custom-call(s32[6]{0:T(128)S(1)} %stack.128.table, bf16[2048,768]{1,0:T(8,128)(2,1)} %get-tuple-element.125.refs_1_.dbr_ref, bf16[2048,384]{1,0:T(8,128)(2,1)S(1)} %copy-done.7, bf16[2048,384]{1,0:T(8,128)(2,1)S(1)} %copy-done.8, bf16[2048,384]{1,0:T(8,128)(2,1)S(1)} %copy-done.9, ...), custom_call_target="tpu_custom_call" | custom-call | flops 14495514624 | bytes 1048576 | tf_op jit(solution)/shard_map/pallas_call | solution.py:266
  532.5 8.3 %collective-permute-done.25.refs_2_ = bf16[96,1152]{1,0:T(8,128)(2,1)S(1)} collective-permute-done((bf16[96,1152]{1,0:T(8,128)(2,1)S(1)}, bf16[96,1152]{1,0:T(8,128)(2,1)S(1)}, u32[]{:S(2)}, u32[]{:S(2)}) %collective-permute-start.25) | collective-permute-done | bytes 221216 | tf_op jit(solution)/shard_map/ppermute | solution.py:57
  547.1 2.9 collective-permute-start.27
  550.0 4.5 collective-permute-done.27.refs_0_
  554.5 4.4 collective-permute-done.28.refs_1_
  566.7 3.0 copy-done
  569.7 7.8 %shard_map.197 = (f32[384,6144]{1,0:T(8,128)}, f32[1536,768]{1,0:T(8,128)}) custom-call(bf16[16,576,384]{2,1,0:T(8,128)(2,1)S(1)} %bitcast.157), custom_call_target="tpu_custom_call" | custom-call | flops 1024 | bytes 1024 | tf_op jit(solution)/shard_map/pallas_call | solution.py:1121
  584.0 3.5 broadcast_select_fusion.refs_0_
  587.5 7.9 %collective-permute-done.35.refs_3_ = bf16[96,1152]{1,0:T(8,128)(2,1)S(1)} collective-permute-done((bf16[96,1152]{1,0:T(8,128)(2,1)S(1)}, bf16[96,1152]{1,0:T(8,128)(2,1)S(1)}, u32[]{:S(2)}, u32[]{:S(2)}) %collective-permute-start.35) | collective-permute-done | bytes 221216 | tf_op jit(solution)/shard_map/ppermute | solution.py:57
  600.8 3.9 shard_map.202.refs_0_
  (396 shorter events, 129.1 us)
Async XLA Ops:
  7.2 52.8 %all-gather.5.cloned.1.call-start = ((), (), s32[]{:S(2)}) async-start(), calls=%async_computation.1 | async-start | bytes 1880064 | tf_op jit(solution)/shard_map/all_gather | solution.py:101
  12.5 131.4 %collective-permute-start.5 = (bf16[2,384]{1,0:T(2,128)(2,1)S(1)}, bf16[2,384]{1,0:T(2,128)(2,1)S(1)}, u32[]{:S(2)}, u32[]{:S(2)}) collective-permute-start(bf16[2,384]{1,0:T(2,128)(2,1)S(1)} %pad_maximum_fusion.6), channel_id=1, source_target_pairs={{0,1},{1,0},{2,3},{3,2},{4,5},{5,4},{6,7},{7,6},{8,9},{9,8},{10,11... | collective-permute-start | bytes 4616 | tf_op jit(solution)/shard_map/ppermute | solution.py:57
  14.8 134.8 %all-gather.7.cloned.1.call-start = ((), (), s32[]{:S(2)}) async-start(), calls=%async_computation.2 | async-start | bytes 5013504 | tf_op jit(solution)/shard_map/all_gather | solution.py:101
  22.6 35.9 %collective-permute-start.1 = (bf16[1024,768]{1,0:T(8,128)(2,1)}, bf16[1024,768]{1,0:T(8,128)(2,1)}, u32[]{:S(2)}, u32[]{:S(2)}) collective-permute-start(bf16[1024,768]{1,0:T(8,128)(2,1)} %shard_map.169), channel_id=1, source_target_pairs={{0,1},{1,0},{2,3},{3,2},{4,5},{5,4},{6,7},{7,6},{8,9},{9,8},{10,11... | collective-permute-start | bytes 4718600 | tf_op jit(solution)/shard_map/ppermute | solution.py:57
  58.5 20.2 %collective-permute-start.2 = (bf16[24,6144]{1,0:T(8,128)(2,1)}, bf16[24,6144]{1,0:T(8,128)(2,1)S(1)}, u32[]{:S(2)}, u32[]{:S(2)}) collective-permute-start(bf16[24,6144]{1,0:T(8,128)(2,1)} %get-tuple-element.96.rest_4_), channel_id=1, source_target_pairs={{0,1},{1,0},{2,3},{3,2},{4,5},{5,4},{6,7},{7,6},{8,9},{9,8},{10,11... | collective-permute-start | bytes 884744 | tf_op jit(solution)/shard_map/ppermute | solution.py:57
  79.4 402.0 %reduce-scatter.2.cloned.1.call-start = ((), (), s32[]{:S(2)}) async-start(), calls=%async_computation.3 | async-start | bytes 14598144 | tf_op jit(solution)/shard_map/reduce_scatter | solution.py:1313
  84.0 57.2 %collective-permute-start.3 = (bf16[192,768]{1,0:T(8,128)(2,1)S(1)}, bf16[192,768]{1,0:T(8,128)(2,1)S(1)}, u32[]{:S(2)}, u32[]{:S(2)}) collective-permute-start(bf16[192,768]{1,0:T(8,128)(2,1)S(1)} %copy-done.13), channel_id=1, source_target_pairs={{0,1},{1,0},{2,3},{3,2},{4,5},{5,4},{6,7},{7,6},{8,9},{9,8},{10,11... | collective-permute-start | bytes 884744 | tf_op jit(solution)/shard_map/ppermute | solution.py:57
  84.7 56.6 %collective-permute-start.4 = (bf16[768,768]{1,0:T(8,128)(2,1)S(1)}, bf16[768,768]{1,0:T(8,128)(2,1)S(1)}, u32[]{:S(2)}, u32[]{:S(2)}) collective-permute-start(bf16[768,768]{1,0:T(8,128)(2,1)S(1)} %copy-done.2), channel_id=1, source_target_pairs={{0,1},{1,0},{2,3},{3,2},{4,5},{5,4},{6,7},{7,6},{8,9},{9,8},{10,11... | collective-permute-start | bytes 3538952 | tf_op jit(solution)/shard_map/ppermute | solution.py:57
  149.0 54.0 %collective-permute-start.8 = (bf16[1024,768]{1,0:T(8,128)(2,1)}, bf16[1024,768]{1,0:T(8,128)(2,1)S(1)}, u32[]{:S(2)}, u32[]{:S(2)}) collective-permute-start(bf16[1024,768]{1,0:T(8,128)(2,1)} %get-tuple-element.191.rest_8_), channel_id=1, source_target_pairs={{0,1},{1,0},{2,3},{3,2},{4,5},{5,4},{6,7},{7,6},{8,9},{9,8},{10,11... | collective-permute-start | bytes 4718600 | tf_op jit(solution)/shard_map/ppermute | solution.py:57
  221.7 12.5 %collective-permute-start.13 = (bf16[128,896]{1,0:T(8,128)(2,1)S(1)}, bf16[128,896]{1,0:T(8,128)(2,1)S(1)}, u32[]{:S(2)}, u32[]{:S(2)}) collective-permute-start(bf16[128,896]{1,0:T(8,128)(2,1)S(1)} %get-tuple-element.195), channel_id=1, source_target_pairs={{0,16},{2,18},{4,20},{6,22},{8,24},{10,26},{12,28},{14,30},{16,0},... | collective-permute-start | bytes 688136 | tf_op jit(solution)/shard_map/ppermute | solution.py:57
  231.5 119.2 %collective-permute-start.14 = (bf16[1024,768]{1,0:T(8,128)(2,1)}, bf16[1024,768]{1,0:T(8,128)(2,1)}, u32[]{:S(2)}, u32[]{:S(2)}) collective-permute-start(bf16[1024,768]{1,0:T(8,128)(2,1)} %get-tuple-element.190), channel_id=1, source_target_pairs={{0,1},{1,0},{2,3},{3,2},{4,5},{5,4},{6,7},{7,6},{8,9},{9,8},{10,11... | collective-permute-start | bytes 4718600 | tf_op jit(solution)/shard_map/ppermute | solution.py:57
  308.6 258.1 %all-gather.9.cloned.1.call-start = ((), (), s32[]{:S(2)}) async-start(), calls=%async_computation.4 | async-start | bytes 7520256 | tf_op jit(solution)/shard_map/all_gather | solution.py:1351
  358.9 51.2 %collective-permute-start.15 = (bf16[2,192,896]{2,1,0:T(8,128)(2,1)S(1)}, bf16[2,192,896]{2,1,0:T(8,128)(2,1)S(1)}, u32[]{:S(2)}, u32[]{:S(2)}) collective-permute-start(bf16[2,192,896]{2,1,0:T(8,128)(2,1)S(1)} %dynamic-slice_bitcast_fusion.6.rest_0_), channel_id=1, source_target_pairs={{0,2},{2,0},{4,6},{6,4},{8,10},{10,8},{12,14},{14,12},{16,18},{18,... | collective-permute-start | bytes 2064392 | tf_op jit(solution)/shard_map/ppermute | solution.py:57
  413.6 11.3 %collective-permute-start.16 = (bf16[1,192,896]{2,1,0:T(8,128)(2,1)S(1)}, bf16[1,192,896]{2,1,0:T(8,128)(2,1)S(1)}, u32[]{:S(2)}, u32[]{:S(2)}) collective-permute-start(bf16[1,192,896]{2,1,0:T(8,128)(2,1)S(1)} %constant_dynamic-slice_fusion.3.refs_4_), channel_id=1, source_target_pairs={{0,1},{1,0},{2,3},{3,2},{4,5},{5,4},{6,7},{7,6},{8,9},{9,8},{10,11... | collective-permute-start | bytes 1032200 | tf_op jit(solution)/shard_map/ppermute | solution.py:57
  426.8 54.0 %collective-permute-start.17 = (bf16[96,896]{1,0:T(8,128)(2,1)S(1)}, bf16[96,896]{1,0:T(8,128)(2,1)S(1)}, u32[]{:S(2)}, u32[]{:S(2)}) collective-permute-start(bf16[96,896]{1,0:T(8,128)(2,1)S(1)} %dynamic-slice_bitcast_fusion.9.rest_0_), channel_id=1, source_target_pairs={{0,4},{2,6},{4,0},{6,2},{8,12},{10,14},{12,8},{14,10},{16,20},{18,... | collective-permute-start | bytes 516104 | tf_op jit(solution)/shard_map/ppermute | solution.py:57
  429.2 51.5 %collective-permute-start.18 = (bf16[2,192,1152]{2,1,0:T(8,128)(2,1)S(1)}, bf16[2,192,1152]{2,1,0:T(8,128)(2,1)}, u32[]{:S(2)}, u32[]{:S(2)}) collective-permute-start(bf16[2,192,1152]{2,1,0:T(8,128)(2,1)S(1)} %dynamic-slice_bitcast_fusion.5.rest_1_), channel_id=1, source_target_pairs={{0,2},{2,0},{4,6},{6,4},{8,10},{10,8},{12,14},{14,12},{16,18},{18,... | collective-permute-start | bytes 2654216 | tf_op jit(solution)/shard_map/ppermute | solution.py:57
  482.4 13.6 %collective-permute-start.19 = (bf16[48,896]{1,0:T(8,128)(2,1)S(1)}, bf16[48,896]{1,0:T(8,128)(2,1)S(1)}, u32[]{:S(2)}, u32[]{:S(2)}) collective-permute-start(bf16[48,896]{1,0:T(8,128)(2,1)S(1)} %dynamic-slice_bitcast_fusion.10.refs_4_), channel_id=1, source_target_pairs={{0,8},{2,10},{4,12},{6,14},{8,0},{10,2},{12,4},{14,6},{16,24},{18,... | collective-permute-start | bytes 258056 | tf_op jit(solution)/shard_map/ppermute | solution.py:57
  484.5 11.9 %collective-permute-start.20 = (bf16[1,192,1152]{2,1,0:T(8,128)(2,1)S(1)}, bf16[1,192,1152]{2,1,0:T(8,128)(2,1)S(1)}, u32[]{:S(2)}, u32[]{:S(2)}) collective-permute-start(bf16[1,192,1152]{2,1,0:T(8,128)(2,1)S(1)} %constant_dynamic-slice_fusion.2.refs_5_), channel_id=1, source_target_pairs={{0,1},{1,0},{2,3},{3,2},{4,5},{5,4},{6,7},{7,6},{8,9},{9,8},{10,11... | collective-permute-start | bytes 1327112 | tf_op jit(solution)/shard_map/ppermute | solution.py:57
  498.4 16.3 %collective-permute-start.21 = (bf16[24,896]{1,0:T(8,128)(2,1)S(1)}, bf16[24,896]{1,0:T(8,128)(2,1)S(1)}, u32[]{:S(2)}, u32[]{:S(2)}) collective-permute-start(bf16[24,896]{1,0:T(8,128)(2,1)S(1)} %dynamic-slice_bitcast_fusion.11.rest_8_), channel_id=1, source_target_pairs={{0,16},{2,18},{4,20},{6,22},{8,24},{10,26},{12,28},{14,30},{16,0},... | collective-permute-start | bytes 129032 | tf_op jit(solution)/shard_map/ppermute | solution.py:57
  503.3 11.4 %collective-permute-start.22 = (bf16[96,1152]{1,0:T(8,128)(2,1)S(1)}, bf16[96,1152]{1,0:T(8,128)(2,1)S(1)}, u32[]{:S(2)}, u32[]{:S(2)}) collective-permute-start(bf16[96,1152]{1,0:T(8,128)(2,1)S(1)} %dynamic-slice_bitcast_fusion.8.rest_9_), channel_id=1, source_target_pairs={{0,4},{2,6},{4,0},{6,2},{8,12},{10,14},{12,8},{14,10},{16,20},{18,... | collective-permute-start | bytes 663560 | tf_op jit(solution)/shard_map/ppermute | solution.py:57
  516.2 16.3 %collective-permute-start.24 = (bf16[24,896]{1,0:T(8,128)(2,1)S(1)}, bf16[24,896]{1,0:T(8,128)(2,1)S(1)}, u32[]{:S(2)}, u32[]{:S(2)}) collective-permute-start(bf16[24,896]{1,0:T(8,128)(2,1)S(1)} %fusion.17.rest_8_), channel_id=1, source_target_pairs={{0,16},{2,18},{4,20},{6,22},{8,24},{10,26},{12,28},{14,30},{16,0},... | collective-permute-start | bytes 129032 | tf_op jit(solution)/shard_map/ppermute | solution.py:57
  518.5 22.2 %collective-permute-start.25 = (bf16[96,1152]{1,0:T(8,128)(2,1)S(1)}, bf16[96,1152]{1,0:T(8,128)(2,1)S(1)}, u32[]{:S(2)}, u32[]{:S(2)}) collective-permute-start(bf16[96,1152]{1,0:T(8,128)(2,1)S(1)} %fusion.9.rest_9_), channel_id=1, source_target_pairs={{0,8},{2,10},{4,12},{6,14},{8,0},{10,2},{12,4},{14,6},{16,24},{18,... | collective-permute-start | bytes 663560 | tf_op jit(solution)/shard_map/ppermute | solution.py:57
  520.7 20.7 %collective-permute-start.26 = (bf16[1,192,1152]{2,1,0:T(8,128)(2,1)S(1)}, bf16[1,192,1152]{2,1,0:T(8,128)(2,1)}, u32[]{:S(2)}, u32[]{:S(2)}) collective-permute-start(bf16[1,192,1152]{2,1,0:T(8,128)(2,1)S(1)} %constant_dynamic-slice_fusion.1.rest_10_), channel_id=1, source_target_pairs={{0,1},{1,0},{2,3},{3,2},{4,5},{5,4},{6,7},{7,6},{8,9},{9,8},{10,11... | collective-permute-start | bytes 1327112 | tf_op jit(solution)/shard_map/ppermute | solution.py:57
  543.2 15.7 %collective-permute-start.28 = (bf16[96,1152]{1,0:T(8,128)(2,1)}, bf16[96,1152]{1,0:T(8,128)(2,1)}, u32[]{:S(2)}, u32[]{:S(2)}) collective-permute-start(bf16[96,1152]{1,0:T(8,128)(2,1)} %add_convert_fusion.6), channel_id=1, source_target_pairs={{0,16},{2,18},{4,20},{6,22},{8,24},{10,26},{12,28},{14,30},{16,0},... | collective-permute-start | bytes 663560 | tf_op jit(solution)/shard_map/ppermute | solution.py:57
  544.5 14.4 %collective-permute-start.29 = (bf16[96,1152]{1,0:T(8,128)(2,1)S(1)}, bf16[96,1152]{1,0:T(8,128)(2,1)S(1)}, u32[]{:S(2)}, u32[]{:S(2)}) collective-permute-start(bf16[96,1152]{1,0:T(8,128)(2,1)S(1)} %dynamic-slice_bitcast_fusion.7), channel_id=1, source_target_pairs={{0,4},{2,6},{4,0},{6,2},{8,12},{10,14},{12,8},{14,10},{16,20},{18,... | collective-permute-start | bytes 663560 | tf_op jit(solution)/shard_map/ppermute | solution.py:57
  560.7 16.9 %collective-permute-start.31 = (bf16[96,1152]{1,0:T(8,128)(2,1)S(1)}, bf16[96,1152]{1,0:T(8,128)(2,1)S(1)}, u32[]{:S(2)}, u32[]{:S(2)}) collective-permute-start(bf16[96,1152]{1,0:T(8,128)(2,1)S(1)} %add_convert_fusion.5), channel_id=1, source_target_pairs={{0,4},{2,6},{4,0},{6,2},{8,12},{10,14},{12,8},{14,10},{16,20},{18,... | collective-permute-start | bytes 663560 | tf_op jit(solution)/shard_map/ppermute | solution.py:57
  563.1 14.5 %collective-permute-start.32 = (bf16[96,1152]{1,0:T(8,128)(2,1)S(1)}, bf16[96,1152]{1,0:T(8,128)(2,1)S(1)}, u32[]{:S(2)}, u32[]{:S(2)}) collective-permute-start(bf16[96,1152]{1,0:T(8,128)(2,1)S(1)} %fusion.8), channel_id=1, source_target_pairs={{0,8},{2,10},{4,12},{6,14},{8,0},{10,2},{12,4},{14,6},{16,24},{18,... | collective-permute-start | bytes 663560 | tf_op jit(solution)/shard_map/ppermute | solution.py:57
  564.3 13.2 %collective-permute-start.30 = (bf16[96,896]{1,0:T(8,128)(2,1)S(1)}, bf16[96,896]{1,0:T(8,128)(2,1)S(1)}, u32[]{:S(2)}, u32[]{:S(2)}) collective-permute-start(bf16[96,896]{1,0:T(8,128)(2,1)S(1)} %bitcast_select_fusion.3), channel_id=1, source_target_pairs={{0,4},{2,6},{4,0},{6,2},{8,12},{10,14},{12,8},{14,10},{16,20},{18,... | collective-permute-start | bytes 516104 | tf_op jit(solution)/shard_map/ppermute | solution.py:57
  565.1 35.7 %collective-permute-start.36 = (bf16[1024,768]{1,0:T(8,128)(2,1)S(1)}, bf16[1024,768]{1,0:T(8,128)(2,1)}, u32[]{:S(2)}, u32[]{:S(2)}) collective-permute-start(bf16[1024,768]{1,0:T(8,128)(2,1)S(1)} %copy-done.6), channel_id=1, source_target_pairs={{0,1},{1,0},{2,3},{3,2},{4,5},{5,4},{6,7},{7,6},{8,9},{9,8},{10,11... | collective-permute-start | bytes 4718600 | tf_op jit(solution)/shard_map/ppermute | solution.py:57
  579.5 15.9 %collective-permute-start.33 = (bf16[192,896]{1,0:T(8,128)(2,1)S(1)}, bf16[192,896]{1,0:T(8,128)(2,1)S(1)}, u32[]{:S(2)}, u32[]{:S(2)}) collective-permute-start(bf16[192,896]{1,0:T(8,128)(2,1)S(1)} %bitcast_select_fusion.2.refs_0_), channel_id=1, source_target_pairs={{0,2},{2,0},{4,6},{6,4},{8,10},{10,8},{12,14},{14,12},{16,18},{18,... | collective-permute-start | bytes 1032200 | tf_op jit(solution)/shard_map/ppermute | solution.py:57
  580.6 15.4 %collective-permute-start.34 = (bf16[192,1152]{1,0:T(8,128)(2,1)S(1)}, bf16[192,1152]{1,0:T(8,128)(2,1)S(1)}, u32[]{:S(2)}, u32[]{:S(2)}) collective-permute-start(bf16[192,1152]{1,0:T(8,128)(2,1)S(1)} %bitcast_select_fusion.1.refs_0_), channel_id=1, source_target_pairs={{0,2},{2,0},{4,6},{6,4},{8,10},{10,8},{12,14},{14,12},{16,18},{18,... | collective-permute-start | bytes 1327112 | tf_op jit(solution)/shard_map/ppermute | solution.py:57
  582.3 13.1 %collective-permute-start.35 = (bf16[96,1152]{1,0:T(8,128)(2,1)S(1)}, bf16[96,1152]{1,0:T(8,128)(2,1)S(1)}, u32[]{:S(2)}, u32[]{:S(2)}) collective-permute-start(bf16[96,1152]{1,0:T(8,128)(2,1)S(1)} %add_convert_fusion.4), channel_id=1, source_target_pairs={{0,16},{2,18},{4,20},{6,22},{8,24},{10,26},{12,28},{14,30},{16,0},... | collective-permute-start | bytes 663560 | tf_op jit(solution)/shard_map/ppermute | solution.py:57
  (91 other events, 757.4 us)
Sparse Core Ops, SparseCore 0:
  14.9 41.8 all-gather.4
  79.5 53.5 all-gather.6
  308.7 162.6 reduce-scatter.1
  481.6 73.5 all-gather.8

commit v6 on v5

--- a/solution.py
+++ b/solution.py
@@ -317,14 +317,16 @@
         whole[:, (2 * g + 1) * LANES : (2 * g + 2) * LANES] = features[...]
 
 
-def staggered(count, load, work, finish):
-    loaded, worked = load(0), None
+def staggered(count, load, work, finish, depth=1):
+    loaded = [load(g) for g in range(min(depth, count))]
+    worked = None
     for g in range(count):
-        ahead = load(g + 1) if g + 1 < count else None
-        result = work(g, loaded)
+        if g + depth < count:
+            loaded.append(load(g + depth))
+        result = work(g, loaded.pop(0))
         if worked is not None:
             finish(g - 1, worked)
-        worked, loaded = result, ahead
+        worked = result
     finish(count - 1, worked)
 
 
@@ -375,7 +377,7 @@
                 values = vt[2 * g + h, :, pl.ds(at, BK_FWD)]
                 accum[g, :, cols] = accum[g, :, cols] * factor[:, cols] + dot(values, soft[:, cols])
 
-        staggered(group, load, work, finish)
+        staggered(group, load, work, finish, 2)
         return state
 
     lax.fori_loop(0, count, step, 0)

time: 631 us -> 628 us (level)
  no operation moved by 1% of the time
where the time goes in v6:
time: 628 us; the launch traced here: 618 us
  Pallas kernels  390 us (62%)
  waiting for transfers between devices  63.2 us (10%)
  local copies, waits for them, and re-layouts  60.9 us (10%)
  other arithmetic  42.9 us (7%)
  starting transfers between devices  42.2 us (7%)
  between operations  17.9 us (3%)
    pallas_call x2, Pallas kernels, attend_back(): pl.pallas_call(functools.partial(attend_back_kernel, group, base, len(aft...  99.7 us
    ppermute x39, waiting for transfers between devices, flipped(): return lax.ppermute(block, axis, route)  63.1 us
    pallas_call x1, Pallas kernels, attend(): pl.pallas_call(functools.partial(attend_kernel, group, len(after)), grid_...  54 us
    pallas_call x1, Pallas kernels, mix(): pl.pallas_call(functools.partial(mix_kernel, counts), grid_spec=pltpu.Pre...  52.6 us
    ppermute x39, starting transfers between devices, flipped(): return lax.ppermute(block, axis, route)  42.1 us
    pallas_call x1, Pallas kernels, branch_back(): pl.pallas_call(functools.partial(branch_back_kernel, counts), grid_spec=p...  39.3 us
    pallas_call x1, Pallas kernels, hidden_back(): pl.pallas_call(functools.partial(hidden_back_kernel, counts, len(cots)),...  30.1 us
    unnamed x165, local copies, waits for them, and re-layouts  27.9 us
  transfers between devices with their start and end apart: 43, of which 14 were waited for; matrix products, arithmetic and copies ran while one was open for 12% of the time, Pallas kernels for 63%

profile of v6, /device:TPU:0, one launch (start us, length us, event | category | flops | bytes accessed | tf_op | source)
XLA Modules:
  0.0 618.0 jit_solution(6949455426082008437)
XLA Ops:
  8.1 3.0 collective-permute-start
  19.4 3.2 dynamic-slice_bitcast_fusion.2
  27.7 5.0 fusion.5
  34.6 23.9 %collective-permute-done.1.refs_3_.rest_1_ = bf16[1024,768]{1,0:T(8,128)(2,1)} collective-permute-done((bf16[1024,768]{1,0:T(8,128)(2,1)}, bf16[1024,768]{1,0:T(8,128)(2,1)}, u32[]{:S(2)}, u32[]{:S(2)}) %collective-permute-start.1) | collective-permute-done | bytes 1572896 | tf_op jit(solution)/shard_map/ppermute | solution.py:57
  64.3 14.3 %shard_map.171 = (bf16[2048,768]{1,0:T(8,128)(2,1)}, bf16[2048,768]{1,0:T(8,128)(2,1)}, bf16[2048,768]{1,0:T(8,128)(2,1)}, bf16[2048,768]{1,0:T(8,128)(2,1)}) custom-call(s32[6]{0:T(128)S(1)} %stack.107.table, f32[2048,128]{1,0:T(8,128)S(1)} %copy-done.16, f32[2048,128]{1,0:T(8,128)S(1)} %get-tuple-element.203.sin_ref.sq_ref.sk_ref, ...), custom_call_target="tpu_custom_call" | custom-call | flops 28991029248 | bytes 1048576 | tf_op jit(solution)/shard_map/pallas_call | solution.py:229
  86.1 54.0 %shard_map.173 = (bf16[2048,768]{1,0:T(8,128)(2,1)}, f32[12,1,2048]{2,1,0:T(1,128)}) custom-call(s32[16]{0:T(128)} %reshape.1313.spans, bf16[2048,768]{1,0:T(8,128)(2,1)} %get-tuple-element.103.q_ref, bf16[2048,768]{1,0:T(8,128)(2,1)} %get-tuple-element.104.k_ref, bf16[2048,768]{1,0:T(8,128)(2,1)} %get-tuple-element.105.v_ref, ...), custom_call_target="tpu_custom_call" | custom-call | flops 51539607552 | bytes 1048576 | tf_op jit(solution)/shard_map/pallas_call | solution.py:401
  148.9 52.6 %shard_map.175 = (bf16[2048,768]{1,0:T(8,128)(2,1)}, f32[2048,128]{1,0:T(8,128)}, bf16[2048,3072]{1,0:T(8,128)(2,1)}, bf16[2048,3072]{1,0:T(8,128)(2,1)}, bf16[2...) custom-call(s32[18]{0:T(128)} %stack.115.table, ...), custom_call_target="tpu_custom_call" | custom-call | flops 125627793408 | bytes 1048576 | tf_op jit(solution)/shard_map/pallas_call | solution.py:675
  209.7 3.0 collective-permute-start.11
  215.1 4.6 collective-permute-done.12
  224.5 3.7 constant_dynamic-slice_fusion
  234.6 30.1 %shard_map.177 = (bf16[2048,768]{1,0:T(8,128)(2,1)}, bf16[2048,6144]{1,0:T(8,128)(2,1)}, f32[8,768]{1,0:T(8,128)}) custom-call(s32[8]{0:T(128)} %stack.114.table, bf16[1024,768]{1,0:T(8,128)(2,1)} %get-tuple-element.192.rest_0_, bf16[1024,768]{1,0:T(8,128)(2,1)} %get-tuple-element.114.rest_1_, bf16[2048,768]{1,0:T(8,128)(2,1)} %get-tuple-element.115.rest_2_, ...), custom_call_target="tpu_custom_call" | custom-call | flops 77309411328 | bytes 1048576 | tf_op jit(solution)/shard_map/pallas_call | solution.py:756
  266.6 24.9 %shard_map.178.old_ref = bf16[16,2,576,384]{3,2,1,0:T(8,128)(2,1)} custom-call(bf16[2048,768]{1,0:T(8,128)(2,1)S(1)} %copy-done.18, bf16[2048,6144]{1,0:T(8,128)(2,1)} %get-tuple-element.122.grad_ref.refs_4_), custom_call_target="tpu_custom_call" | custom-call | flops 77309411328 | bytes 1048576 | tf_op jit(solution)/shard_map/pallas_call | solution.py:1013
  291.6 14.5 %shard_map.179.refs_14_ = bf16[16,2,576,384]{3,2,1,0:T(8,128)(2,1)} custom-call(bf16[2048,3072]{1,0:T(8,128)(2,1)} %get-tuple-element.123.hidden_ref, bf16[2048,768]{1,0:T(8,128)(2,1)S(1)} %copy-done.17, bf16[16,2,576,384]{3,2,1,0:T(8,128)(2,1)} %shard_map.178.old_ref), custom_call_target="tpu_custom_call", output_to_operand_aliasing={{}: (2, {})} | custom-call | flops 38654705664 | bytes 1048576 | tf_op jit(solution)/shard_map/pallas_call | solution.py:1025
  306.2 39.3 %shard_map.180 = (bf16[2048,768]{1,0:T(8,128)(2,1)}, bf16[2048,768]{1,0:T(8,128)(2,1)}, bf16[2048,128]{1,0:T(8,128)(2,1)}, f32[8,768]{1,0:T(8,128)}) custom-call(s32[12]{0:T(128)} %stack.110.table, bf16[2048,768]{1,0:T(8,128)(2,1)} %get-tuple-element.120.dffn_ref.refs_0_, bf16[2048,768]{1,0:T(8,128)(2,1)} %get-tuple-element.121.low_ref.refs_1_, ...), custom_call_target="tpu_custom_call" | custom-call | flops 86973087744 | bytes 1048576 | tf_op jit(solution)/shard_map/pallas_call | solution.py:837
  348.5 6.8 %shard_map.182 = bf16[768,896]{1,0:T(8,128)(2,1)} custom-call(bf16[2048,768]{1,0:T(8,128)(2,1)} %get-tuple-element.108.att_ref.refs_5_.refs_0_, bf16[2048,768]{1,0:T(8,128)(2,1)} %get-tuple-element.125.refs_1_.dbr_ref, bf16[768,128]{1,0:T(8,128)(2,1)} %pad.24.refs_2_), custom_call_target="tpu_custom_call" | custom-call | flops 11274289152 | bytes 1048576 | tf_op jit(solution)/shard_map/pallas_call | solution.py:1071
  357.4 50.1 %shard_map.183 = (bf16[2048,384]{1,0:T(8,128)(2,1)}, bf16[2048,384]{1,0:T(8,128)(2,1)}, bf16[2048,384]{1,0:T(8,128)(2,1)}) custom-call(s32[16]{0:T(128)} %reshape.1322.spans, bf16[2048,768]{1,0:T(8,128)(2,1)} %get-tuple-element.103.q_ref, bf16[2048,768]{1,0:T(8,128)(2,1)} %get-tuple-element.128.do_ref, bf16[2048,768]{1,0:T(8,128)(2,1)} %get-tuple-element.104.k_ref, ...), custom_call_target="tpu_custom_call" | custom-call | flops 51539607552 | bytes 1048576 | tf_op jit(solution)/shard_map/pallas_call | solution.py:526
  411.0 2.5 collective-permute-start.16
  413.5 9.6 %shard_map.185.refs_0_ = bf16[768,1152]{1,0:T(8,128)(2,1)} custom-call(bf16[2048,768]{1,0:T(8,128)(2,1)} %get-tuple-element.109.x_ref.refs_0_, bf16[2048,384]{1,0:T(8,128)(2,1)} %get-tuple-element.134.refs_1_.rest_0_, bf16[2048,384]{1,0:T(8,128)(2,1)} %get-tuple-element.135.refs_2_.rest_1_, bf16[2048,384]{1,0:T(8,128)(2,1)} %get-tuple-element.136.refs_3_.rest_2_, ...), custom_call_target="tpu_custom_call" | custom-call | flops 14495514624 | bytes 1048576 | tf_op jit(solution)/shard_map/pallas_call | solution.py:1071
  428.8 49.6 %shard_map.187 = (bf16[2048,384]{1,0:T(8,128)(2,1)}, bf16[2048,384]{1,0:T(8,128)(2,1)}, bf16[2048,384]{1,0:T(8,128)(2,1)}) custom-call(s32[16]{0:T(128)} %reshape.1322.spans, bf16[2048,768]{1,0:T(8,128)(2,1)} %get-tuple-element.103.q_ref, bf16[2048,768]{1,0:T(8,128)(2,1)} %get-tuple-element.128.do_ref, bf16[2048,768]{1,0:T(8,128)(2,1)} %get-tuple-element.104.k_ref, ...), custom_call_target="tpu_custom_call" | custom-call | flops 51539607552 | bytes 1048576 | tf_op jit(solution)/shard_map/pallas_call | solution.py:526
  483.0 9.9 %shard_map.190.refs_0_ = bf16[768,1152]{1,0:T(8,128)(2,1)} custom-call(bf16[2048,768]{1,0:T(8,128)(2,1)} %get-tuple-element.109.x_ref.refs_0_, bf16[2048,384]{1,0:T(8,128)(2,1)} %get-tuple-element.146.refs_1_.rest_3_, bf16[2048,384]{1,0:T(8,128)(2,1)} %get-tuple-element.147.refs_2_.rest_4_, bf16[2048,384]{1,0:T(8,128)(2,1)} %get-tuple-element.148.refs_3_.rest_5_, ...), custom_call_target="tpu_custom_call" | custom-call | flops 14495514624 | bytes 1048576 | tf_op jit(solution)/shard_map/pallas_call | solution.py:1071
  500.8 8.8 %shard_map.192.refs_0_ = bf16[1024,768]{1,0:T(8,128)(2,1)S(1)} custom-call(s32[6]{0:T(128)S(1)} %stack.126.table, bf16[2048,768]{1,0:T(8,128)(2,1)} %get-tuple-element.125.refs_1_.dbr_ref, bf16[2048,384]{1,0:T(8,128)(2,1)S(1)} %copy-done.7, bf16[2048,384]{1,0:T(8,128)(2,1)S(1)} %copy-done.8, bf16[2048,384]{1,0:T(8,128)(2,1)} %get-tuple-element.136.refs_3_.rest_2_, ...), custom_call_target="tpu_custom_call" | custom-call | flops 14495514624 | bytes 1048576 | tf_op jit(solution)/shard_map/pallas_call | solution.py:266
  512.2 2.9 collective-permute-start.24
  521.1 10.0 %shard_map.194.refs_0_ = f32[2048,768]{1,0:T(8,128)} custom-call(s32[6]{0:T(128)S(1)} %stack.128.table, bf16[2048,768]{1,0:T(8,128)(2,1)} %get-tuple-element.125.refs_1_.dbr_ref, bf16[2048,384]{1,0:T(8,128)(2,1)S(1)} %copy-done.7, bf16[2048,384]{1,0:T(8,128)(2,1)S(1)} %copy-done.8, bf16[2048,384]{1,0:T(8,128)(2,1)S(1)} %copy-done.9, ...), custom_call_target="tpu_custom_call" | custom-call | flops 14495514624 | bytes 1048576 | tf_op jit(solution)/shard_map/pallas_call | solution.py:266
  531.1 6.6 %collective-permute-done.25.refs_2_ = bf16[96,1152]{1,0:T(8,128)(2,1)S(1)} collective-permute-done((bf16[96,1152]{1,0:T(8,128)(2,1)S(1)}, bf16[96,1152]{1,0:T(8,128)(2,1)S(1)}, u32[]{:S(2)}, u32[]{:S(2)}) %collective-permute-start.25) | collective-permute-done | bytes 221216 | tf_op jit(solution)/shard_map/ppermute | solution.py:57
  543.2 2.9 collective-permute-start.27
  546.1 4.9 collective-permute-done.27.refs_0_
  551.0 4.4 collective-permute-done.28.refs_1_
  563.3 3.0 copy-done
  566.3 7.8 %shard_map.197 = (f32[384,6144]{1,0:T(8,128)}, f32[1536,768]{1,0:T(8,128)}) custom-call(bf16[16,576,384]{2,1,0:T(8,128)(2,1)S(1)} %bitcast.157), custom_call_target="tpu_custom_call" | custom-call | flops 1024 | bytes 1024 | tf_op jit(solution)/shard_map/pallas_call | solution.py:1123
  580.6 3.5 broadcast_select_fusion.refs_0_
  584.1 7.9 %collective-permute-done.35.refs_3_ = bf16[96,1152]{1,0:T(8,128)(2,1)S(1)} collective-permute-done((bf16[96,1152]{1,0:T(8,128)(2,1)S(1)}, bf16[96,1152]{1,0:T(8,128)(2,1)S(1)}, u32[]{:S(2)}, u32[]{:S(2)}) %collective-permute-start.35) | collective-permute-done | bytes 221216 | tf_op jit(solution)/shard_map/ppermute | solution.py:57
  597.6 3.9 shard_map.202.refs_0_
  (396 shorter events, 128.8 us)
Async XLA Ops:
  7.2 52.8 %all-gather.5.cloned.1.call-start = ((), (), s32[]{:S(2)}) async-start(), calls=%async_computation.1 | async-start | bytes 1880064 | tf_op jit(solution)/shard_map/all_gather | solution.py:101
  12.5 130.2 %collective-permute-start.5 = (bf16[2,384]{1,0:T(2,128)(2,1)S(1)}, bf16[2,384]{1,0:T(2,128)(2,1)S(1)}, u32[]{:S(2)}, u32[]{:S(2)}) collective-permute-start(bf16[2,384]{1,0:T(2,128)(2,1)S(1)} %pad_maximum_fusion.6), channel_id=1, source_target_pairs={{0,1},{1,0},{2,3},{3,2},{4,5},{5,4},{6,7},{7,6},{8,9},{9,8},{10,11... | collective-permute-start | bytes 4616 | tf_op jit(solution)/shard_map/ppermute | solution.py:57
  14.8 133.4 %all-gather.7.cloned.1.call-start = ((), (), s32[]{:S(2)}) async-start(), calls=%async_computation.2 | async-start | bytes 5013504 | tf_op jit(solution)/shard_map/all_gather | solution.py:101
  22.6 35.9 %collective-permute-start.1 = (bf16[1024,768]{1,0:T(8,128)(2,1)}, bf16[1024,768]{1,0:T(8,128)(2,1)}, u32[]{:S(2)}, u32[]{:S(2)}) collective-permute-start(bf16[1024,768]{1,0:T(8,128)(2,1)} %shard_map.169), channel_id=1, source_target_pairs={{0,1},{1,0},{2,3},{3,2},{4,5},{5,4},{6,7},{7,6},{8,9},{9,8},{10,11... | collective-permute-start | bytes 4718600 | tf_op jit(solution)/shard_map/ppermute | solution.py:57
  58.5 20.2 %collective-permute-start.2 = (bf16[24,6144]{1,0:T(8,128)(2,1)}, bf16[24,6144]{1,0:T(8,128)(2,1)S(1)}, u32[]{:S(2)}, u32[]{:S(2)}) collective-permute-start(bf16[24,6144]{1,0:T(8,128)(2,1)} %get-tuple-element.96.rest_4_), channel_id=1, source_target_pairs={{0,1},{1,0},{2,3},{3,2},{4,5},{5,4},{6,7},{7,6},{8,9},{9,8},{10,11... | collective-permute-start | bytes 884744 | tf_op jit(solution)/shard_map/ppermute | solution.py:57
  79.4 399.7 %reduce-scatter.2.cloned.1.call-start = ((), (), s32[]{:S(2)}) async-start(), calls=%async_computation.3 | async-start | bytes 14598144 | tf_op jit(solution)/shard_map/reduce_scatter | solution.py:1315
  84.0 56.1 %collective-permute-start.3 = (bf16[192,768]{1,0:T(8,128)(2,1)S(1)}, bf16[192,768]{1,0:T(8,128)(2,1)S(1)}, u32[]{:S(2)}, u32[]{:S(2)}) collective-permute-start(bf16[192,768]{1,0:T(8,128)(2,1)S(1)} %copy-done.13), channel_id=1, source_target_pairs={{0,1},{1,0},{2,3},{3,2},{4,5},{5,4},{6,7},{7,6},{8,9},{9,8},{10,11... | collective-permute-start | bytes 884744 | tf_op jit(solution)/shard_map/ppermute | solution.py:57
  84.7 55.5 %collective-permute-start.4 = (bf16[768,768]{1,0:T(8,128)(2,1)S(1)}, bf16[768,768]{1,0:T(8,128)(2,1)S(1)}, u32[]{:S(2)}, u32[]{:S(2)}) collective-permute-start(bf16[768,768]{1,0:T(8,128)(2,1)S(1)} %copy-done.2), channel_id=1, source_target_pairs={{0,1},{1,0},{2,3},{3,2},{4,5},{5,4},{6,7},{7,6},{8,9},{9,8},{10,11... | collective-permute-start | bytes 3538952 | tf_op jit(solution)/shard_map/ppermute | solution.py:57
  147.8 53.8 %collective-permute-start.8 = (bf16[1024,768]{1,0:T(8,128)(2,1)}, bf16[1024,768]{1,0:T(8,128)(2,1)S(1)}, u32[]{:S(2)}, u32[]{:S(2)}) collective-permute-start(bf16[1024,768]{1,0:T(8,128)(2,1)} %get-tuple-element.191.rest_8_), channel_id=1, source_target_pairs={{0,1},{1,0},{2,3},{3,2},{4,5},{5,4},{6,7},{7,6},{8,9},{9,8},{10,11... | collective-permute-start | bytes 4718600 | tf_op jit(solution)/shard_map/ppermute | solution.py:57
  219.8 11.9 %collective-permute-start.13 = (bf16[128,896]{1,0:T(8,128)(2,1)S(1)}, bf16[128,896]{1,0:T(8,128)(2,1)S(1)}, u32[]{:S(2)}, u32[]{:S(2)}) collective-permute-start(bf16[128,896]{1,0:T(8,128)(2,1)S(1)} %get-tuple-element.195), channel_id=1, source_target_pairs={{0,16},{2,18},{4,20},{6,22},{8,24},{10,26},{12,28},{14,30},{16,0},... | collective-permute-start | bytes 688136 | tf_op jit(solution)/shard_map/ppermute | solution.py:57
  228.2 120.4 %collective-permute-start.14 = (bf16[1024,768]{1,0:T(8,128)(2,1)}, bf16[1024,768]{1,0:T(8,128)(2,1)}, u32[]{:S(2)}, u32[]{:S(2)}) collective-permute-start(bf16[1024,768]{1,0:T(8,128)(2,1)} %get-tuple-element.190), channel_id=1, source_target_pairs={{0,1},{1,0},{2,3},{3,2},{4,5},{5,4},{6,7},{7,6},{8,9},{9,8},{10,11... | collective-permute-start | bytes 4718600 | tf_op jit(solution)/shard_map/ppermute | solution.py:57
  306.1 257.2 %all-gather.9.cloned.1.call-start = ((), (), s32[]{:S(2)}) async-start(), calls=%async_computation.4 | async-start | bytes 7520256 | tf_op jit(solution)/shard_map/all_gather | solution.py:1353
  356.6 50.9 %collective-permute-start.15 = (bf16[2,192,896]{2,1,0:T(8,128)(2,1)S(1)}, bf16[2,192,896]{2,1,0:T(8,128)(2,1)S(1)}, u32[]{:S(2)}, u32[]{:S(2)}) collective-permute-start(bf16[2,192,896]{2,1,0:T(8,128)(2,1)S(1)} %dynamic-slice_bitcast_fusion.6.rest_0_), channel_id=1, source_target_pairs={{0,2},{2,0},{4,6},{6,4},{8,10},{10,8},{12,14},{14,12},{16,18},{18,... | collective-permute-start | bytes 2064392 | tf_op jit(solution)/shard_map/ppermute | solution.py:57
  411.0 12.1 %collective-permute-start.16 = (bf16[1,192,896]{2,1,0:T(8,128)(2,1)S(1)}, bf16[1,192,896]{2,1,0:T(8,128)(2,1)S(1)}, u32[]{:S(2)}, u32[]{:S(2)}) collective-permute-start(bf16[1,192,896]{2,1,0:T(8,128)(2,1)S(1)} %constant_dynamic-slice_fusion.3.refs_4_), channel_id=1, source_target_pairs={{0,1},{1,0},{2,3},{3,2},{4,5},{5,4},{6,7},{7,6},{8,9},{9,8},{10,11... | collective-permute-start | bytes 1032200 | tf_op jit(solution)/shard_map/ppermute | solution.py:57
  424.9 53.5 %collective-permute-start.17 = (bf16[96,896]{1,0:T(8,128)(2,1)S(1)}, bf16[96,896]{1,0:T(8,128)(2,1)S(1)}, u32[]{:S(2)}, u32[]{:S(2)}) collective-permute-start(bf16[96,896]{1,0:T(8,128)(2,1)S(1)} %dynamic-slice_bitcast_fusion.9.rest_0_), channel_id=1, source_target_pairs={{0,4},{2,6},{4,0},{6,2},{8,12},{10,14},{12,8},{14,10},{16,20},{18,... | collective-permute-start | bytes 516104 | tf_op jit(solution)/shard_map/ppermute | solution.py:57
  427.9 50.5 %collective-permute-start.18 = (bf16[2,192,1152]{2,1,0:T(8,128)(2,1)S(1)}, bf16[2,192,1152]{2,1,0:T(8,128)(2,1)}, u32[]{:S(2)}, u32[]{:S(2)}) collective-permute-start(bf16[2,192,1152]{2,1,0:T(8,128)(2,1)S(1)} %dynamic-slice_bitcast_fusion.5.rest_1_), channel_id=1, source_target_pairs={{0,2},{2,0},{4,6},{6,4},{8,10},{10,8},{12,14},{14,12},{16,18},{18,... | collective-permute-start | bytes 2654216 | tf_op jit(solution)/shard_map/ppermute | solution.py:57
  480.1 12.8 %collective-permute-start.19 = (bf16[48,896]{1,0:T(8,128)(2,1)S(1)}, bf16[48,896]{1,0:T(8,128)(2,1)S(1)}, u32[]{:S(2)}, u32[]{:S(2)}) collective-permute-start(bf16[48,896]{1,0:T(8,128)(2,1)S(1)} %dynamic-slice_bitcast_fusion.10.refs_4_), channel_id=1, source_target_pairs={{0,8},{2,10},{4,12},{6,14},{8,0},{10,2},{12,4},{14,6},{16,24},{18,... | collective-permute-start | bytes 258056 | tf_op jit(solution)/shard_map/ppermute | solution.py:57
  482.2 12.3 %collective-permute-start.20 = (bf16[1,192,1152]{2,1,0:T(8,128)(2,1)S(1)}, bf16[1,192,1152]{2,1,0:T(8,128)(2,1)S(1)}, u32[]{:S(2)}, u32[]{:S(2)}) collective-permute-start(bf16[1,192,1152]{2,1,0:T(8,128)(2,1)S(1)} %constant_dynamic-slice_fusion.2.refs_5_), channel_id=1, source_target_pairs={{0,1},{1,0},{2,3},{3,2},{4,5},{5,4},{6,7},{7,6},{8,9},{9,8},{10,11... | collective-permute-start | bytes 1327112 | tf_op jit(solution)/shard_map/ppermute | solution.py:57
  496.2 14.5 %collective-permute-start.21 = (bf16[24,896]{1,0:T(8,128)(2,1)S(1)}, bf16[24,896]{1,0:T(8,128)(2,1)S(1)}, u32[]{:S(2)}, u32[]{:S(2)}) collective-permute-start(bf16[24,896]{1,0:T(8,128)(2,1)S(1)} %dynamic-slice_bitcast_fusion.11.rest_8_), channel_id=1, source_target_pairs={{0,16},{2,18},{4,20},{6,22},{8,24},{10,26},{12,28},{14,30},{16,0},... | collective-permute-start | bytes 129032 | tf_op jit(solution)/shard_map/ppermute | solution.py:57
  497.7 13.0 %collective-permute-start.22 = (bf16[96,1152]{1,0:T(8,128)(2,1)S(1)}, bf16[96,1152]{1,0:T(8,128)(2,1)S(1)}, u32[]{:S(2)}, u32[]{:S(2)}) collective-permute-start(bf16[96,1152]{1,0:T(8,128)(2,1)S(1)} %dynamic-slice_bitcast_fusion.8.rest_9_), channel_id=1, source_target_pairs={{0,4},{2,6},{4,0},{6,2},{8,12},{10,14},{12,8},{14,10},{16,20},{18,... | collective-permute-start | bytes 663560 | tf_op jit(solution)/shard_map/ppermute | solution.py:57
  512.2 18.9 %collective-permute-start.24 = (bf16[24,896]{1,0:T(8,128)(2,1)S(1)}, bf16[24,896]{1,0:T(8,128)(2,1)S(1)}, u32[]{:S(2)}, u32[]{:S(2)}) collective-permute-start(bf16[24,896]{1,0:T(8,128)(2,1)S(1)} %fusion.17.rest_8_), channel_id=1, source_target_pairs={{0,16},{2,18},{4,20},{6,22},{8,24},{10,26},{12,28},{14,30},{16,0},... | collective-permute-start | bytes 129032 | tf_op jit(solution)/shard_map/ppermute | solution.py:57
  516.3 21.4 %collective-permute-start.25 = (bf16[96,1152]{1,0:T(8,128)(2,1)S(1)}, bf16[96,1152]{1,0:T(8,128)(2,1)S(1)}, u32[]{:S(2)}, u32[]{:S(2)}) collective-permute-start(bf16[96,1152]{1,0:T(8,128)(2,1)S(1)} %fusion.9.rest_9_), channel_id=1, source_target_pairs={{0,8},{2,10},{4,12},{6,14},{8,0},{10,2},{12,4},{14,6},{16,24},{18,... | collective-permute-start | bytes 663560 | tf_op jit(solution)/shard_map/ppermute | solution.py:57
  519.7 18.7 %collective-permute-start.26 = (bf16[1,192,1152]{2,1,0:T(8,128)(2,1)S(1)}, bf16[1,192,1152]{2,1,0:T(8,128)(2,1)}, u32[]{:S(2)}, u32[]{:S(2)}) collective-permute-start(bf16[1,192,1152]{2,1,0:T(8,128)(2,1)S(1)} %constant_dynamic-slice_fusion.1.rest_10_), channel_id=1, source_target_pairs={{0,1},{1,0},{2,3},{3,2},{4,5},{5,4},{6,7},{7,6},{8,9},{9,8},{10,11... | collective-permute-start | bytes 1327112 | tf_op jit(solution)/shard_map/ppermute | solution.py:57
  540.1 15.4 %collective-permute-start.28 = (bf16[96,1152]{1,0:T(8,128)(2,1)}, bf16[96,1152]{1,0:T(8,128)(2,1)}, u32[]{:S(2)}, u32[]{:S(2)}) collective-permute-start(bf16[96,1152]{1,0:T(8,128)(2,1)} %add_convert_fusion.6), channel_id=1, source_target_pairs={{0,16},{2,18},{4,20},{6,22},{8,24},{10,26},{12,28},{14,30},{16,0},... | collective-permute-start | bytes 663560 | tf_op jit(solution)/shard_map/ppermute | solution.py:57
  541.4 14.1 %collective-permute-start.29 = (bf16[96,1152]{1,0:T(8,128)(2,1)S(1)}, bf16[96,1152]{1,0:T(8,128)(2,1)S(1)}, u32[]{:S(2)}, u32[]{:S(2)}) collective-permute-start(bf16[96,1152]{1,0:T(8,128)(2,1)S(1)} %dynamic-slice_bitcast_fusion.7), channel_id=1, source_target_pairs={{0,4},{2,6},{4,0},{6,2},{8,12},{10,14},{12,8},{14,10},{16,20},{18,... | collective-permute-start | bytes 663560 | tf_op jit(solution)/shard_map/ppermute | solution.py:57
  557.3 16.9 %collective-permute-start.31 = (bf16[96,1152]{1,0:T(8,128)(2,1)S(1)}, bf16[96,1152]{1,0:T(8,128)(2,1)S(1)}, u32[]{:S(2)}, u32[]{:S(2)}) collective-permute-start(bf16[96,1152]{1,0:T(8,128)(2,1)S(1)} %add_convert_fusion.5), channel_id=1, source_target_pairs={{0,4},{2,6},{4,0},{6,2},{8,12},{10,14},{12,8},{14,10},{16,20},{18,... | collective-permute-start | bytes 663560 | tf_op jit(solution)/shard_map/ppermute | solution.py:57
  559.6 14.5 %collective-permute-start.32 = (bf16[96,1152]{1,0:T(8,128)(2,1)S(1)}, bf16[96,1152]{1,0:T(8,128)(2,1)S(1)}, u32[]{:S(2)}, u32[]{:S(2)}) collective-permute-start(bf16[96,1152]{1,0:T(8,128)(2,1)S(1)} %fusion.8), channel_id=1, source_target_pairs={{0,8},{2,10},{4,12},{6,14},{8,0},{10,2},{12,4},{14,6},{16,24},{18,... | collective-permute-start | bytes 663560 | tf_op jit(solution)/shard_map/ppermute | solution.py:57
  560.9 13.2 %collective-permute-start.30 = (bf16[96,896]{1,0:T(8,128)(2,1)S(1)}, bf16[96,896]{1,0:T(8,128)(2,1)S(1)}, u32[]{:S(2)}, u32[]{:S(2)}) collective-permute-start(bf16[96,896]{1,0:T(8,128)(2,1)S(1)} %bitcast_select_fusion.3), channel_id=1, source_target_pairs={{0,4},{2,6},{4,0},{6,2},{8,12},{10,14},{12,8},{14,10},{16,20},{18,... | collective-permute-start | bytes 516104 | tf_op jit(solution)/shard_map/ppermute | solution.py:57
  561.7 35.9 %collective-permute-start.36 = (bf16[1024,768]{1,0:T(8,128)(2,1)S(1)}, bf16[1024,768]{1,0:T(8,128)(2,1)}, u32[]{:S(2)}, u32[]{:S(2)}) collective-permute-start(bf16[1024,768]{1,0:T(8,128)(2,1)S(1)} %copy-done.6), channel_id=1, source_target_pairs={{0,1},{1,0},{2,3},{3,2},{4,5},{5,4},{6,7},{7,6},{8,9},{9,8},{10,11... | collective-permute-start | bytes 4718600 | tf_op jit(solution)/shard_map/ppermute | solution.py:57
  576.1 15.9 %collective-permute-start.33 = (bf16[192,896]{1,0:T(8,128)(2,1)S(1)}, bf16[192,896]{1,0:T(8,128)(2,1)S(1)}, u32[]{:S(2)}, u32[]{:S(2)}) collective-permute-start(bf16[192,896]{1,0:T(8,128)(2,1)S(1)} %bitcast_select_fusion.2.refs_0_), channel_id=1, source_target_pairs={{0,2},{2,0},{4,6},{6,4},{8,10},{10,8},{12,14},{14,12},{16,18},{18,... | collective-permute-start | bytes 1032200 | tf_op jit(solution)/shard_map/ppermute | solution.py:57
  577.3 15.4 %collective-permute-start.34 = (bf16[192,1152]{1,0:T(8,128)(2,1)S(1)}, bf16[192,1152]{1,0:T(8,128)(2,1)S(1)}, u32[]{:S(2)}, u32[]{:S(2)}) collective-permute-start(bf16[192,1152]{1,0:T(8,128)(2,1)S(1)} %bitcast_select_fusion.1.refs_0_), channel_id=1, source_target_pairs={{0,2},{2,0},{4,6},{6,4},{8,10},{10,8},{12,14},{14,12},{16,18},{18,... | collective-permute-start | bytes 1327112 | tf_op jit(solution)/shard_map/ppermute | solution.py:57
  578.9 13.1 %collective-permute-start.35 = (bf16[96,1152]{1,0:T(8,128)(2,1)S(1)}, bf16[96,1152]{1,0:T(8,128)(2,1)S(1)}, u32[]{:S(2)}, u32[]{:S(2)}) collective-permute-start(bf16[96,1152]{1,0:T(8,128)(2,1)S(1)} %add_convert_fusion.4), channel_id=1, source_target_pairs={{0,16},{2,18},{4,20},{6,22},{8,24},{10,26},{12,28},{14,30},{16,0},... | collective-permute-start | bytes 663560 | tf_op jit(solution)/shard_map/ppermute | solution.py:57
  (91 other events, 757.5 us)
Sparse Core Ops, SparseCore 0:
  14.9 41.8 all-gather.4
  79.5 53.5 all-gather.6
  306.2 161.1 reduce-scatter.1
  479.3 70.2 all-gather.8
